TPU v7x, 128 devices: a whole 4x4x4 slice. The times are simulated.
128 devices in a mesh: region: 4 (over z), member: 32 (over x, y, core).
Axes of the slice: x: 4, y: 4, z: 4, core: 2. Of those that a mesh axis runs over, the one named last changes fastest.
Arguments:
- source: float32 [128, 1024, 128], P('region', 'member'), may hold values from -6 to 6
- inverse_density: float32 [3, 128, 1024, 128], P(None, 'region', 'member'), may hold values from 0.1 to 10
- block_level: int32 [512], P(('region', 'member')), may hold values from 0 to 2, as said below
- level_sweeps: int32 [3], replicated, may hold values from 1 to 6, as said below
- new_owner: int32 [512], replicated, may hold values from 0 to 127, as said below
Outputs:
- moved_pressure: float32 [768, 32768], P(('region', 'member'))
- moved_residual: float32 [768, 32768], P(('region', 'member'))
Inputs may be any that keep to these rules, and one draw needn't show every extreme that they name: `block_level`: the blocks of one run of 64 consecutive blocks all have level 2. `level_sweeps`: Nondecreasing; level 0 takes one sweep and level 2 takes 6. `new_owner`: nondecreasing in b; block b goes to device b // 4 - 1, b // 4 or b // 4 + 1; block 3 goes to device 1; every device receives at most 6 blocks and some device exactly 6.
All inputs are finite; a program needn't handle non-finite values.
Results may differ from a plain program's by a relative error of at most 0.00018.
Values sent between devices are 32-bit elements; how exact they have to be, the bound alone decides.
No kernel may reach another device: no remote copies, remote signals or barrier semaphores. Data moves between devices by JAX's collectives and lax.ppermute only.
A program may use at most 128 MiB of HBM per device.

v0:
```python
import functools

import jax
import jax.numpy as jnp
from jax import lax
from jax.experimental import pallas as pl
from jax.experimental.pallas import tpu as pltpu
from jax.sharding import PartitionSpec as P


BS = 32
BLK = 4
CSWEEPS = 8
CYCLES = 2
CAP = 6
SWEEP_MAX = 6
RELAX = 0.8
KEEP = 0.2
PART = 1.0 / 64.0
LANES = 128
ROWS = BS * BS
XC = BS // 4
CROWS = XC * XC
UNROLL = 2
ZERO = functools.partial(jnp.zeros, (BS, LANES), jnp.float32)
F32 = jnp.float32


def vmem(*shape):
    return pltpu.VMEM(shape, F32)


def call(body, out_rows, args, scalars=(), scratch=(), aliases=None, flops=2e6, mib=48):
    outs = [jax.ShapeDtypeStruct(s, F32) for s in out_rows]
    moved = sum(a.size * 4 for a in args) + sum(o.size * 4 for o in outs)
    return pl.pallas_call(
        body,
        out_shape=outs,
        in_specs=[pl.BlockSpec(memory_space=pltpu.SMEM)] * len(scalars)
        + [pl.BlockSpec(memory_space=pltpu.VMEM)] * len(args),
        out_specs=[pl.BlockSpec(memory_space=pltpu.VMEM)] * len(outs),
        scratch_shapes=list(scratch),
        input_output_aliases={len(scalars) + k: v for k, v in (aliases or {}).items()},
        compiler_params=pltpu.CompilerParams(vmem_limit_bytes=mib << 20),
        cost_estimate=pl.CostEstimate(flops=int(flops), bytes_accessed=int(moved), transcendentals=0),
    )(*scalars, *args)


class Place:
    def __init__(self):
        region, member = lax.axis_index("region"), lax.axis_index("member")
        self.device = region * lax.axis_size("member") + member
        self.even = (member % 2 == 0, region % 2 == 0)
        self.low = (member > 0, region > 0)
        self.high = (member < lax.axis_size("member") - 1, region < lax.axis_size("region") - 1)


def lane_ids(rows):
    return lax.broadcasted_iota(jnp.int32, (rows, LANES), 1)


def row_ids(rows):
    return lax.broadcasted_iota(jnp.int32, (rows, LANES), 0)


def next_y(v):
    return jnp.concatenate([v[8:32], pltpu.roll(v[0:8], 7, 0)], axis=0)


def prev_y(v):
    return jnp.concatenate([pltpu.roll(v[24:32], 1, 0), v[0:24]], axis=0)


def next_z(v):
    return pltpu.roll(v, LANES - 1, 1)


def prev_z(v):
    return pltpu.roll(v, 1, 1)


def fold(v):
    return v[0:8] + v[8:16] + v[16:24] + v[24:32]


def tiled(v):
    return jnp.concatenate([v, v, v, v], axis=0)


def plane(x):
    return pl.ds(pl.multiple_of(x * BS, BS), BS)


def pick(flag, yes, no):
    return jnp.where(jnp.full(yes.shape, flag.astype(jnp.int32), jnp.int32) == 1, yes, no)


def low_high(place, axis, first, second):
    low = pick(place.even[axis], second, first) * place.low[axis].astype(F32)
    high = pick(place.even[axis], first, second) * place.high[axis].astype(F32)
    return low, high


def group_matrix():
    return jnp.where(
        row_ids(LANES) // 4 == lane_ids(LANES) // 4, jnp.float32(1.0), jnp.float32(0.0)
    )


def group_sum(v, ones):
    return lax.dot_general(
        v, ones, (((1,), (0,)), ((), ())), precision=lax.Precision.HIGHEST, preferred_element_type=F32
    )


def by_fours(ref, base):
    total = ref[pl.ds(base, 8, stride=4), :]
    for j in range(1, 4):
        total = total + ref[pl.ds(base + j, 8, stride=4), :]
    return total


def weights_kernel(new_owner, src, inv, owned, src_t, f0, fy, fz, fzs, c0, fx, fyf, czu, czd):
    row, lane = row_ids(BS), lane_ids(BS)

    def load(ref, x, offset):
        return jnp.concatenate(
            [ref[pl.ds(offset + x * BS + k, 8, stride=4), :] for k in range(4)], axis=0
        )

    def body(xc, carry):
        before, here = carry
        total_up = jnp.zeros((8, LANES), F32)
        total_down = jnp.zeros((8, LANES), F32)
        for j in range(4):
            x = xc * 4 + j
            src_t[plane(x), :] = load(src, x, 0)
            inside = (x < BS - 1).astype(F32)
            after = load(inv, jnp.minimum(x + 1, BS - 1), 0) * inside
            one = load(inv, x, ROWS)
            two = load(inv, x, 2 * ROWS)
            one_n = jnp.where(row == BS - 1, 0.0, next_y(one))
            one_p = jnp.where(row == 0, 0.0, prev_y(one))
            two_n = jnp.where(lane == LANES - 1, 0.0, next_z(two))
            two_p = jnp.where(lane == 0, 0.0, prev_z(two))
            up0 = 0.5 * (here + after)
            upy = 0.5 * (one + one_n)
            upz = 0.5 * (two + two_n)
            downz = 0.5 * (two + two_p)
            f0[plane(x), :] = up0 * inside
            fy[plane(x), :] = jnp.where(row == BS - 1, 0.0, upy)
            fz[plane(x), :] = jnp.where(lane == LANES - 1, 0.0, upz)
            fzs[plane(x), :] = jnp.where(lane % BS == BS - 1, 0.0, upz)
            c0[plane(x), :] = up0 + upy + upz + 0.5 * (here + before) + 0.5 * (one + one_p) + downz
            total_up = total_up + fold(upz)
            total_down = total_down + fold(downz)
            before, here = here, after
        at = pl.ds(pl.multiple_of(xc * 8, 8), 8)
        czu[at, :] = total_up
        czd[at, :] = total_down
        return before, here

    lax.fori_loop(0, XC, body, (ZERO(), load(inv, 0, 0)))
    fx[0:BS, :] = load(inv, 0, 0)
    fx[BS : 2 * BS, :] = load(inv, BS - 1, 0)
    for g in range(4):
        fyf[8 * g : 8 * g + 8, :] = inv[pl.ds(ROWS + 256 * g, 8, stride=BS), :]
        fyf[BS + 8 * g : BS + 8 * g + 8, :] = inv[pl.ds(ROWS + 256 * g + 31, 8, stride=BS), :]
    device = Place().device
    owner = new_owner[...]
    block = lax.broadcasted_iota(jnp.int32, owner.shape, 0) * owner.shape[1]
    block = block + lax.broadcasted_iota(jnp.int32, owner.shape, 1)
    home, place = block // BLK, block % BLK
    leaving = jnp.where(owner > home, BLK - place, jnp.where(owner < home, place + 1, 0))
    owned[0] = jnp.sum((owner < device).astype(F32)).astype(jnp.int32)
    owned[1] = jnp.sum((owner == device).astype(F32)).astype(jnp.int32)
    owned[2] = jnp.max(leaving.astype(F32)).astype(jnp.int32)


def add_faces_y(ref, low, high):
    for g in range(4):
        at = pl.ds(256 * g, 8, stride=BS)
        ref[at, :] = ref[at, :] + low[8 * g : 8 * g + 8]
        at = pl.ds(256 * g + 31, 8, stride=BS)
        ref[at, :] = ref[at, :] + high[8 * g : 8 * g + 8]


def add_faces_x(ref, low, high):
    ref[0:BS, :] = ref[0:BS, :] + low
    ref[ROWS - BS : ROWS, :] = ref[ROWS - BS : ROWS, :] + high


def send_faces(place, p, sa, sb, sc, sd):
    even = place.even[0]
    for g in range(4):
        low = p[pl.ds(256 * g, 8, stride=BS), :]
        high = p[pl.ds(256 * g + 31, 8, stride=BS), :]
        sa[8 * g : 8 * g + 8, :] = pick(even, high, low)
        sb[8 * g : 8 * g + 8, :] = pick(even, low, high)
    low = p[0:BS, :]
    high = p[ROWS - BS : ROWS, :]
    sc[...] = pick(place.even[1], high, low)
    sd[...] = pick(place.even[1], low, high)


def sweep_limits(levels, level_sweeps):
    block = lane_ids(BS) // BS
    limit = jnp.zeros((BS, LANES), jnp.int32)
    for b in range(BLK):
        limit = jnp.where(block == b, level_sweeps[levels[b]], limit)
    return limit


def relax(limit, r, e, f0, fy, fzs, d, finish):
    def sweep(i, load, store):
        active = limit > i

        def body(x, carry):
            t0, here = carry
            at = plane(x)
            after = load(plane(jnp.minimum(x + 1, BS - 1)))
            w0, wy, wz = f0[at, :], fy[at, :], fzs[at, :]
            t1 = w0 * here
            total = r[at, :] + t0 + w0 * after
            total = total + wy * next_y(here) + prev_y(wy * here)
            total = total + wz * next_z(here) + prev_z(wz * here)
            store(at, jnp.where(active, KEEP * here + d[at, :] * total, here))
            return t1, after

        lax.fori_loop(0, BS, body, (ZERO(), load(plane(0))), unroll=UNROLL)

    def first(at):
        return d[at, :] * r[at, :]

    def held(at):
        return e[at, :]

    def keep(at, value):
        e[at, :] = value

    def middle(i, _):
        sweep(i, held, keep)
        return 0

    sweep(1, first, keep)
    lax.fori_loop(2, SWEEP_MAX - 1, middle, 0)
    sweep(SWEEP_MAX - 1, held, finish)


def first_kernel(
    levels, level_sweeps, src, f0, fy, fzs, c0, fx, fyf, ra, rb, rc, rd,
    c, d, gx, gy, p, sa, sb, sc, sd, e,
):
    def natural(ref):
        return jnp.concatenate([ref[pl.ds(k, 8, stride=4), :] for k in range(4)], axis=0)

    place = Place()
    xlo, xhi = low_high(place, 1, natural(rc), natural(rd))
    ylo, yhi = low_high(place, 0, ra[...], rb[...])
    gx[0:BS, :] = 0.5 * (fx[0:BS, :] + xlo)
    gx[BS : 2 * BS, :] = 0.5 * (fx[BS : 2 * BS, :] + xhi)
    gy[0:BS, :] = 0.5 * (fyf[0:BS, :] + ylo)
    gy[BS : 2 * BS, :] = 0.5 * (fyf[BS : 2 * BS, :] + yhi)
    add_faces_x(c, 0.5 * xlo, 0.5 * xhi)
    add_faces_y(c, 0.5 * ylo, 0.5 * yhi)

    def begin(x, _):
        at = plane(x)
        d[at, :] = RELAX / c[at, :]
        return 0

    lax.fori_loop(0, BS, begin, 0, unroll=UNROLL)

    def finish(at, value):
        p[at, :] = value

    relax(sweep_limits(levels, level_sweeps), src, e, f0, fy, fzs, d, finish)
    send_faces(place, p, sa, sb, sc, sd)


def residual_plane(src, c, f0, fy, fz, at, t0, here, after):
    w0, wy, wz = f0[at, :], fy[at, :], fz[at, :]
    total = src[at, :] - c[at, :] * here + t0 + w0 * after
    total = total + wy * next_y(here) + prev_y(wy * here)
    total = total + wz * next_z(here) + prev_z(wz * here)
    return total, w0 * here


def coarse_rhs_kernel(src, c, f0, fy, fz, p, q, scr):
    def body(xc, carry):
        t0, here = carry
        total = jnp.zeros((8, LANES), F32)
        for j in range(4):
            x = xc * 4 + j
            after = p[plane(jnp.minimum(x + 1, BS - 1)), :]
            r, t0 = residual_plane(src, c, f0, fy, fz, plane(x), t0, here, after)
            total = total + fold(r)
            here = after
        scr[pl.ds(pl.multiple_of(xc * 8, 8), 8), :] = total
        return t0, here

    lax.fori_loop(0, XC, body, (ZERO(), p[0:BS, :]))
    q[...] = group_sum(scr[...], group_matrix()) * PART


def coarse_weights_kernel(f0, fy, gx, gy, czu, czd, packed, scr, cy):
    ones = group_matrix()
    lane = lane_ids(CROWS)
    row = row_ids(CROWS)
    for xc in range(XC):
        scr[8 * xc : 8 * xc + 8, :] = fold(f0[(4 * xc + 3) * BS : (4 * xc + 4) * BS, :])
        total = fy[4 * xc * BS + 24 : 4 * xc * BS + 32, :]
        for j in range(1, 4):
            at = (4 * xc + j) * BS
            total = total + fy[at + 24 : at + 32, :]
        cy[8 * xc : 8 * xc + 8, :] = total
    c0 = group_sum(scr[...], ones) * PART
    cy[pl.ds(7, 8, stride=8), :] = by_fours(gy, BS)
    up_y = group_sum(cy[...], ones) * PART
    gxlo = group_sum(fold(gx[0:BS, :]), ones) * PART
    gxhi = group_sum(fold(gx[BS : 2 * BS, :]), ones) * PART
    up_z = group_sum(jnp.where(lane % 4 == 3, czu[...], 0.0), ones) * PART
    down_z = group_sum(jnp.where(lane % 4 == 0, czd[...], 0.0), ones) * PART
    up_0 = jnp.concatenate([c0[0 : CROWS - 8], gxhi], axis=0)
    down_0 = jnp.concatenate([gxlo, c0[0 : CROWS - 8]], axis=0)
    cy[...] = jnp.concatenate(
        [pltpu.roll(up_y[8 * xc : 8 * xc + 8], 1, 0) for xc in range(XC)], axis=0
    )
    cy[pl.ds(0, 8, stride=8), :] = group_sum(by_fours(gy, 0), ones) * PART
    scale = RELAX / (up_0 + up_y + up_z + down_0 + cy[...] + down_z)
    couple_y = jnp.where(row % 8 == 7, up_y * Place().high[0].astype(F32), up_y)
    couple_z = jnp.where(lane >= LANES - 4, 0.0, up_z)
    slot = lane % 4
    packed[...] = jnp.where(
        slot == 0, c0, jnp.where(slot == 1, couple_y, jnp.where(slot == 2, couple_z, scale))
    )


def coarse_faces_kernel(qi, gx, gy, ra, rc, rd, sb, *rest):
    packed, (ma, mb, scr) = rest[:-3], rest[-3:]
    place = Place()
    xlo, xhi = low_high(place, 1, rc[...], rd[...])
    even = place.even[0]
    own = jnp.where(jnp.full(ra.shape, even.astype(jnp.int32)) == 1, gy[BS : 2 * BS, :], gy[0:BS, :])
    scr[...] = own * ra[...]
    faces = jnp.concatenate(
        [fold(gx[0:BS, :] * xlo), fold(gx[BS : 2 * BS, :] * xhi), by_fours(scr, 0)], axis=0
    )
    faces = group_sum(faces, group_matrix()) * PART
    ma[0:CROWS, :] = qi[...]
    ma[0:8, :] = ma[0:8, :] + faces[0:8]
    ma[CROWS - 8 : CROWS, :] = ma[CROWS - 8 : CROWS, :] + faces[8:16]
    nothing = jnp.zeros((8, LANES), F32)
    at = pl.ds(0, 8, stride=8)
    ma[at, :] = ma[at, :] + pick(even, nothing, faces[16:24])
    at = pl.ds(7, 8, stride=8)
    ma[at, :] = ma[at, :] + pick(even, faces[16:24], nothing)
    mb[0:CROWS, :] = ma[0:CROWS, :]
    mb[CROWS : CROWS + BS, :] = sb[...]
    for w in packed:
        ma[CROWS : 2 * CROWS, :] = w[...]
        mb[CROWS + BS : 2 * CROWS + BS, :] = w[...]


def joined(place, own, first, second):
    low, high = low_high(place, 0, first, second)
    parts = []
    for xc in range(XC):
        at = slice(8 * xc, 8 * xc + 8)
        parts += [low[at], own[at], high[at]]
    return jnp.concatenate(parts, axis=0)


def coarse_solve(place, ma, qa, qb, sb, gy, weights, c, cyb, sa, sc, sd, scr, two):
    even = place.even[0]
    w0, wy, wz, scale = weights
    scr[...] = joined(place, ma[0:CROWS, :], qa[0:CROWS, :], qb[0:CROWS, :])
    side = pick(even, gy[0:BS, :], gy[BS : 2 * BS, :])
    there = jnp.where(even, place.low[0].astype(F32), place.high[0].astype(F32))
    two[0:BS, :] = side * qb[CROWS : CROWS + BS, :] * there
    two[BS : 2 * BS, :] = side * sb[...]
    faces = jnp.concatenate([by_fours(two, 0), by_fours(two, BS)], axis=0)
    faces = group_sum(faces, group_matrix()) * PART
    mine, theirs = faces[0:8], faces[8:16]
    nothing = jnp.zeros((8, LANES), F32)
    for row, value in (
        (8, pick(even, mine, nothing)),
        (7, pick(even, theirs, nothing)),
        (15, pick(even, nothing, mine)),
        (16, pick(even, nothing, theirs)),
    ):
        at = pl.ds(row, 8, stride=24)
        scr[at, :] = scr[at, :] + value
    rhs = scr[...]

    def up_x(v):
        return jnp.concatenate([v[24:], v[:24]], axis=0)

    def down_x(v):
        return jnp.concatenate([v[-24:], v[:-24]], axis=0)

    def by_plane(v, shift):
        return jnp.concatenate(
            [pltpu.roll(v[24 * xc : 24 * xc + 24], shift, 0) for xc in range(XC)], axis=0
        )

    field = scale * rhs
    for _ in range(CSWEEPS - 1):
        total = rhs + w0 * up_x(field) + down_x(w0 * field)
        total = total + wy * by_plane(field, 23) + by_plane(wy * field, 1)
        total = total + wz * pltpu.roll(field, LANES - 4, 1) + pltpu.roll(wz * field, 4, 1)
        field = KEEP * field + scale * total
    scr[...] = field
    for xc in range(XC):
        c[8 * xc : 8 * xc + 8, :] = field[24 * xc + 8 : 24 * xc + 16]
    cyb[...] = pick(even, scr[pl.ds(7, 8, stride=24), :], scr[pl.ds(16, 8, stride=24), :])
    sa[...] = pick(even, scr[pl.ds(15, 8, stride=24), :], scr[pl.ds(8, 8, stride=24), :])
    low, high = field[8:16], field[24 * 7 + 8 : 24 * 7 + 16]
    sc[...] = pick(place.even[1], high, low)
    sd[...] = pick(place.even[1], low, high)


def first_coarse_kernel(ma, qa, qb, sb, gy, c, cyb, sa, sc, sd, wide, scr, two):
    place = Place()
    packed = joined(
        place, ma[CROWS : 2 * CROWS, :], qa[CROWS : 2 * CROWS, :], qb[CROWS + BS :, :]
    )
    ones = group_matrix()
    slot = lane_ids(3 * CROWS) % 4
    weights = [group_sum(jnp.where(slot == j, packed, 0.0), ones) for j in range(4)]
    for j in range(4):
        wide[3 * CROWS * j : 3 * CROWS * (j + 1), :] = weights[j]
    coarse_solve(place, ma, qa, qb, sb, gy, weights, c, cyb, sa, sc, sd, scr, two)


def later_coarse_kernel(ma, qa, qb, sb, gy, wide, c, cyb, sa, sc, sd, scr, two):
    weights = [wide[3 * CROWS * j : 3 * CROWS * (j + 1), :] for j in range(4)]
    coarse_solve(Place(), ma, qa, qb, sb, gy, weights, c, cyb, sa, sc, sd, scr, two)


def spread_rows(scr, value):
    for j in range(4):
        scr[pl.ds(j, 8, stride=4), :] = value
    return scr[...]


def correct_kernel(src, c, f0, fy, fz, p, gy, qb, cc, cyb, p2, r, scr):
    def body(xc, carry):
        t0, here = carry
        add = tiled(cc[pl.ds(pl.multiple_of(xc * 8, 8), 8), :])
        later = pl.ds(pl.multiple_of(jnp.minimum(xc + 1, XC - 1) * 8, 8), 8)
        add_next = tiled(cc[later, :])
        for j in range(4):
            x = xc * 4 + j
            at = plane(x)
            after = p[plane(jnp.minimum(x + 1, BS - 1)), :] + (add if j < 3 else add_next)
            p2[at, :] = here
            r[at, :], t0 = residual_plane(src, c, f0, fy, fz, at, t0, here, after)
            here = after
        return t0, here

    lax.fori_loop(0, XC, body, (ZERO(), p[0:BS, :] + tiled(cc[0:8, :])))
    halo = qb[CROWS : CROWS + BS, :] + spread_rows(scr, cyb[...])
    ylo, yhi = low_high(Place(), 0, ZERO(), halo)
    add_faces_y(r, gy[0:BS, :] * ylo, gy[BS : 2 * BS, :] * yhi)


def residual_kernel(src, c, f0, fy, fz, p, r):
    def body(x, carry):
        t0, here = carry
        at = plane(x)
        after = p[plane(jnp.minimum(x + 1, BS - 1)), :]
        r[at, :], t1 = residual_plane(src, c, f0, fy, fz, at, t0, here, after)
        return t1, after

    lax.fori_loop(0, BS, body, (ZERO(), p[0:BS, :]), unroll=UNROLL)


def add_all(place, gx, gy, ra, rb, rc, rd, ref):
    xlo, xhi = low_high(place, 1, rc, rd)
    add_faces_x(ref, gx[0:BS, :] * xlo, gx[BS : 2 * BS, :] * xhi)
    ylo, yhi = low_high(place, 0, ra, rb)
    add_faces_y(ref, gy[0:BS, :] * ylo, gy[BS : 2 * BS, :] * yhi)


def finish_smooth(place, limit, r, f0, fy, fzs, d, p, p_out, sends, e):
    def finish(at, value):
        p_out[at, :] = p[at, :] + value

    relax(limit, r, e, f0, fy, fzs, d, finish)
    send_faces(place, p_out, *sends)


def smooth_corrected_kernel(
    levels, level_sweeps, ri, f0, fy, fzs, d, p, gx, gy, ra, rc, rd, ka, kc, kd,
    r, p_out, sa, sb, sc, sd, e, scr,
):
    place = Place()
    near = ra[...] + spread_rows(scr, ka[...])
    add_all(place, gx, gy, near, ZERO(), rc[...] + tiled(kc[...]), rd[...] + tiled(kd[...]), r)
    limit = sweep_limits(levels, level_sweeps)
    finish_smooth(place, limit, r, f0, fy, fzs, d, p, p_out, (sa, sb, sc, sd), e)


def smooth_kernel(
    levels, level_sweeps, ri, f0, fy, fzs, d, p, gx, gy, ra, rb, rc, rd,
    r, p_out, sa, sb, sc, sd, e,
):
    place = Place()
    add_all(place, gx, gy, ra[...], rb[...], rc[...], rd[...], r)
    limit = sweep_limits(levels, level_sweeps)
    finish_smooth(place, limit, r, f0, fy, fzs, d, p, p_out, (sa, sb, sc, sd), e)


def plane_to_blocks(v, x, out):
    lane = lane_ids(8)
    half = lane < 64
    even = (lane // BS) % 2 == 0
    v = [v[8 * k : 8 * k + 8] for k in range(4)]
    u = [None] * 4
    for k in range(2):
        low, high = v[k], v[k + 2]
        u[k] = jnp.where(half, low, pltpu.roll(high, 64, 1))
        u[k + 2] = jnp.where(half, pltpu.roll(low, 64, 1), high)
    for b in (0, 2):
        low, high = u[b], u[b + 1]
        first = jnp.where(even, low, pltpu.roll(high, BS, 1))
        second = jnp.where(even, pltpu.roll(low, LANES - BS, 1), high)
        out[pl.ds(pl.multiple_of(b * 256 + x * 8, 8), 8), :] = first
        out[pl.ds(pl.multiple_of((b + 1) * 256 + x * 8, 8), 8), :] = second


def last_residual_kernel(src, c, f0, fy, fz, p, r, blocks):
    def body(x, carry):
        t0, here = carry
        at = plane(x)
        after = p[plane(jnp.minimum(x + 1, BS - 1)), :]
        r[at, :], t1 = residual_plane(src, c, f0, fy, fz, at, t0, here, after)
        plane_to_blocks(here, x, blocks)
        return t1, after

    lax.fori_loop(0, BS, body, (ZERO(), p[0:BS, :]), unroll=UNROLL)


def final_kernel(ri, gx, gy, ra, rb, rc, rd, pblocks, r, blocks, sa, sb, *, count):
    place = Place()
    even = place.even[0]
    add_all(place, gx, gy, ra[...], rb[...], rc[...], rd[...], r)

    def body(x, _):
        plane_to_blocks(r[plane(x), :], x, blocks)
        return 0

    lax.fori_loop(0, BS, body, 0, unroll=UNROLL)
    size, last = count * 256, (BLK - count) * 256

    def send(t, _):
        for n, ref in enumerate((pblocks, blocks)):
            at = pl.ds(pl.multiple_of(n * size + t * 32, 32), 32)
            low = ref[pl.ds(pl.multiple_of(t * 32, 32), 32), :]
            high = ref[pl.ds(pl.multiple_of(last + t * 32, 32), 32), :]
            sa[at, :] = pick(even, high, low)
            sb[at, :] = pick(even, low, high)
        return 0

    lax.fori_loop(0, size // 32, send, 0)


def place_kernel(owned, own_p, own_r, ra, rb, out_p, out_r, nothing, sems, *, count):
    place = Place()
    even = place.even[0]
    nothing[...] = jnp.zeros_like(nothing)
    start, held = owned[0], owned[1]

    def copy(ref, base, out, n, j):
        rows = ref.at[pl.ds(pl.multiple_of(base, 256), 256), :]
        pltpu.make_async_copy(rows, out.at[:, j, :], sems.at[n, j]).start()

    outs = ((0, own_p, out_p), (1, own_r, out_r))
    for j in range(CAP):
        where = start + j - place.device * BLK
        used = j < held
        mine = used & (where >= 0) & (where < BLK)
        low = used & (where < 0)
        high = used & (where >= BLK)
        own_base = jnp.clip(where, 0, BLK - 1) * 256
        base = jnp.where(
            low, jnp.clip(where + count, 0, count - 1), jnp.clip(where - BLK, 0, count - 1)
        ) * 256
        from_a = (low & jnp.logical_not(even)) | (high & even)
        from_b = (low & even) | (high & jnp.logical_not(even))

        @pl.when(mine)
        def _():
            for n, own, out in outs:
                copy(own, own_base, out, n, j)

        @pl.when(from_a)
        def _():
            for n, own, out in outs:
                copy(ra, base + n * count * 256, out, n, j)

        @pl.when(from_b)
        def _():
            for n, own, out in outs:
                copy(rb, base + n * count * 256, out, n, j)

        @pl.when(jnp.logical_not(used))
        def _():
            for n, own, out in outs:
                pltpu.make_async_copy(nothing, out.at[:, j, :], sems.at[n, j]).start()

    for n, own, out in outs:
        for j in range(CAP):
            pltpu.make_async_copy(nothing, out.at[:, j, :], sems.at[n, j]).wait()


BOTH = ("region", "member")


def swap_near(value):
    return lax.ppermute(value, "member", [(i, i ^ 1) for i in range(lax.axis_size("member"))])


def swap_far(value):
    regions, members = lax.axis_size("region"), lax.axis_size("member")
    pairs = []
    for r in range(regions):
        for m in range(members):
            other = m + 1 if m % 2 else m - 1
            inside = 0 <= other < members
            target = r * members + other if inside else (r ^ 1) * members + m
            pairs.append((r * members + m, target))
    return lax.ppermute(value, BOTH, pairs)


def swap_regions(inner, outer):
    regions, members = lax.axis_size("region"), lax.axis_size("member")
    pairs = []
    for r in range(regions):
        other = r + 1 if r % 2 else r - 1
        inside = 0 <= other < regions
        for m in range(members):
            target = other * members + m if inside else r * members + (m ^ 1)
            pairs.append((r * members + m, target))
    inner = lax.ppermute(inner, "region", [(i, i ^ 1) for i in range(regions)])
    return inner, lax.ppermute(outer, BOTH, pairs)


def swap_blocks(first, second):
    count = lax.axis_size(BOTH)
    inner = [(i, i ^ 1) for i in range(count)]
    outer = [(i, (i + 1) % count if i % 2 else (i - 1) % count) for i in range(count)]
    return lax.ppermute(first, BOTH, inner), lax.ppermute(second, BOTH, outer)


def swap_faces(sa, sb, sc, sd):
    return (swap_near(sa), swap_far(sb), *swap_regions(sc, sd))


FULL, TWO, CFIELD = (ROWS, LANES), (2 * BS, LANES), (CROWS, LANES)
FACE, CFACE = (BS, LANES), (8, LANES)


def set_up(new_owner, src, inv):
    outs = [jax.ShapeDtypeStruct((3,), jnp.int32)] + [
        jax.ShapeDtypeStruct(s, F32) for s in [FULL] * 6 + [TWO] * 2 + [CFIELD] * 2
    ]
    vm, sm = pl.BlockSpec(memory_space=pltpu.VMEM), pl.BlockSpec(memory_space=pltpu.SMEM)
    return pl.pallas_call(
        weights_kernel,
        out_shape=outs,
        in_specs=[vm] * 3,
        out_specs=[sm] + [vm] * 10,
        compiler_params=pltpu.CompilerParams(vmem_limit_bytes=48 << 20),
        cost_estimate=pl.CostEstimate(flops=4000000, bytes_accessed=6 << 20, transcendentals=0),
    )(new_owner.reshape(-1, min(LANES, new_owner.size)), src, inv)


def place_blocks(count, owned, *arrays):
    anywhere = pl.BlockSpec(memory_space=pl.ANY)
    slots = jax.ShapeDtypeStruct((256, CAP, LANES), F32)
    outs = pl.pallas_call(
        functools.partial(place_kernel, count=count),
        out_shape=[slots, slots],
        in_specs=[pl.BlockSpec(memory_space=pltpu.SMEM)] + [anywhere] * 4,
        out_specs=[anywhere] * 2,
        scratch_shapes=[vmem(256, LANES), pltpu.SemaphoreType.DMA((2, CAP))],
    )(owned, *arrays)
    return tuple(o.transpose(1, 0, 2).reshape(CAP, 256 * LANES) for o in outs)


def on_device(source, inverse_density, block_level, level_sweeps, new_owner):
    region, member = lax.axis_index("region"), lax.axis_index("member")
    levels = (block_level, level_sweeps)
    edge = jnp.where(member % 2 == 0, BS - 1, 0)
    ia = lax.dynamic_slice_in_dim(inverse_density[1], edge, 1, axis=1)[:, 0]
    ib = lax.dynamic_slice_in_dim(inverse_density[1], BS - 1 - edge, 1, axis=1)[:, 0]
    edge = jnp.where(region % 2 == 0, BS - 1, 0)
    ic = lax.dynamic_slice_in_dim(inverse_density[0], edge, 1, axis=0)[0]
    id_ = lax.dynamic_slice_in_dim(inverse_density[0], BS - 1 - edge, 1, axis=0)[0]
    halos = swap_faces(ia, ib, ic, id_)
    owned, src, f0, fy, fz, fzs, c0, fx, fyf, czu, czd = set_up(
        new_owner, source.reshape(ROWS, LANES), inverse_density.reshape(3 * ROWS, LANES)
    )
    c, d, gx, gy, p, *sends = call(
        first_kernel,
        [FULL, FULL, TWO, TWO, FULL] + [FACE] * 4,
        [src, f0, fy, fzs, c0, fx, fyf, *halos],
        levels,
        [vmem(*FULL)],
        {4: 0},
    )
    fine = [src, c, f0, fy, fz]
    wide = None
    for cycle in range(CYCLES):
        if cycle > 0:
            halos = swap_faces(*sends)
            (ri,) = call(residual_kernel, [FULL], [*fine, p])
            _, p, *sends = call(
                smooth_kernel,
                [FULL, FULL] + [FACE] * 4,
                [ri, f0, fy, fzs, d, p, gx, gy, *halos],
                levels,
                [vmem(*FULL)],
                {0: 0},
            )
        sa, sb, sc, sd = sends
        ra = swap_near(sa)
        rc, rd = swap_regions(sc, sd)
        (qi,) = call(coarse_rhs_kernel, [CFIELD], [*fine, p], scratch=[vmem(*CFIELD)])
        packed, rows = [], CROWS
        if wide is None:
            packed = call(
                coarse_weights_kernel,
                [CFIELD],
                [f0, fy, gx, gy, czu, czd],
                scratch=[vmem(*CFIELD)] * 2,
            )
            rows = 2 * CROWS
        ma, mb = call(
            coarse_faces_kernel,
            [(rows, LANES), (rows + BS, LANES)],
            [qi, gx, gy, ra, rc, rd, sb, *packed],
            scratch=[vmem(*FACE)],
        )
        qa, qb = swap_near(ma), swap_far(mb)
        outs = [CFIELD] + [CFACE] * 4
        arrays = [ma, qa, qb, sb, gy]
        scratch = [vmem(3 * CROWS, LANES), vmem(*TWO)]
        if wide is None:
            cc, cyb, ta, tc, td, wide = call(
                first_coarse_kernel, outs + [(12 * CROWS, LANES)], arrays, scratch=scratch
            )
        else:
            cc, cyb, ta, tc, td = call(later_coarse_kernel, outs, [*arrays, wide], scratch=scratch)
        ka = swap_near(ta)
        kc, kd = swap_regions(tc, td)
        p, ri = call(
            correct_kernel, [FULL, FULL], [*fine, p, gy, qb, cc, cyb], scratch=[vmem(*FACE)]
        )
        _, p, *sends = call(
            smooth_corrected_kernel,
            [FULL, FULL] + [FACE] * 4,
            [ri, f0, fy, fzs, d, p, gx, gy, ra, rc, rd, ka, kc, kd],
            levels,
            [vmem(*FULL), vmem(*FACE)],
            {0: 0},
        )

    def tail(count, p, sends, fine, gx, gy, owned):
        halos = swap_faces(*sends)
        ri, blocks_p = call(last_residual_kernel, [FULL, FULL], [*fine, p])
        part = (2 * count * 256, LANES)
        _, blocks_r, sa, sb = call(
            functools.partial(final_kernel, count=count),
            [FULL, FULL, part, part],
            [ri, gx, gy, *halos, blocks_p],
            aliases={0: 0},
        )
        return place_blocks(count, owned, blocks_p, blocks_r, *swap_blocks(sa, sb))

    return lax.cond(
        owned[2] <= 1,
        functools.partial(tail, 1),
        functools.partial(tail, BLK),
        p, sends, fine, gx, gy, owned,
    )


def solution(mesh):
    placed = (
        P("region", "member", None),
        P(None, "region", "member", None),
        P(("region", "member")),
        P(),
        P(),
    )
    return jax.shard_map(
        on_device,
        mesh=mesh,
        in_specs=placed,
        out_specs=(P(("region", "member"), None), P(("region", "member"), None)),
        check_vma=False,
    )
```

profile of v0, /device:TPU:11, one launch (start us, length us, event | category | flops | bytes accessed | tf_op | source)
XLA Modules:
  0.0 145.1 jit_solution(12504220823290631816)
XLA Ops:
  0.7 1.4 fusion
  2.1 0.0 copy-start.6
  2.1 0.0 copy-start.7
  2.1 0.8 collective-permute-start.15
  2.9 2.6 %collective-permute-start.14 = (f32[32,128]{1,0:T(8,128)S(1)}, f32[32,128]{1,0:T(8,128)S(1)}, u32[]{:S(2)}, u32[]{:S(2)}) collective-permute-start(f32[32,128]{1,0:T(8,128)S(1)} %get-tuple-element.207), channel_id=1, source_target_pairs={{0,32},{32,0},{64,96},{96,64},{1,33},{33,1},{65,97},{97,65},{2,34}... | collective-permute-start | bytes 49160 | tf_op jit(solution)/shard_map/ppermute | solution.py:646
  5.5 1.3 collective-permute-start.12
  6.8 1.3 collective-permute-start.13
  8.1 1.6 %shard_map.72 = (s32[3]{0:T(128)S(1)}, f32[1024,128]{1,0:T(8,128)S(1)}, f32[1024,128]{1,0:T(8,128)S(1)}, f32[1024,128]{1,0:T(8,128)S(1)}, f32[1024,128]{1,0:T(8,...) custom-call(s32[4,128]{1,0:T(4,128)S(1)} %bitcast.24, ...), custom_call_target="tpu_custom_call" | custom-call | flops 4000000 | bytes 6291456 | tf_op jit(solution)/shard_map/pallas_call | solution.py:670
  9.8 0.0 collective-permute-done.14.rc
  9.8 0.0 collective-permute-done.12.ra
  9.8 0.2 collective-permute-done.13.rb
  10.0 8.3 %shard_map.73 = (f32[1024,128]{1,0:T(8,128)S(1)}, f32[1024,128]{1,0:T(8,128)S(1)}, f32[64,128]{1,0:T(8,128)S(1)}, f32[64,128]{1,0:T(8,128)S(1)}, f32[1024,128]{1...) custom-call(s32[4]{0:T(128)S(1)} %copy-done.6, ...), custom_call_target="tpu_custom_call", output_to_operand_aliasing={{0}: (6, {})} | custom-call | flops 2000000 | bytes 4456448 | tf_op jit(solution)/shard_map/pallas_call | solution.py:36
  18.4 0.2 collective-permute-start.16
  18.5 0.1 collective-permute-start.17
  18.7 0.4 collective-permute-start.18
  19.0 1.1 shard_map.74.qi
  20.1 0.5 shard_map.75.rest_0_
  20.6 0.5 collective-permute-done.17.rc
  21.1 0.2 shard_map.76
  21.3 2.8 %collective-permute-start.19 = (f32[160,128]{1,0:T(8,128)S(1)}, f32[160,128]{1,0:T(8,128)S(1)}, u32[]{:S(2)}, u32[]{:S(2)}) collective-permute-start(f32[160,128]{1,0:T(8,128)S(1)} %get-tuple-element.167), channel_id=1, source_target_pairs={{0,32},{1,2},{2,1},{3,4},{4,3},{5,6},{6,5},{7,8},{8,7},{9,10},{10,... | collective-permute-start | bytes 245768 | tf_op jit(solution)/shard_map/ppermute | solution.py:634
  24.1 1.3 collective-permute-done.20.qa
  25.4 1.0 collective-permute-done.19.qb
  26.4 1.3 shard_map.77
  27.7 0.5 collective-permute-start.21
  28.2 1.8 %collective-permute-start.22 = (f32[8,128]{1,0:T(8,128)S(1)}, f32[8,128]{1,0:T(8,128)S(1)}, u32[]{:S(2)}, u32[]{:S(2)}) collective-permute-start(f32[8,128]{1,0:T(8,128)S(1)} %get-tuple-element.175), channel_id=1, source_target_pairs={{0,32},{32,0},{64,96},{96,64},{1,33},{33,1},{65,97},{97,65},{2,34}... | collective-permute-start | bytes 12296 | tf_op jit(solution)/shard_map/ppermute | solution.py:646
  30.0 0.4 collective-permute-start.23
  30.3 0.9 shard_map.78
  31.3 8.0 %shard_map.79 = (f32[1024,128]{1,0:T(8,128)S(1)}, f32[1024,128]{1,0:T(8,128)S(1)}, f32[32,128]{1,0:T(8,128)S(1)}, f32[32,128]{1,0:T(8,128)S(1)}, f32[32,128]{1,0:T(8,128)S(1)}, /*index=5*/f32[32,128]{1,0:T(8,128)S(1)}) custom-call(s32[4]{0:T(128)S(1)} %copy-done.6, s32[3]{0:T(128)S(1)} %copy-done.7, ...), custom_call_target="tpu_custom_call", output_to_operand_aliasing={{0}: (2, {})} | custom-call | flops 2000000 | bytes 4386816 | tf_op jit(solution)/shard_map/pallas_call | solution.py:36
  39.3 0.7 collective-permute-start.24
  40.1 2.9 %collective-permute-start.25 = (f32[32,128]{1,0:T(8,128)S(1)}, f32[32,128]{1,0:T(8,128)S(1)}, u32[]{:S(2)}, u32[]{:S(2)}) collective-permute-start(f32[32,128]{1,0:T(8,128)S(1)} %get-tuple-element.179), channel_id=1, source_target_pairs={{0,32},{1,2},{2,1},{3,4},{4,3},{5,6},{6,5},{7,8},{8,7},{9,10},{10,... | collective-permute-start | bytes 49160 | tf_op jit(solution)/shard_map/ppermute | solution.py:634
  43.0 1.7 %collective-permute-start.26 = (f32[32,128]{1,0:T(8,128)S(1)}, f32[32,128]{1,0:T(8,128)S(1)}, u32[]{:S(2)}, u32[]{:S(2)}) collective-permute-start(f32[32,128]{1,0:T(8,128)S(1)} %get-tuple-element.180), channel_id=1, source_target_pairs={{0,32},{32,0},{64,96},{96,64},{1,33},{33,1},{65,97},{97,65},{2,34}... | collective-permute-start | bytes 49160 | tf_op jit(solution)/shard_map/ppermute | solution.py:646
  44.7 1.9 %collective-permute-start.27 = (f32[32,128]{1,0:T(8,128)S(1)}, f32[32,128]{1,0:T(8,128)S(1)}, u32[]{:S(2)}, u32[]{:S(2)}) collective-permute-start(f32[32,128]{1,0:T(8,128)S(1)} %get-tuple-element.181), channel_id=1, source_target_pairs={{0,1},{1,0},{2,3},{3,2},{4,5},{5,4},{6,7},{7,6},{8,9},{9,8},{10,11... | collective-permute-start | bytes 49160 | tf_op jit(solution)/shard_map/ppermute | solution.py:647
  46.6 1.4 shard_map.80.ri
  48.0 7.9 %shard_map.81 = (f32[1024,128]{1,0:T(8,128)S(1)}, f32[1024,128]{1,0:T(8,128)S(1)}, f32[32,128]{1,0:T(8,128)S(1)}, f32[32,128]{1,0:T(8,128)S(1)}, f32[32,128]{1,0:T(8,128)S(1)}, /*index=5*/f32[32,128]{1,0:T(8,128)S(1)}) custom-call(s32[4]{0:T(128)S(1)} %copy-done.6, s32[3]{0:T(128)S(1)} %copy-done.7, ...), custom_call_target="tpu_custom_call", output_to_operand_aliasing={{0}: (2, {})} | custom-call | flops 2000000 | bytes 4390912 | tf_op jit(solution)/shard_map/pallas_call | solution.py:36
  55.9 0.4 collective-permute-start.28
  56.3 1.8 %collective-permute-start.29 = (f32[32,128]{1,0:T(8,128)S(1)}, f32[32,128]{1,0:T(8,128)S(1)}, u32[]{:S(2)}, u32[]{:S(2)}) collective-permute-start(f32[32,128]{1,0:T(8,128)S(1)} %get-tuple-element.184), channel_id=1, source_target_pairs={{0,32},{32,0},{64,96},{96,64},{1,33},{33,1},{65,97},{97,65},{2,34}... | collective-permute-start | bytes 49160 | tf_op jit(solution)/shard_map/ppermute | solution.py:646
  58.1 0.4 collective-permute-start.30
  58.4 1.1 shard_map.82.qi
  59.5 0.2 shard_map.83
  59.7 1.3 collective-permute-start.31
  61.1 0.9 collective-permute-start.32
  62.0 0.9 collective-permute-done.32.qa
  62.9 0.8 collective-permute-done.31.qb
  63.6 0.9 shard_map.84
  64.6 0.5 collective-permute-start.33
  65.1 1.8 %collective-permute-start.34 = (f32[8,128]{1,0:T(8,128)S(1)}, f32[8,128]{1,0:T(8,128)S(1)}, u32[]{:S(2)}, u32[]{:S(2)}) collective-permute-start(f32[8,128]{1,0:T(8,128)S(1)} %get-tuple-element.195), channel_id=1, source_target_pairs={{0,32},{32,0},{64,96},{96,64},{1,33},{33,1},{65,97},{97,65},{2,34}... | collective-permute-start | bytes 12296 | tf_op jit(solution)/shard_map/ppermute | solution.py:646
  66.9 0.4 collective-permute-start.35
  67.2 0.6 slice.11
  68.5 0.9 shard_map.85
  69.4 8.0 %shard_map.86 = (f32[1024,128]{1,0:T(8,128)S(1)}, f32[1024,128]{1,0:T(8,128)S(1)}, f32[32,128]{1,0:T(8,128)S(1)}, f32[32,128]{1,0:T(8,128)S(1)}, f32[32,128]{1,0:T(8,128)S(1)}, /*index=5*/f32[32,128]{1,0:T(8,128)S(1)}) custom-call(s32[4]{0:T(128)S(1)} %copy-done.6, s32[3]{0:T(128)S(1)} %copy-done.7, ...), custom_call_target="tpu_custom_call", output_to_operand_aliasing={{0}: (2, {})} | custom-call | flops 2000000 | bytes 4386816 | tf_op jit(solution)/shard_map/pallas_call | solution.py:36
  77.4 67.6 %conditional.1 = (f32[6,32768]{1,0:T(8,128)}, f32[6,32768]{1,0:T(8,128)}) conditional(s32[]{:T(128)} %bitcast.15, (f32[1024,128]{1,0:T(8,128)S(1)}, f32[1024,128]{1,0:T(8,128)S(1)}, f32[1024,128]{1,0:T(8,128)S(1)}, f32[1024,128]{1,0:T(8,128)S(1)}, f32[1024,128]{1,0:T(8,128)S(1)}, /*index=5*/f32[1024,128]{1,0:T(8,128)S(1)}, f32[32,128]{1,0:T(8,128)S(1)}, ...), branch_computations={%region_0.1_spmd, %region_1.2_spmd} | conditional | flops 4000000 | bytes 29753712 | solution.py:783
  77.5 0.2 collective-permute-start.6
  77.7 1.5 %collective-permute-start.7 = (f32[32,128]{1,0:T(8,128)S(1)}, f32[32,128]{1,0:T(8,128)S(1)}, u32[]{:S(2)}, u32[]{:S(2)}) collective-permute-start(f32[32,128]{1,0:T(8,128)S(1)} %get-tuple-element.84), channel_id=1, source_target_pairs={{0,32},{1,2},{2,1},{3,4},{4,3},{5,6},{6,5},{7,8},{8,7},{9,10},{10,... | collective-permute-start | bytes 49160 | tf_op jit(solution)/shard_map/cond/branch_1_fun/ppermute | solution.py:634
  79.2 0.7 collective-permute-start.8
  79.9 3.5 %collective-permute-start.9 = (f32[32,128]{1,0:T(8,128)S(1)}, f32[32,128]{1,0:T(8,128)S(1)}, u32[]{:S(2)}, u32[]{:S(2)}) collective-permute-start(f32[32,128]{1,0:T(8,128)S(1)} %get-tuple-element.86), channel_id=1, source_target_pairs={{0,1},{1,0},{2,3},{3,2},{4,5},{5,4},{6,7},{7,6},{8,9},{9,8},{10,11... | collective-permute-start | bytes 49160 | tf_op jit(solution)/shard_map/cond/branch_1_fun/ppermute | solution.py:647
  83.4 2.3 %branch_1_fun.3 = (f32[1024,128]{1,0:T(8,128)S(1)}, f32[1024,128]{1,0:T(8,128)S(1)}) custom-call(f32[1024,128]{1,0:T(8,128)S(1)} %get-tuple-element.73.src, f32[1024,128]{1,0:T(8,128)S(1)} %get-tuple-element.74.c, f32[1024,128]{1,0:T(8,128)S(1)} %get-tuple-element.75.f0, f32[1024,128]{1,0:T(8,128)S(1)} %get-tuple-element.76.fy, ...), custom_call_target="tpu_custom_call" | custom-call | flops 2000000 | bytes 4194304 | tf_op jit(solution)/shard_map/cond/branch_1_fun/pallas_call | solution.py:36
  85.8 2.5 %branch_1_fun.4 = (f32[1024,128]{1,0:T(8,128)S(1)}, f32[1024,128]{1,0:T(8,128)S(1)}, f32[512,128]{1,0:T(8,128)S(1)}, f32[512,128]{1,0:T(8,128)S(1)}) custom-call(f32[1024,128]{1,0:T(8,128)S(1)} %get-tuple-element.80.ri, f32[64,128]{1,0:T(8,128)S(1)} %get-tuple-element.81.gx, f32[64,128]{1,0:T(8,128)S(1)} %get-tuple-element.82.gy, ...), custom_call_target="tpu_custom_call", output_to_operand_aliasing={{0}: (0, {})} | custom-call | flops 2000000 | bytes 2752512 | tf_op jit(solution)/shard_map/cond/branch_1_fun/pallas_call | solution.py:36
  88.3 0.8 copy-done.4
  89.0 0.0 collective-permute-start.10
  89.0 0.3 collective-permute-start.11
  89.3 1.3 collective-permute-done.10.ra
  90.6 4.4 %collective-permute-done.11.rb = f32[512,128]{1,0:T(8,128)S(1)} collective-permute-done((f32[512,128]{1,0:T(8,128)S(1)}, f32[512,128]{1,0:T(8,128)S(1)}, u32[]{:S(2)}, u32[]{:S(2)}) %collective-permute-start.11) | collective-permute-done | bytes 262176 | tf_op jit(solution)/shard_map/cond/branch_1_fun/ppermute | solution.py:654
  95.0 0.7 copy-done.12
  95.7 49.4 %branch_1_fun.5 = (f32[256,6,128]{2,1,0:T(8,128)}, f32[256,6,128]{2,1,0:T(8,128)}) custom-call(s32[3]{0:T(128)S(1)} %get-tuple-element.72.owned, f32[1024,128]{1,0:T(8,128)} %copy-done.1, f32[1024,128]{1,0:T(8,128)} %copy-done.4, f32[512,128]{1,0:T(8,128)} %copy-done.11, f32[512,128]{1,0:T(8,128)} %copy-done.12), custom_call_target="tpu_custom_call" | custom-call | tf_op jit(solution)/shard_map/cond/branch_1_fun/pallas_call | solution.py:683
  (37 shorter events, 0.1 us)
Async XLA Ops:
  0.6 7.5 %copy-start = (f32[3,32,32,128]{3,2,1,0:T(8,128)S(1)}, f32[3,32,32,128]{3,2,1,0:T(8,128)}, u32[]{:S(2)}) copy-start(f32[3,32,32,128]{3,2,1,0:T(8,128)} %param.8) | copy-start | bytes 4718596
  0.6 7.5 %copy-start.8 = (s32[512]{0:T(512)S(1)}, s32[512]{0:T(512)}, u32[]{:S(2)}) copy-start(s32[512]{0:T(512)} %param.11) | copy-start | bytes 6148
  0.6 7.5 %copy-start.3 = (f32[32,32,128]{2,1,0:T(8,128)S(1)}, f32[32,32,128]{2,1,0:T(8,128)}, u32[]{:S(2)}) copy-start(f32[32,32,128]{2,1,0:T(8,128)} %param.7) | copy-start | bytes 1572868
  2.1 7.9 %copy-start.6 = (s32[4]{0:T(128)S(1)}, s32[4]{0:T(128)}, u32[]{:S(2)}) copy-start(s32[4]{0:T(128)} %levels.7) | copy-start | bytes 52
  2.1 7.9 %copy-start.7 = (s32[3]{0:T(128)S(1)}, s32[3]{0:T(128)}, u32[]{:S(2)}) copy-start(s32[3]{0:T(128)} %level_sweeps.7) | copy-start | bytes 40
  2.1 7.7 %collective-permute-start.15 = (f32[32,128]{1,0:T(8,128)S(1)}, f32[32,128]{1,0:T(8,128)S(1)}, u32[]{:S(2)}, u32[]{:S(2)}) collective-permute-start(f32[32,128]{1,0:T(8,128)S(1)} %get-tuple-element.206), channel_id=1, source_target_pairs={{0,1},{1,0},{2,3},{3,2},{4,5},{5,4},{6,7},{7,6},{8,9},{9,8},{10,11... | collective-permute-start | bytes 49160 | tf_op jit(solution)/shard_map/ppermute | solution.py:647
  2.9 6.9 %collective-permute-start.14 = (f32[32,128]{1,0:T(8,128)S(1)}, f32[32,128]{1,0:T(8,128)S(1)}, u32[]{:S(2)}, u32[]{:S(2)}) collective-permute-start(f32[32,128]{1,0:T(8,128)S(1)} %get-tuple-element.207), channel_id=1, source_target_pairs={{0,32},{32,0},{64,96},{96,64},{1,33},{33,1},{65,97},{97,65},{2,34}... | collective-permute-start | bytes 49160 | tf_op jit(solution)/shard_map/ppermute | solution.py:646
  5.5 4.3 %collective-permute-start.12 = (f32[32,128]{1,0:T(8,128)S(1)}, f32[32,128]{1,0:T(8,128)S(1)}, u32[]{:S(2)}, u32[]{:S(2)}) collective-permute-start(f32[32,128]{1,0:T(8,128)S(1)} %bitcast.26), channel_id=1, source_target_pairs={{0,1},{1,0},{2,3},{3,2},{4,5},{5,4},{6,7},{7,6},{8,9},{9,8},{10,11... | collective-permute-start | bytes 49160 | tf_op jit(solution)/shard_map/ppermute | solution.py:622
  6.8 3.2 %collective-permute-start.13 = (f32[32,128]{1,0:T(8,128)S(1)}, f32[32,128]{1,0:T(8,128)S(1)}, u32[]{:S(2)}, u32[]{:S(2)}) collective-permute-start(f32[32,128]{1,0:T(8,128)S(1)} %bitcast.25), channel_id=1, source_target_pairs={{0,32},{1,2},{2,1},{3,4},{4,3},{5,6},{6,5},{7,8},{8,7},{9,10},{10,... | collective-permute-start | bytes 49160 | tf_op jit(solution)/shard_map/ppermute | solution.py:634
  18.4 2.2 %collective-permute-start.16 = (f32[32,128]{1,0:T(8,128)S(1)}, f32[32,128]{1,0:T(8,128)S(1)}, u32[]{:S(2)}, u32[]{:S(2)}) collective-permute-start(f32[32,128]{1,0:T(8,128)S(1)} %get-tuple-element.161), channel_id=1, source_target_pairs={{0,1},{1,0},{2,3},{3,2},{4,5},{5,4},{6,7},{7,6},{8,9},{9,8},{10,11... | collective-permute-start | bytes 49160 | tf_op jit(solution)/shard_map/ppermute | solution.py:622
  18.5 2.6 %collective-permute-start.17 = (f32[32,128]{1,0:T(8,128)S(1)}, f32[32,128]{1,0:T(8,128)S(1)}, u32[]{:S(2)}, u32[]{:S(2)}) collective-permute-start(f32[32,128]{1,0:T(8,128)S(1)} %get-tuple-element.162), channel_id=1, source_target_pairs={{0,32},{32,0},{64,96},{96,64},{1,33},{33,1},{65,97},{97,65},{2,34}... | collective-permute-start | bytes 49160 | tf_op jit(solution)/shard_map/ppermute | solution.py:646
  18.7 2.5 %collective-permute-start.18 = (f32[32,128]{1,0:T(8,128)S(1)}, f32[32,128]{1,0:T(8,128)S(1)}, u32[]{:S(2)}, u32[]{:S(2)}) collective-permute-start(f32[32,128]{1,0:T(8,128)S(1)} %get-tuple-element.163), channel_id=1, source_target_pairs={{0,1},{1,0},{2,3},{3,2},{4,5},{5,4},{6,7},{7,6},{8,9},{9,8},{10,11... | collective-permute-start | bytes 49160 | tf_op jit(solution)/shard_map/ppermute | solution.py:647
  21.3 5.1 %collective-permute-start.19 = (f32[160,128]{1,0:T(8,128)S(1)}, f32[160,128]{1,0:T(8,128)S(1)}, u32[]{:S(2)}, u32[]{:S(2)}) collective-permute-start(f32[160,128]{1,0:T(8,128)S(1)} %get-tuple-element.167), channel_id=1, source_target_pairs={{0,32},{1,2},{2,1},{3,4},{4,3},{5,6},{6,5},{7,8},{8,7},{9,10},{10,... | collective-permute-start | bytes 245768 | tf_op jit(solution)/shard_map/ppermute | solution.py:634
  24.1 1.3 collective-permute-start.20
  27.7 3.5 %collective-permute-start.21 = (f32[8,128]{1,0:T(8,128)S(1)}, f32[8,128]{1,0:T(8,128)S(1)}, u32[]{:S(2)}, u32[]{:S(2)}) collective-permute-start(f32[8,128]{1,0:T(8,128)S(1)} %get-tuple-element.174), channel_id=1, source_target_pairs={{0,1},{1,0},{2,3},{3,2},{4,5},{5,4},{6,7},{7,6},{8,9},{9,8},{10,11... | collective-permute-start | bytes 12296 | tf_op jit(solution)/shard_map/ppermute | solution.py:622
  28.2 3.1 %collective-permute-start.22 = (f32[8,128]{1,0:T(8,128)S(1)}, f32[8,128]{1,0:T(8,128)S(1)}, u32[]{:S(2)}, u32[]{:S(2)}) collective-permute-start(f32[8,128]{1,0:T(8,128)S(1)} %get-tuple-element.175), channel_id=1, source_target_pairs={{0,32},{32,0},{64,96},{96,64},{1,33},{33,1},{65,97},{97,65},{2,34}... | collective-permute-start | bytes 12296 | tf_op jit(solution)/shard_map/ppermute | solution.py:646
  30.0 1.3 collective-permute-start.23
  39.3 8.6 %collective-permute-start.24 = (f32[32,128]{1,0:T(8,128)S(1)}, f32[32,128]{1,0:T(8,128)S(1)}, u32[]{:S(2)}, u32[]{:S(2)}) collective-permute-start(f32[32,128]{1,0:T(8,128)S(1)} %get-tuple-element.178), channel_id=1, source_target_pairs={{0,1},{1,0},{2,3},{3,2},{4,5},{5,4},{6,7},{7,6},{8,9},{9,8},{10,11... | collective-permute-start | bytes 49160 | tf_op jit(solution)/shard_map/ppermute | solution.py:622
  40.1 7.9 %collective-permute-start.25 = (f32[32,128]{1,0:T(8,128)S(1)}, f32[32,128]{1,0:T(8,128)S(1)}, u32[]{:S(2)}, u32[]{:S(2)}) collective-permute-start(f32[32,128]{1,0:T(8,128)S(1)} %get-tuple-element.179), channel_id=1, source_target_pairs={{0,32},{1,2},{2,1},{3,4},{4,3},{5,6},{6,5},{7,8},{8,7},{9,10},{10,... | collective-permute-start | bytes 49160 | tf_op jit(solution)/shard_map/ppermute | solution.py:634
  43.0 5.0 %collective-permute-start.26 = (f32[32,128]{1,0:T(8,128)S(1)}, f32[32,128]{1,0:T(8,128)S(1)}, u32[]{:S(2)}, u32[]{:S(2)}) collective-permute-start(f32[32,128]{1,0:T(8,128)S(1)} %get-tuple-element.180), channel_id=1, source_target_pairs={{0,32},{32,0},{64,96},{96,64},{1,33},{33,1},{65,97},{97,65},{2,34}... | collective-permute-start | bytes 49160 | tf_op jit(solution)/shard_map/ppermute | solution.py:646
  44.7 3.3 %collective-permute-start.27 = (f32[32,128]{1,0:T(8,128)S(1)}, f32[32,128]{1,0:T(8,128)S(1)}, u32[]{:S(2)}, u32[]{:S(2)}) collective-permute-start(f32[32,128]{1,0:T(8,128)S(1)} %get-tuple-element.181), channel_id=1, source_target_pairs={{0,1},{1,0},{2,3},{3,2},{4,5},{5,4},{6,7},{7,6},{8,9},{9,8},{10,11... | collective-permute-start | bytes 49160 | tf_op jit(solution)/shard_map/ppermute | solution.py:647
  55.9 3.6 %collective-permute-start.28 = (f32[32,128]{1,0:T(8,128)S(1)}, f32[32,128]{1,0:T(8,128)S(1)}, u32[]{:S(2)}, u32[]{:S(2)}) collective-permute-start(f32[32,128]{1,0:T(8,128)S(1)} %get-tuple-element.183), channel_id=1, source_target_pairs={{0,1},{1,0},{2,3},{3,2},{4,5},{5,4},{6,7},{7,6},{8,9},{9,8},{10,11... | collective-permute-start | bytes 49160 | tf_op jit(solution)/shard_map/ppermute | solution.py:622
  56.3 3.2 %collective-permute-start.29 = (f32[32,128]{1,0:T(8,128)S(1)}, f32[32,128]{1,0:T(8,128)S(1)}, u32[]{:S(2)}, u32[]{:S(2)}) collective-permute-start(f32[32,128]{1,0:T(8,128)S(1)} %get-tuple-element.184), channel_id=1, source_target_pairs={{0,32},{32,0},{64,96},{96,64},{1,33},{33,1},{65,97},{97,65},{2,34}... | collective-permute-start | bytes 49160 | tf_op jit(solution)/shard_map/ppermute | solution.py:646
  58.1 1.5 %collective-permute-start.30 = (f32[32,128]{1,0:T(8,128)S(1)}, f32[32,128]{1,0:T(8,128)S(1)}, u32[]{:S(2)}, u32[]{:S(2)}) collective-permute-start(f32[32,128]{1,0:T(8,128)S(1)} %get-tuple-element.185), channel_id=1, source_target_pairs={{0,1},{1,0},{2,3},{3,2},{4,5},{5,4},{6,7},{7,6},{8,9},{9,8},{10,11... | collective-permute-start | bytes 49160 | tf_op jit(solution)/shard_map/ppermute | solution.py:647
  59.7 3.9 %collective-permute-start.31 = (f32[96,128]{1,0:T(8,128)S(1)}, f32[96,128]{1,0:T(8,128)S(1)}, u32[]{:S(2)}, u32[]{:S(2)}) collective-permute-start(f32[96,128]{1,0:T(8,128)S(1)} %get-tuple-element.187), channel_id=1, source_target_pairs={{0,32},{1,2},{2,1},{3,4},{4,3},{5,6},{6,5},{7,8},{8,7},{9,10},{10,... | collective-permute-start | bytes 147464 | tf_op jit(solution)/shard_map/ppermute | solution.py:634
  61.1 1.8 %collective-permute-start.32 = (f32[64,128]{1,0:T(8,128)S(1)}, f32[64,128]{1,0:T(8,128)S(1)}, u32[]{:S(2)}, u32[]{:S(2)}) collective-permute-start(f32[64,128]{1,0:T(8,128)S(1)} %get-tuple-element.188.ma), channel_id=1, source_target_pairs={{0,1},{1,0},{2,3},{3,2},{4,5},{5,4},{6,7},{7,6},{8,9},{9,8},{10,11... | collective-permute-start | bytes 98312 | tf_op jit(solution)/shard_map/ppermute | solution.py:622
  64.6 4.8 %collective-permute-start.33 = (f32[8,128]{1,0:T(8,128)S(1)}, f32[8,128]{1,0:T(8,128)S(1)}, u32[]{:S(2)}, u32[]{:S(2)}) collective-permute-start(f32[8,128]{1,0:T(8,128)S(1)} %get-tuple-element.194), channel_id=1, source_target_pairs={{0,1},{1,0},{2,3},{3,2},{4,5},{5,4},{6,7},{7,6},{8,9},{9,8},{10,11... | collective-permute-start | bytes 12296 | tf_op jit(solution)/shard_map/ppermute | solution.py:622
  65.1 4.3 %collective-permute-start.34 = (f32[8,128]{1,0:T(8,128)S(1)}, f32[8,128]{1,0:T(8,128)S(1)}, u32[]{:S(2)}, u32[]{:S(2)}) collective-permute-start(f32[8,128]{1,0:T(8,128)S(1)} %get-tuple-element.195), channel_id=1, source_target_pairs={{0,32},{32,0},{64,96},{96,64},{1,33},{33,1},{65,97},{97,65},{2,34}... | collective-permute-start | bytes 12296 | tf_op jit(solution)/shard_map/ppermute | solution.py:646
  66.9 2.5 %collective-permute-start.35 = (f32[8,128]{1,0:T(8,128)S(1)}, f32[8,128]{1,0:T(8,128)S(1)}, u32[]{:S(2)}, u32[]{:S(2)}) collective-permute-start(f32[8,128]{1,0:T(8,128)S(1)} %get-tuple-element.196), channel_id=1, source_target_pairs={{0,1},{1,0},{2,3},{3,2},{4,5},{5,4},{6,7},{7,6},{8,9},{9,8},{10,11... | collective-permute-start | bytes 12296 | tf_op jit(solution)/shard_map/ppermute | solution.py:647
  77.5 8.2 %collective-permute-start.6 = (f32[32,128]{1,0:T(8,128)S(1)}, f32[32,128]{1,0:T(8,128)S(1)}, u32[]{:S(2)}, u32[]{:S(2)}) collective-permute-start(f32[32,128]{1,0:T(8,128)S(1)} %get-tuple-element.83), channel_id=1, source_target_pairs={{0,1},{1,0},{2,3},{3,2},{4,5},{5,4},{6,7},{7,6},{8,9},{9,8},{10,11... | collective-permute-start | bytes 49160 | tf_op jit(solution)/shard_map/cond/branch_1_fun/ppermute | solution.py:622
  77.7 8.0 %collective-permute-start.7 = (f32[32,128]{1,0:T(8,128)S(1)}, f32[32,128]{1,0:T(8,128)S(1)}, u32[]{:S(2)}, u32[]{:S(2)}) collective-permute-start(f32[32,128]{1,0:T(8,128)S(1)} %get-tuple-element.84), channel_id=1, source_target_pairs={{0,32},{1,2},{2,1},{3,4},{4,3},{5,6},{6,5},{7,8},{8,7},{9,10},{10,... | collective-permute-start | bytes 49160 | tf_op jit(solution)/shard_map/cond/branch_1_fun/ppermute | solution.py:634
  79.2 6.6 %collective-permute-start.8 = (f32[32,128]{1,0:T(8,128)S(1)}, f32[32,128]{1,0:T(8,128)S(1)}, u32[]{:S(2)}, u32[]{:S(2)}) collective-permute-start(f32[32,128]{1,0:T(8,128)S(1)} %get-tuple-element.85), channel_id=1, source_target_pairs={{0,32},{32,0},{64,96},{96,64},{1,33},{33,1},{65,97},{97,65},{2,34}... | collective-permute-start | bytes 49160 | tf_op jit(solution)/shard_map/cond/branch_1_fun/ppermute | solution.py:646
  79.9 5.9 %collective-permute-start.9 = (f32[32,128]{1,0:T(8,128)S(1)}, f32[32,128]{1,0:T(8,128)S(1)}, u32[]{:S(2)}, u32[]{:S(2)}) collective-permute-start(f32[32,128]{1,0:T(8,128)S(1)} %get-tuple-element.86), channel_id=1, source_target_pairs={{0,1},{1,0},{2,3},{3,2},{4,5},{5,4},{6,7},{7,6},{8,9},{9,8},{10,11... | collective-permute-start | bytes 49160 | tf_op jit(solution)/shard_map/cond/branch_1_fun/ppermute | solution.py:647
  85.7 9.3 %copy-start.1 = (f32[1024,128]{1,0:T(8,128)}, f32[1024,128]{1,0:T(8,128)S(1)}, u32[]{:S(2)}) copy-start(f32[1024,128]{1,0:T(8,128)S(1)} %get-tuple-element.79.pblocks.own_p) | copy-start | bytes 1572868 | tf_op jit(solution)/shard_map/cond
  88.2 0.8 copy-start.4
  89.0 1.5 %collective-permute-start.10 = (f32[512,128]{1,0:T(8,128)S(1)}, f32[512,128]{1,0:T(8,128)S(1)}, u32[]{:S(2)}, u32[]{:S(2)}) collective-permute-start(f32[512,128]{1,0:T(8,128)S(1)} %get-tuple-element.88), channel_id=1, source_target_pairs={{0,1},{1,0},{2,3},{3,2},{4,5},{5,4},{6,7},{7,6},{8,9},{9,8},{10,11... | collective-permute-start | bytes 786440 | tf_op jit(solution)/shard_map/cond/branch_1_fun/ppermute | solution.py:654
  89.0 5.9 %collective-permute-start.11 = (f32[512,128]{1,0:T(8,128)S(1)}, f32[512,128]{1,0:T(8,128)S(1)}, u32[]{:S(2)}, u32[]{:S(2)}) collective-permute-start(f32[512,128]{1,0:T(8,128)S(1)} %get-tuple-element.89), channel_id=1, source_target_pairs={{0,127},{1,2},{2,1},{3,4},{4,3},{5,6},{6,5},{7,8},{8,7},{9,10},{10... | collective-permute-start | bytes 786440 | tf_op jit(solution)/shard_map/cond/branch_1_fun/ppermute | solution.py:654
  90.6 4.4 %copy-start.11 = (f32[512,128]{1,0:T(8,128)}, f32[512,128]{1,0:T(8,128)S(1)}, u32[]{:S(2)}) copy-start(f32[512,128]{1,0:T(8,128)S(1)} %collective-permute-done.10.ra) | copy-start | bytes 786436 | tf_op jit(solution)/shard_map/cond
  95.0 0.7 copy-start.12
where the time goes:
time: 148 us; the launch traced here: 145 us
  Pallas kernels  96.7 us (65%)
  starting transfers between devices  32.9 us (22%)
  waiting for transfers between devices  10.3 us (7%)
  local copies, waits for them, and re-layouts  3.55 us (2%)
  between operations  1.59 us (1%)
    pallas_call x1, Pallas kernels, place_blocks(): pl.pallas_call(functools.partial(place_kernel, count=count), out_shape=[s...  49.4 us
    pallas_call x16, Pallas kernels, call(): pl.pallas_call(body, out_shape=outs, in_specs=[pl.BlockSpec(memory_space=...  45.6 us
    ppermute x7, starting transfers between devices, swap_regions(): inner = lax.ppermute(inner, 'region', [(i, i ^ 1) for i in range(regions)])  10.5 us
    ppermute x5, starting transfers between devices, swap_far(): return lax.ppermute(value, BOTH, pairs)  9.77 us
    ppermute x7, starting transfers between devices, swap_regions(): return (inner, lax.ppermute(outer, BOTH, pairs))  7.54 us
    ppermute x2, waiting for transfers between devices, swap_blocks(): return (lax.ppermute(first, BOTH, inner), lax.ppermute(second, BOTH, outer))  5.63 us
    ppermute x9, starting transfers between devices, swap_near(): lax.ppermute(value, 'member', [(i, i ^ 1) for i in range(lax.axis_size('m...  4.78 us
  transfers between devices with their start and end apart: 30, of which 8 were waited for; matrix products, arithmetic and copies ran while one was open for 0% of the time, Pallas kernels for 7%

commit v1 on v0

--- a/solution.py
+++ b/solution.py
@@ -21,7 +21,6 @@
 ROWS = BS * BS
 XC = BS // 4
 CROWS = XC * XC
-UNROLL = 2
 ZERO = functools.partial(jnp.zeros, (BS, LANES), jnp.float32)
 F32 = jnp.float32
 
@@ -88,7 +87,11 @@
 
 
 def plane(x):
-    return pl.ds(pl.multiple_of(x * BS, BS), BS)
+    return slice(x * BS, (x + 1) * BS)
+
+
+def after_plane(x):
+    return plane(min(x + 1, BS - 1))
 
 
 def pick(flag, yes, no):
@@ -128,15 +131,14 @@
             [ref[pl.ds(offset + x * BS + k, 8, stride=4), :] for k in range(4)], axis=0
         )
 
-    def body(xc, carry):
-        before, here = carry
+    before, here = ZERO(), load(inv, 0, 0)
+    for xc in range(XC):
         total_up = jnp.zeros((8, LANES), F32)
         total_down = jnp.zeros((8, LANES), F32)
         for j in range(4):
             x = xc * 4 + j
             src_t[plane(x), :] = load(src, x, 0)
-            inside = (x < BS - 1).astype(F32)
-            after = load(inv, jnp.minimum(x + 1, BS - 1), 0) * inside
+            after = load(inv, x + 1, 0) if x < BS - 1 else ZERO()
             one = load(inv, x, ROWS)
             two = load(inv, x, 2 * ROWS)
             one_n = jnp.where(row == BS - 1, 0.0, next_y(one))
@@ -147,7 +149,7 @@
             upy = 0.5 * (one + one_n)
             upz = 0.5 * (two + two_n)
             downz = 0.5 * (two + two_p)
-            f0[plane(x), :] = up0 * inside
+            f0[plane(x), :] = up0 if x < BS - 1 else ZERO()
             fy[plane(x), :] = jnp.where(row == BS - 1, 0.0, upy)
             fz[plane(x), :] = jnp.where(lane == LANES - 1, 0.0, upz)
             fzs[plane(x), :] = jnp.where(lane % BS == BS - 1, 0.0, upz)
@@ -155,12 +157,8 @@
             total_up = total_up + fold(upz)
             total_down = total_down + fold(downz)
             before, here = here, after
-        at = pl.ds(pl.multiple_of(xc * 8, 8), 8)
-        czu[at, :] = total_up
-        czd[at, :] = total_down
-        return before, here
-
-    lax.fori_loop(0, XC, body, (ZERO(), load(inv, 0, 0)))
+        czu[8 * xc : 8 * xc + 8, :] = total_up
+        czd[8 * xc : 8 * xc + 8, :] = total_down
     fx[0:BS, :] = load(inv, 0, 0)
     fx[BS : 2 * BS, :] = load(inv, BS - 1, 0)
     for g in range(4):
@@ -215,19 +213,17 @@
     def sweep(i, load, store):
         active = limit > i
 
-        def body(x, carry):
-            t0, here = carry
+        t0, here = ZERO(), load(plane(0))
+        for x in range(BS):
             at = plane(x)
-            after = load(plane(jnp.minimum(x + 1, BS - 1)))
+            after = load(after_plane(x))
             w0, wy, wz = f0[at, :], fy[at, :], fzs[at, :]
             t1 = w0 * here
             total = r[at, :] + t0 + w0 * after
             total = total + wy * next_y(here) + prev_y(wy * here)
             total = total + wz * next_z(here) + prev_z(wz * here)
             store(at, jnp.where(active, KEEP * here + d[at, :] * total, here))
-            return t1, after
-
-        lax.fori_loop(0, BS, body, (ZERO(), load(plane(0))), unroll=UNROLL)
+            t0, here = t1, after
 
     def first(at):
         return d[at, :] * r[at, :]
@@ -264,12 +260,9 @@
     add_faces_x(c, 0.5 * xlo, 0.5 * xhi)
     add_faces_y(c, 0.5 * ylo, 0.5 * yhi)
 
-    def begin(x, _):
+    for x in range(BS):
         at = plane(x)
         d[at, :] = RELAX / c[at, :]
-        return 0
-
-    lax.fori_loop(0, BS, begin, 0, unroll=UNROLL)
 
     def finish(at, value):
         p[at, :] = value
@@ -287,19 +280,16 @@
 
 
 def coarse_rhs_kernel(src, c, f0, fy, fz, p, q, scr):
-    def body(xc, carry):
-        t0, here = carry
+    t0, here = ZERO(), p[0:BS, :]
+    for xc in range(XC):
         total = jnp.zeros((8, LANES), F32)
         for j in range(4):
             x = xc * 4 + j
-            after = p[plane(jnp.minimum(x + 1, BS - 1)), :]
+            after = p[after_plane(x), :]
             r, t0 = residual_plane(src, c, f0, fy, fz, plane(x), t0, here, after)
             total = total + fold(r)
             here = after
-        scr[pl.ds(pl.multiple_of(xc * 8, 8), 8), :] = total
-        return t0, here
-
-    lax.fori_loop(0, XC, body, (ZERO(), p[0:BS, :]))
+        scr[8 * xc : 8 * xc + 8, :] = total
     q[...] = group_sum(scr[...], group_matrix()) * PART
 
 
@@ -445,35 +435,28 @@
 
 
 def correct_kernel(src, c, f0, fy, fz, p, gy, qb, cc, cyb, p2, r, scr):
-    def body(xc, carry):
-        t0, here = carry
-        add = tiled(cc[pl.ds(pl.multiple_of(xc * 8, 8), 8), :])
-        later = pl.ds(pl.multiple_of(jnp.minimum(xc + 1, XC - 1) * 8, 8), 8)
-        add_next = tiled(cc[later, :])
-        for j in range(4):
-            x = xc * 4 + j
-            at = plane(x)
-            after = p[plane(jnp.minimum(x + 1, BS - 1)), :] + (add if j < 3 else add_next)
-            p2[at, :] = here
-            r[at, :], t0 = residual_plane(src, c, f0, fy, fz, at, t0, here, after)
-            here = after
-        return t0, here
-
-    lax.fori_loop(0, XC, body, (ZERO(), p[0:BS, :] + tiled(cc[0:8, :])))
+    def corrected(x):
+        return p[plane(x), :] + tiled(cc[8 * (x // 4) : 8 * (x // 4) + 8, :])
+
+    t0, here = ZERO(), corrected(0)
+    for x in range(BS):
+        at = plane(x)
+        after = corrected(min(x + 1, BS - 1))
+        p2[at, :] = here
+        r[at, :], t0 = residual_plane(src, c, f0, fy, fz, at, t0, here, after)
+        here = after
     halo = qb[CROWS : CROWS + BS, :] + spread_rows(scr, cyb[...])
     ylo, yhi = low_high(Place(), 0, ZERO(), halo)
     add_faces_y(r, gy[0:BS, :] * ylo, gy[BS : 2 * BS, :] * yhi)
 
 
 def residual_kernel(src, c, f0, fy, fz, p, r):
-    def body(x, carry):
-        t0, here = carry
+    t0, here = ZERO(), p[0:BS, :]
+    for x in range(BS):
         at = plane(x)
-        after = p[plane(jnp.minimum(x + 1, BS - 1)), :]
-        r[at, :], t1 = residual_plane(src, c, f0, fy, fz, at, t0, here, after)
-        return t1, after
-
-    lax.fori_loop(0, BS, body, (ZERO(), p[0:BS, :]), unroll=UNROLL)
+        after = p[after_plane(x), :]
+        r[at, :], t0 = residual_plane(src, c, f0, fy, fz, at, t0, here, after)
+        here = after
 
 
 def add_all(place, gx, gy, ra, rb, rc, rd, ref):
@@ -526,20 +509,18 @@
         low, high = u[b], u[b + 1]
         first = jnp.where(even, low, pltpu.roll(high, BS, 1))
         second = jnp.where(even, pltpu.roll(low, LANES - BS, 1), high)
-        out[pl.ds(pl.multiple_of(b * 256 + x * 8, 8), 8), :] = first
-        out[pl.ds(pl.multiple_of((b + 1) * 256 + x * 8, 8), 8), :] = second
+        out[b * 256 + x * 8 : b * 256 + x * 8 + 8, :] = first
+        out[(b + 1) * 256 + x * 8 : (b + 1) * 256 + x * 8 + 8, :] = second
 
 
 def last_residual_kernel(src, c, f0, fy, fz, p, r, blocks):
-    def body(x, carry):
-        t0, here = carry
+    t0, here = ZERO(), p[0:BS, :]
+    for x in range(BS):
         at = plane(x)
-        after = p[plane(jnp.minimum(x + 1, BS - 1)), :]
-        r[at, :], t1 = residual_plane(src, c, f0, fy, fz, at, t0, here, after)
+        after = p[after_plane(x), :]
+        r[at, :], t0 = residual_plane(src, c, f0, fy, fz, at, t0, here, after)
         plane_to_blocks(here, x, blocks)
-        return t1, after
-
-    lax.fori_loop(0, BS, body, (ZERO(), p[0:BS, :]), unroll=UNROLL)
+        here = after
 
 
 def final_kernel(ri, gx, gy, ra, rb, rc, rd, pblocks, r, blocks, sa, sb, *, count):
@@ -547,36 +528,27 @@
     even = place.even[0]
     add_all(place, gx, gy, ra[...], rb[...], rc[...], rd[...], r)
 
-    def body(x, _):
+    for x in range(BS):
         plane_to_blocks(r[plane(x), :], x, blocks)
-        return 0
-
-    lax.fori_loop(0, BS, body, 0, unroll=UNROLL)
     size, last = count * 256, (BLK - count) * 256
-
-    def send(t, _):
-        for n, ref in enumerate((pblocks, blocks)):
-            at = pl.ds(pl.multiple_of(n * size + t * 32, 32), 32)
-            low = ref[pl.ds(pl.multiple_of(t * 32, 32), 32), :]
-            high = ref[pl.ds(pl.multiple_of(last + t * 32, 32), 32), :]
+    for n, ref in enumerate((pblocks, blocks)):
+        for t in range(0, size, 32):
+            low, high = ref[t : t + 32, :], ref[last + t : last + t + 32, :]
+            at = slice(n * size + t, n * size + t + 32)
             sa[at, :] = pick(even, high, low)
             sb[at, :] = pick(even, low, high)
-        return 0
-
-    lax.fori_loop(0, size // 32, send, 0)
-
-
-def place_kernel(owned, own_p, own_r, ra, rb, out_p, out_r, nothing, sems, *, count):
+
+
+def place_kernel(owned, own_p, own_r, ra, rb, out_p, out_r, *, count):
     place = Place()
     even = place.even[0]
-    nothing[...] = jnp.zeros_like(nothing)
     start, held = owned[0], owned[1]
-
-    def copy(ref, base, out, n, j):
-        rows = ref.at[pl.ds(pl.multiple_of(base, 256), 256), :]
-        pltpu.make_async_copy(rows, out.at[:, j, :], sems.at[n, j]).start()
-
-    outs = ((0, own_p, out_p), (1, own_r, out_r))
+    fields = ((0, own_p, out_p), (1, own_r, out_r))
+
+    def fill(ref, base, out, j):
+        for t in range(0, 256, 8):
+            out[t : t + 8, j, :] = ref[pl.ds(pl.multiple_of(base + t, 8), 8), :]
+
     for j in range(CAP):
         where = start + j - place.device * BLK
         used = j < held
@@ -592,27 +564,24 @@
 
         @pl.when(mine)
         def _():
-            for n, own, out in outs:
-                copy(own, own_base, out, n, j)
+            for n, own, out in fields:
+                fill(own, own_base, out, j)
 
         @pl.when(from_a)
         def _():
-            for n, own, out in outs:
-                copy(ra, base + n * count * 256, out, n, j)
+            for n, own, out in fields:
+                fill(ra, base + n * count * 256, out, j)
 
         @pl.when(from_b)
         def _():
-            for n, own, out in outs:
-                copy(rb, base + n * count * 256, out, n, j)
+            for n, own, out in fields:
+                fill(rb, base + n * count * 256, out, j)
 
         @pl.when(jnp.logical_not(used))
         def _():
-            for n, own, out in outs:
-                pltpu.make_async_copy(nothing, out.at[:, j, :], sems.at[n, j]).start()
-
-    for n, own, out in outs:
-        for j in range(CAP):
-            pltpu.make_async_copy(nothing, out.at[:, j, :], sems.at[n, j]).wait()
+            for n, own, out in fields:
+                for t in range(0, 256, 8):
+                    out[t : t + 8, j, :] = jnp.zeros((8, LANES), F32)
 
 
 BOTH = ("region", "member")
@@ -678,15 +647,8 @@
 
 
 def place_blocks(count, owned, *arrays):
-    anywhere = pl.BlockSpec(memory_space=pl.ANY)
-    slots = jax.ShapeDtypeStruct((256, CAP, LANES), F32)
-    outs = pl.pallas_call(
-        functools.partial(place_kernel, count=count),
-        out_shape=[slots, slots],
-        in_specs=[pl.BlockSpec(memory_space=pltpu.SMEM)] + [anywhere] * 4,
-        out_specs=[anywhere] * 2,
-        scratch_shapes=[vmem(256, LANES), pltpu.SemaphoreType.DMA((2, CAP))],
-    )(owned, *arrays)
+    slots = (256, CAP, LANES)
+    outs = call(functools.partial(place_kernel, count=count), [slots, slots], arrays, [owned])
     return tuple(o.transpose(1, 0, 2).reshape(CAP, 256 * LANES) for o in outs)
 
 

time: 148 us -> 77.4 us (0.52)
  the two profiles are of different devices: /device:TPU:11 before, /device:TPU:6 now
where the time goes in v1:
time: 77.4 us; the launch traced here: 77.3 us
  starting transfers between devices  29.1 us (38%)
  Pallas kernels  24 us (31%)
  waiting for transfers between devices  20.4 us (26%)
  local copies, waits for them, and re-layouts  2.07 us (3%)
  between operations  1.61 us (2%)
    pallas_call x17, Pallas kernels, call(): pl.pallas_call(body, out_shape=outs, in_specs=[pl.BlockSpec(memory_space=...  23 us
    ppermute x7, starting transfers between devices, swap_regions(): inner = lax.ppermute(inner, 'region', [(i, i ^ 1) for i in range(regions)])  14.5 us
    ppermute x5, starting transfers between devices, swap_far(): return lax.ppermute(value, BOTH, pairs)  9.91 us
    ppermute x5, waiting for transfers between devices, swap_far(): return lax.ppermute(value, BOTH, pairs)  7.58 us
    ppermute x2, waiting for transfers between devices, swap_blocks(): return (lax.ppermute(first, BOTH, inner), lax.ppermute(second, BOTH, outer))  5.37 us
    ppermute x7, waiting for transfers between devices, swap_regions(): inner = lax.ppermute(inner, 'region', [(i, i ^ 1) for i in range(regions)])  4.94 us
    ppermute x2, starting transfers between devices, swap_blocks(): return (lax.ppermute(first, BOTH, inner), lax.ppermute(second, BOTH, outer))  2.78 us
    ppermute x9, waiting for transfers between devices, swap_near(): lax.ppermute(value, 'member', [(i, i ^ 1) for i in range(lax.axis_size('m...  2.47 us
  transfers between devices with their start and end apart: 30, of which 12 were waited for; matrix products, arithmetic and copies ran while one was open for 1% of the time, Pallas kernels for 8%

profile of v1, /device:TPU:6, one launch (start us, length us, event | category | flops | bytes accessed | tf_op | source)
XLA Modules:
  0.0 77.3 jit_solution(9537415427691834773)
XLA Ops:
  0.7 1.4 %fusion = (f32[1,32,32,128]{3,2,1,0:T(8,128)S(1)}, f32[1,32,32,128]{3,2,1,0:T(8,128)S(1)}) fusion(f32[3,32,32,128]{3,2,1,0:T(8,128)} %param.8), kind=kLoop, calls=%fused_computation.4 | loop fusion | bytes 2097152 | tf_op jit(solution)/shard_map/slice | solution.py:662
  2.1 0.0 copy-start.2
  2.1 0.0 copy-start.3
  2.1 0.1 collective-permute-start.15
  2.2 3.8 %collective-permute-start.14 = (f32[32,128]{1,0:T(8,128)S(1)}, f32[32,128]{1,0:T(8,128)S(1)}, u32[]{:S(2)}, u32[]{:S(2)}) collective-permute-start(f32[32,128]{1,0:T(8,128)S(1)} %get-tuple-element.207), channel_id=1, source_target_pairs={{0,32},{32,0},{64,96},{96,64},{1,33},{33,1},{65,97},{97,65},{2,34}... | collective-permute-start | bytes 49160 | tf_op jit(solution)/shard_map/ppermute | solution.py:615
  6.1 0.1 collective-permute-start.12
  6.2 3.4 %collective-permute-start.13 = (f32[32,128]{1,0:T(8,128)S(1)}, f32[32,128]{1,0:T(8,128)S(1)}, u32[]{:S(2)}, u32[]{:S(2)}) collective-permute-start(f32[32,128]{1,0:T(8,128)S(1)} %bitcast.25), channel_id=1, source_target_pairs={{0,32},{1,2},{2,1},{3,4},{4,3},{5,6},{6,5},{7,8},{8,7},{9,10},{10,... | collective-permute-start | bytes 49160 | tf_op jit(solution)/shard_map/ppermute | solution.py:603
  9.6 1.0 %shard_map.72 = (s32[3]{0:T(128)S(1)}, f32[1024,128]{1,0:T(8,128)S(1)}, f32[1024,128]{1,0:T(8,128)S(1)}, f32[1024,128]{1,0:T(8,128)S(1)}, f32[1024,128]{1,0:T(8,...) custom-call(s32[4,128]{1,0:T(4,128)S(1)} %bitcast.24, ...), custom_call_target="tpu_custom_call" | custom-call | flops 4000000 | bytes 6291456 | tf_op jit(solution)/shard_map/pallas_call | solution.py:639
  10.6 0.0 collective-permute-done.15.rd
  10.6 0.0 collective-permute-done.14.rc
  10.6 0.9 %collective-permute-done.13.rb = f32[32,128]{1,0:T(8,128)S(1)} collective-permute-done((f32[32,128]{1,0:T(8,128)S(1)}, f32[32,128]{1,0:T(8,128)S(1)}, u32[]{:S(2)}, u32[]{:S(2)}) %collective-permute-start.13) | collective-permute-done | bytes 16416 | tf_op jit(solution)/shard_map/ppermute | solution.py:603
  11.5 2.7 %shard_map.73 = (f32[1024,128]{1,0:T(8,128)S(1)}, f32[1024,128]{1,0:T(8,128)S(1)}, f32[64,128]{1,0:T(8,128)S(1)}, f32[64,128]{1,0:T(8,128)S(1)}, f32[1024,128]{1...) custom-call(s32[4]{0:T(128)S(1)} %copy-done.2, ...), custom_call_target="tpu_custom_call", output_to_operand_aliasing={{0}: (6, {})} | custom-call | flops 2000000 | bytes 4456448 | tf_op jit(solution)/shard_map/pallas_call | solution.py:35
  14.2 0.1 collective-permute-start.16
  14.3 0.1 collective-permute-start.17
  14.4 0.4 collective-permute-start.18
  14.8 0.7 shard_map.74.qi
  15.5 0.5 shard_map.75.rest_0_
  16.0 0.0 collective-permute-done.16.ra
  16.0 2.1 %collective-permute-done.17.rc = f32[32,128]{1,0:T(8,128)S(1)} collective-permute-done((f32[32,128]{1,0:T(8,128)S(1)}, f32[32,128]{1,0:T(8,128)S(1)}, u32[]{:S(2)}, u32[]{:S(2)}) %collective-permute-start.17) | collective-permute-done | bytes 16416 | tf_op jit(solution)/shard_map/ppermute | solution.py:615
  18.2 0.2 shard_map.76
  18.4 2.2 %collective-permute-start.19 = (f32[160,128]{1,0:T(8,128)S(1)}, f32[160,128]{1,0:T(8,128)S(1)}, u32[]{:S(2)}, u32[]{:S(2)}) collective-permute-start(f32[160,128]{1,0:T(8,128)S(1)} %get-tuple-element.167), channel_id=1, source_target_pairs={{0,32},{1,2},{2,1},{3,4},{4,3},{5,6},{6,5},{7,8},{8,7},{9,10},{10,... | collective-permute-start | bytes 245768 | tf_op jit(solution)/shard_map/ppermute | solution.py:603
  20.6 1.3 %collective-permute-done.20.qa = f32[128,128]{1,0:T(8,128)S(1)} collective-permute-done((f32[128,128]{1,0:T(8,128)S(1)}, f32[128,128]{1,0:T(8,128)S(1)}, u32[]{:S(2)}, u32[]{:S(2)}) %collective-permute-start.20) | collective-permute-done | bytes 65568 | tf_op jit(solution)/shard_map/ppermute | solution.py:591
  21.8 2.6 %collective-permute-done.19.qb = f32[160,128]{1,0:T(8,128)S(1)} collective-permute-done((f32[160,128]{1,0:T(8,128)S(1)}, f32[160,128]{1,0:T(8,128)S(1)}, u32[]{:S(2)}, u32[]{:S(2)}) %collective-permute-start.19) | collective-permute-done | bytes 81952 | tf_op jit(solution)/shard_map/ppermute | solution.py:603
  24.4 1.3 %shard_map.77 = (f32[64,128]{1,0:T(8,128)S(1)}, f32[8,128]{1,0:T(8,128)S(1)}, f32[8,128]{1,0:T(8,128)S(1)}, f32[8,128]{1,0:T(8,128)S(1)}, f32[8,128]{1,0:T(8,128)S(1)}, /*index=5*/f32[768,128]{1,0:T(8,128)S(1)}) custom-call(f32[128,128]{1,0:T(8,128)S(1)} %get-tuple-element.168.ma, f32[128,128]{1,0:T(8,128)S(1)} %collective-permute-done.20.qa, ...), custom_call_target="tpu_custom_call" | custom-call | flops 2000000 | bytes 704512 | tf_op jit(solution)/shard_map/pallas_call | solution.py:35
  25.7 0.1 collective-permute-start.21
  25.8 2.1 %collective-permute-start.22 = (f32[8,128]{1,0:T(8,128)S(1)}, f32[8,128]{1,0:T(8,128)S(1)}, u32[]{:S(2)}, u32[]{:S(2)}) collective-permute-start(f32[8,128]{1,0:T(8,128)S(1)} %get-tuple-element.175), channel_id=1, source_target_pairs={{0,32},{32,0},{64,96},{96,64},{1,33},{33,1},{65,97},{97,65},{2,34}... | collective-permute-start | bytes 12296 | tf_op jit(solution)/shard_map/ppermute | solution.py:615
  27.9 0.2 collective-permute-start.23
  28.0 0.4 shard_map.78
  28.5 1.0 %collective-permute-done.22.kc = f32[8,128]{1,0:T(8,128)S(1)} collective-permute-done((f32[8,128]{1,0:T(8,128)S(1)}, f32[8,128]{1,0:T(8,128)S(1)}, u32[]{:S(2)}, u32[]{:S(2)}) %collective-permute-start.22) | collective-permute-done | bytes 4128 | tf_op jit(solution)/shard_map/ppermute | solution.py:615
  29.5 2.8 %shard_map.79 = (f32[1024,128]{1,0:T(8,128)S(1)}, f32[1024,128]{1,0:T(8,128)S(1)}, f32[32,128]{1,0:T(8,128)S(1)}, f32[32,128]{1,0:T(8,128)S(1)}, f32[32,128]{1,0:T(8,128)S(1)}, /*index=5*/f32[32,128]{1,0:T(8,128)S(1)}) custom-call(s32[4]{0:T(128)S(1)} %copy-done.2, s32[3]{0:T(128)S(1)} %copy-done.3, ...), custom_call_target="tpu_custom_call", output_to_operand_aliasing={{0}: (2, {})} | custom-call | flops 2000000 | bytes 4386816 | tf_op jit(solution)/shard_map/pallas_call | solution.py:35
  32.3 0.1 collective-permute-start.24
  32.4 2.6 %collective-permute-start.25 = (f32[32,128]{1,0:T(8,128)S(1)}, f32[32,128]{1,0:T(8,128)S(1)}, u32[]{:S(2)}, u32[]{:S(2)}) collective-permute-start(f32[32,128]{1,0:T(8,128)S(1)} %get-tuple-element.179), channel_id=1, source_target_pairs={{0,32},{1,2},{2,1},{3,4},{4,3},{5,6},{6,5},{7,8},{8,7},{9,10},{10,... | collective-permute-start | bytes 49160 | tf_op jit(solution)/shard_map/ppermute | solution.py:603
  34.9 2.0 %collective-permute-start.26 = (f32[32,128]{1,0:T(8,128)S(1)}, f32[32,128]{1,0:T(8,128)S(1)}, u32[]{:S(2)}, u32[]{:S(2)}) collective-permute-start(f32[32,128]{1,0:T(8,128)S(1)} %get-tuple-element.180), channel_id=1, source_target_pairs={{0,32},{32,0},{64,96},{96,64},{1,33},{33,1},{65,97},{97,65},{2,34}... | collective-permute-start | bytes 49160 | tf_op jit(solution)/shard_map/ppermute | solution.py:615
  36.9 0.4 shard_map.80.ri
  37.3 0.4 collective-permute-done.25.rb
  37.7 0.9 %collective-permute-done.26.rc = f32[32,128]{1,0:T(8,128)S(1)} collective-permute-done((f32[32,128]{1,0:T(8,128)S(1)}, f32[32,128]{1,0:T(8,128)S(1)}, u32[]{:S(2)}, u32[]{:S(2)}) %collective-permute-start.26) | collective-permute-done | bytes 16416 | tf_op jit(solution)/shard_map/ppermute | solution.py:615
  38.7 2.8 %shard_map.81 = (f32[1024,128]{1,0:T(8,128)S(1)}, f32[1024,128]{1,0:T(8,128)S(1)}, f32[32,128]{1,0:T(8,128)S(1)}, f32[32,128]{1,0:T(8,128)S(1)}, f32[32,128]{1,0:T(8,128)S(1)}, /*index=5*/f32[32,128]{1,0:T(8,128)S(1)}) custom-call(s32[4]{0:T(128)S(1)} %copy-done.2, s32[3]{0:T(128)S(1)} %copy-done.3, ...), custom_call_target="tpu_custom_call", output_to_operand_aliasing={{0}: (2, {})} | custom-call | flops 2000000 | bytes 4390912 | tf_op jit(solution)/shard_map/pallas_call | solution.py:35
  41.4 0.1 collective-permute-start.28
  41.5 2.1 %collective-permute-start.29 = (f32[32,128]{1,0:T(8,128)S(1)}, f32[32,128]{1,0:T(8,128)S(1)}, u32[]{:S(2)}, u32[]{:S(2)}) collective-permute-start(f32[32,128]{1,0:T(8,128)S(1)} %get-tuple-element.184), channel_id=1, source_target_pairs={{0,32},{32,0},{64,96},{96,64},{1,33},{33,1},{65,97},{97,65},{2,34}... | collective-permute-start | bytes 49160 | tf_op jit(solution)/shard_map/ppermute | solution.py:615
  43.6 0.2 collective-permute-start.30
  43.8 0.7 shard_map.82.qi
  44.4 0.9 %collective-permute-done.29.rc = f32[32,128]{1,0:T(8,128)S(1)} collective-permute-done((f32[32,128]{1,0:T(8,128)S(1)}, f32[32,128]{1,0:T(8,128)S(1)}, u32[]{:S(2)}, u32[]{:S(2)}) %collective-permute-start.29) | collective-permute-done | bytes 16416 | tf_op jit(solution)/shard_map/ppermute | solution.py:615
  45.3 0.2 shard_map.83
  45.5 1.2 %collective-permute-start.31 = (f32[96,128]{1,0:T(8,128)S(1)}, f32[96,128]{1,0:T(8,128)S(1)}, u32[]{:S(2)}, u32[]{:S(2)}) collective-permute-start(f32[96,128]{1,0:T(8,128)S(1)} %get-tuple-element.187), channel_id=1, source_target_pairs={{0,32},{1,2},{2,1},{3,4},{4,3},{5,6},{6,5},{7,8},{8,7},{9,10},{10,... | collective-permute-start | bytes 147464 | tf_op jit(solution)/shard_map/ppermute | solution.py:603
  46.7 1.2 %collective-permute-done.32.qa = f32[64,128]{1,0:T(8,128)S(1)} collective-permute-done((f32[64,128]{1,0:T(8,128)S(1)}, f32[64,128]{1,0:T(8,128)S(1)}, u32[]{:S(2)}, u32[]{:S(2)}) %collective-permute-start.32) | collective-permute-done | bytes 32800 | tf_op jit(solution)/shard_map/ppermute | solution.py:591
  47.9 3.3 %collective-permute-done.31.qb = f32[96,128]{1,0:T(8,128)S(1)} collective-permute-done((f32[96,128]{1,0:T(8,128)S(1)}, f32[96,128]{1,0:T(8,128)S(1)}, u32[]{:S(2)}, u32[]{:S(2)}) %collective-permute-start.31) | collective-permute-done | bytes 49184 | tf_op jit(solution)/shard_map/ppermute | solution.py:603
  51.2 0.9 %shard_map.84 = (f32[64,128]{1,0:T(8,128)S(1)}, f32[8,128]{1,0:T(8,128)S(1)}, f32[8,128]{1,0:T(8,128)S(1)}, f32[8,128]{1,0:T(8,128)S(1)}, f32[8,128]{1,0:T(8,128)S(1)}) custom-call(f32[64,128]{1,0:T(8,128)S(1)} %get-tuple-element.188.ma, f32[64,128]{1,0:T(8,128)S(1)} %collective-permute-done.32.qa, f32[96,128]{1,0:T(8,128)S(1)} %collective-permute-done.31.qb, ...), custom_call_target="tpu_custom_call" | custom-call | flops 2000000 | bytes 606208 | tf_op jit(solution)/shard_map/pallas_call | solution.py:35
  52.2 0.1 collective-permute-start.33
  52.3 2.4 %collective-permute-start.34 = (f32[8,128]{1,0:T(8,128)S(1)}, f32[8,128]{1,0:T(8,128)S(1)}, u32[]{:S(2)}, u32[]{:S(2)}) collective-permute-start(f32[8,128]{1,0:T(8,128)S(1)} %get-tuple-element.195), channel_id=1, source_target_pairs={{0,32},{32,0},{64,96},{96,64},{1,33},{33,1},{65,97},{97,65},{2,34}... | collective-permute-start | bytes 12296 | tf_op jit(solution)/shard_map/ppermute | solution.py:615
  54.7 0.2 collective-permute-start.35
  54.8 0.6 slice.11
  56.0 0.4 shard_map.85
  56.5 2.8 %shard_map.86 = (f32[1024,128]{1,0:T(8,128)S(1)}, f32[1024,128]{1,0:T(8,128)S(1)}, f32[32,128]{1,0:T(8,128)S(1)}, f32[32,128]{1,0:T(8,128)S(1)}, f32[32,128]{1,0:T(8,128)S(1)}, /*index=5*/f32[32,128]{1,0:T(8,128)S(1)}) custom-call(s32[4]{0:T(128)S(1)} %copy-done.2, s32[3]{0:T(128)S(1)} %copy-done.3, ...), custom_call_target="tpu_custom_call", output_to_operand_aliasing={{0}: (2, {})} | custom-call | flops 2000000 | bytes 4386816 | tf_op jit(solution)/shard_map/pallas_call | solution.py:35
  59.3 18.0 %conditional.1 = (f32[6,32768]{1,0:T(8,128)}, f32[6,32768]{1,0:T(8,128)}) conditional(s32[]{:T(128)} %bitcast.15, (f32[1024,128]{1,0:T(8,128)S(1)}, f32[1024,128]{1,0:T(8,128)S(1)}, f32[1024,128]{1,0:T(8,128)S(1)}, f32[1024,128]{1,0:T(8,128)S(1)}, f32[1024,128]{1,0:T(8,128)S(1)}, /*index=5*/f32[1024,128]{1,0:T(8,128)S(1)}, f32[32,128]{1,0:T(8,128)S(1)}, ...), branch_computations={%region_0.1_spmd, %region_1.2_spmd} | conditional | flops 6000000 | bytes 21889280 | solution.py:745
  59.3 0.4 collective-permute-start.6
  59.7 0.6 collective-permute-start.7
  60.3 2.0 %collective-permute-start.8 = (f32[32,128]{1,0:T(8,128)S(1)}, f32[32,128]{1,0:T(8,128)S(1)}, u32[]{:S(2)}, u32[]{:S(2)}) collective-permute-start(f32[32,128]{1,0:T(8,128)S(1)} %get-tuple-element.85), channel_id=1, source_target_pairs={{0,32},{32,0},{64,96},{96,64},{1,33},{33,1},{65,97},{97,65},{2,34}... | collective-permute-start | bytes 49160 | tf_op jit(solution)/shard_map/cond/branch_1_fun/ppermute | solution.py:615
  62.4 2.3 %branch_1_fun.3 = (f32[1024,128]{1,0:T(8,128)S(1)}, f32[1024,128]{1,0:T(8,128)S(1)}) custom-call(f32[1024,128]{1,0:T(8,128)S(1)} %get-tuple-element.73.src, f32[1024,128]{1,0:T(8,128)S(1)} %get-tuple-element.74.c, f32[1024,128]{1,0:T(8,128)S(1)} %get-tuple-element.75.f0, f32[1024,128]{1,0:T(8,128)S(1)} %get-tuple-element.76.fy, ...), custom_call_target="tpu_custom_call" | custom-call | flops 2000000 | bytes 4194304 | tf_op jit(solution)/shard_map/cond/branch_1_fun/pallas_call | solution.py:35
  64.7 0.4 collective-permute-done.7.rb
  65.0 1.2 %branch_1_fun.4 = (f32[1024,128]{1,0:T(8,128)S(1)}, f32[1024,128]{1,0:T(8,128)S(1)}, f32[512,128]{1,0:T(8,128)S(1)}, f32[512,128]{1,0:T(8,128)S(1)}) custom-call(f32[1024,128]{1,0:T(8,128)S(1)} %get-tuple-element.80.ri, f32[64,128]{1,0:T(8,128)S(1)} %get-tuple-element.81.gx, f32[64,128]{1,0:T(8,128)S(1)} %get-tuple-element.82.gy, ...), custom_call_target="tpu_custom_call", output_to_operand_aliasing={{0}: (0, {})} | custom-call | flops 2000000 | bytes 2752512 | tf_op jit(solution)/shard_map/cond/branch_1_fun/pallas_call | solution.py:35
  66.3 0.2 collective-permute-start.10
  66.5 2.5 %collective-permute-start.11 = (f32[512,128]{1,0:T(8,128)S(1)}, f32[512,128]{1,0:T(8,128)S(1)}, u32[]{:S(2)}, u32[]{:S(2)}) collective-permute-start(f32[512,128]{1,0:T(8,128)S(1)} %get-tuple-element.89), channel_id=1, source_target_pairs={{0,127},{1,2},{2,1},{3,4},{4,3},{5,6},{6,5},{7,8},{8,7},{9,10},{10... | collective-permute-start | bytes 786440 | tf_op jit(solution)/shard_map/cond/branch_1_fun/ppermute | solution.py:623
  69.1 5.4 %collective-permute-done.11.rb = f32[512,128]{1,0:T(8,128)S(1)} collective-permute-done((f32[512,128]{1,0:T(8,128)S(1)}, f32[512,128]{1,0:T(8,128)S(1)}, u32[]{:S(2)}, u32[]{:S(2)}) %collective-permute-start.11) | collective-permute-done | bytes 262176 | tf_op jit(solution)/shard_map/cond/branch_1_fun/ppermute | solution.py:623
  74.4 2.8 %branch_1_fun.5 = (f32[256,6,128]{2,1,0:T(8,128)}, f32[256,6,128]{2,1,0:T(8,128)}) custom-call(s32[3]{0:T(128)S(1)} %get-tuple-element.72.owned, f32[1024,128]{1,0:T(8,128)S(1)} %get-tuple-element.79.pblocks.own_p, f32[1024,128]{1,0:T(8,128)S(1)} %get-tuple-element.87.own_r, f32[512,128]{1,0:T(8,128)S(1)} %collective-permute-done.10.ra, ...), custom_call_target="tpu_custom_call" | custom-call | flops 2000000 | bytes 3145728 | tf_op jit(solution)/shard_map/cond/branch_1_fun/pallas_call | solution.py:35
  (29 shorter events, 0.1 us)
Async XLA Ops:
  0.6 8.9 %copy-start = (f32[3,32,32,128]{3,2,1,0:T(8,128)S(1)}, f32[3,32,32,128]{3,2,1,0:T(8,128)}, u32[]{:S(2)}) copy-start(f32[3,32,32,128]{3,2,1,0:T(8,128)} %param.8) | copy-start | bytes 4718596
  0.6 8.9 %copy-start.4 = (s32[512]{0:T(512)S(1)}, s32[512]{0:T(512)}, u32[]{:S(2)}) copy-start(s32[512]{0:T(512)} %param.11) | copy-start | bytes 6148
  0.6 8.9 %copy-start.1 = (f32[32,32,128]{2,1,0:T(8,128)S(1)}, f32[32,32,128]{2,1,0:T(8,128)}, u32[]{:S(2)}) copy-start(f32[32,32,128]{2,1,0:T(8,128)} %param.7) | copy-start | bytes 1572868
  2.1 9.5 %copy-start.2 = (s32[4]{0:T(128)S(1)}, s32[4]{0:T(128)}, u32[]{:S(2)}) copy-start(s32[4]{0:T(128)} %levels.7) | copy-start | bytes 52
  2.1 9.4 %copy-start.3 = (s32[3]{0:T(128)S(1)}, s32[3]{0:T(128)}, u32[]{:S(2)}) copy-start(s32[3]{0:T(128)} %level_sweeps.7) | copy-start | bytes 40
  2.1 8.5 %collective-permute-start.15 = (f32[32,128]{1,0:T(8,128)S(1)}, f32[32,128]{1,0:T(8,128)S(1)}, u32[]{:S(2)}, u32[]{:S(2)}) collective-permute-start(f32[32,128]{1,0:T(8,128)S(1)} %get-tuple-element.206), channel_id=1, source_target_pairs={{0,1},{1,0},{2,3},{3,2},{4,5},{5,4},{6,7},{7,6},{8,9},{9,8},{10,11... | collective-permute-start | bytes 49160 | tf_op jit(solution)/shard_map/ppermute | solution.py:616
  2.2 8.4 %collective-permute-start.14 = (f32[32,128]{1,0:T(8,128)S(1)}, f32[32,128]{1,0:T(8,128)S(1)}, u32[]{:S(2)}, u32[]{:S(2)}) collective-permute-start(f32[32,128]{1,0:T(8,128)S(1)} %get-tuple-element.207), channel_id=1, source_target_pairs={{0,32},{32,0},{64,96},{96,64},{1,33},{33,1},{65,97},{97,65},{2,34}... | collective-permute-start | bytes 49160 | tf_op jit(solution)/shard_map/ppermute | solution.py:615
  6.1 4.5 %collective-permute-start.12 = (f32[32,128]{1,0:T(8,128)S(1)}, f32[32,128]{1,0:T(8,128)S(1)}, u32[]{:S(2)}, u32[]{:S(2)}) collective-permute-start(f32[32,128]{1,0:T(8,128)S(1)} %bitcast.26), channel_id=1, source_target_pairs={{0,1},{1,0},{2,3},{3,2},{4,5},{5,4},{6,7},{7,6},{8,9},{9,8},{10,11... | collective-permute-start | bytes 49160 | tf_op jit(solution)/shard_map/ppermute | solution.py:591
  6.2 5.4 %collective-permute-start.13 = (f32[32,128]{1,0:T(8,128)S(1)}, f32[32,128]{1,0:T(8,128)S(1)}, u32[]{:S(2)}, u32[]{:S(2)}) collective-permute-start(f32[32,128]{1,0:T(8,128)S(1)} %bitcast.25), channel_id=1, source_target_pairs={{0,32},{1,2},{2,1},{3,4},{4,3},{5,6},{6,5},{7,8},{8,7},{9,10},{10,... | collective-permute-start | bytes 49160 | tf_op jit(solution)/shard_map/ppermute | solution.py:603
  14.2 1.8 %collective-permute-start.16 = (f32[32,128]{1,0:T(8,128)S(1)}, f32[32,128]{1,0:T(8,128)S(1)}, u32[]{:S(2)}, u32[]{:S(2)}) collective-permute-start(f32[32,128]{1,0:T(8,128)S(1)} %get-tuple-element.161), channel_id=1, source_target_pairs={{0,1},{1,0},{2,3},{3,2},{4,5},{5,4},{6,7},{7,6},{8,9},{9,8},{10,11... | collective-permute-start | bytes 49160 | tf_op jit(solution)/shard_map/ppermute | solution.py:591
  14.3 3.8 %collective-permute-start.17 = (f32[32,128]{1,0:T(8,128)S(1)}, f32[32,128]{1,0:T(8,128)S(1)}, u32[]{:S(2)}, u32[]{:S(2)}) collective-permute-start(f32[32,128]{1,0:T(8,128)S(1)} %get-tuple-element.162), channel_id=1, source_target_pairs={{0,32},{32,0},{64,96},{96,64},{1,33},{33,1},{65,97},{97,65},{2,34}... | collective-permute-start | bytes 49160 | tf_op jit(solution)/shard_map/ppermute | solution.py:615
  14.4 3.7 %collective-permute-start.18 = (f32[32,128]{1,0:T(8,128)S(1)}, f32[32,128]{1,0:T(8,128)S(1)}, u32[]{:S(2)}, u32[]{:S(2)}) collective-permute-start(f32[32,128]{1,0:T(8,128)S(1)} %get-tuple-element.163), channel_id=1, source_target_pairs={{0,1},{1,0},{2,3},{3,2},{4,5},{5,4},{6,7},{7,6},{8,9},{9,8},{10,11... | collective-permute-start | bytes 49160 | tf_op jit(solution)/shard_map/ppermute | solution.py:616
  18.4 6.1 %collective-permute-start.19 = (f32[160,128]{1,0:T(8,128)S(1)}, f32[160,128]{1,0:T(8,128)S(1)}, u32[]{:S(2)}, u32[]{:S(2)}) collective-permute-start(f32[160,128]{1,0:T(8,128)S(1)} %get-tuple-element.167), channel_id=1, source_target_pairs={{0,32},{1,2},{2,1},{3,4},{4,3},{5,6},{6,5},{7,8},{8,7},{9,10},{10,... | collective-permute-start | bytes 245768 | tf_op jit(solution)/shard_map/ppermute | solution.py:603
  20.6 1.3 %collective-permute-start.20 = (f32[128,128]{1,0:T(8,128)S(1)}, f32[128,128]{1,0:T(8,128)S(1)}, u32[]{:S(2)}, u32[]{:S(2)}) collective-permute-start(f32[128,128]{1,0:T(8,128)S(1)} %get-tuple-element.168.ma), channel_id=1, source_target_pairs={{0,1},{1,0},{2,3},{3,2},{4,5},{5,4},{6,7},{7,6},{8,9},{9,8},{10,11... | collective-permute-start | bytes 196616 | tf_op jit(solution)/shard_map/ppermute | solution.py:591
  25.7 2.8 %collective-permute-start.21 = (f32[8,128]{1,0:T(8,128)S(1)}, f32[8,128]{1,0:T(8,128)S(1)}, u32[]{:S(2)}, u32[]{:S(2)}) collective-permute-start(f32[8,128]{1,0:T(8,128)S(1)} %get-tuple-element.174), channel_id=1, source_target_pairs={{0,1},{1,0},{2,3},{3,2},{4,5},{5,4},{6,7},{7,6},{8,9},{9,8},{10,11... | collective-permute-start | bytes 12296 | tf_op jit(solution)/shard_map/ppermute | solution.py:591
  25.8 3.7 %collective-permute-start.22 = (f32[8,128]{1,0:T(8,128)S(1)}, f32[8,128]{1,0:T(8,128)S(1)}, u32[]{:S(2)}, u32[]{:S(2)}) collective-permute-start(f32[8,128]{1,0:T(8,128)S(1)} %get-tuple-element.175), channel_id=1, source_target_pairs={{0,32},{32,0},{64,96},{96,64},{1,33},{33,1},{65,97},{97,65},{2,34}... | collective-permute-start | bytes 12296 | tf_op jit(solution)/shard_map/ppermute | solution.py:615
  27.9 1.6 %collective-permute-start.23 = (f32[8,128]{1,0:T(8,128)S(1)}, f32[8,128]{1,0:T(8,128)S(1)}, u32[]{:S(2)}, u32[]{:S(2)}) collective-permute-start(f32[8,128]{1,0:T(8,128)S(1)} %get-tuple-element.176), channel_id=1, source_target_pairs={{0,1},{1,0},{2,3},{3,2},{4,5},{5,4},{6,7},{7,6},{8,9},{9,8},{10,11... | collective-permute-start | bytes 12296 | tf_op jit(solution)/shard_map/ppermute | solution.py:616
  32.3 5.1 %collective-permute-start.24 = (f32[32,128]{1,0:T(8,128)S(1)}, f32[32,128]{1,0:T(8,128)S(1)}, u32[]{:S(2)}, u32[]{:S(2)}) collective-permute-start(f32[32,128]{1,0:T(8,128)S(1)} %get-tuple-element.178), channel_id=1, source_target_pairs={{0,1},{1,0},{2,3},{3,2},{4,5},{5,4},{6,7},{7,6},{8,9},{9,8},{10,11... | collective-permute-start | bytes 49160 | tf_op jit(solution)/shard_map/ppermute | solution.py:591
  32.4 5.4 %collective-permute-start.25 = (f32[32,128]{1,0:T(8,128)S(1)}, f32[32,128]{1,0:T(8,128)S(1)}, u32[]{:S(2)}, u32[]{:S(2)}) collective-permute-start(f32[32,128]{1,0:T(8,128)S(1)} %get-tuple-element.179), channel_id=1, source_target_pairs={{0,32},{1,2},{2,1},{3,4},{4,3},{5,6},{6,5},{7,8},{8,7},{9,10},{10,... | collective-permute-start | bytes 49160 | tf_op jit(solution)/shard_map/ppermute | solution.py:603
  34.9 3.7 %collective-permute-start.26 = (f32[32,128]{1,0:T(8,128)S(1)}, f32[32,128]{1,0:T(8,128)S(1)}, u32[]{:S(2)}, u32[]{:S(2)}) collective-permute-start(f32[32,128]{1,0:T(8,128)S(1)} %get-tuple-element.180), channel_id=1, source_target_pairs={{0,32},{32,0},{64,96},{96,64},{1,33},{33,1},{65,97},{97,65},{2,34}... | collective-permute-start | bytes 49160 | tf_op jit(solution)/shard_map/ppermute | solution.py:615
  36.9 1.7 %collective-permute-start.27 = (f32[32,128]{1,0:T(8,128)S(1)}, f32[32,128]{1,0:T(8,128)S(1)}, u32[]{:S(2)}, u32[]{:S(2)}) collective-permute-start(f32[32,128]{1,0:T(8,128)S(1)} %get-tuple-element.181), channel_id=1, source_target_pairs={{0,1},{1,0},{2,3},{3,2},{4,5},{5,4},{6,7},{7,6},{8,9},{9,8},{10,11... | collective-permute-start | bytes 49160 | tf_op jit(solution)/shard_map/ppermute | solution.py:616
  41.4 3.0 %collective-permute-start.28 = (f32[32,128]{1,0:T(8,128)S(1)}, f32[32,128]{1,0:T(8,128)S(1)}, u32[]{:S(2)}, u32[]{:S(2)}) collective-permute-start(f32[32,128]{1,0:T(8,128)S(1)} %get-tuple-element.183), channel_id=1, source_target_pairs={{0,1},{1,0},{2,3},{3,2},{4,5},{5,4},{6,7},{7,6},{8,9},{9,8},{10,11... | collective-permute-start | bytes 49160 | tf_op jit(solution)/shard_map/ppermute | solution.py:591
  41.5 3.8 %collective-permute-start.29 = (f32[32,128]{1,0:T(8,128)S(1)}, f32[32,128]{1,0:T(8,128)S(1)}, u32[]{:S(2)}, u32[]{:S(2)}) collective-permute-start(f32[32,128]{1,0:T(8,128)S(1)} %get-tuple-element.184), channel_id=1, source_target_pairs={{0,32},{32,0},{64,96},{96,64},{1,33},{33,1},{65,97},{97,65},{2,34}... | collective-permute-start | bytes 49160 | tf_op jit(solution)/shard_map/ppermute | solution.py:615
  43.6 1.7 %collective-permute-start.30 = (f32[32,128]{1,0:T(8,128)S(1)}, f32[32,128]{1,0:T(8,128)S(1)}, u32[]{:S(2)}, u32[]{:S(2)}) collective-permute-start(f32[32,128]{1,0:T(8,128)S(1)} %get-tuple-element.185), channel_id=1, source_target_pairs={{0,1},{1,0},{2,3},{3,2},{4,5},{5,4},{6,7},{7,6},{8,9},{9,8},{10,11... | collective-permute-start | bytes 49160 | tf_op jit(solution)/shard_map/ppermute | solution.py:616
  45.5 5.7 %collective-permute-start.31 = (f32[96,128]{1,0:T(8,128)S(1)}, f32[96,128]{1,0:T(8,128)S(1)}, u32[]{:S(2)}, u32[]{:S(2)}) collective-permute-start(f32[96,128]{1,0:T(8,128)S(1)} %get-tuple-element.187), channel_id=1, source_target_pairs={{0,32},{1,2},{2,1},{3,4},{4,3},{5,6},{6,5},{7,8},{8,7},{9,10},{10,... | collective-permute-start | bytes 147464 | tf_op jit(solution)/shard_map/ppermute | solution.py:603
  46.7 1.2 %collective-permute-start.32 = (f32[64,128]{1,0:T(8,128)S(1)}, f32[64,128]{1,0:T(8,128)S(1)}, u32[]{:S(2)}, u32[]{:S(2)}) collective-permute-start(f32[64,128]{1,0:T(8,128)S(1)} %get-tuple-element.188.ma), channel_id=1, source_target_pairs={{0,1},{1,0},{2,3},{3,2},{4,5},{5,4},{6,7},{7,6},{8,9},{9,8},{10,11... | collective-permute-start | bytes 98312 | tf_op jit(solution)/shard_map/ppermute | solution.py:591
  52.2 4.3 %collective-permute-start.33 = (f32[8,128]{1,0:T(8,128)S(1)}, f32[8,128]{1,0:T(8,128)S(1)}, u32[]{:S(2)}, u32[]{:S(2)}) collective-permute-start(f32[8,128]{1,0:T(8,128)S(1)} %get-tuple-element.194), channel_id=1, source_target_pairs={{0,1},{1,0},{2,3},{3,2},{4,5},{5,4},{6,7},{7,6},{8,9},{9,8},{10,11... | collective-permute-start | bytes 12296 | tf_op jit(solution)/shard_map/ppermute | solution.py:591
  52.3 4.2 %collective-permute-start.34 = (f32[8,128]{1,0:T(8,128)S(1)}, f32[8,128]{1,0:T(8,128)S(1)}, u32[]{:S(2)}, u32[]{:S(2)}) collective-permute-start(f32[8,128]{1,0:T(8,128)S(1)} %get-tuple-element.195), channel_id=1, source_target_pairs={{0,32},{32,0},{64,96},{96,64},{1,33},{33,1},{65,97},{97,65},{2,34}... | collective-permute-start | bytes 12296 | tf_op jit(solution)/shard_map/ppermute | solution.py:615
  54.7 1.8 %collective-permute-start.35 = (f32[8,128]{1,0:T(8,128)S(1)}, f32[8,128]{1,0:T(8,128)S(1)}, u32[]{:S(2)}, u32[]{:S(2)}) collective-permute-start(f32[8,128]{1,0:T(8,128)S(1)} %get-tuple-element.196), channel_id=1, source_target_pairs={{0,1},{1,0},{2,3},{3,2},{4,5},{5,4},{6,7},{7,6},{8,9},{9,8},{10,11... | collective-permute-start | bytes 12296 | tf_op jit(solution)/shard_map/ppermute | solution.py:616
  59.3 5.3 %collective-permute-start.6 = (f32[32,128]{1,0:T(8,128)S(1)}, f32[32,128]{1,0:T(8,128)S(1)}, u32[]{:S(2)}, u32[]{:S(2)}) collective-permute-start(f32[32,128]{1,0:T(8,128)S(1)} %get-tuple-element.83), channel_id=1, source_target_pairs={{0,1},{1,0},{2,3},{3,2},{4,5},{5,4},{6,7},{7,6},{8,9},{9,8},{10,11... | collective-permute-start | bytes 49160 | tf_op jit(solution)/shard_map/cond/branch_1_fun/ppermute | solution.py:591
  59.7 5.3 %collective-permute-start.7 = (f32[32,128]{1,0:T(8,128)S(1)}, f32[32,128]{1,0:T(8,128)S(1)}, u32[]{:S(2)}, u32[]{:S(2)}) collective-permute-start(f32[32,128]{1,0:T(8,128)S(1)} %get-tuple-element.84), channel_id=1, source_target_pairs={{0,32},{1,2},{2,1},{3,4},{4,3},{5,6},{6,5},{7,8},{8,7},{9,10},{10,... | collective-permute-start | bytes 49160 | tf_op jit(solution)/shard_map/cond/branch_1_fun/ppermute | solution.py:603
  60.3 4.7 %collective-permute-start.8 = (f32[32,128]{1,0:T(8,128)S(1)}, f32[32,128]{1,0:T(8,128)S(1)}, u32[]{:S(2)}, u32[]{:S(2)}) collective-permute-start(f32[32,128]{1,0:T(8,128)S(1)} %get-tuple-element.85), channel_id=1, source_target_pairs={{0,32},{32,0},{64,96},{96,64},{1,33},{33,1},{65,97},{97,65},{2,34}... | collective-permute-start | bytes 49160 | tf_op jit(solution)/shard_map/cond/branch_1_fun/ppermute | solution.py:615
  62.4 2.7 %collective-permute-start.9 = (f32[32,128]{1,0:T(8,128)S(1)}, f32[32,128]{1,0:T(8,128)S(1)}, u32[]{:S(2)}, u32[]{:S(2)}) collective-permute-start(f32[32,128]{1,0:T(8,128)S(1)} %get-tuple-element.86), channel_id=1, source_target_pairs={{0,1},{1,0},{2,3},{3,2},{4,5},{5,4},{6,7},{7,6},{8,9},{9,8},{10,11... | collective-permute-start | bytes 49160 | tf_op jit(solution)/shard_map/cond/branch_1_fun/ppermute | solution.py:616
  66.3 2.8 %collective-permute-start.10 = (f32[512,128]{1,0:T(8,128)S(1)}, f32[512,128]{1,0:T(8,128)S(1)}, u32[]{:S(2)}, u32[]{:S(2)}) collective-permute-start(f32[512,128]{1,0:T(8,128)S(1)} %get-tuple-element.88), channel_id=1, source_target_pairs={{0,1},{1,0},{2,3},{3,2},{4,5},{5,4},{6,7},{7,6},{8,9},{9,8},{10,11... | collective-permute-start | bytes 786440 | tf_op jit(solution)/shard_map/cond/branch_1_fun/ppermute | solution.py:623
  66.5 7.9 %collective-permute-start.11 = (f32[512,128]{1,0:T(8,128)S(1)}, f32[512,128]{1,0:T(8,128)S(1)}, u32[]{:S(2)}, u32[]{:S(2)}) collective-permute-start(f32[512,128]{1,0:T(8,128)S(1)} %get-tuple-element.89), channel_id=1, source_target_pairs={{0,127},{1,2},{2,1},{3,4},{4,3},{5,6},{6,5},{7,8},{8,7},{9,10},{10... | collective-permute-start | bytes 786440 | tf_op jit(solution)/shard_map/cond/branch_1_fun/ppermute | solution.py:623

commit v2 on v1

--- a/solution.py
+++ b/solution.py
@@ -17,6 +17,7 @@
 RELAX = 0.8
 KEEP = 0.2
 PART = 1.0 / 64.0
+STEP = 264
 LANES = 128
 ROWS = BS * BS
 XC = BS // 4
@@ -123,7 +124,7 @@
     return total
 
 
-def weights_kernel(new_owner, src, inv, owned, src_t, f0, fy, fz, fzs, c0, fx, fyf, czu, czd):
+def weights_kernel(new_owner, src, inv, owned, most, src_t, f0, fy, fz, fzs, c0, fx, fyf, czu, czd):
     row, lane = row_ids(BS), lane_ids(BS)
 
     def load(ref, x, offset):
@@ -172,7 +173,7 @@
     leaving = jnp.where(owner > home, BLK - place, jnp.where(owner < home, place + 1, 0))
     owned[0] = jnp.sum((owner < device).astype(F32)).astype(jnp.int32)
     owned[1] = jnp.sum((owner == device).astype(F32)).astype(jnp.int32)
-    owned[2] = jnp.max(leaving.astype(F32)).astype(jnp.int32)
+    most[0] = jnp.max(leaving.astype(F32)).astype(jnp.int32)
 
 
 def add_faces_y(ref, low, high):
@@ -234,12 +235,9 @@
     def keep(at, value):
         e[at, :] = value
 
-    def middle(i, _):
+    sweep(1, first, keep)
+    for i in range(2, SWEEP_MAX - 1):
         sweep(i, held, keep)
-        return 0
-
-    sweep(1, first, keep)
-    lax.fori_loop(2, SWEEP_MAX - 1, middle, 0)
     sweep(SWEEP_MAX - 1, held, finish)
 
 
@@ -495,7 +493,7 @@
     finish_smooth(place, limit, r, f0, fy, fzs, d, p, p_out, (sa, sb, sc, sd), e)
 
 
-def plane_to_blocks(v, x, out):
+def plane_to_blocks(v, x, out, base):
     lane = lane_ids(8)
     half = lane < 64
     even = (lane // BS) % 2 == 0
@@ -509,17 +507,18 @@
         low, high = u[b], u[b + 1]
         first = jnp.where(even, low, pltpu.roll(high, BS, 1))
         second = jnp.where(even, pltpu.roll(low, LANES - BS, 1), high)
-        out[b * 256 + x * 8 : b * 256 + x * 8 + 8, :] = first
-        out[(b + 1) * 256 + x * 8 : (b + 1) * 256 + x * 8 + 8, :] = second
-
-
-def last_residual_kernel(src, c, f0, fy, fz, p, r, blocks):
+        at = base + b * STEP + x * 8
+        out[at : at + 8, :] = first
+        out[at + STEP : at + STEP + 8, :] = second
+
+
+def last_residual_kernel(src, c, f0, fy, fz, p, r, blocks, *, count):
     t0, here = ZERO(), p[0:BS, :]
     for x in range(BS):
         at = plane(x)
         after = p[after_plane(x), :]
         r[at, :], t0 = residual_plane(src, c, f0, fy, fz, at, t0, here, after)
-        plane_to_blocks(here, x, blocks)
+        plane_to_blocks(here, x, blocks, count * STEP)
         here = after
 
 
@@ -529,59 +528,34 @@
     add_all(place, gx, gy, ra[...], rb[...], rc[...], rd[...], r)
 
     for x in range(BS):
-        plane_to_blocks(r[plane(x), :], x, blocks)
-    size, last = count * 256, (BLK - count) * 256
+        plane_to_blocks(r[plane(x), :], x, blocks, count * STEP)
     for n, ref in enumerate((pblocks, blocks)):
-        for t in range(0, size, 32):
-            low, high = ref[t : t + 32, :], ref[last + t : last + t + 32, :]
-            at = slice(n * size + t, n * size + t + 32)
-            sa[at, :] = pick(even, high, low)
-            sb[at, :] = pick(even, low, high)
-
-
-def place_kernel(owned, own_p, own_r, ra, rb, out_p, out_r, *, count):
+        for b in range(count):
+            for t in range(0, 256, 32):
+                low = (count + b) * STEP + t
+                high = (BLK + b) * STEP + t
+                low, high = ref[low : low + 32, :], ref[high : high + 32, :]
+                at = slice((n * count + b) * 256 + t, (n * count + b) * 256 + t + 32)
+                sa[at, :] = pick(even, high, low)
+                sb[at, :] = pick(even, low, high)
+
+
+def place_kernel(owned, in_p, in_r, ra, rb, out_p, out_r, seq_p, seq_r, *, count):
     place = Place()
     even = place.even[0]
     start, held = owned[0], owned[1]
-    fields = ((0, own_p, out_p), (1, own_r, out_r))
-
-    def fill(ref, base, out, j):
-        for t in range(0, 256, 8):
-            out[t : t + 8, j, :] = ref[pl.ds(pl.multiple_of(base + t, 8), 8), :]
-
-    for j in range(CAP):
-        where = start + j - place.device * BLK
-        used = j < held
-        mine = used & (where >= 0) & (where < BLK)
-        low = used & (where < 0)
-        high = used & (where >= BLK)
-        own_base = jnp.clip(where, 0, BLK - 1) * 256
-        base = jnp.where(
-            low, jnp.clip(where + count, 0, count - 1), jnp.clip(where - BLK, 0, count - 1)
-        ) * 256
-        from_a = (low & jnp.logical_not(even)) | (high & even)
-        from_b = (low & even) | (high & jnp.logical_not(even))
-
-        @pl.when(mine)
-        def _():
-            for n, own, out in fields:
-                fill(own, own_base, out, j)
-
-        @pl.when(from_a)
-        def _():
-            for n, own, out in fields:
-                fill(ra, base + n * count * 256, out, j)
-
-        @pl.when(from_b)
-        def _():
-            for n, own, out in fields:
-                fill(rb, base + n * count * 256, out, j)
-
-        @pl.when(jnp.logical_not(used))
-        def _():
-            for n, own, out in fields:
-                for t in range(0, 256, 8):
-                    out[t : t + 8, j, :] = jnp.zeros((8, LANES), F32)
+    base = jnp.clip(start - place.device * BLK + count, 0, 2 * count) * STEP
+    valid = row_ids(8) < held
+    for n, (seq, out) in enumerate(((seq_p, out_p), (seq_r, out_r))):
+        for b in range(count):
+            for t in range(0, 256, 32):
+                at = slice((n * count + b) * 256 + t, (n * count + b) * 256 + t + 32)
+                low, high = b * STEP + t, (count + BLK + b) * STEP + t
+                seq[low : low + 32, :] = pick(even, rb[at, :], ra[at, :])
+                seq[high : high + 32, :] = pick(even, ra[at, :], rb[at, :])
+        for t in range(256):
+            rows = seq[pl.ds(base + t, 8, stride=STEP), :]
+            out[t, :, :] = jnp.where(valid, rows, 0.0)[0:CAP]
 
 
 BOTH = ("region", "member")
@@ -632,7 +606,7 @@
 
 
 def set_up(new_owner, src, inv):
-    outs = [jax.ShapeDtypeStruct((3,), jnp.int32)] + [
+    outs = [jax.ShapeDtypeStruct((2,), jnp.int32), jax.ShapeDtypeStruct((1,), jnp.int32)] + [
         jax.ShapeDtypeStruct(s, F32) for s in [FULL] * 6 + [TWO] * 2 + [CFIELD] * 2
     ]
     vm, sm = pl.BlockSpec(memory_space=pltpu.VMEM), pl.BlockSpec(memory_space=pltpu.SMEM)
@@ -640,29 +614,38 @@
         weights_kernel,
         out_shape=outs,
         in_specs=[vm] * 3,
-        out_specs=[sm] + [vm] * 10,
+        out_specs=[sm] * 2 + [vm] * 10,
         compiler_params=pltpu.CompilerParams(vmem_limit_bytes=48 << 20),
         cost_estimate=pl.CostEstimate(flops=4000000, bytes_accessed=6 << 20, transcendentals=0),
     )(new_owner.reshape(-1, min(LANES, new_owner.size)), src, inv)
 
 
+def row_shape(count):
+    return ((2 * count + 8) * STEP, LANES)
+
+
 def place_blocks(count, owned, *arrays):
-    slots = (256, CAP, LANES)
-    outs = call(functools.partial(place_kernel, count=count), [slots, slots], arrays, [owned])
-    return tuple(o.transpose(1, 0, 2).reshape(CAP, 256 * LANES) for o in outs)
+    slots, row = (256, CAP, LANES), row_shape(count)
+    body = functools.partial(place_kernel, count=count)
+    outs = call(body, [slots, slots, row, row], arrays, [owned], aliases={0: 2, 1: 3})
+    return tuple(o.transpose(1, 0, 2).reshape(CAP, 256 * LANES) for o in outs[:2])
 
 
 def on_device(source, inverse_density, block_level, level_sweeps, new_owner):
     region, member = lax.axis_index("region"), lax.axis_index("member")
     levels = (block_level, level_sweeps)
-    edge = jnp.where(member % 2 == 0, BS - 1, 0)
-    ia = lax.dynamic_slice_in_dim(inverse_density[1], edge, 1, axis=1)[:, 0]
-    ib = lax.dynamic_slice_in_dim(inverse_density[1], BS - 1 - edge, 1, axis=1)[:, 0]
-    edge = jnp.where(region % 2 == 0, BS - 1, 0)
-    ic = lax.dynamic_slice_in_dim(inverse_density[0], edge, 1, axis=0)[0]
-    id_ = lax.dynamic_slice_in_dim(inverse_density[0], BS - 1 - edge, 1, axis=0)[0]
-    halos = swap_faces(ia, ib, ic, id_)
-    owned, src, f0, fy, fz, fzs, c0, fx, fyf, czu, czd = set_up(
+    edge_y = jnp.where(member % 2 == 0, BS - 1, 0)
+    edge_x = jnp.where(region % 2 == 0, BS - 1, 0)
+
+    def face(direction, x, y):
+        extent = (1, BS, 1, LANES) if direction == 1 else (1, 1, BS, LANES)
+        return lax.dynamic_slice(inverse_density, (direction, x, y, 0), extent).reshape(FACE)
+
+    faces = (
+        face(1, 0, edge_y), face(1, 0, BS - 1 - edge_y), face(0, edge_x, 0), face(0, BS - 1 - edge_x, 0)
+    )
+    halos = swap_faces(*lax.optimization_barrier(faces))
+    owned, most, src, f0, fy, fz, fzs, c0, fx, fyf, czu, czd = set_up(
         new_owner, source.reshape(ROWS, LANES), inverse_density.reshape(3 * ROWS, LANES)
     )
     c, d, gx, gy, p, *sends = call(
@@ -732,18 +715,20 @@
 
     def tail(count, p, sends, fine, gx, gy, owned):
         halos = swap_faces(*sends)
-        ri, blocks_p = call(last_residual_kernel, [FULL, FULL], [*fine, p])
+        row = row_shape(count)
+        body = functools.partial(last_residual_kernel, count=count)
+        ri, blocks_p = call(body, [FULL, row], [*fine, p])
         part = (2 * count * 256, LANES)
         _, blocks_r, sa, sb = call(
             functools.partial(final_kernel, count=count),
-            [FULL, FULL, part, part],
+            [FULL, row, part, part],
             [ri, gx, gy, *halos, blocks_p],
             aliases={0: 0},
         )
         return place_blocks(count, owned, blocks_p, blocks_r, *swap_blocks(sa, sb))
 
     return lax.cond(
-        owned[2] <= 1,
+        most.reshape(()) <= 1,
         functools.partial(tail, 1),
         functools.partial(tail, BLK),
         p, sends, fine, gx, gy, owned,

time: 77.4 us -> 76.8 us (level)
  local copies, waits for them, and re-layouts: 2.07 us -> 4.88 us
  starting transfers between devices: 29.1 us -> 26.9 us
  Pallas kernels: 24 us -> 22.2 us
    ppermute x5, starting transfers between devices: 9.91 us -> 6.22 us  [swap_far(): return lax.ppermute(value, BOTH, pairs)]
    unnamed x10, local copies, waits for them, and re-layouts: 0.03 us -> 3.14 us
    ppermute x5, waiting for transfers between devices: 7.58 us -> 10.4 us  [swap_far(): return lax.ppermute(value, BOTH, pairs)]
    ppermute x7, waiting for transfers between devices: 4.94 us -> 2.75 us  [swap_regions(): inner = lax.ppermute(inner, 'region', [(i, i ^ 1) for i in range(regions)])]
    slice x2 -> x0, local copies, waits for them, and re-layouts: 1.99 us -> none  [the longest x1 1.41 us: on_device(): ic = lax.dynamic_slice_in_dim(inverse_density[0], edge, 1, axis=0)[0]]
    pallas_call x17, Pallas kernels: 23 us -> 21.2 us  [call(): pl.pallas_call(body, out_shape=outs, in_specs=[pl.BlockSpec(memory_space=...]
    ppermute x7, starting transfers between devices: 14.5 us -> 15.7 us  [swap_regions(): inner = lax.ppermute(inner, 'region', [(i, i ^ 1) for i in range(regions)])]
    dynamic_slice x1, local copies, waits for them, and re-layouts: 0.04 us -> 0.99 us  [face(): lax.dynamic_slice(inverse_density, (direction, x, y, 0), extent)]
  transfers between devices with their start and end apart: 30 -> 30, of which waited for: 12 -> 10; matrix products, arithmetic and copies ran while one was open for 1% -> 0% of each run, Pallas kernels for 8% -> 8%
where the time goes in v2:
time: 76.8 us; the launch traced here: 76.5 us
  starting transfers between devices  26.9 us (35%)
  Pallas kernels  22.2 us (29%)
  waiting for transfers between devices  20.8 us (27%)
  local copies, waits for them, and re-layouts  4.88 us (6%)
  between operations  1.57 us (2%)
    pallas_call x17, Pallas kernels, call(): pl.pallas_call(body, out_shape=outs, in_specs=[pl.BlockSpec(memory_space=...  21.2 us
    ppermute x7, starting transfers between devices, swap_regions(): inner = lax.ppermute(inner, 'region', [(i, i ^ 1) for i in range(regions)])  15.7 us
    ppermute x5, waiting for transfers between devices, swap_far(): return lax.ppermute(value, BOTH, pairs)  10.4 us
    ppermute x5, starting transfers between devices, swap_far(): return lax.ppermute(value, BOTH, pairs)  6.22 us
    ppermute x2, waiting for transfers between devices, swap_blocks(): return (lax.ppermute(first, BOTH, inner), lax.ppermute(second, BOTH, outer))  5.18 us
    ppermute x2, starting transfers between devices, swap_blocks(): return (lax.ppermute(first, BOTH, inner), lax.ppermute(second, BOTH, outer))  3.31 us
    unnamed x10, local copies, waits for them, and re-layouts  3.14 us
    ppermute x7, waiting for transfers between devices, swap_regions(): inner = lax.ppermute(inner, 'region', [(i, i ^ 1) for i in range(regions)])  2.75 us
  transfers between devices with their start and end apart: 30, of which 10 were waited for; matrix products, arithmetic and copies ran while one was open for 0% of the time, Pallas kernels for 8%

profile of v2, /device:TPU:6, one launch (start us, length us, event | category | flops | bytes accessed | tf_op | source)
XLA Modules:
  0.0 76.5 jit_solution(12001631502360935330)
XLA Ops:
  0.7 0.7 dynamic-slice_bitcast_fusion
  1.4 1.0 %constant_dynamic-slice_fusion = (f32[1,32,1,128]{3,2,1,0:T(1,128)S(1)}, f32[1,32,1,128]{3,2,1,0:T(1,128)S(1)}) fusion(f32[3,32,32,128]{3,2,1,0:T(8,128)} %param.8, s32[]{:T(128)S(6)} %select_n.28, s32[]{:T(128)S(6)} %select_n.27), kind=kLoop, calls=%fused_computation.2 | loop fusion | bytes 65544 | tf_op jit(solution)/shard_map/dynamic_slice | solution.py:642
  2.4 0.1 collective-permute-start.12
  2.5 3.4 %collective-permute-start.13 = (f32[32,128]{1,0:T(8,128)S(1)}, f32[32,128]{1,0:T(8,128)S(1)}, u32[]{:S(2)}, u32[]{:S(2)}) collective-permute-start(f32[32,128]{1,0:T(8,128)S(1)} %bitcast.25), channel_id=1, source_target_pairs={{0,32},{1,2},{2,1},{3,4},{4,3},{5,6},{6,5},{7,8},{8,7},{9,10},{10,... | collective-permute-start | bytes 49160 | tf_op jit(solution)/shard_map/ppermute | solution.py:577
  5.9 1.9 %collective-permute-start.14 = (f32[32,128]{1,0:T(8,128)S(1)}, f32[32,128]{1,0:T(8,128)S(1)}, u32[]{:S(2)}, u32[]{:S(2)}) collective-permute-start(f32[32,128]{1,0:T(8,128)S(1)} %get-tuple-element.163), channel_id=1, source_target_pairs={{0,32},{32,0},{64,96},{96,64},{1,33},{33,1},{65,97},{97,65},{2,34}... | collective-permute-start | bytes 49160 | tf_op jit(solution)/shard_map/ppermute | solution.py:589
  7.8 1.4 %copy-done.3 = f32[3,32,32,128]{3,2,1,0:T(8,128)S(1)} copy-done((f32[3,32,32,128]{3,2,1,0:T(8,128)S(1)}, f32[3,32,32,128]{3,2,1,0:T(8,128)}, u32[]{:S(2)}) %copy-start.3) | copy-done | bytes 1572888
  9.2 1.0 %copy-done.4 = f32[32,32,128]{2,1,0:T(8,128)S(1)} copy-done((f32[32,32,128]{2,1,0:T(8,128)S(1)}, f32[32,32,128]{2,1,0:T(8,128)}, u32[]{:S(2)}) %copy-start.4) | copy-done | bytes 524312
  10.3 0.7 copy-done.7
  10.9 1.0 %shard_map.72 = (s32[2]{0:T(128)S(1)}, s32[1]{0:T(128)}, f32[1024,128]{1,0:T(8,128)S(1)}, f32[1024,128]{1,0:T(8,128)S(1)}, f32[1024,128]{1,0:T(8,128)S(1)}, /*in...) custom-call(s32[4,128]{1,0:T(4,128)S(1)} %bitcast.24, ...), custom_call_target="tpu_custom_call" | custom-call | flops 4000000 | bytes 6291456 | tf_op jit(solution)/shard_map/pallas_call | solution.py:613
  12.0 0.0 collective-permute-done.14.rc
  12.0 0.0 collective-permute-done.15.rd
  12.0 2.3 %shard_map.73 = (f32[1024,128]{1,0:T(8,128)S(1)}, f32[1024,128]{1,0:T(8,128)S(1)}, f32[64,128]{1,0:T(8,128)S(1)}, f32[64,128]{1,0:T(8,128)S(1)}, f32[1024,128]{1...) custom-call(s32[4]{0:T(128)S(1)} %copy-done.5, ...), custom_call_target="tpu_custom_call", output_to_operand_aliasing={{0}: (6, {})} | custom-call | flops 2000000 | bytes 4456448 | tf_op jit(solution)/shard_map/pallas_call | solution.py:36
  14.4 0.6 collective-permute-start.16
  14.9 3.1 %collective-permute-start.17 = (f32[32,128]{1,0:T(8,128)S(1)}, f32[32,128]{1,0:T(8,128)S(1)}, u32[]{:S(2)}, u32[]{:S(2)}) collective-permute-start(f32[32,128]{1,0:T(8,128)S(1)} %get-tuple-element.171), channel_id=1, source_target_pairs={{0,32},{32,0},{64,96},{96,64},{1,33},{33,1},{65,97},{97,65},{2,34}... | collective-permute-start | bytes 49160 | tf_op jit(solution)/shard_map/ppermute | solution.py:589
  18.1 0.2 collective-permute-start.18
  18.2 0.6 shard_map.74.qi
  18.9 0.5 shard_map.75.rest_0_
  19.4 0.4 collective-permute-done.17.rc
  19.8 0.2 shard_map.76
  20.0 0.4 collective-permute-start.19
  20.4 1.3 %collective-permute-done.20.qa = f32[128,128]{1,0:T(8,128)S(1)} collective-permute-done((f32[128,128]{1,0:T(8,128)S(1)}, f32[128,128]{1,0:T(8,128)S(1)}, u32[]{:S(2)}, u32[]{:S(2)}) %collective-permute-start.20) | collective-permute-done | bytes 65568 | tf_op jit(solution)/shard_map/ppermute | solution.py:565
  21.6 4.4 %collective-permute-done.19.qb = f32[160,128]{1,0:T(8,128)S(1)} collective-permute-done((f32[160,128]{1,0:T(8,128)S(1)}, f32[160,128]{1,0:T(8,128)S(1)}, u32[]{:S(2)}, u32[]{:S(2)}) %collective-permute-start.19) | collective-permute-done | bytes 81952 | tf_op jit(solution)/shard_map/ppermute | solution.py:577
  26.0 1.3 %shard_map.77 = (f32[64,128]{1,0:T(8,128)S(1)}, f32[8,128]{1,0:T(8,128)S(1)}, f32[8,128]{1,0:T(8,128)S(1)}, f32[8,128]{1,0:T(8,128)S(1)}, f32[8,128]{1,0:T(8,128)S(1)}, /*index=5*/f32[768,128]{1,0:T(8,128)S(1)}) custom-call(f32[128,128]{1,0:T(8,128)S(1)} %get-tuple-element.177.ma, f32[128,128]{1,0:T(8,128)S(1)} %collective-permute-done.20.qa, ...), custom_call_target="tpu_custom_call" | custom-call | flops 2000000 | bytes 704512 | tf_op jit(solution)/shard_map/pallas_call | solution.py:36
  27.3 0.1 collective-permute-start.21
  27.4 2.2 %collective-permute-start.22 = (f32[8,128]{1,0:T(8,128)S(1)}, f32[8,128]{1,0:T(8,128)S(1)}, u32[]{:S(2)}, u32[]{:S(2)}) collective-permute-start(f32[8,128]{1,0:T(8,128)S(1)} %get-tuple-element.184), channel_id=1, source_target_pairs={{0,32},{32,0},{64,96},{96,64},{1,33},{33,1},{65,97},{97,65},{2,34}... | collective-permute-start | bytes 12296 | tf_op jit(solution)/shard_map/ppermute | solution.py:589
  29.6 0.2 collective-permute-start.23
  29.8 0.4 shard_map.78
  30.1 0.0 collective-permute-done.21.ka
  30.1 1.1 %collective-permute-done.22.kc = f32[8,128]{1,0:T(8,128)S(1)} collective-permute-done((f32[8,128]{1,0:T(8,128)S(1)}, f32[8,128]{1,0:T(8,128)S(1)}, u32[]{:S(2)}, u32[]{:S(2)}) %collective-permute-start.22) | collective-permute-done | bytes 4128 | tf_op jit(solution)/shard_map/ppermute | solution.py:589
  31.2 2.5 %shard_map.79 = (f32[1024,128]{1,0:T(8,128)S(1)}, f32[1024,128]{1,0:T(8,128)S(1)}, f32[32,128]{1,0:T(8,128)S(1)}, f32[32,128]{1,0:T(8,128)S(1)}, f32[32,128]{1,0:T(8,128)S(1)}, /*index=5*/f32[32,128]{1,0:T(8,128)S(1)}) custom-call(s32[4]{0:T(128)S(1)} %copy-done.5, s32[3]{0:T(128)S(1)} %copy-done.6, ...), custom_call_target="tpu_custom_call", output_to_operand_aliasing={{0}: (2, {})} | custom-call | flops 2000000 | bytes 4386816 | tf_op jit(solution)/shard_map/pallas_call | solution.py:36
  33.7 0.1 collective-permute-start.24
  33.8 0.6 collective-permute-start.25
  34.4 2.0 %collective-permute-start.26 = (f32[32,128]{1,0:T(8,128)S(1)}, f32[32,128]{1,0:T(8,128)S(1)}, u32[]{:S(2)}, u32[]{:S(2)}) collective-permute-start(f32[32,128]{1,0:T(8,128)S(1)} %get-tuple-element.189), channel_id=1, source_target_pairs={{0,32},{32,0},{64,96},{96,64},{1,33},{33,1},{65,97},{97,65},{2,34}... | collective-permute-start | bytes 49160 | tf_op jit(solution)/shard_map/ppermute | solution.py:589
  36.5 0.0 collective-permute-start.27
  36.5 0.4 shard_map.80.ri
  36.9 2.3 %collective-permute-done.25.rb = f32[32,128]{1,0:T(8,128)S(1)} collective-permute-done((f32[32,128]{1,0:T(8,128)S(1)}, f32[32,128]{1,0:T(8,128)S(1)}, u32[]{:S(2)}, u32[]{:S(2)}) %collective-permute-start.25) | collective-permute-done | bytes 16416 | tf_op jit(solution)/shard_map/ppermute | solution.py:577
  39.2 2.5 %shard_map.81 = (f32[1024,128]{1,0:T(8,128)S(1)}, f32[1024,128]{1,0:T(8,128)S(1)}, f32[32,128]{1,0:T(8,128)S(1)}, f32[32,128]{1,0:T(8,128)S(1)}, f32[32,128]{1,0:T(8,128)S(1)}, /*index=5*/f32[32,128]{1,0:T(8,128)S(1)}) custom-call(s32[4]{0:T(128)S(1)} %copy-done.5, s32[3]{0:T(128)S(1)} %copy-done.6, ...), custom_call_target="tpu_custom_call", output_to_operand_aliasing={{0}: (2, {})} | custom-call | flops 2000000 | bytes 4390912 | tf_op jit(solution)/shard_map/pallas_call | solution.py:36
  41.7 0.1 collective-permute-start.28
  41.8 2.2 %collective-permute-start.29 = (f32[32,128]{1,0:T(8,128)S(1)}, f32[32,128]{1,0:T(8,128)S(1)}, u32[]{:S(2)}, u32[]{:S(2)}) collective-permute-start(f32[32,128]{1,0:T(8,128)S(1)} %get-tuple-element.193), channel_id=1, source_target_pairs={{0,32},{32,0},{64,96},{96,64},{1,33},{33,1},{65,97},{97,65},{2,34}... | collective-permute-start | bytes 49160 | tf_op jit(solution)/shard_map/ppermute | solution.py:589
  44.0 0.2 collective-permute-start.30
  44.1 0.6 shard_map.82.qi
  44.8 0.9 %collective-permute-done.29.rc = f32[32,128]{1,0:T(8,128)S(1)} collective-permute-done((f32[32,128]{1,0:T(8,128)S(1)}, f32[32,128]{1,0:T(8,128)S(1)}, u32[]{:S(2)}, u32[]{:S(2)}) %collective-permute-start.29) | collective-permute-done | bytes 16416 | tf_op jit(solution)/shard_map/ppermute | solution.py:589
  45.7 0.2 shard_map.83
  45.9 0.8 %collective-permute-start.31 = (f32[96,128]{1,0:T(8,128)S(1)}, f32[96,128]{1,0:T(8,128)S(1)}, u32[]{:S(2)}, u32[]{:S(2)}) collective-permute-start(f32[96,128]{1,0:T(8,128)S(1)} %get-tuple-element.196), channel_id=1, source_target_pairs={{0,32},{1,2},{2,1},{3,4},{4,3},{5,6},{6,5},{7,8},{8,7},{9,10},{10,... | collective-permute-start | bytes 147464 | tf_op jit(solution)/shard_map/ppermute | solution.py:577
  46.7 1.2 %collective-permute-done.32.qa = f32[64,128]{1,0:T(8,128)S(1)} collective-permute-done((f32[64,128]{1,0:T(8,128)S(1)}, f32[64,128]{1,0:T(8,128)S(1)}, u32[]{:S(2)}, u32[]{:S(2)}) %collective-permute-start.32) | collective-permute-done | bytes 32800 | tf_op jit(solution)/shard_map/ppermute | solution.py:565
  47.9 3.7 %collective-permute-done.31.qb = f32[96,128]{1,0:T(8,128)S(1)} collective-permute-done((f32[96,128]{1,0:T(8,128)S(1)}, f32[96,128]{1,0:T(8,128)S(1)}, u32[]{:S(2)}, u32[]{:S(2)}) %collective-permute-start.31) | collective-permute-done | bytes 49184 | tf_op jit(solution)/shard_map/ppermute | solution.py:577
  51.6 0.9 %shard_map.84 = (f32[64,128]{1,0:T(8,128)S(1)}, f32[8,128]{1,0:T(8,128)S(1)}, f32[8,128]{1,0:T(8,128)S(1)}, f32[8,128]{1,0:T(8,128)S(1)}, f32[8,128]{1,0:T(8,128)S(1)}) custom-call(f32[64,128]{1,0:T(8,128)S(1)} %get-tuple-element.197.ma, f32[64,128]{1,0:T(8,128)S(1)} %collective-permute-done.32.qa, f32[96,128]{1,0:T(8,128)S(1)} %collective-permute-done.31.qb, ...), custom_call_target="tpu_custom_call" | custom-call | flops 2000000 | bytes 606208 | tf_op jit(solution)/shard_map/pallas_call | solution.py:36
  52.5 0.1 collective-permute-start.33
  52.6 2.2 %collective-permute-start.34 = (f32[8,128]{1,0:T(8,128)S(1)}, f32[8,128]{1,0:T(8,128)S(1)}, u32[]{:S(2)}, u32[]{:S(2)}) collective-permute-start(f32[8,128]{1,0:T(8,128)S(1)} %get-tuple-element.204), channel_id=1, source_target_pairs={{0,32},{32,0},{64,96},{96,64},{1,33},{33,1},{65,97},{97,65},{2,34}... | collective-permute-start | bytes 12296 | tf_op jit(solution)/shard_map/ppermute | solution.py:589
  54.8 0.2 collective-permute-start.35
  55.6 0.4 shard_map.85
  56.0 0.4 collective-permute-done.34.kc
  56.4 2.5 %shard_map.86 = (f32[1024,128]{1,0:T(8,128)S(1)}, f32[1024,128]{1,0:T(8,128)S(1)}, f32[32,128]{1,0:T(8,128)S(1)}, f32[32,128]{1,0:T(8,128)S(1)}, f32[32,128]{1,0:T(8,128)S(1)}, /*index=5*/f32[32,128]{1,0:T(8,128)S(1)}) custom-call(s32[4]{0:T(128)S(1)} %copy-done.5, s32[3]{0:T(128)S(1)} %copy-done.6, ...), custom_call_target="tpu_custom_call", output_to_operand_aliasing={{0}: (2, {})} | custom-call | flops 2000000 | bytes 4386816 | tf_op jit(solution)/shard_map/pallas_call | solution.py:36
  58.9 17.6 %conditional.1 = (f32[6,32768]{1,0:T(8,128)}, f32[6,32768]{1,0:T(8,128)}) conditional(s32[]{:T(128)} %bitcast.15, (f32[1024,128]{1,0:T(8,128)S(1)}, f32[1024,128]{1,0:T(8,128)S(1)}, f32[1024,128]{1,0:T(8,128)S(1)}, f32[1024,128]{1,0:T(8,128)S(1)}, f32[1024,128]{1,0:T(8,128)S(1)}, /*index=5*/f32[1024,128]{1,0:T(8,128)S(1)}, f32[32,128]{1,0:T(8,128)S(1)}, ...), branch_computations={%region_0.1_spmd, %region_1.2_spmd} | conditional | flops 6000000 | bytes 60358996 | solution.py:730
  58.9 0.1 collective-permute-start.6
  59.0 1.0 %collective-permute-start.7 = (f32[32,128]{1,0:T(8,128)S(1)}, f32[32,128]{1,0:T(8,128)S(1)}, u32[]{:S(2)}, u32[]{:S(2)}) collective-permute-start(f32[32,128]{1,0:T(8,128)S(1)} %get-tuple-element.84), channel_id=1, source_target_pairs={{0,32},{1,2},{2,1},{3,4},{4,3},{5,6},{6,5},{7,8},{8,7},{9,10},{10,... | collective-permute-start | bytes 49160 | tf_op jit(solution)/shard_map/cond/branch_1_fun/ppermute | solution.py:577
  60.0 2.0 %collective-permute-start.8 = (f32[32,128]{1,0:T(8,128)S(1)}, f32[32,128]{1,0:T(8,128)S(1)}, u32[]{:S(2)}, u32[]{:S(2)}) collective-permute-start(f32[32,128]{1,0:T(8,128)S(1)} %get-tuple-element.85), channel_id=1, source_target_pairs={{0,32},{32,0},{64,96},{96,64},{1,33},{33,1},{65,97},{97,65},{2,34}... | collective-permute-start | bytes 49160 | tf_op jit(solution)/shard_map/cond/branch_1_fun/ppermute | solution.py:589
  62.1 2.3 %branch_1_fun.3 = (f32[1024,128]{1,0:T(8,128)S(1)}, f32[2640,128]{1,0:T(8,128)S(1)}) custom-call(f32[1024,128]{1,0:T(8,128)S(1)} %get-tuple-element.73.src, f32[1024,128]{1,0:T(8,128)S(1)} %get-tuple-element.74.c, f32[1024,128]{1,0:T(8,128)S(1)} %get-tuple-element.75.f0, f32[1024,128]{1,0:T(8,128)S(1)} %get-tuple-element.76.fy, ...), custom_call_target="tpu_custom_call" | custom-call | flops 2000000 | bytes 5021696 | tf_op jit(solution)/shard_map/cond/branch_1_fun/pallas_call | solution.py:36
  64.3 0.0 collective-permute-done.7.rb
  64.4 1.2 %branch_1_fun.4 = (f32[1024,128]{1,0:T(8,128)S(1)}, f32[2640,128]{1,0:T(8,128)S(1)}, f32[512,128]{1,0:T(8,128)S(1)}, f32[512,128]{1,0:T(8,128)S(1)}) custom-call(f32[1024,128]{1,0:T(8,128)S(1)} %get-tuple-element.80.ri, f32[64,128]{1,0:T(8,128)S(1)} %get-tuple-element.81.gx, f32[64,128]{1,0:T(8,128)S(1)} %get-tuple-element.82.gy, ...), custom_call_target="tpu_custom_call", output_to_operand_aliasing={{0}: (0, {})} | custom-call | flops 2000000 | bytes 4407296 | tf_op jit(solution)/shard_map/cond/branch_1_fun/pallas_call | solution.py:36
  65.6 0.6 collective-permute-start.10
  66.2 2.7 %collective-permute-start.11 = (f32[512,128]{1,0:T(8,128)S(1)}, f32[512,128]{1,0:T(8,128)S(1)}, u32[]{:S(2)}, u32[]{:S(2)}) collective-permute-start(f32[512,128]{1,0:T(8,128)S(1)} %get-tuple-element.89), channel_id=1, source_target_pairs={{0,127},{1,2},{2,1},{3,4},{4,3},{5,6},{6,5},{7,8},{8,7},{9,10},{10... | collective-permute-start | bytes 786440 | tf_op jit(solution)/shard_map/cond/branch_1_fun/ppermute | solution.py:597
  68.9 5.2 %collective-permute-done.11.rb = f32[512,128]{1,0:T(8,128)S(1)} collective-permute-done((f32[512,128]{1,0:T(8,128)S(1)}, f32[512,128]{1,0:T(8,128)S(1)}, u32[]{:S(2)}, u32[]{:S(2)}) %collective-permute-start.11) | collective-permute-done | bytes 262176 | tf_op jit(solution)/shard_map/cond/branch_1_fun/ppermute | solution.py:597
  74.1 2.4 %branch_1_fun.5 = (f32[256,6,128]{2,1,0:T(8,128)}, f32[256,6,128]{2,1,0:T(8,128)}, f32[2640,128]{1,0:T(8,128)S(1)}, f32[2640,128]{1,0:T(8,128)S(1)}) custom-call(s32[2]{0:T(128)S(1)} %get-tuple-element.72.owned, f32[2640,128]{1,0:T(8,128)S(1)} %get-tuple-element.79.pblocks.in_p, ...), custom_call_target="tpu_custom_call", output_to_operand_aliasing={{2}: (1, {}), {3}: (2, {})} | custom-call | flops 2000000 | bytes 7503872 | tf_op jit(solution)/shard_map/cond/branch_1_fun/pallas_call | solution.py:36
  (27 shorter events, 0.1 us)
Async XLA Ops:
  0.6 11.4 %copy-start.6 = (s32[3]{0:T(128)S(1)}, s32[3]{0:T(128)}, u32[]{:S(2)}) copy-start(s32[3]{0:T(128)} %level_sweeps.7) | copy-start | bytes 40
  0.6 11.4 %copy-start.5 = (s32[4]{0:T(128)S(1)}, s32[4]{0:T(128)}, u32[]{:S(2)}) copy-start(s32[4]{0:T(128)} %levels.7) | copy-start | bytes 52
  2.4 9.5 %collective-permute-start.12 = (f32[32,128]{1,0:T(8,128)S(1)}, f32[32,128]{1,0:T(8,128)S(1)}, u32[]{:S(2)}, u32[]{:S(2)}) collective-permute-start(f32[32,128]{1,0:T(8,128)S(1)} %bitcast.26), channel_id=1, source_target_pairs={{0,1},{1,0},{2,3},{3,2},{4,5},{5,4},{6,7},{7,6},{8,9},{9,8},{10,11... | collective-permute-start | bytes 49160 | tf_op jit(solution)/shard_map/ppermute | solution.py:565
  2.5 9.5 %collective-permute-start.13 = (f32[32,128]{1,0:T(8,128)S(1)}, f32[32,128]{1,0:T(8,128)S(1)}, u32[]{:S(2)}, u32[]{:S(2)}) collective-permute-start(f32[32,128]{1,0:T(8,128)S(1)} %bitcast.25), channel_id=1, source_target_pairs={{0,32},{1,2},{2,1},{3,4},{4,3},{5,6},{6,5},{7,8},{8,7},{9,10},{10,... | collective-permute-start | bytes 49160 | tf_op jit(solution)/shard_map/ppermute | solution.py:577
  5.9 6.1 %collective-permute-start.14 = (f32[32,128]{1,0:T(8,128)S(1)}, f32[32,128]{1,0:T(8,128)S(1)}, u32[]{:S(2)}, u32[]{:S(2)}) collective-permute-start(f32[32,128]{1,0:T(8,128)S(1)} %get-tuple-element.163), channel_id=1, source_target_pairs={{0,32},{32,0},{64,96},{96,64},{1,33},{33,1},{65,97},{97,65},{2,34}... | collective-permute-start | bytes 49160 | tf_op jit(solution)/shard_map/ppermute | solution.py:589
  7.8 4.2 %collective-permute-start.15 = (f32[32,128]{1,0:T(8,128)S(1)}, f32[32,128]{1,0:T(8,128)S(1)}, u32[]{:S(2)}, u32[]{:S(2)}) collective-permute-start(f32[32,128]{1,0:T(8,128)S(1)} %get-tuple-element.164), channel_id=1, source_target_pairs={{0,1},{1,0},{2,3},{3,2},{4,5},{5,4},{6,7},{7,6},{8,9},{9,8},{10,11... | collective-permute-start | bytes 49160 | tf_op jit(solution)/shard_map/ppermute | solution.py:590
  7.8 1.4 %copy-start.3 = (f32[3,32,32,128]{3,2,1,0:T(8,128)S(1)}, f32[3,32,32,128]{3,2,1,0:T(8,128)}, u32[]{:S(2)}) copy-start(f32[3,32,32,128]{3,2,1,0:T(8,128)} %param.8) | copy-start | bytes 4718596
  9.2 1.0 %copy-start.4 = (f32[32,32,128]{2,1,0:T(8,128)S(1)}, f32[32,32,128]{2,1,0:T(8,128)}, u32[]{:S(2)}) copy-start(f32[32,32,128]{2,1,0:T(8,128)} %param.7) | copy-start | bytes 1572868
  10.3 0.7 copy-start.7
  14.4 5.0 %collective-permute-start.16 = (f32[32,128]{1,0:T(8,128)S(1)}, f32[32,128]{1,0:T(8,128)S(1)}, u32[]{:S(2)}, u32[]{:S(2)}) collective-permute-start(f32[32,128]{1,0:T(8,128)S(1)} %get-tuple-element.170), channel_id=1, source_target_pairs={{0,1},{1,0},{2,3},{3,2},{4,5},{5,4},{6,7},{7,6},{8,9},{9,8},{10,11... | collective-permute-start | bytes 49160 | tf_op jit(solution)/shard_map/ppermute | solution.py:565
  14.9 4.8 %collective-permute-start.17 = (f32[32,128]{1,0:T(8,128)S(1)}, f32[32,128]{1,0:T(8,128)S(1)}, u32[]{:S(2)}, u32[]{:S(2)}) collective-permute-start(f32[32,128]{1,0:T(8,128)S(1)} %get-tuple-element.171), channel_id=1, source_target_pairs={{0,32},{32,0},{64,96},{96,64},{1,33},{33,1},{65,97},{97,65},{2,34}... | collective-permute-start | bytes 49160 | tf_op jit(solution)/shard_map/ppermute | solution.py:589
  18.1 1.7 %collective-permute-start.18 = (f32[32,128]{1,0:T(8,128)S(1)}, f32[32,128]{1,0:T(8,128)S(1)}, u32[]{:S(2)}, u32[]{:S(2)}) collective-permute-start(f32[32,128]{1,0:T(8,128)S(1)} %get-tuple-element.172), channel_id=1, source_target_pairs={{0,1},{1,0},{2,3},{3,2},{4,5},{5,4},{6,7},{7,6},{8,9},{9,8},{10,11... | collective-permute-start | bytes 49160 | tf_op jit(solution)/shard_map/ppermute | solution.py:590
  20.0 6.1 %collective-permute-start.19 = (f32[160,128]{1,0:T(8,128)S(1)}, f32[160,128]{1,0:T(8,128)S(1)}, u32[]{:S(2)}, u32[]{:S(2)}) collective-permute-start(f32[160,128]{1,0:T(8,128)S(1)} %get-tuple-element.176), channel_id=1, source_target_pairs={{0,32},{1,2},{2,1},{3,4},{4,3},{5,6},{6,5},{7,8},{8,7},{9,10},{10,... | collective-permute-start | bytes 245768 | tf_op jit(solution)/shard_map/ppermute | solution.py:577
  20.4 1.3 %collective-permute-start.20 = (f32[128,128]{1,0:T(8,128)S(1)}, f32[128,128]{1,0:T(8,128)S(1)}, u32[]{:S(2)}, u32[]{:S(2)}) collective-permute-start(f32[128,128]{1,0:T(8,128)S(1)} %get-tuple-element.177.ma), channel_id=1, source_target_pairs={{0,1},{1,0},{2,3},{3,2},{4,5},{5,4},{6,7},{7,6},{8,9},{9,8},{10,11... | collective-permute-start | bytes 196616 | tf_op jit(solution)/shard_map/ppermute | solution.py:565
  27.3 2.8 %collective-permute-start.21 = (f32[8,128]{1,0:T(8,128)S(1)}, f32[8,128]{1,0:T(8,128)S(1)}, u32[]{:S(2)}, u32[]{:S(2)}) collective-permute-start(f32[8,128]{1,0:T(8,128)S(1)} %get-tuple-element.183), channel_id=1, source_target_pairs={{0,1},{1,0},{2,3},{3,2},{4,5},{5,4},{6,7},{7,6},{8,9},{9,8},{10,11... | collective-permute-start | bytes 12296 | tf_op jit(solution)/shard_map/ppermute | solution.py:565
  27.4 3.8 %collective-permute-start.22 = (f32[8,128]{1,0:T(8,128)S(1)}, f32[8,128]{1,0:T(8,128)S(1)}, u32[]{:S(2)}, u32[]{:S(2)}) collective-permute-start(f32[8,128]{1,0:T(8,128)S(1)} %get-tuple-element.184), channel_id=1, source_target_pairs={{0,32},{32,0},{64,96},{96,64},{1,33},{33,1},{65,97},{97,65},{2,34}... | collective-permute-start | bytes 12296 | tf_op jit(solution)/shard_map/ppermute | solution.py:589
  29.6 1.6 %collective-permute-start.23 = (f32[8,128]{1,0:T(8,128)S(1)}, f32[8,128]{1,0:T(8,128)S(1)}, u32[]{:S(2)}, u32[]{:S(2)}) collective-permute-start(f32[8,128]{1,0:T(8,128)S(1)} %get-tuple-element.185), channel_id=1, source_target_pairs={{0,1},{1,0},{2,3},{3,2},{4,5},{5,4},{6,7},{7,6},{8,9},{9,8},{10,11... | collective-permute-start | bytes 12296 | tf_op jit(solution)/shard_map/ppermute | solution.py:590
  33.7 3.1 %collective-permute-start.24 = (f32[32,128]{1,0:T(8,128)S(1)}, f32[32,128]{1,0:T(8,128)S(1)}, u32[]{:S(2)}, u32[]{:S(2)}) collective-permute-start(f32[32,128]{1,0:T(8,128)S(1)} %get-tuple-element.187), channel_id=1, source_target_pairs={{0,1},{1,0},{2,3},{3,2},{4,5},{5,4},{6,7},{7,6},{8,9},{9,8},{10,11... | collective-permute-start | bytes 49160 | tf_op jit(solution)/shard_map/ppermute | solution.py:565
  33.8 5.4 %collective-permute-start.25 = (f32[32,128]{1,0:T(8,128)S(1)}, f32[32,128]{1,0:T(8,128)S(1)}, u32[]{:S(2)}, u32[]{:S(2)}) collective-permute-start(f32[32,128]{1,0:T(8,128)S(1)} %get-tuple-element.188), channel_id=1, source_target_pairs={{0,32},{1,2},{2,1},{3,4},{4,3},{5,6},{6,5},{7,8},{8,7},{9,10},{10,... | collective-permute-start | bytes 49160 | tf_op jit(solution)/shard_map/ppermute | solution.py:577
  34.4 4.7 %collective-permute-start.26 = (f32[32,128]{1,0:T(8,128)S(1)}, f32[32,128]{1,0:T(8,128)S(1)}, u32[]{:S(2)}, u32[]{:S(2)}) collective-permute-start(f32[32,128]{1,0:T(8,128)S(1)} %get-tuple-element.189), channel_id=1, source_target_pairs={{0,32},{32,0},{64,96},{96,64},{1,33},{33,1},{65,97},{97,65},{2,34}... | collective-permute-start | bytes 49160 | tf_op jit(solution)/shard_map/ppermute | solution.py:589
  36.5 2.7 %collective-permute-start.27 = (f32[32,128]{1,0:T(8,128)S(1)}, f32[32,128]{1,0:T(8,128)S(1)}, u32[]{:S(2)}, u32[]{:S(2)}) collective-permute-start(f32[32,128]{1,0:T(8,128)S(1)} %get-tuple-element.190), channel_id=1, source_target_pairs={{0,1},{1,0},{2,3},{3,2},{4,5},{5,4},{6,7},{7,6},{8,9},{9,8},{10,11... | collective-permute-start | bytes 49160 | tf_op jit(solution)/shard_map/ppermute | solution.py:590
  41.7 3.1 %collective-permute-start.28 = (f32[32,128]{1,0:T(8,128)S(1)}, f32[32,128]{1,0:T(8,128)S(1)}, u32[]{:S(2)}, u32[]{:S(2)}) collective-permute-start(f32[32,128]{1,0:T(8,128)S(1)} %get-tuple-element.192), channel_id=1, source_target_pairs={{0,1},{1,0},{2,3},{3,2},{4,5},{5,4},{6,7},{7,6},{8,9},{9,8},{10,11... | collective-permute-start | bytes 49160 | tf_op jit(solution)/shard_map/ppermute | solution.py:565
  41.8 3.9 %collective-permute-start.29 = (f32[32,128]{1,0:T(8,128)S(1)}, f32[32,128]{1,0:T(8,128)S(1)}, u32[]{:S(2)}, u32[]{:S(2)}) collective-permute-start(f32[32,128]{1,0:T(8,128)S(1)} %get-tuple-element.193), channel_id=1, source_target_pairs={{0,32},{32,0},{64,96},{96,64},{1,33},{33,1},{65,97},{97,65},{2,34}... | collective-permute-start | bytes 49160 | tf_op jit(solution)/shard_map/ppermute | solution.py:589
  44.0 1.7 %collective-permute-start.30 = (f32[32,128]{1,0:T(8,128)S(1)}, f32[32,128]{1,0:T(8,128)S(1)}, u32[]{:S(2)}, u32[]{:S(2)}) collective-permute-start(f32[32,128]{1,0:T(8,128)S(1)} %get-tuple-element.194), channel_id=1, source_target_pairs={{0,1},{1,0},{2,3},{3,2},{4,5},{5,4},{6,7},{7,6},{8,9},{9,8},{10,11... | collective-permute-start | bytes 49160 | tf_op jit(solution)/shard_map/ppermute | solution.py:590
  45.9 5.7 %collective-permute-start.31 = (f32[96,128]{1,0:T(8,128)S(1)}, f32[96,128]{1,0:T(8,128)S(1)}, u32[]{:S(2)}, u32[]{:S(2)}) collective-permute-start(f32[96,128]{1,0:T(8,128)S(1)} %get-tuple-element.196), channel_id=1, source_target_pairs={{0,32},{1,2},{2,1},{3,4},{4,3},{5,6},{6,5},{7,8},{8,7},{9,10},{10,... | collective-permute-start | bytes 147464 | tf_op jit(solution)/shard_map/ppermute | solution.py:577
  46.7 1.2 %collective-permute-start.32 = (f32[64,128]{1,0:T(8,128)S(1)}, f32[64,128]{1,0:T(8,128)S(1)}, u32[]{:S(2)}, u32[]{:S(2)}) collective-permute-start(f32[64,128]{1,0:T(8,128)S(1)} %get-tuple-element.197.ma), channel_id=1, source_target_pairs={{0,1},{1,0},{2,3},{3,2},{4,5},{5,4},{6,7},{7,6},{8,9},{9,8},{10,11... | collective-permute-start | bytes 98312 | tf_op jit(solution)/shard_map/ppermute | solution.py:565
  52.5 3.5 %collective-permute-start.33 = (f32[8,128]{1,0:T(8,128)S(1)}, f32[8,128]{1,0:T(8,128)S(1)}, u32[]{:S(2)}, u32[]{:S(2)}) collective-permute-start(f32[8,128]{1,0:T(8,128)S(1)} %get-tuple-element.203), channel_id=1, source_target_pairs={{0,1},{1,0},{2,3},{3,2},{4,5},{5,4},{6,7},{7,6},{8,9},{9,8},{10,11... | collective-permute-start | bytes 12296 | tf_op jit(solution)/shard_map/ppermute | solution.py:565
  52.6 3.8 %collective-permute-start.34 = (f32[8,128]{1,0:T(8,128)S(1)}, f32[8,128]{1,0:T(8,128)S(1)}, u32[]{:S(2)}, u32[]{:S(2)}) collective-permute-start(f32[8,128]{1,0:T(8,128)S(1)} %get-tuple-element.204), channel_id=1, source_target_pairs={{0,32},{32,0},{64,96},{96,64},{1,33},{33,1},{65,97},{97,65},{2,34}... | collective-permute-start | bytes 12296 | tf_op jit(solution)/shard_map/ppermute | solution.py:589
  54.8 1.6 %collective-permute-start.35 = (f32[8,128]{1,0:T(8,128)S(1)}, f32[8,128]{1,0:T(8,128)S(1)}, u32[]{:S(2)}, u32[]{:S(2)}) collective-permute-start(f32[8,128]{1,0:T(8,128)S(1)} %get-tuple-element.205), channel_id=1, source_target_pairs={{0,1},{1,0},{2,3},{3,2},{4,5},{5,4},{6,7},{7,6},{8,9},{9,8},{10,11... | collective-permute-start | bytes 12296 | tf_op jit(solution)/shard_map/ppermute | solution.py:590
  58.9 5.4 %collective-permute-start.6 = (f32[32,128]{1,0:T(8,128)S(1)}, f32[32,128]{1,0:T(8,128)S(1)}, u32[]{:S(2)}, u32[]{:S(2)}) collective-permute-start(f32[32,128]{1,0:T(8,128)S(1)} %get-tuple-element.83), channel_id=1, source_target_pairs={{0,1},{1,0},{2,3},{3,2},{4,5},{5,4},{6,7},{7,6},{8,9},{9,8},{10,11... | collective-permute-start | bytes 49160 | tf_op jit(solution)/shard_map/cond/branch_1_fun/ppermute | solution.py:565
  59.0 5.3 %collective-permute-start.7 = (f32[32,128]{1,0:T(8,128)S(1)}, f32[32,128]{1,0:T(8,128)S(1)}, u32[]{:S(2)}, u32[]{:S(2)}) collective-permute-start(f32[32,128]{1,0:T(8,128)S(1)} %get-tuple-element.84), channel_id=1, source_target_pairs={{0,32},{1,2},{2,1},{3,4},{4,3},{5,6},{6,5},{7,8},{8,7},{9,10},{10,... | collective-permute-start | bytes 49160 | tf_op jit(solution)/shard_map/cond/branch_1_fun/ppermute | solution.py:577
  60.0 4.3 %collective-permute-start.8 = (f32[32,128]{1,0:T(8,128)S(1)}, f32[32,128]{1,0:T(8,128)S(1)}, u32[]{:S(2)}, u32[]{:S(2)}) collective-permute-start(f32[32,128]{1,0:T(8,128)S(1)} %get-tuple-element.85), channel_id=1, source_target_pairs={{0,32},{32,0},{64,96},{96,64},{1,33},{33,1},{65,97},{97,65},{2,34}... | collective-permute-start | bytes 49160 | tf_op jit(solution)/shard_map/cond/branch_1_fun/ppermute | solution.py:589
  62.1 2.3 %collective-permute-start.9 = (f32[32,128]{1,0:T(8,128)S(1)}, f32[32,128]{1,0:T(8,128)S(1)}, u32[]{:S(2)}, u32[]{:S(2)}) collective-permute-start(f32[32,128]{1,0:T(8,128)S(1)} %get-tuple-element.86), channel_id=1, source_target_pairs={{0,1},{1,0},{2,3},{3,2},{4,5},{5,4},{6,7},{7,6},{8,9},{9,8},{10,11... | collective-permute-start | bytes 49160 | tf_op jit(solution)/shard_map/cond/branch_1_fun/ppermute | solution.py:590
  65.6 3.3 %collective-permute-start.10 = (f32[512,128]{1,0:T(8,128)S(1)}, f32[512,128]{1,0:T(8,128)S(1)}, u32[]{:S(2)}, u32[]{:S(2)}) collective-permute-start(f32[512,128]{1,0:T(8,128)S(1)} %get-tuple-element.88), channel_id=1, source_target_pairs={{0,1},{1,0},{2,3},{3,2},{4,5},{5,4},{6,7},{7,6},{8,9},{9,8},{10,11... | collective-permute-start | bytes 786440 | tf_op jit(solution)/shard_map/cond/branch_1_fun/ppermute | solution.py:597
  66.2 7.9 %collective-permute-start.11 = (f32[512,128]{1,0:T(8,128)S(1)}, f32[512,128]{1,0:T(8,128)S(1)}, u32[]{:S(2)}, u32[]{:S(2)}) collective-permute-start(f32[512,128]{1,0:T(8,128)S(1)} %get-tuple-element.89), channel_id=1, source_target_pairs={{0,127},{1,2},{2,1},{3,4},{4,3},{5,6},{6,5},{7,8},{8,7},{9,10},{10... | collective-permute-start | bytes 786440 | tf_op jit(solution)/shard_map/cond/branch_1_fun/ppermute | solution.py:597

commit v3 on v2

--- a/solution.py
+++ b/solution.py
@@ -17,6 +17,8 @@
 RELAX = 0.8
 KEEP = 0.2
 PART = 1.0 / 64.0
+PIECES = 4
+PIECE = 256 // PIECES
 STEP = 264
 LANES = 128
 ROWS = BS * BS
@@ -540,22 +542,31 @@
                 sb[at, :] = pick(even, low, high)
 
 
-def place_kernel(owned, in_p, in_r, ra, rb, out_p, out_r, seq_p, seq_r, *, count):
+def place_kernel(owned, in_p, in_r, ra, rb, out_p, out_r, seq_p, seq_r, held_p, held_r, sems, *, count):
     place = Place()
     even = place.even[0]
     start, held = owned[0], owned[1]
     base = jnp.clip(start - place.device * BLK + count, 0, 2 * count) * STEP
     valid = row_ids(8) < held
-    for n, (seq, out) in enumerate(((seq_p, out_p), (seq_r, out_r))):
+    copies = []
+    fields = ((seq_p, held_p, out_p), (seq_r, held_r, out_r))
+    for n, (seq, tiles, out) in enumerate(fields):
         for b in range(count):
             for t in range(0, 256, 32):
                 at = slice((n * count + b) * 256 + t, (n * count + b) * 256 + t + 32)
                 low, high = b * STEP + t, (count + BLK + b) * STEP + t
                 seq[low : low + 32, :] = pick(even, rb[at, :], ra[at, :])
                 seq[high : high + 32, :] = pick(even, ra[at, :], rb[at, :])
-        for t in range(256):
-            rows = seq[pl.ds(base + t, 8, stride=STEP), :]
-            out[t, :, :] = jnp.where(valid, rows, 0.0)[0:CAP]
+        for part in range(PIECES):
+            for t in range(part * PIECE, (part + 1) * PIECE):
+                rows = seq[pl.ds(base + t, 8, stride=STEP), :]
+                tiles[t, :, :] = jnp.where(valid, rows, 0.0)[0:CAP]
+            at = pl.ds(part * PIECE, PIECE)
+            copy = pltpu.make_async_copy(tiles.at[at], out.at[at], sems.at[n, part])
+            copy.start()
+            copies.append(copy)
+    for copy in copies:
+        copy.wait()
 
 
 BOTH = ("region", "member")
@@ -624,27 +635,68 @@
     return ((2 * count + 8) * STEP, LANES)
 
 
+def faces_kernel(inv, sa, sb, sc, sd, sems):
+    place = Place()
+    low, high = (0, BS - 1)
+
+    def copies(first, second, axis):
+        if axis == 0:
+            pair = ((inv.at[1, :, first, :], sa), (inv.at[1, :, second, :], sb))
+        else:
+            pair = ((inv.at[0, first], sc), (inv.at[0, second], sd))
+        return [
+            pltpu.make_async_copy(source, to, sems.at[2 * axis + n])
+            for n, (source, to) in enumerate(pair)
+        ]
+
+    for axis in range(2):
+
+        @pl.when(place.even[axis])
+        def _():
+            for copy in copies(high, low, axis):
+                copy.start()
+
+        @pl.when(jnp.logical_not(place.even[axis]))
+        def _():
+            for copy in copies(low, high, axis):
+                copy.start()
+
+    for axis in range(2):
+        for copy in copies(low, high, axis):
+            copy.wait()
+
+
+def density_faces(inverse_density):
+    return pl.pallas_call(
+        faces_kernel,
+        out_shape=[jax.ShapeDtypeStruct(FACE, F32)] * 4,
+        in_specs=[pl.BlockSpec(memory_space=pl.ANY)],
+        out_specs=[pl.BlockSpec(memory_space=pltpu.VMEM)] * 4,
+        scratch_shapes=[pltpu.SemaphoreType.DMA((4,))],
+        cost_estimate=pl.CostEstimate(flops=2000000000, bytes_accessed=131072, transcendentals=0),
+    )(inverse_density)
+
+
 def place_blocks(count, owned, *arrays):
     slots, row = (256, CAP, LANES), row_shape(count)
-    body = functools.partial(place_kernel, count=count)
-    outs = call(body, [slots, slots, row, row], arrays, [owned], aliases={0: 2, 1: 3})
+    vm = pl.BlockSpec(memory_space=pltpu.VMEM)
+    anywhere = pl.BlockSpec(memory_space=pl.ANY)
+    outs = pl.pallas_call(
+        functools.partial(place_kernel, count=count),
+        out_shape=[jax.ShapeDtypeStruct(shape, F32) for shape in (slots, slots, row, row)],
+        in_specs=[pl.BlockSpec(memory_space=pltpu.SMEM)] + [vm] * 4,
+        out_specs=[anywhere] * 2 + [vm] * 2,
+        scratch_shapes=[vmem(*slots), vmem(*slots), pltpu.SemaphoreType.DMA((2, PIECES))],
+        input_output_aliases={1: 2, 2: 3},
+        compiler_params=pltpu.CompilerParams(vmem_limit_bytes=48 << 20),
+        cost_estimate=pl.CostEstimate(flops=2000000, bytes_accessed=6 << 20, transcendentals=0),
+    )(owned, *arrays)
     return tuple(o.transpose(1, 0, 2).reshape(CAP, 256 * LANES) for o in outs[:2])
 
 
 def on_device(source, inverse_density, block_level, level_sweeps, new_owner):
-    region, member = lax.axis_index("region"), lax.axis_index("member")
     levels = (block_level, level_sweeps)
-    edge_y = jnp.where(member % 2 == 0, BS - 1, 0)
-    edge_x = jnp.where(region % 2 == 0, BS - 1, 0)
-
-    def face(direction, x, y):
-        extent = (1, BS, 1, LANES) if direction == 1 else (1, 1, BS, LANES)
-        return lax.dynamic_slice(inverse_density, (direction, x, y, 0), extent).reshape(FACE)
-
-    faces = (
-        face(1, 0, edge_y), face(1, 0, BS - 1 - edge_y), face(0, edge_x, 0), face(0, BS - 1 - edge_x, 0)
-    )
-    halos = swap_faces(*lax.optimization_barrier(faces))
+    halos = swap_faces(*density_faces(inverse_density))
     owned, most, src, f0, fy, fz, fzs, c0, fx, fyf, czu, czd = set_up(
         new_owner, source.reshape(ROWS, LANES), inverse_density.reshape(3 * ROWS, LANES)
     )

time: 76.8 us -> 74.7 us (0.973)
  local copies, waits for them, and re-layouts: 4.88 us -> 0.03 us
  Pallas kernels: 22.2 us -> 23.9 us
  waiting for transfers between devices: 20.8 us -> 21.6 us
    pallas_call x0 -> x2, Pallas kernels: none -> 3.4 us  [the longest x1 1.83 us: place_blocks(): pl.pallas_call(functools.partial(place_kernel, count=count), out_shape=[j...]
    unnamed x10, local copies, waits for them, and re-layouts: 3.14 us -> 0.03 us
    pallas_call x17 -> x16, Pallas kernels: 21.2 us -> 19.5 us  [call(): pl.pallas_call(body, out_shape=outs, in_specs=[pl.BlockSpec(memory_space=...]
    dynamic_slice x1 -> x0, local copies, waits for them, and re-layouts: 0.99 us -> none  [face(): lax.dynamic_slice(inverse_density, (direction, x, y, 0), extent)]
    ppermute x7, waiting for transfers between devices: 2.75 us -> 3.68 us  [swap_regions(): inner = lax.ppermute(inner, 'region', [(i, i ^ 1) for i in range(regions)])]
  transfers between devices with their start and end apart: 30 -> 30, of which waited for: 10 -> 11; matrix products, arithmetic and copies ran while one was open for 0% -> 0% of each run, Pallas kernels for 8% -> 8%
where the time goes in v3:
time: 74.7 us; the launch traced here: 74.5 us
  starting transfers between devices  27.2 us (36%)
  Pallas kernels  23.9 us (32%)
  waiting for transfers between devices  21.6 us (29%)
  between operations  1.64 us (2%)
    pallas_call x16, Pallas kernels, call(): pl.pallas_call(body, out_shape=outs, in_specs=[pl.BlockSpec(memory_space=...  19.5 us
    ppermute x7, starting transfers between devices, swap_regions(): inner = lax.ppermute(inner, 'region', [(i, i ^ 1) for i in range(regions)])  16 us
    ppermute x5, waiting for transfers between devices, swap_far(): return lax.ppermute(value, BOTH, pairs)  9.95 us
    ppermute x5, starting transfers between devices, swap_far(): return lax.ppermute(value, BOTH, pairs)  6.96 us
    ppermute x2, waiting for transfers between devices, swap_blocks(): return (lax.ppermute(first, BOTH, inner), lax.ppermute(second, BOTH, outer))  5.45 us
    ppermute x7, waiting for transfers between devices, swap_regions(): inner = lax.ppermute(inner, 'region', [(i, i ^ 1) for i in range(regions)])  3.68 us
    ppermute x2, starting transfers between devices, swap_blocks(): return (lax.ppermute(first, BOTH, inner), lax.ppermute(second, BOTH, outer))  3.04 us
    ppermute x9, waiting for transfers between devices, swap_near(): lax.ppermute(value, 'member', [(i, i ^ 1) for i in range(lax.axis_size('m...  2.47 us
  transfers between devices with their start and end apart: 30, of which 11 were waited for; matrix products, arithmetic and copies ran while one was open for 0% of the time, Pallas kernels for 8%

profile of v3, /device:TPU:6, one launch (start us, length us, event | category | flops | bytes accessed | tf_op | source)
XLA Modules:
  0.0 74.5 jit_solution(17222315833184560646)
XLA Ops:
  0.7 1.6 %shard_map.73 = (f32[32,128]{1,0:T(8,128)}, f32[32,128]{1,0:T(8,128)}, f32[32,128]{1,0:T(8,128)}, f32[32,128]{1,0:T(8,128)}) custom-call(f32[3,32,32,128]{3,2,1,0:T(8,128)} %inv.1), custom_call_target="tpu_custom_call" | custom-call | flops 2000000000 | bytes 131072 | tf_op jit(solution)/shard_map/pallas_call | solution.py:670
  2.2 0.0 copy-start.5
  2.2 0.0 copy-start.6
  2.3 0.1 collective-permute-start.12
  2.4 3.4 %collective-permute-start.13 = (f32[32,128]{1,0:T(8,128)}, f32[32,128]{1,0:T(8,128)S(1)}, u32[]{:S(2)}, u32[]{:S(2)}) collective-permute-start(f32[32,128]{1,0:T(8,128)} %get-tuple-element.162), channel_id=1, source_target_pairs={{0,32},{1,2},{2,1},{3,4},{4,3},{5,6},{6,5},{7,8},{8,7},{9,10},{10,... | collective-permute-start | bytes 49160 | tf_op jit(solution)/shard_map/ppermute | solution.py:588
  5.7 1.9 %collective-permute-start.14 = (f32[32,128]{1,0:T(8,128)}, f32[32,128]{1,0:T(8,128)S(1)}, u32[]{:S(2)}, u32[]{:S(2)}) collective-permute-start(f32[32,128]{1,0:T(8,128)} %get-tuple-element.163), channel_id=1, source_target_pairs={{0,32},{32,0},{64,96},{96,64},{1,33},{33,1},{65,97},{97,65},{2,34}... | collective-permute-start | bytes 49160 | tf_op jit(solution)/shard_map/ppermute | solution.py:600
  7.7 0.0 collective-permute-start.15
  7.7 1.0 %shard_map.72 = (s32[2]{0:T(128)S(1)}, s32[1]{0:T(128)}, f32[1024,128]{1,0:T(8,128)S(1)}, f32[1024,128]{1,0:T(8,128)S(1)}, f32[1024,128]{1,0:T(8,128)S(1)}, /*in...) custom-call(s32[4,128]{1,0:T(4,128)S(1)} %bitcast.18, ...), custom_call_target="tpu_custom_call" | custom-call | flops 4000000 | bytes 6291456 | tf_op jit(solution)/shard_map/pallas_call | solution.py:624
  8.7 1.0 %collective-permute-done.14.rc = f32[32,128]{1,0:T(8,128)S(1)} collective-permute-done((f32[32,128]{1,0:T(8,128)}, f32[32,128]{1,0:T(8,128)S(1)}, u32[]{:S(2)}, u32[]{:S(2)}) %collective-permute-start.14) | collective-permute-done | bytes 16416 | tf_op jit(solution)/shard_map/ppermute | solution.py:600
  9.7 2.5 %shard_map.74 = (f32[1024,128]{1,0:T(8,128)S(1)}, f32[1024,128]{1,0:T(8,128)S(1)}, f32[64,128]{1,0:T(8,128)S(1)}, f32[64,128]{1,0:T(8,128)S(1)}, f32[1024,128]{1...) custom-call(s32[4]{0:T(128)S(1)} %copy-done.5, ...), custom_call_target="tpu_custom_call", output_to_operand_aliasing={{0}: (6, {})} | custom-call | flops 2000000 | bytes 4456448 | tf_op jit(solution)/shard_map/pallas_call | solution.py:38
  12.2 0.1 collective-permute-start.16
  12.3 3.5 %collective-permute-start.17 = (f32[32,128]{1,0:T(8,128)S(1)}, f32[32,128]{1,0:T(8,128)S(1)}, u32[]{:S(2)}, u32[]{:S(2)}) collective-permute-start(f32[32,128]{1,0:T(8,128)S(1)} %get-tuple-element.171), channel_id=1, source_target_pairs={{0,32},{32,0},{64,96},{96,64},{1,33},{33,1},{65,97},{97,65},{2,34}... | collective-permute-start | bytes 49160 | tf_op jit(solution)/shard_map/ppermute | solution.py:600
  15.8 0.2 collective-permute-start.18
  15.9 0.7 shard_map.75.qi
  16.6 0.5 shard_map.76.rest_0_
  17.1 0.4 collective-permute-done.17.rc
  17.5 0.2 shard_map.77
  17.7 0.4 collective-permute-start.19
  18.1 0.0 collective-permute-start.20
  18.1 1.3 %collective-permute-done.20.qa = f32[128,128]{1,0:T(8,128)S(1)} collective-permute-done((f32[128,128]{1,0:T(8,128)S(1)}, f32[128,128]{1,0:T(8,128)S(1)}, u32[]{:S(2)}, u32[]{:S(2)}) %collective-permute-start.20) | collective-permute-done | bytes 65568 | tf_op jit(solution)/shard_map/ppermute | solution.py:576
  19.4 4.4 %collective-permute-done.19.qb = f32[160,128]{1,0:T(8,128)S(1)} collective-permute-done((f32[160,128]{1,0:T(8,128)S(1)}, f32[160,128]{1,0:T(8,128)S(1)}, u32[]{:S(2)}, u32[]{:S(2)}) %collective-permute-start.19) | collective-permute-done | bytes 81952 | tf_op jit(solution)/shard_map/ppermute | solution.py:588
  23.8 1.3 %shard_map.78 = (f32[64,128]{1,0:T(8,128)S(1)}, f32[8,128]{1,0:T(8,128)S(1)}, f32[8,128]{1,0:T(8,128)S(1)}, f32[8,128]{1,0:T(8,128)S(1)}, f32[8,128]{1,0:T(8,128)S(1)}, /*index=5*/f32[768,128]{1,0:T(8,128)S(1)}) custom-call(f32[128,128]{1,0:T(8,128)S(1)} %get-tuple-element.177.ma, f32[128,128]{1,0:T(8,128)S(1)} %collective-permute-done.20.qa, ...), custom_call_target="tpu_custom_call" | custom-call | flops 2000000 | bytes 704512 | tf_op jit(solution)/shard_map/pallas_call | solution.py:38
  25.0 0.1 collective-permute-start.21
  25.1 2.2 %collective-permute-start.22 = (f32[8,128]{1,0:T(8,128)S(1)}, f32[8,128]{1,0:T(8,128)S(1)}, u32[]{:S(2)}, u32[]{:S(2)}) collective-permute-start(f32[8,128]{1,0:T(8,128)S(1)} %get-tuple-element.184), channel_id=1, source_target_pairs={{0,32},{32,0},{64,96},{96,64},{1,33},{33,1},{65,97},{97,65},{2,34}... | collective-permute-start | bytes 12296 | tf_op jit(solution)/shard_map/ppermute | solution.py:600
  27.3 0.2 collective-permute-start.23
  27.5 0.4 shard_map.79
  27.9 0.0 collective-permute-done.21.ka
  27.9 1.0 %collective-permute-done.22.kc = f32[8,128]{1,0:T(8,128)S(1)} collective-permute-done((f32[8,128]{1,0:T(8,128)S(1)}, f32[8,128]{1,0:T(8,128)S(1)}, u32[]{:S(2)}, u32[]{:S(2)}) %collective-permute-start.22) | collective-permute-done | bytes 4128 | tf_op jit(solution)/shard_map/ppermute | solution.py:600
  28.9 2.6 %shard_map.80 = (f32[1024,128]{1,0:T(8,128)S(1)}, f32[1024,128]{1,0:T(8,128)S(1)}, f32[32,128]{1,0:T(8,128)S(1)}, f32[32,128]{1,0:T(8,128)S(1)}, f32[32,128]{1,0:T(8,128)S(1)}, /*index=5*/f32[32,128]{1,0:T(8,128)S(1)}) custom-call(s32[4]{0:T(128)S(1)} %copy-done.5, s32[3]{0:T(128)S(1)} %copy-done.6, ...), custom_call_target="tpu_custom_call", output_to_operand_aliasing={{0}: (2, {})} | custom-call | flops 2000000 | bytes 4386816 | tf_op jit(solution)/shard_map/pallas_call | solution.py:38
  31.5 0.1 collective-permute-start.24
  31.6 0.8 %collective-permute-start.25 = (f32[32,128]{1,0:T(8,128)S(1)}, f32[32,128]{1,0:T(8,128)S(1)}, u32[]{:S(2)}, u32[]{:S(2)}) collective-permute-start(f32[32,128]{1,0:T(8,128)S(1)} %get-tuple-element.188), channel_id=1, source_target_pairs={{0,32},{1,2},{2,1},{3,4},{4,3},{5,6},{6,5},{7,8},{8,7},{9,10},{10,... | collective-permute-start | bytes 49160 | tf_op jit(solution)/shard_map/ppermute | solution.py:588
  32.4 2.0 %collective-permute-start.26 = (f32[32,128]{1,0:T(8,128)S(1)}, f32[32,128]{1,0:T(8,128)S(1)}, u32[]{:S(2)}, u32[]{:S(2)}) collective-permute-start(f32[32,128]{1,0:T(8,128)S(1)} %get-tuple-element.189), channel_id=1, source_target_pairs={{0,32},{32,0},{64,96},{96,64},{1,33},{33,1},{65,97},{97,65},{2,34}... | collective-permute-start | bytes 49160 | tf_op jit(solution)/shard_map/ppermute | solution.py:600
  34.5 0.0 collective-permute-start.27
  34.5 0.4 shard_map.81.ri
  34.9 2.1 %collective-permute-done.25.rb = f32[32,128]{1,0:T(8,128)S(1)} collective-permute-done((f32[32,128]{1,0:T(8,128)S(1)}, f32[32,128]{1,0:T(8,128)S(1)}, u32[]{:S(2)}, u32[]{:S(2)}) %collective-permute-start.25) | collective-permute-done | bytes 16416 | tf_op jit(solution)/shard_map/ppermute | solution.py:588
  37.0 0.0 collective-permute-done.26.rc
  37.0 0.0 collective-permute-done.27.rd
  37.0 2.6 %shard_map.82 = (f32[1024,128]{1,0:T(8,128)S(1)}, f32[1024,128]{1,0:T(8,128)S(1)}, f32[32,128]{1,0:T(8,128)S(1)}, f32[32,128]{1,0:T(8,128)S(1)}, f32[32,128]{1,0:T(8,128)S(1)}, /*index=5*/f32[32,128]{1,0:T(8,128)S(1)}) custom-call(s32[4]{0:T(128)S(1)} %copy-done.5, s32[3]{0:T(128)S(1)} %copy-done.6, ...), custom_call_target="tpu_custom_call", output_to_operand_aliasing={{0}: (2, {})} | custom-call | flops 2000000 | bytes 4390912 | tf_op jit(solution)/shard_map/pallas_call | solution.py:38
  39.6 0.1 collective-permute-start.28
  39.7 2.2 %collective-permute-start.29 = (f32[32,128]{1,0:T(8,128)S(1)}, f32[32,128]{1,0:T(8,128)S(1)}, u32[]{:S(2)}, u32[]{:S(2)}) collective-permute-start(f32[32,128]{1,0:T(8,128)S(1)} %get-tuple-element.193), channel_id=1, source_target_pairs={{0,32},{32,0},{64,96},{96,64},{1,33},{33,1},{65,97},{97,65},{2,34}... | collective-permute-start | bytes 49160 | tf_op jit(solution)/shard_map/ppermute | solution.py:600
  41.9 0.2 collective-permute-start.30
  42.1 0.6 shard_map.83.qi
  42.7 0.9 %collective-permute-done.29.rc = f32[32,128]{1,0:T(8,128)S(1)} collective-permute-done((f32[32,128]{1,0:T(8,128)S(1)}, f32[32,128]{1,0:T(8,128)S(1)}, u32[]{:S(2)}, u32[]{:S(2)}) %collective-permute-start.29) | collective-permute-done | bytes 16416 | tf_op jit(solution)/shard_map/ppermute | solution.py:600
  43.7 0.2 shard_map.84
  43.8 1.1 %collective-permute-start.31 = (f32[96,128]{1,0:T(8,128)S(1)}, f32[96,128]{1,0:T(8,128)S(1)}, u32[]{:S(2)}, u32[]{:S(2)}) collective-permute-start(f32[96,128]{1,0:T(8,128)S(1)} %get-tuple-element.196), channel_id=1, source_target_pairs={{0,32},{1,2},{2,1},{3,4},{4,3},{5,6},{6,5},{7,8},{8,7},{9,10},{10,... | collective-permute-start | bytes 147464 | tf_op jit(solution)/shard_map/ppermute | solution.py:588
  44.9 1.2 %collective-permute-done.32.qa = f32[64,128]{1,0:T(8,128)S(1)} collective-permute-done((f32[64,128]{1,0:T(8,128)S(1)}, f32[64,128]{1,0:T(8,128)S(1)}, u32[]{:S(2)}, u32[]{:S(2)}) %collective-permute-start.32) | collective-permute-done | bytes 32800 | tf_op jit(solution)/shard_map/ppermute | solution.py:576
  46.1 3.4 %collective-permute-done.31.qb = f32[96,128]{1,0:T(8,128)S(1)} collective-permute-done((f32[96,128]{1,0:T(8,128)S(1)}, f32[96,128]{1,0:T(8,128)S(1)}, u32[]{:S(2)}, u32[]{:S(2)}) %collective-permute-start.31) | collective-permute-done | bytes 49184 | tf_op jit(solution)/shard_map/ppermute | solution.py:588
  49.5 0.9 %shard_map.85 = (f32[64,128]{1,0:T(8,128)S(1)}, f32[8,128]{1,0:T(8,128)S(1)}, f32[8,128]{1,0:T(8,128)S(1)}, f32[8,128]{1,0:T(8,128)S(1)}, f32[8,128]{1,0:T(8,128)S(1)}) custom-call(f32[64,128]{1,0:T(8,128)S(1)} %get-tuple-element.197.ma, f32[64,128]{1,0:T(8,128)S(1)} %collective-permute-done.32.qa, f32[96,128]{1,0:T(8,128)S(1)} %collective-permute-done.31.qb, ...), custom_call_target="tpu_custom_call" | custom-call | flops 2000000 | bytes 606208 | tf_op jit(solution)/shard_map/pallas_call | solution.py:38
  50.5 0.1 collective-permute-start.33
  50.6 2.2 %collective-permute-start.34 = (f32[8,128]{1,0:T(8,128)S(1)}, f32[8,128]{1,0:T(8,128)S(1)}, u32[]{:S(2)}, u32[]{:S(2)}) collective-permute-start(f32[8,128]{1,0:T(8,128)S(1)} %get-tuple-element.204), channel_id=1, source_target_pairs={{0,32},{32,0},{64,96},{96,64},{1,33},{33,1},{65,97},{97,65},{2,34}... | collective-permute-start | bytes 12296 | tf_op jit(solution)/shard_map/ppermute | solution.py:600
  52.8 0.2 collective-permute-start.35
  53.5 0.4 shard_map.86
  53.9 0.4 collective-permute-done.34.kc
  54.4 2.6 %shard_map.87 = (f32[1024,128]{1,0:T(8,128)S(1)}, f32[1024,128]{1,0:T(8,128)S(1)}, f32[32,128]{1,0:T(8,128)S(1)}, f32[32,128]{1,0:T(8,128)S(1)}, f32[32,128]{1,0:T(8,128)S(1)}, /*index=5*/f32[32,128]{1,0:T(8,128)S(1)}) custom-call(s32[4]{0:T(128)S(1)} %copy-done.5, s32[3]{0:T(128)S(1)} %copy-done.6, ...), custom_call_target="tpu_custom_call", output_to_operand_aliasing={{0}: (2, {})} | custom-call | flops 2000000 | bytes 4386816 | tf_op jit(solution)/shard_map/pallas_call | solution.py:38
  57.0 17.3 %conditional.1 = (f32[6,32768]{1,0:T(8,128)}, f32[6,32768]{1,0:T(8,128)}) conditional(s32[]{:T(128)} %bitcast.15, (f32[1024,128]{1,0:T(8,128)S(1)}, f32[1024,128]{1,0:T(8,128)S(1)}, f32[1024,128]{1,0:T(8,128)S(1)}, f32[1024,128]{1,0:T(8,128)S(1)}, f32[1024,128]{1,0:T(8,128)S(1)}, /*index=5*/f32[1024,128]{1,0:T(8,128)S(1)}, f32[32,128]{1,0:T(8,128)S(1)}, ...), branch_computations={%region_0.0_spmd, %region_1.0_spmd} | conditional | flops 6000000 | bytes 54329684 | solution.py:782
  57.0 0.1 collective-permute-start.6
  57.1 1.3 %collective-permute-start.7 = (f32[32,128]{1,0:T(8,128)S(1)}, f32[32,128]{1,0:T(8,128)S(1)}, u32[]{:S(2)}, u32[]{:S(2)}) collective-permute-start(f32[32,128]{1,0:T(8,128)S(1)} %get-tuple-element.84), channel_id=1, source_target_pairs={{0,32},{1,2},{2,1},{3,4},{4,3},{5,6},{6,5},{7,8},{8,7},{9,10},{10,... | collective-permute-start | bytes 49160 | tf_op jit(solution)/shard_map/cond/branch_1_fun/ppermute | solution.py:588
  58.4 2.0 %collective-permute-start.8 = (f32[32,128]{1,0:T(8,128)S(1)}, f32[32,128]{1,0:T(8,128)S(1)}, u32[]{:S(2)}, u32[]{:S(2)}) collective-permute-start(f32[32,128]{1,0:T(8,128)S(1)} %get-tuple-element.85), channel_id=1, source_target_pairs={{0,32},{32,0},{64,96},{96,64},{1,33},{33,1},{65,97},{97,65},{2,34}... | collective-permute-start | bytes 49160 | tf_op jit(solution)/shard_map/cond/branch_1_fun/ppermute | solution.py:600
  60.4 2.3 %branch_1_fun.3 = (f32[1024,128]{1,0:T(8,128)S(1)}, f32[2640,128]{1,0:T(8,128)S(1)}) custom-call(f32[1024,128]{1,0:T(8,128)S(1)} %get-tuple-element.73.src, f32[1024,128]{1,0:T(8,128)S(1)} %get-tuple-element.74.c, f32[1024,128]{1,0:T(8,128)S(1)} %get-tuple-element.75.f0, f32[1024,128]{1,0:T(8,128)S(1)} %get-tuple-element.76.fy, ...), custom_call_target="tpu_custom_call" | custom-call | flops 2000000 | bytes 5021696 | tf_op jit(solution)/shard_map/cond/branch_1_fun/pallas_call | solution.py:38
  62.8 1.2 %branch_1_fun.4 = (f32[1024,128]{1,0:T(8,128)S(1)}, f32[2640,128]{1,0:T(8,128)S(1)}, f32[512,128]{1,0:T(8,128)S(1)}, f32[512,128]{1,0:T(8,128)S(1)}) custom-call(f32[1024,128]{1,0:T(8,128)S(1)} %get-tuple-element.80.ri, f32[64,128]{1,0:T(8,128)S(1)} %get-tuple-element.81.gx, f32[64,128]{1,0:T(8,128)S(1)} %get-tuple-element.82.gy, ...), custom_call_target="tpu_custom_call", output_to_operand_aliasing={{0}: (0, {})} | custom-call | flops 2000000 | bytes 4407296 | tf_op jit(solution)/shard_map/cond/branch_1_fun/pallas_call | solution.py:38
  64.0 0.6 collective-permute-start.10
  64.6 2.5 %collective-permute-start.11 = (f32[512,128]{1,0:T(8,128)S(1)}, f32[512,128]{1,0:T(8,128)S(1)}, u32[]{:S(2)}, u32[]{:S(2)}) collective-permute-start(f32[512,128]{1,0:T(8,128)S(1)} %get-tuple-element.89), channel_id=1, source_target_pairs={{0,127},{1,2},{2,1},{3,4},{4,3},{5,6},{6,5},{7,8},{8,7},{9,10},{10... | collective-permute-start | bytes 786440 | tf_op jit(solution)/shard_map/cond/branch_1_fun/ppermute | solution.py:608
  67.0 5.5 %collective-permute-done.11.rb = f32[512,128]{1,0:T(8,128)S(1)} collective-permute-done((f32[512,128]{1,0:T(8,128)S(1)}, f32[512,128]{1,0:T(8,128)S(1)}, u32[]{:S(2)}, u32[]{:S(2)}) %collective-permute-start.11) | collective-permute-done | bytes 262176 | tf_op jit(solution)/shard_map/cond/branch_1_fun/ppermute | solution.py:608
  72.5 1.8 %branch_1_fun.5 = (f32[256,6,128]{2,1,0:T(8,128)}, f32[256,6,128]{2,1,0:T(8,128)}, f32[2640,128]{1,0:T(8,128)S(1)}, f32[2640,128]{1,0:T(8,128)S(1)}) custom-call(s32[2]{0:T(128)S(1)} %get-tuple-element.72.owned, f32[2640,128]{1,0:T(8,128)S(1)} %get-tuple-element.79.pblocks.in_p, ...), custom_call_target="tpu_custom_call", output_to_operand_aliasing={{2}: (1, {}), {3}: (2, {})} | custom-call | flops 2000000 | bytes 6291456 | tf_op jit(solution)/shard_map/cond/branch_1_fun/pallas_call | solution.py:684
  (26 shorter events, 0.1 us)
Async XLA Ops:
  0.6 7.0 %copy-start.3 = (f32[3,32,32,128]{3,2,1,0:T(8,128)S(1)}, f32[3,32,32,128]{3,2,1,0:T(8,128)}, u32[]{:S(2)}) copy-start(f32[3,32,32,128]{3,2,1,0:T(8,128)} %inv.1) | copy-start | bytes 4718596
  0.6 7.0 %copy-start.7 = (s32[512]{0:T(512)S(1)}, s32[512]{0:T(512)}, u32[]{:S(2)}) copy-start(s32[512]{0:T(512)} %param.11) | copy-start | bytes 6148
  0.6 7.0 %copy-start.4 = (f32[32,32,128]{2,1,0:T(8,128)S(1)}, f32[32,32,128]{2,1,0:T(8,128)}, u32[]{:S(2)}) copy-start(f32[32,32,128]{2,1,0:T(8,128)} %param.7) | copy-start | bytes 1572868
  2.2 7.5 %copy-start.5 = (s32[4]{0:T(128)S(1)}, s32[4]{0:T(128)}, u32[]{:S(2)}) copy-start(s32[4]{0:T(128)} %levels.7) | copy-start | bytes 52
  2.2 7.4 %copy-start.6 = (s32[3]{0:T(128)S(1)}, s32[3]{0:T(128)}, u32[]{:S(2)}) copy-start(s32[3]{0:T(128)} %level_sweeps.7) | copy-start | bytes 40
  2.3 6.4 %collective-permute-start.12 = (f32[32,128]{1,0:T(8,128)}, f32[32,128]{1,0:T(8,128)S(1)}, u32[]{:S(2)}, u32[]{:S(2)}) collective-permute-start(f32[32,128]{1,0:T(8,128)} %get-tuple-element.161), channel_id=1, source_target_pairs={{0,1},{1,0},{2,3},{3,2},{4,5},{5,4},{6,7},{7,6},{8,9},{9,8},{10,11... | collective-permute-start | bytes 49160 | tf_op jit(solution)/shard_map/ppermute | solution.py:576
  2.4 6.3 %collective-permute-start.13 = (f32[32,128]{1,0:T(8,128)}, f32[32,128]{1,0:T(8,128)S(1)}, u32[]{:S(2)}, u32[]{:S(2)}) collective-permute-start(f32[32,128]{1,0:T(8,128)} %get-tuple-element.162), channel_id=1, source_target_pairs={{0,32},{1,2},{2,1},{3,4},{4,3},{5,6},{6,5},{7,8},{8,7},{9,10},{10,... | collective-permute-start | bytes 49160 | tf_op jit(solution)/shard_map/ppermute | solution.py:588
  5.7 3.9 %collective-permute-start.14 = (f32[32,128]{1,0:T(8,128)}, f32[32,128]{1,0:T(8,128)S(1)}, u32[]{:S(2)}, u32[]{:S(2)}) collective-permute-start(f32[32,128]{1,0:T(8,128)} %get-tuple-element.163), channel_id=1, source_target_pairs={{0,32},{32,0},{64,96},{96,64},{1,33},{33,1},{65,97},{97,65},{2,34}... | collective-permute-start | bytes 49160 | tf_op jit(solution)/shard_map/ppermute | solution.py:600
  7.7 2.0 %collective-permute-start.15 = (f32[32,128]{1,0:T(8,128)}, f32[32,128]{1,0:T(8,128)S(1)}, u32[]{:S(2)}, u32[]{:S(2)}) collective-permute-start(f32[32,128]{1,0:T(8,128)} %get-tuple-element.164), channel_id=1, source_target_pairs={{0,1},{1,0},{2,3},{3,2},{4,5},{5,4},{6,7},{7,6},{8,9},{9,8},{10,11... | collective-permute-start | bytes 49160 | tf_op jit(solution)/shard_map/ppermute | solution.py:601
  12.2 4.9 %collective-permute-start.16 = (f32[32,128]{1,0:T(8,128)S(1)}, f32[32,128]{1,0:T(8,128)S(1)}, u32[]{:S(2)}, u32[]{:S(2)}) collective-permute-start(f32[32,128]{1,0:T(8,128)S(1)} %get-tuple-element.170), channel_id=1, source_target_pairs={{0,1},{1,0},{2,3},{3,2},{4,5},{5,4},{6,7},{7,6},{8,9},{9,8},{10,11... | collective-permute-start | bytes 49160 | tf_op jit(solution)/shard_map/ppermute | solution.py:576
  12.3 5.2 %collective-permute-start.17 = (f32[32,128]{1,0:T(8,128)S(1)}, f32[32,128]{1,0:T(8,128)S(1)}, u32[]{:S(2)}, u32[]{:S(2)}) collective-permute-start(f32[32,128]{1,0:T(8,128)S(1)} %get-tuple-element.171), channel_id=1, source_target_pairs={{0,32},{32,0},{64,96},{96,64},{1,33},{33,1},{65,97},{97,65},{2,34}... | collective-permute-start | bytes 49160 | tf_op jit(solution)/shard_map/ppermute | solution.py:600
  15.8 1.7 %collective-permute-start.18 = (f32[32,128]{1,0:T(8,128)S(1)}, f32[32,128]{1,0:T(8,128)S(1)}, u32[]{:S(2)}, u32[]{:S(2)}) collective-permute-start(f32[32,128]{1,0:T(8,128)S(1)} %get-tuple-element.172), channel_id=1, source_target_pairs={{0,1},{1,0},{2,3},{3,2},{4,5},{5,4},{6,7},{7,6},{8,9},{9,8},{10,11... | collective-permute-start | bytes 49160 | tf_op jit(solution)/shard_map/ppermute | solution.py:601
  17.7 6.1 %collective-permute-start.19 = (f32[160,128]{1,0:T(8,128)S(1)}, f32[160,128]{1,0:T(8,128)S(1)}, u32[]{:S(2)}, u32[]{:S(2)}) collective-permute-start(f32[160,128]{1,0:T(8,128)S(1)} %get-tuple-element.176), channel_id=1, source_target_pairs={{0,32},{1,2},{2,1},{3,4},{4,3},{5,6},{6,5},{7,8},{8,7},{9,10},{10,... | collective-permute-start | bytes 245768 | tf_op jit(solution)/shard_map/ppermute | solution.py:588
  18.1 1.3 %collective-permute-start.20 = (f32[128,128]{1,0:T(8,128)S(1)}, f32[128,128]{1,0:T(8,128)S(1)}, u32[]{:S(2)}, u32[]{:S(2)}) collective-permute-start(f32[128,128]{1,0:T(8,128)S(1)} %get-tuple-element.177.ma), channel_id=1, source_target_pairs={{0,1},{1,0},{2,3},{3,2},{4,5},{5,4},{6,7},{7,6},{8,9},{9,8},{10,11... | collective-permute-start | bytes 196616 | tf_op jit(solution)/shard_map/ppermute | solution.py:576
  25.0 2.9 %collective-permute-start.21 = (f32[8,128]{1,0:T(8,128)S(1)}, f32[8,128]{1,0:T(8,128)S(1)}, u32[]{:S(2)}, u32[]{:S(2)}) collective-permute-start(f32[8,128]{1,0:T(8,128)S(1)} %get-tuple-element.183), channel_id=1, source_target_pairs={{0,1},{1,0},{2,3},{3,2},{4,5},{5,4},{6,7},{7,6},{8,9},{9,8},{10,11... | collective-permute-start | bytes 12296 | tf_op jit(solution)/shard_map/ppermute | solution.py:576
  25.1 3.8 %collective-permute-start.22 = (f32[8,128]{1,0:T(8,128)S(1)}, f32[8,128]{1,0:T(8,128)S(1)}, u32[]{:S(2)}, u32[]{:S(2)}) collective-permute-start(f32[8,128]{1,0:T(8,128)S(1)} %get-tuple-element.184), channel_id=1, source_target_pairs={{0,32},{32,0},{64,96},{96,64},{1,33},{33,1},{65,97},{97,65},{2,34}... | collective-permute-start | bytes 12296 | tf_op jit(solution)/shard_map/ppermute | solution.py:600
  27.3 1.6 %collective-permute-start.23 = (f32[8,128]{1,0:T(8,128)S(1)}, f32[8,128]{1,0:T(8,128)S(1)}, u32[]{:S(2)}, u32[]{:S(2)}) collective-permute-start(f32[8,128]{1,0:T(8,128)S(1)} %get-tuple-element.185), channel_id=1, source_target_pairs={{0,1},{1,0},{2,3},{3,2},{4,5},{5,4},{6,7},{7,6},{8,9},{9,8},{10,11... | collective-permute-start | bytes 12296 | tf_op jit(solution)/shard_map/ppermute | solution.py:601
  31.5 3.3 %collective-permute-start.24 = (f32[32,128]{1,0:T(8,128)S(1)}, f32[32,128]{1,0:T(8,128)S(1)}, u32[]{:S(2)}, u32[]{:S(2)}) collective-permute-start(f32[32,128]{1,0:T(8,128)S(1)} %get-tuple-element.187), channel_id=1, source_target_pairs={{0,1},{1,0},{2,3},{3,2},{4,5},{5,4},{6,7},{7,6},{8,9},{9,8},{10,11... | collective-permute-start | bytes 49160 | tf_op jit(solution)/shard_map/ppermute | solution.py:576
  31.6 5.4 %collective-permute-start.25 = (f32[32,128]{1,0:T(8,128)S(1)}, f32[32,128]{1,0:T(8,128)S(1)}, u32[]{:S(2)}, u32[]{:S(2)}) collective-permute-start(f32[32,128]{1,0:T(8,128)S(1)} %get-tuple-element.188), channel_id=1, source_target_pairs={{0,32},{1,2},{2,1},{3,4},{4,3},{5,6},{6,5},{7,8},{8,7},{9,10},{10,... | collective-permute-start | bytes 49160 | tf_op jit(solution)/shard_map/ppermute | solution.py:588
  32.4 4.6 %collective-permute-start.26 = (f32[32,128]{1,0:T(8,128)S(1)}, f32[32,128]{1,0:T(8,128)S(1)}, u32[]{:S(2)}, u32[]{:S(2)}) collective-permute-start(f32[32,128]{1,0:T(8,128)S(1)} %get-tuple-element.189), channel_id=1, source_target_pairs={{0,32},{32,0},{64,96},{96,64},{1,33},{33,1},{65,97},{97,65},{2,34}... | collective-permute-start | bytes 49160 | tf_op jit(solution)/shard_map/ppermute | solution.py:600
  34.5 2.5 %collective-permute-start.27 = (f32[32,128]{1,0:T(8,128)S(1)}, f32[32,128]{1,0:T(8,128)S(1)}, u32[]{:S(2)}, u32[]{:S(2)}) collective-permute-start(f32[32,128]{1,0:T(8,128)S(1)} %get-tuple-element.190), channel_id=1, source_target_pairs={{0,1},{1,0},{2,3},{3,2},{4,5},{5,4},{6,7},{7,6},{8,9},{9,8},{10,11... | collective-permute-start | bytes 49160 | tf_op jit(solution)/shard_map/ppermute | solution.py:601
  39.6 3.1 %collective-permute-start.28 = (f32[32,128]{1,0:T(8,128)S(1)}, f32[32,128]{1,0:T(8,128)S(1)}, u32[]{:S(2)}, u32[]{:S(2)}) collective-permute-start(f32[32,128]{1,0:T(8,128)S(1)} %get-tuple-element.192), channel_id=1, source_target_pairs={{0,1},{1,0},{2,3},{3,2},{4,5},{5,4},{6,7},{7,6},{8,9},{9,8},{10,11... | collective-permute-start | bytes 49160 | tf_op jit(solution)/shard_map/ppermute | solution.py:576
  39.7 3.9 %collective-permute-start.29 = (f32[32,128]{1,0:T(8,128)S(1)}, f32[32,128]{1,0:T(8,128)S(1)}, u32[]{:S(2)}, u32[]{:S(2)}) collective-permute-start(f32[32,128]{1,0:T(8,128)S(1)} %get-tuple-element.193), channel_id=1, source_target_pairs={{0,32},{32,0},{64,96},{96,64},{1,33},{33,1},{65,97},{97,65},{2,34}... | collective-permute-start | bytes 49160 | tf_op jit(solution)/shard_map/ppermute | solution.py:600
  41.9 1.7 %collective-permute-start.30 = (f32[32,128]{1,0:T(8,128)S(1)}, f32[32,128]{1,0:T(8,128)S(1)}, u32[]{:S(2)}, u32[]{:S(2)}) collective-permute-start(f32[32,128]{1,0:T(8,128)S(1)} %get-tuple-element.194), channel_id=1, source_target_pairs={{0,1},{1,0},{2,3},{3,2},{4,5},{5,4},{6,7},{7,6},{8,9},{9,8},{10,11... | collective-permute-start | bytes 49160 | tf_op jit(solution)/shard_map/ppermute | solution.py:601
  43.8 5.7 %collective-permute-start.31 = (f32[96,128]{1,0:T(8,128)S(1)}, f32[96,128]{1,0:T(8,128)S(1)}, u32[]{:S(2)}, u32[]{:S(2)}) collective-permute-start(f32[96,128]{1,0:T(8,128)S(1)} %get-tuple-element.196), channel_id=1, source_target_pairs={{0,32},{1,2},{2,1},{3,4},{4,3},{5,6},{6,5},{7,8},{8,7},{9,10},{10,... | collective-permute-start | bytes 147464 | tf_op jit(solution)/shard_map/ppermute | solution.py:588
  44.9 1.2 %collective-permute-start.32 = (f32[64,128]{1,0:T(8,128)S(1)}, f32[64,128]{1,0:T(8,128)S(1)}, u32[]{:S(2)}, u32[]{:S(2)}) collective-permute-start(f32[64,128]{1,0:T(8,128)S(1)} %get-tuple-element.197.ma), channel_id=1, source_target_pairs={{0,1},{1,0},{2,3},{3,2},{4,5},{5,4},{6,7},{7,6},{8,9},{9,8},{10,11... | collective-permute-start | bytes 98312 | tf_op jit(solution)/shard_map/ppermute | solution.py:576
  50.5 3.4 %collective-permute-start.33 = (f32[8,128]{1,0:T(8,128)S(1)}, f32[8,128]{1,0:T(8,128)S(1)}, u32[]{:S(2)}, u32[]{:S(2)}) collective-permute-start(f32[8,128]{1,0:T(8,128)S(1)} %get-tuple-element.203), channel_id=1, source_target_pairs={{0,1},{1,0},{2,3},{3,2},{4,5},{5,4},{6,7},{7,6},{8,9},{9,8},{10,11... | collective-permute-start | bytes 12296 | tf_op jit(solution)/shard_map/ppermute | solution.py:576
  50.6 3.8 %collective-permute-start.34 = (f32[8,128]{1,0:T(8,128)S(1)}, f32[8,128]{1,0:T(8,128)S(1)}, u32[]{:S(2)}, u32[]{:S(2)}) collective-permute-start(f32[8,128]{1,0:T(8,128)S(1)} %get-tuple-element.204), channel_id=1, source_target_pairs={{0,32},{32,0},{64,96},{96,64},{1,33},{33,1},{65,97},{97,65},{2,34}... | collective-permute-start | bytes 12296 | tf_op jit(solution)/shard_map/ppermute | solution.py:600
  52.8 1.6 %collective-permute-start.35 = (f32[8,128]{1,0:T(8,128)S(1)}, f32[8,128]{1,0:T(8,128)S(1)}, u32[]{:S(2)}, u32[]{:S(2)}) collective-permute-start(f32[8,128]{1,0:T(8,128)S(1)} %get-tuple-element.205), channel_id=1, source_target_pairs={{0,1},{1,0},{2,3},{3,2},{4,5},{5,4},{6,7},{7,6},{8,9},{9,8},{10,11... | collective-permute-start | bytes 12296 | tf_op jit(solution)/shard_map/ppermute | solution.py:601
  57.0 5.7 %collective-permute-start.6 = (f32[32,128]{1,0:T(8,128)S(1)}, f32[32,128]{1,0:T(8,128)S(1)}, u32[]{:S(2)}, u32[]{:S(2)}) collective-permute-start(f32[32,128]{1,0:T(8,128)S(1)} %get-tuple-element.83), channel_id=1, source_target_pairs={{0,1},{1,0},{2,3},{3,2},{4,5},{5,4},{6,7},{7,6},{8,9},{9,8},{10,11... | collective-permute-start | bytes 49160 | tf_op jit(solution)/shard_map/cond/branch_1_fun/ppermute | solution.py:576
  57.1 5.6 %collective-permute-start.7 = (f32[32,128]{1,0:T(8,128)S(1)}, f32[32,128]{1,0:T(8,128)S(1)}, u32[]{:S(2)}, u32[]{:S(2)}) collective-permute-start(f32[32,128]{1,0:T(8,128)S(1)} %get-tuple-element.84), channel_id=1, source_target_pairs={{0,32},{1,2},{2,1},{3,4},{4,3},{5,6},{6,5},{7,8},{8,7},{9,10},{10,... | collective-permute-start | bytes 49160 | tf_op jit(solution)/shard_map/cond/branch_1_fun/ppermute | solution.py:588
  58.4 4.3 %collective-permute-start.8 = (f32[32,128]{1,0:T(8,128)S(1)}, f32[32,128]{1,0:T(8,128)S(1)}, u32[]{:S(2)}, u32[]{:S(2)}) collective-permute-start(f32[32,128]{1,0:T(8,128)S(1)} %get-tuple-element.85), channel_id=1, source_target_pairs={{0,32},{32,0},{64,96},{96,64},{1,33},{33,1},{65,97},{97,65},{2,34}... | collective-permute-start | bytes 49160 | tf_op jit(solution)/shard_map/cond/branch_1_fun/ppermute | solution.py:600
  60.4 2.3 %collective-permute-start.9 = (f32[32,128]{1,0:T(8,128)S(1)}, f32[32,128]{1,0:T(8,128)S(1)}, u32[]{:S(2)}, u32[]{:S(2)}) collective-permute-start(f32[32,128]{1,0:T(8,128)S(1)} %get-tuple-element.86), channel_id=1, source_target_pairs={{0,1},{1,0},{2,3},{3,2},{4,5},{5,4},{6,7},{7,6},{8,9},{9,8},{10,11... | collective-permute-start | bytes 49160 | tf_op jit(solution)/shard_map/cond/branch_1_fun/ppermute | solution.py:601
  64.0 3.0 %collective-permute-start.10 = (f32[512,128]{1,0:T(8,128)S(1)}, f32[512,128]{1,0:T(8,128)S(1)}, u32[]{:S(2)}, u32[]{:S(2)}) collective-permute-start(f32[512,128]{1,0:T(8,128)S(1)} %get-tuple-element.88), channel_id=1, source_target_pairs={{0,1},{1,0},{2,3},{3,2},{4,5},{5,4},{6,7},{7,6},{8,9},{9,8},{10,11... | collective-permute-start | bytes 786440 | tf_op jit(solution)/shard_map/cond/branch_1_fun/ppermute | solution.py:608
  64.6 7.9 %collective-permute-start.11 = (f32[512,128]{1,0:T(8,128)S(1)}, f32[512,128]{1,0:T(8,128)S(1)}, u32[]{:S(2)}, u32[]{:S(2)}) collective-permute-start(f32[512,128]{1,0:T(8,128)S(1)} %get-tuple-element.89), channel_id=1, source_target_pairs={{0,127},{1,2},{2,1},{3,4},{4,3},{5,6},{6,5},{7,8},{8,7},{9,10},{10... | collective-permute-start | bytes 786440 | tf_op jit(solution)/shard_map/cond/branch_1_fun/ppermute | solution.py:608

commit v4 on v3

--- a/solution.py
+++ b/solution.py
@@ -126,7 +126,10 @@
     return total
 
 
-def weights_kernel(new_owner, src, inv, owned, most, src_t, f0, fy, fz, fzs, c0, fx, fyf, czu, czd):
+def weights_kernel(
+    levels, level_sweeps, new_owner, src, inv,
+    owned, most, src_t, f0, fy, fz, fzs, c0, fx, fyf, czu, czd, limit,
+):
     row, lane = row_ids(BS), lane_ids(BS)
 
     def load(ref, x, offset):
@@ -167,6 +170,7 @@
     for g in range(4):
         fyf[8 * g : 8 * g + 8, :] = inv[pl.ds(ROWS + 256 * g, 8, stride=BS), :]
         fyf[BS + 8 * g : BS + 8 * g + 8, :] = inv[pl.ds(ROWS + 256 * g + 31, 8, stride=BS), :]
+    limit[...] = sweep_limits(levels, level_sweeps)
     device = Place().device
     owner = new_owner[...]
     block = lax.broadcasted_iota(jnp.int32, owner.shape, 0) * owner.shape[1]
@@ -209,12 +213,12 @@
     limit = jnp.zeros((BS, LANES), jnp.int32)
     for b in range(BLK):
         limit = jnp.where(block == b, level_sweeps[levels[b]], limit)
-    return limit
+    return limit.astype(F32)
 
 
 def relax(limit, r, e, f0, fy, fzs, d, finish):
     def sweep(i, load, store):
-        active = limit > i
+        active = limit > float(i)
 
         t0, here = ZERO(), load(plane(0))
         for x in range(BS):
@@ -244,7 +248,7 @@
 
 
 def first_kernel(
-    levels, level_sweeps, src, f0, fy, fzs, c0, fx, fyf, ra, rb, rc, rd,
+    limit, src, f0, fy, fzs, c0, fx, fyf, ra, rb, rc, rd,
     c, d, gx, gy, p, sa, sb, sc, sd, e,
 ):
     def natural(ref):
@@ -267,7 +271,7 @@
     def finish(at, value):
         p[at, :] = value
 
-    relax(sweep_limits(levels, level_sweeps), src, e, f0, fy, fzs, d, finish)
+    relax(limit[...], src, e, f0, fy, fzs, d, finish)
     send_faces(place, p, sa, sb, sc, sd)
 
 
@@ -475,24 +479,22 @@
 
 
 def smooth_corrected_kernel(
-    levels, level_sweeps, ri, f0, fy, fzs, d, p, gx, gy, ra, rc, rd, ka, kc, kd,
+    ri, limit, f0, fy, fzs, d, p, gx, gy, ra, rc, rd, ka, kc, kd,
     r, p_out, sa, sb, sc, sd, e, scr,
 ):
     place = Place()
     near = ra[...] + spread_rows(scr, ka[...])
     add_all(place, gx, gy, near, ZERO(), rc[...] + tiled(kc[...]), rd[...] + tiled(kd[...]), r)
-    limit = sweep_limits(levels, level_sweeps)
-    finish_smooth(place, limit, r, f0, fy, fzs, d, p, p_out, (sa, sb, sc, sd), e)
+    finish_smooth(place, limit[...], r, f0, fy, fzs, d, p, p_out, (sa, sb, sc, sd), e)
 
 
 def smooth_kernel(
-    levels, level_sweeps, ri, f0, fy, fzs, d, p, gx, gy, ra, rb, rc, rd,
+    ri, limit, f0, fy, fzs, d, p, gx, gy, ra, rb, rc, rd,
     r, p_out, sa, sb, sc, sd, e,
 ):
     place = Place()
     add_all(place, gx, gy, ra[...], rb[...], rc[...], rd[...], r)
-    limit = sweep_limits(levels, level_sweeps)
-    finish_smooth(place, limit, r, f0, fy, fzs, d, p, p_out, (sa, sb, sc, sd), e)
+    finish_smooth(place, limit[...], r, f0, fy, fzs, d, p, p_out, (sa, sb, sc, sd), e)
 
 
 def plane_to_blocks(v, x, out, base):
@@ -520,8 +522,9 @@
         at = plane(x)
         after = p[after_plane(x), :]
         r[at, :], t0 = residual_plane(src, c, f0, fy, fz, at, t0, here, after)
-        plane_to_blocks(here, x, blocks, count * STEP)
         here = after
+    for x in range(BS):
+        plane_to_blocks(p[plane(x), :], x, blocks, count * STEP)
 
 
 def final_kernel(ri, gx, gy, ra, rb, rc, rd, pblocks, r, blocks, sa, sb, *, count):
@@ -616,19 +619,19 @@
 FACE, CFACE = (BS, LANES), (8, LANES)
 
 
-def set_up(new_owner, src, inv):
+def set_up(levels, new_owner, src, inv):
     outs = [jax.ShapeDtypeStruct((2,), jnp.int32), jax.ShapeDtypeStruct((1,), jnp.int32)] + [
-        jax.ShapeDtypeStruct(s, F32) for s in [FULL] * 6 + [TWO] * 2 + [CFIELD] * 2
+        jax.ShapeDtypeStruct(s, F32) for s in [FULL] * 6 + [TWO] * 2 + [CFIELD] * 2 + [FACE]
     ]
     vm, sm = pl.BlockSpec(memory_space=pltpu.VMEM), pl.BlockSpec(memory_space=pltpu.SMEM)
     return pl.pallas_call(
         weights_kernel,
         out_shape=outs,
-        in_specs=[vm] * 3,
-        out_specs=[sm] * 2 + [vm] * 10,
+        in_specs=[sm] * 2 + [vm] * 3,
+        out_specs=[sm] * 2 + [vm] * 11,
         compiler_params=pltpu.CompilerParams(vmem_limit_bytes=48 << 20),
         cost_estimate=pl.CostEstimate(flops=4000000, bytes_accessed=6 << 20, transcendentals=0),
-    )(new_owner.reshape(-1, min(LANES, new_owner.size)), src, inv)
+    )(*levels, new_owner.reshape(-1, min(LANES, new_owner.size)), src, inv)
 
 
 def row_shape(count):
@@ -673,6 +676,7 @@
         in_specs=[pl.BlockSpec(memory_space=pl.ANY)],
         out_specs=[pl.BlockSpec(memory_space=pltpu.VMEM)] * 4,
         scratch_shapes=[pltpu.SemaphoreType.DMA((4,))],
+        compiler_params=pltpu.CompilerParams(vmem_limit_bytes=48 << 20),
         cost_estimate=pl.CostEstimate(flops=2000000000, bytes_accessed=131072, transcendentals=0),
     )(inverse_density)
 
@@ -697,16 +701,16 @@
 def on_device(source, inverse_density, block_level, level_sweeps, new_owner):
     levels = (block_level, level_sweeps)
     halos = swap_faces(*density_faces(inverse_density))
-    owned, most, src, f0, fy, fz, fzs, c0, fx, fyf, czu, czd = set_up(
-        new_owner, source.reshape(ROWS, LANES), inverse_density.reshape(3 * ROWS, LANES)
+    owned, most, src, f0, fy, fz, fzs, c0, fx, fyf, czu, czd, limit = set_up(
+        levels, new_owner, source.reshape(ROWS, LANES), inverse_density.reshape(3 * ROWS, LANES)
     )
     c, d, gx, gy, p, *sends = call(
         first_kernel,
         [FULL, FULL, TWO, TWO, FULL] + [FACE] * 4,
-        [src, f0, fy, fzs, c0, fx, fyf, *halos],
-        levels,
+        [limit, src, f0, fy, fzs, c0, fx, fyf, *halos],
+        (),
         [vmem(*FULL)],
-        {4: 0},
+        {5: 0},
     )
     fine = [src, c, f0, fy, fz]
     wide = None
@@ -717,8 +721,8 @@
             _, p, *sends = call(
                 smooth_kernel,
                 [FULL, FULL] + [FACE] * 4,
-                [ri, f0, fy, fzs, d, p, gx, gy, *halos],
-                levels,
+                [ri, limit, f0, fy, fzs, d, p, gx, gy, *halos],
+                (),
                 [vmem(*FULL)],
                 {0: 0},
             )
@@ -759,8 +763,8 @@
         _, p, *sends = call(
             smooth_corrected_kernel,
             [FULL, FULL] + [FACE] * 4,
-            [ri, f0, fy, fzs, d, p, gx, gy, ra, rc, rd, ka, kc, kd],
-            levels,
+            [ri, limit, f0, fy, fzs, d, p, gx, gy, ra, rc, rd, ka, kc, kd],
+            (),
             [vmem(*FULL), vmem(*FACE)],
             {0: 0},
         )

time: 74.7 us -> 70.4 us (0.942)
  Pallas kernels: 23.9 us -> 18.6 us
  local copies, waits for them, and re-layouts: 0.03 us -> 1.42 us
    pallas_call x16, Pallas kernels: 19.5 us -> 15.1 us  [call(): pl.pallas_call(body, out_shape=outs, in_specs=[pl.BlockSpec(memory_space=...]
    pallas_call x1, Pallas kernels: 1.57 us -> 0.15 us  [density_faces(): pl.pallas_call(faces_kernel, out_shape=[jax.ShapeDtypeStruct(FACE, F32)]...]
    unnamed x10 -> x12, local copies, waits for them, and re-layouts: 0.03 us -> 1.42 us
  transfers between devices with their start and end apart: 30 -> 30, of which waited for: 11 -> 11; matrix products, arithmetic and copies ran while one was open for 0% -> 0% of each run, Pallas kernels for 8% -> 9%
where the time goes in v4:
time: 70.4 us; the launch traced here: 70.2 us
  starting transfers between devices  27.1 us (38%)
  waiting for transfers between devices  21.3 us (30%)
  Pallas kernels  18.6 us (26%)
  between operations  1.71 us (2%)
  local copies, waits for them, and re-layouts  1.42 us (2%)
    ppermute x7, starting transfers between devices, swap_regions(): inner = lax.ppermute(inner, 'region', [(i, i ^ 1) for i in range(regions)])  15.7 us
    pallas_call x16, Pallas kernels, call(): pl.pallas_call(body, out_shape=outs, in_specs=[pl.BlockSpec(memory_space=...  15.1 us
    ppermute x5, waiting for transfers between devices, swap_far(): return lax.ppermute(value, BOTH, pairs)  10.1 us
    ppermute x5, starting transfers between devices, swap_far(): return lax.ppermute(value, BOTH, pairs)  6.82 us
    ppermute x2, waiting for transfers between devices, swap_blocks(): return (lax.ppermute(first, BOTH, inner), lax.ppermute(second, BOTH, outer))  5.45 us
    ppermute x7, waiting for transfers between devices, swap_regions(): inner = lax.ppermute(inner, 'region', [(i, i ^ 1) for i in range(regions)])  3.17 us
    ppermute x2, starting transfers between devices, swap_blocks(): return (lax.ppermute(first, BOTH, inner), lax.ppermute(second, BOTH, outer))  3.04 us
    ppermute x9, waiting for transfers between devices, swap_near(): lax.ppermute(value, 'member', [(i, i ^ 1) for i in range(lax.axis_size('m...  2.47 us
  transfers between devices with their start and end apart: 30, of which 11 were waited for; matrix products, arithmetic and copies ran while one was open for 0% of the time, Pallas kernels for 9%

profile of v4, /device:TPU:6, one launch (start us, length us, event | category | flops | bytes accessed | tf_op | source)
XLA Modules:
  0.0 70.2 jit_solution(16862054779461647974)
XLA Ops:
  0.6 1.4 %copy-done.3 = f32[3,32,32,128]{3,2,1,0:T(8,128)S(1)} copy-done((f32[3,32,32,128]{3,2,1,0:T(8,128)S(1)}, f32[3,32,32,128]{3,2,1,0:T(8,128)}, u32[]{:S(2)}) %copy-start.3) | copy-done | bytes 1572888
  2.1 0.1 shard_map.73
  2.2 0.1 collective-permute-start.12
  2.3 3.4 %collective-permute-start.13 = (f32[32,128]{1,0:T(8,128)S(1)}, f32[32,128]{1,0:T(8,128)S(1)}, u32[]{:S(2)}, u32[]{:S(2)}) collective-permute-start(f32[32,128]{1,0:T(8,128)S(1)} %get-tuple-element.164), channel_id=1, source_target_pairs={{0,32},{1,2},{2,1},{3,4},{4,3},{5,6},{6,5},{7,8},{8,7},{9,10},{10,... | collective-permute-start | bytes 49160 | tf_op jit(solution)/shard_map/ppermute | solution.py:591
  5.7 1.9 %collective-permute-start.14 = (f32[32,128]{1,0:T(8,128)S(1)}, f32[32,128]{1,0:T(8,128)S(1)}, u32[]{:S(2)}, u32[]{:S(2)}) collective-permute-start(f32[32,128]{1,0:T(8,128)S(1)} %get-tuple-element.165), channel_id=1, source_target_pairs={{0,32},{32,0},{64,96},{96,64},{1,33},{33,1},{65,97},{97,65},{2,34}... | collective-permute-start | bytes 49160 | tf_op jit(solution)/shard_map/ppermute | solution.py:603
  7.6 0.0 collective-permute-start.15
  7.6 1.5 %shard_map.72 = (s32[2]{0:T(128)S(1)}, s32[1]{0:T(128)}, f32[1024,128]{1,0:T(8,128)S(1)}, f32[1024,128]{1,0:T(8,128)S(1)}, f32[1024,128]{1,0:T(8,128)S(1)}, /*in...) custom-call(s32[4]{0:T(128)S(1)} %copy-done.7, ...), custom_call_target="tpu_custom_call" | custom-call | flops 4000000 | bytes 6291456 | tf_op jit(solution)/shard_map/pallas_call | solution.py:627
  9.2 0.0 collective-permute-done.12.ra
  9.2 0.2 collective-permute-done.14.rc
  9.4 0.0 collective-permute-done.15.rd
  9.4 1.6 %shard_map.74 = (f32[1024,128]{1,0:T(8,128)S(1)}, f32[1024,128]{1,0:T(8,128)S(1)}, f32[64,128]{1,0:T(8,128)S(1)}, f32[64,128]{1,0:T(8,128)S(1)}, f32[1024,128]{1...) custom-call(f32[32,128]{1,0:T(8,128)S(1)} %get-tuple-element.156.lim, ...), custom_call_target="tpu_custom_call", output_to_operand_aliasing={{0}: (5, {})} | custom-call | flops 2000000 | bytes 4472832 | tf_op jit(solution)/shard_map/pallas_call | solution.py:38
  11.0 0.4 collective-permute-start.16
  11.4 3.2 %collective-permute-start.17 = (f32[32,128]{1,0:T(8,128)S(1)}, f32[32,128]{1,0:T(8,128)S(1)}, u32[]{:S(2)}, u32[]{:S(2)}) collective-permute-start(f32[32,128]{1,0:T(8,128)S(1)} %get-tuple-element.173), channel_id=1, source_target_pairs={{0,32},{32,0},{64,96},{96,64},{1,33},{33,1},{65,97},{97,65},{2,34}... | collective-permute-start | bytes 49160 | tf_op jit(solution)/shard_map/ppermute | solution.py:603
  14.6 0.2 collective-permute-start.18
  14.8 0.5 shard_map.75.qi
  15.3 0.5 shard_map.76.rest_0_
  15.9 0.5 collective-permute-done.17.rc
  16.4 0.0 collective-permute-done.18.rd
  16.4 0.2 shard_map.77
  16.6 0.3 collective-permute-start.19
  16.9 0.0 collective-permute-start.20
  16.9 1.3 %collective-permute-done.20.qa = f32[128,128]{1,0:T(8,128)S(1)} collective-permute-done((f32[128,128]{1,0:T(8,128)S(1)}, f32[128,128]{1,0:T(8,128)S(1)}, u32[]{:S(2)}, u32[]{:S(2)}) %collective-permute-start.20) | collective-permute-done | bytes 65568 | tf_op jit(solution)/shard_map/ppermute | solution.py:579
  18.1 4.5 %collective-permute-done.19.qb = f32[160,128]{1,0:T(8,128)S(1)} collective-permute-done((f32[160,128]{1,0:T(8,128)S(1)}, f32[160,128]{1,0:T(8,128)S(1)}, u32[]{:S(2)}, u32[]{:S(2)}) %collective-permute-start.19) | collective-permute-done | bytes 81952 | tf_op jit(solution)/shard_map/ppermute | solution.py:591
  22.6 1.3 %shard_map.78 = (f32[64,128]{1,0:T(8,128)S(1)}, f32[8,128]{1,0:T(8,128)S(1)}, f32[8,128]{1,0:T(8,128)S(1)}, f32[8,128]{1,0:T(8,128)S(1)}, f32[8,128]{1,0:T(8,128)S(1)}, /*index=5*/f32[768,128]{1,0:T(8,128)S(1)}) custom-call(f32[128,128]{1,0:T(8,128)S(1)} %get-tuple-element.179.ma, f32[128,128]{1,0:T(8,128)S(1)} %collective-permute-done.20.qa, ...), custom_call_target="tpu_custom_call" | custom-call | flops 2000000 | bytes 704512 | tf_op jit(solution)/shard_map/pallas_call | solution.py:38
  23.9 0.1 collective-permute-start.21
  24.0 2.2 %collective-permute-start.22 = (f32[8,128]{1,0:T(8,128)S(1)}, f32[8,128]{1,0:T(8,128)S(1)}, u32[]{:S(2)}, u32[]{:S(2)}) collective-permute-start(f32[8,128]{1,0:T(8,128)S(1)} %get-tuple-element.186), channel_id=1, source_target_pairs={{0,32},{32,0},{64,96},{96,64},{1,33},{33,1},{65,97},{97,65},{2,34}... | collective-permute-start | bytes 12296 | tf_op jit(solution)/shard_map/ppermute | solution.py:603
  26.2 0.2 collective-permute-start.23
  26.3 0.3 shard_map.79
  26.7 1.1 %collective-permute-done.22.kc = f32[8,128]{1,0:T(8,128)S(1)} collective-permute-done((f32[8,128]{1,0:T(8,128)S(1)}, f32[8,128]{1,0:T(8,128)S(1)}, u32[]{:S(2)}, u32[]{:S(2)}) %collective-permute-start.22) | collective-permute-done | bytes 4128 | tf_op jit(solution)/shard_map/ppermute | solution.py:603
  27.7 1.6 %shard_map.80 = (f32[1024,128]{1,0:T(8,128)S(1)}, f32[1024,128]{1,0:T(8,128)S(1)}, f32[32,128]{1,0:T(8,128)S(1)}, f32[32,128]{1,0:T(8,128)S(1)}, f32[32,128]{1,0:T(8,128)S(1)}, /*index=5*/f32[32,128]{1,0:T(8,128)S(1)}) custom-call(f32[1024,128]{1,0:T(8,128)S(1)} %get-tuple-element.182.ri, ...), custom_call_target="tpu_custom_call", output_to_operand_aliasing={{0}: (0, {})} | custom-call | flops 2000000 | bytes 4403200 | tf_op jit(solution)/shard_map/pallas_call | solution.py:38
  29.4 0.1 collective-permute-start.24
  29.5 0.8 %collective-permute-start.25 = (f32[32,128]{1,0:T(8,128)S(1)}, f32[32,128]{1,0:T(8,128)S(1)}, u32[]{:S(2)}, u32[]{:S(2)}) collective-permute-start(f32[32,128]{1,0:T(8,128)S(1)} %get-tuple-element.190), channel_id=1, source_target_pairs={{0,32},{1,2},{2,1},{3,4},{4,3},{5,6},{6,5},{7,8},{8,7},{9,10},{10,... | collective-permute-start | bytes 49160 | tf_op jit(solution)/shard_map/ppermute | solution.py:591
  30.2 2.0 %collective-permute-start.26 = (f32[32,128]{1,0:T(8,128)S(1)}, f32[32,128]{1,0:T(8,128)S(1)}, u32[]{:S(2)}, u32[]{:S(2)}) collective-permute-start(f32[32,128]{1,0:T(8,128)S(1)} %get-tuple-element.191), channel_id=1, source_target_pairs={{0,32},{32,0},{64,96},{96,64},{1,33},{33,1},{65,97},{97,65},{2,34}... | collective-permute-start | bytes 49160 | tf_op jit(solution)/shard_map/ppermute | solution.py:603
  32.3 0.0 collective-permute-start.27
  32.3 0.3 shard_map.81.ri
  32.6 0.0 collective-permute-done.24.ra
  32.6 2.2 %collective-permute-done.25.rb = f32[32,128]{1,0:T(8,128)S(1)} collective-permute-done((f32[32,128]{1,0:T(8,128)S(1)}, f32[32,128]{1,0:T(8,128)S(1)}, u32[]{:S(2)}, u32[]{:S(2)}) %collective-permute-start.25) | collective-permute-done | bytes 16416 | tf_op jit(solution)/shard_map/ppermute | solution.py:591
  34.8 1.6 %shard_map.82 = (f32[1024,128]{1,0:T(8,128)S(1)}, f32[1024,128]{1,0:T(8,128)S(1)}, f32[32,128]{1,0:T(8,128)S(1)}, f32[32,128]{1,0:T(8,128)S(1)}, f32[32,128]{1,0:T(8,128)S(1)}, /*index=5*/f32[32,128]{1,0:T(8,128)S(1)}) custom-call(f32[1024,128]{1,0:T(8,128)S(1)} %shard_map.81.ri, ...), custom_call_target="tpu_custom_call", output_to_operand_aliasing={{0}: (0, {})} | custom-call | flops 2000000 | bytes 4407296 | tf_op jit(solution)/shard_map/pallas_call | solution.py:38
  36.5 0.1 collective-permute-start.28
  36.6 2.2 %collective-permute-start.29 = (f32[32,128]{1,0:T(8,128)S(1)}, f32[32,128]{1,0:T(8,128)S(1)}, u32[]{:S(2)}, u32[]{:S(2)}) collective-permute-start(f32[32,128]{1,0:T(8,128)S(1)} %get-tuple-element.195), channel_id=1, source_target_pairs={{0,32},{32,0},{64,96},{96,64},{1,33},{33,1},{65,97},{97,65},{2,34}... | collective-permute-start | bytes 49160 | tf_op jit(solution)/shard_map/ppermute | solution.py:603
  38.7 0.2 collective-permute-start.30
  38.9 0.5 shard_map.83.qi
  39.5 1.0 %collective-permute-done.29.rc = f32[32,128]{1,0:T(8,128)S(1)} collective-permute-done((f32[32,128]{1,0:T(8,128)S(1)}, f32[32,128]{1,0:T(8,128)S(1)}, u32[]{:S(2)}, u32[]{:S(2)}) %collective-permute-start.29) | collective-permute-done | bytes 16416 | tf_op jit(solution)/shard_map/ppermute | solution.py:603
  40.5 0.2 shard_map.84
  40.7 1.1 %collective-permute-start.31 = (f32[96,128]{1,0:T(8,128)S(1)}, f32[96,128]{1,0:T(8,128)S(1)}, u32[]{:S(2)}, u32[]{:S(2)}) collective-permute-start(f32[96,128]{1,0:T(8,128)S(1)} %get-tuple-element.198), channel_id=1, source_target_pairs={{0,32},{1,2},{2,1},{3,4},{4,3},{5,6},{6,5},{7,8},{8,7},{9,10},{10,... | collective-permute-start | bytes 147464 | tf_op jit(solution)/shard_map/ppermute | solution.py:591
  41.7 1.2 %collective-permute-done.32.qa = f32[64,128]{1,0:T(8,128)S(1)} collective-permute-done((f32[64,128]{1,0:T(8,128)S(1)}, f32[64,128]{1,0:T(8,128)S(1)}, u32[]{:S(2)}, u32[]{:S(2)}) %collective-permute-start.32) | collective-permute-done | bytes 32800 | tf_op jit(solution)/shard_map/ppermute | solution.py:579
  42.9 3.4 %collective-permute-done.31.qb = f32[96,128]{1,0:T(8,128)S(1)} collective-permute-done((f32[96,128]{1,0:T(8,128)S(1)}, f32[96,128]{1,0:T(8,128)S(1)}, u32[]{:S(2)}, u32[]{:S(2)}) %collective-permute-start.31) | collective-permute-done | bytes 49184 | tf_op jit(solution)/shard_map/ppermute | solution.py:591
  46.4 0.9 %shard_map.85 = (f32[64,128]{1,0:T(8,128)S(1)}, f32[8,128]{1,0:T(8,128)S(1)}, f32[8,128]{1,0:T(8,128)S(1)}, f32[8,128]{1,0:T(8,128)S(1)}, f32[8,128]{1,0:T(8,128)S(1)}) custom-call(f32[64,128]{1,0:T(8,128)S(1)} %get-tuple-element.199.ma, f32[64,128]{1,0:T(8,128)S(1)} %collective-permute-done.32.qa, f32[96,128]{1,0:T(8,128)S(1)} %collective-permute-done.31.qb, ...), custom_call_target="tpu_custom_call" | custom-call | flops 2000000 | bytes 606208 | tf_op jit(solution)/shard_map/pallas_call | solution.py:38
  47.3 0.1 collective-permute-start.33
  47.4 2.2 %collective-permute-start.34 = (f32[8,128]{1,0:T(8,128)S(1)}, f32[8,128]{1,0:T(8,128)S(1)}, u32[]{:S(2)}, u32[]{:S(2)}) collective-permute-start(f32[8,128]{1,0:T(8,128)S(1)} %get-tuple-element.206), channel_id=1, source_target_pairs={{0,32},{32,0},{64,96},{96,64},{1,33},{33,1},{65,97},{97,65},{2,34}... | collective-permute-start | bytes 12296 | tf_op jit(solution)/shard_map/ppermute | solution.py:603
  49.6 0.2 collective-permute-start.35
  50.4 0.4 shard_map.86
  50.7 0.4 collective-permute-done.34.kc
  51.2 1.6 %shard_map.87 = (f32[1024,128]{1,0:T(8,128)S(1)}, f32[1024,128]{1,0:T(8,128)S(1)}, f32[32,128]{1,0:T(8,128)S(1)}, f32[32,128]{1,0:T(8,128)S(1)}, f32[32,128]{1,0:T(8,128)S(1)}, /*index=5*/f32[32,128]{1,0:T(8,128)S(1)}) custom-call(f32[1024,128]{1,0:T(8,128)S(1)} %get-tuple-element.203.ri, ...), custom_call_target="tpu_custom_call", output_to_operand_aliasing={{0}: (0, {})} | custom-call | flops 2000000 | bytes 4403200 | tf_op jit(solution)/shard_map/pallas_call | solution.py:38
  52.8 17.3 %conditional.1 = (f32[6,32768]{1,0:T(8,128)}, f32[6,32768]{1,0:T(8,128)}) conditional(s32[]{:T(128)} %bitcast.15, (f32[1024,128]{1,0:T(8,128)S(1)}, f32[1024,128]{1,0:T(8,128)S(1)}, f32[1024,128]{1,0:T(8,128)S(1)}, f32[1024,128]{1,0:T(8,128)S(1)}, f32[1024,128]{1,0:T(8,128)S(1)}, /*index=5*/f32[1024,128]{1,0:T(8,128)S(1)}, f32[32,128]{1,0:T(8,128)S(1)}, ...), branch_computations={%region_0.0_spmd, %region_1.0_spmd} | conditional | flops 6000000 | bytes 54329684 | solution.py:786
  52.8 0.1 collective-permute-start.6
  52.9 1.3 %collective-permute-start.7 = (f32[32,128]{1,0:T(8,128)S(1)}, f32[32,128]{1,0:T(8,128)S(1)}, u32[]{:S(2)}, u32[]{:S(2)}) collective-permute-start(f32[32,128]{1,0:T(8,128)S(1)} %get-tuple-element.84), channel_id=1, source_target_pairs={{0,32},{1,2},{2,1},{3,4},{4,3},{5,6},{6,5},{7,8},{8,7},{9,10},{10,... | collective-permute-start | bytes 49160 | tf_op jit(solution)/shard_map/cond/branch_1_fun/ppermute | solution.py:591
  54.2 2.0 %collective-permute-start.8 = (f32[32,128]{1,0:T(8,128)S(1)}, f32[32,128]{1,0:T(8,128)S(1)}, u32[]{:S(2)}, u32[]{:S(2)}) collective-permute-start(f32[32,128]{1,0:T(8,128)S(1)} %get-tuple-element.85), channel_id=1, source_target_pairs={{0,32},{32,0},{64,96},{96,64},{1,33},{33,1},{65,97},{97,65},{2,34}... | collective-permute-start | bytes 49160 | tf_op jit(solution)/shard_map/cond/branch_1_fun/ppermute | solution.py:603
  56.2 2.2 %branch_1_fun.3 = (f32[1024,128]{1,0:T(8,128)S(1)}, f32[2640,128]{1,0:T(8,128)S(1)}) custom-call(f32[1024,128]{1,0:T(8,128)S(1)} %get-tuple-element.73.src, f32[1024,128]{1,0:T(8,128)S(1)} %get-tuple-element.74.c, f32[1024,128]{1,0:T(8,128)S(1)} %get-tuple-element.75.f0, f32[1024,128]{1,0:T(8,128)S(1)} %get-tuple-element.76.fy, ...), custom_call_target="tpu_custom_call" | custom-call | flops 2000000 | bytes 5021696 | tf_op jit(solution)/shard_map/cond/branch_1_fun/pallas_call | solution.py:38
  58.5 1.2 %branch_1_fun.4 = (f32[1024,128]{1,0:T(8,128)S(1)}, f32[2640,128]{1,0:T(8,128)S(1)}, f32[512,128]{1,0:T(8,128)S(1)}, f32[512,128]{1,0:T(8,128)S(1)}) custom-call(f32[1024,128]{1,0:T(8,128)S(1)} %get-tuple-element.80.ri, f32[64,128]{1,0:T(8,128)S(1)} %get-tuple-element.81.gx, f32[64,128]{1,0:T(8,128)S(1)} %get-tuple-element.82.gy, ...), custom_call_target="tpu_custom_call", output_to_operand_aliasing={{0}: (0, {})} | custom-call | flops 2000000 | bytes 4407296 | tf_op jit(solution)/shard_map/cond/branch_1_fun/pallas_call | solution.py:38
  59.7 0.6 collective-permute-start.10
  60.3 2.5 %collective-permute-start.11 = (f32[512,128]{1,0:T(8,128)S(1)}, f32[512,128]{1,0:T(8,128)S(1)}, u32[]{:S(2)}, u32[]{:S(2)}) collective-permute-start(f32[512,128]{1,0:T(8,128)S(1)} %get-tuple-element.89), channel_id=1, source_target_pairs={{0,127},{1,2},{2,1},{3,4},{4,3},{5,6},{6,5},{7,8},{8,7},{9,10},{10... | collective-permute-start | bytes 786440 | tf_op jit(solution)/shard_map/cond/branch_1_fun/ppermute | solution.py:611
  62.8 5.5 %collective-permute-done.11.rb = f32[512,128]{1,0:T(8,128)S(1)} collective-permute-done((f32[512,128]{1,0:T(8,128)S(1)}, f32[512,128]{1,0:T(8,128)S(1)}, u32[]{:S(2)}, u32[]{:S(2)}) %collective-permute-start.11) | collective-permute-done | bytes 262176 | tf_op jit(solution)/shard_map/cond/branch_1_fun/ppermute | solution.py:611
  68.2 1.8 %branch_1_fun.5 = (f32[256,6,128]{2,1,0:T(8,128)}, f32[256,6,128]{2,1,0:T(8,128)}, f32[2640,128]{1,0:T(8,128)S(1)}, f32[2640,128]{1,0:T(8,128)S(1)}) custom-call(s32[2]{0:T(128)S(1)} %get-tuple-element.72.owned, f32[2640,128]{1,0:T(8,128)S(1)} %get-tuple-element.79.pblocks.in_p, ...), custom_call_target="tpu_custom_call", output_to_operand_aliasing={{2}: (1, {}), {3}: (2, {})} | custom-call | flops 2000000 | bytes 6291456 | tf_op jit(solution)/shard_map/cond/branch_1_fun/pallas_call | solution.py:688
  (28 shorter events, 0.1 us)
Async XLA Ops:
  0.6 1.4 %copy-start.3 = (f32[3,32,32,128]{3,2,1,0:T(8,128)S(1)}, f32[3,32,32,128]{3,2,1,0:T(8,128)}, u32[]{:S(2)}) copy-start(f32[3,32,32,128]{3,2,1,0:T(8,128)} %inv.1) | copy-start | bytes 4718596
  2.0 5.6 %copy-start.4 = (f32[3,32,32,128]{3,2,1,0:T(8,128)S(1)}, f32[3,32,32,128]{3,2,1,0:T(8,128)}, u32[]{:S(2)}) copy-start(f32[3,32,32,128]{3,2,1,0:T(8,128)} %inv.1) | copy-start | bytes 4718596
  2.0 5.6 %copy-start.5 = (f32[32,32,128]{2,1,0:T(8,128)S(1)}, f32[32,32,128]{2,1,0:T(8,128)}, u32[]{:S(2)}) copy-start(f32[32,32,128]{2,1,0:T(8,128)} %param.7) | copy-start | bytes 1572868
  2.0 5.6 %copy-start.6 = (s32[512]{0:T(512)S(1)}, s32[512]{0:T(512)}, u32[]{:S(2)}) copy-start(s32[512]{0:T(512)} %param.11) | copy-start | bytes 6148
  2.0 5.6 %copy-start.7 = (s32[4]{0:T(128)S(1)}, s32[4]{0:T(128)}, u32[]{:S(2)}) copy-start(s32[4]{0:T(128)} %levels.1) | copy-start | bytes 52
  2.1 5.6 %copy-start.8 = (s32[3]{0:T(128)S(1)}, s32[3]{0:T(128)}, u32[]{:S(2)}) copy-start(s32[3]{0:T(128)} %level_sweeps.1) | copy-start | bytes 40
  2.2 7.0 %collective-permute-start.12 = (f32[32,128]{1,0:T(8,128)S(1)}, f32[32,128]{1,0:T(8,128)S(1)}, u32[]{:S(2)}, u32[]{:S(2)}) collective-permute-start(f32[32,128]{1,0:T(8,128)S(1)} %get-tuple-element.163), channel_id=1, source_target_pairs={{0,1},{1,0},{2,3},{3,2},{4,5},{5,4},{6,7},{7,6},{8,9},{9,8},{10,11... | collective-permute-start | bytes 49160 | tf_op jit(solution)/shard_map/ppermute | solution.py:579
  2.3 6.9 %collective-permute-start.13 = (f32[32,128]{1,0:T(8,128)S(1)}, f32[32,128]{1,0:T(8,128)S(1)}, u32[]{:S(2)}, u32[]{:S(2)}) collective-permute-start(f32[32,128]{1,0:T(8,128)S(1)} %get-tuple-element.164), channel_id=1, source_target_pairs={{0,32},{1,2},{2,1},{3,4},{4,3},{5,6},{6,5},{7,8},{8,7},{9,10},{10,... | collective-permute-start | bytes 49160 | tf_op jit(solution)/shard_map/ppermute | solution.py:591
  5.7 3.7 %collective-permute-start.14 = (f32[32,128]{1,0:T(8,128)S(1)}, f32[32,128]{1,0:T(8,128)S(1)}, u32[]{:S(2)}, u32[]{:S(2)}) collective-permute-start(f32[32,128]{1,0:T(8,128)S(1)} %get-tuple-element.165), channel_id=1, source_target_pairs={{0,32},{32,0},{64,96},{96,64},{1,33},{33,1},{65,97},{97,65},{2,34}... | collective-permute-start | bytes 49160 | tf_op jit(solution)/shard_map/ppermute | solution.py:603
  7.6 1.8 %collective-permute-start.15 = (f32[32,128]{1,0:T(8,128)S(1)}, f32[32,128]{1,0:T(8,128)S(1)}, u32[]{:S(2)}, u32[]{:S(2)}) collective-permute-start(f32[32,128]{1,0:T(8,128)S(1)} %get-tuple-element.166), channel_id=1, source_target_pairs={{0,1},{1,0},{2,3},{3,2},{4,5},{5,4},{6,7},{7,6},{8,9},{9,8},{10,11... | collective-permute-start | bytes 49160 | tf_op jit(solution)/shard_map/ppermute | solution.py:604
  11.0 4.8 %collective-permute-start.16 = (f32[32,128]{1,0:T(8,128)S(1)}, f32[32,128]{1,0:T(8,128)S(1)}, u32[]{:S(2)}, u32[]{:S(2)}) collective-permute-start(f32[32,128]{1,0:T(8,128)S(1)} %get-tuple-element.172), channel_id=1, source_target_pairs={{0,1},{1,0},{2,3},{3,2},{4,5},{5,4},{6,7},{7,6},{8,9},{9,8},{10,11... | collective-permute-start | bytes 49160 | tf_op jit(solution)/shard_map/ppermute | solution.py:579
  11.4 4.9 %collective-permute-start.17 = (f32[32,128]{1,0:T(8,128)S(1)}, f32[32,128]{1,0:T(8,128)S(1)}, u32[]{:S(2)}, u32[]{:S(2)}) collective-permute-start(f32[32,128]{1,0:T(8,128)S(1)} %get-tuple-element.173), channel_id=1, source_target_pairs={{0,32},{32,0},{64,96},{96,64},{1,33},{33,1},{65,97},{97,65},{2,34}... | collective-permute-start | bytes 49160 | tf_op jit(solution)/shard_map/ppermute | solution.py:603
  14.6 1.7 %collective-permute-start.18 = (f32[32,128]{1,0:T(8,128)S(1)}, f32[32,128]{1,0:T(8,128)S(1)}, u32[]{:S(2)}, u32[]{:S(2)}) collective-permute-start(f32[32,128]{1,0:T(8,128)S(1)} %get-tuple-element.174), channel_id=1, source_target_pairs={{0,1},{1,0},{2,3},{3,2},{4,5},{5,4},{6,7},{7,6},{8,9},{9,8},{10,11... | collective-permute-start | bytes 49160 | tf_op jit(solution)/shard_map/ppermute | solution.py:604
  16.6 6.1 %collective-permute-start.19 = (f32[160,128]{1,0:T(8,128)S(1)}, f32[160,128]{1,0:T(8,128)S(1)}, u32[]{:S(2)}, u32[]{:S(2)}) collective-permute-start(f32[160,128]{1,0:T(8,128)S(1)} %get-tuple-element.178), channel_id=1, source_target_pairs={{0,32},{1,2},{2,1},{3,4},{4,3},{5,6},{6,5},{7,8},{8,7},{9,10},{10,... | collective-permute-start | bytes 245768 | tf_op jit(solution)/shard_map/ppermute | solution.py:591
  16.9 1.3 %collective-permute-start.20 = (f32[128,128]{1,0:T(8,128)S(1)}, f32[128,128]{1,0:T(8,128)S(1)}, u32[]{:S(2)}, u32[]{:S(2)}) collective-permute-start(f32[128,128]{1,0:T(8,128)S(1)} %get-tuple-element.179.ma), channel_id=1, source_target_pairs={{0,1},{1,0},{2,3},{3,2},{4,5},{5,4},{6,7},{7,6},{8,9},{9,8},{10,11... | collective-permute-start | bytes 196616 | tf_op jit(solution)/shard_map/ppermute | solution.py:579
  23.9 2.8 %collective-permute-start.21 = (f32[8,128]{1,0:T(8,128)S(1)}, f32[8,128]{1,0:T(8,128)S(1)}, u32[]{:S(2)}, u32[]{:S(2)}) collective-permute-start(f32[8,128]{1,0:T(8,128)S(1)} %get-tuple-element.185), channel_id=1, source_target_pairs={{0,1},{1,0},{2,3},{3,2},{4,5},{5,4},{6,7},{7,6},{8,9},{9,8},{10,11... | collective-permute-start | bytes 12296 | tf_op jit(solution)/shard_map/ppermute | solution.py:579
  24.0 3.8 %collective-permute-start.22 = (f32[8,128]{1,0:T(8,128)S(1)}, f32[8,128]{1,0:T(8,128)S(1)}, u32[]{:S(2)}, u32[]{:S(2)}) collective-permute-start(f32[8,128]{1,0:T(8,128)S(1)} %get-tuple-element.186), channel_id=1, source_target_pairs={{0,32},{32,0},{64,96},{96,64},{1,33},{33,1},{65,97},{97,65},{2,34}... | collective-permute-start | bytes 12296 | tf_op jit(solution)/shard_map/ppermute | solution.py:603
  26.2 1.6 %collective-permute-start.23 = (f32[8,128]{1,0:T(8,128)S(1)}, f32[8,128]{1,0:T(8,128)S(1)}, u32[]{:S(2)}, u32[]{:S(2)}) collective-permute-start(f32[8,128]{1,0:T(8,128)S(1)} %get-tuple-element.187), channel_id=1, source_target_pairs={{0,1},{1,0},{2,3},{3,2},{4,5},{5,4},{6,7},{7,6},{8,9},{9,8},{10,11... | collective-permute-start | bytes 12296 | tf_op jit(solution)/shard_map/ppermute | solution.py:604
  29.4 3.2 %collective-permute-start.24 = (f32[32,128]{1,0:T(8,128)S(1)}, f32[32,128]{1,0:T(8,128)S(1)}, u32[]{:S(2)}, u32[]{:S(2)}) collective-permute-start(f32[32,128]{1,0:T(8,128)S(1)} %get-tuple-element.189), channel_id=1, source_target_pairs={{0,1},{1,0},{2,3},{3,2},{4,5},{5,4},{6,7},{7,6},{8,9},{9,8},{10,11... | collective-permute-start | bytes 49160 | tf_op jit(solution)/shard_map/ppermute | solution.py:579
  29.5 5.4 %collective-permute-start.25 = (f32[32,128]{1,0:T(8,128)S(1)}, f32[32,128]{1,0:T(8,128)S(1)}, u32[]{:S(2)}, u32[]{:S(2)}) collective-permute-start(f32[32,128]{1,0:T(8,128)S(1)} %get-tuple-element.190), channel_id=1, source_target_pairs={{0,32},{1,2},{2,1},{3,4},{4,3},{5,6},{6,5},{7,8},{8,7},{9,10},{10,... | collective-permute-start | bytes 49160 | tf_op jit(solution)/shard_map/ppermute | solution.py:591
  30.2 4.6 %collective-permute-start.26 = (f32[32,128]{1,0:T(8,128)S(1)}, f32[32,128]{1,0:T(8,128)S(1)}, u32[]{:S(2)}, u32[]{:S(2)}) collective-permute-start(f32[32,128]{1,0:T(8,128)S(1)} %get-tuple-element.191), channel_id=1, source_target_pairs={{0,32},{32,0},{64,96},{96,64},{1,33},{33,1},{65,97},{97,65},{2,34}... | collective-permute-start | bytes 49160 | tf_op jit(solution)/shard_map/ppermute | solution.py:603
  32.3 2.6 %collective-permute-start.27 = (f32[32,128]{1,0:T(8,128)S(1)}, f32[32,128]{1,0:T(8,128)S(1)}, u32[]{:S(2)}, u32[]{:S(2)}) collective-permute-start(f32[32,128]{1,0:T(8,128)S(1)} %get-tuple-element.192), channel_id=1, source_target_pairs={{0,1},{1,0},{2,3},{3,2},{4,5},{5,4},{6,7},{7,6},{8,9},{9,8},{10,11... | collective-permute-start | bytes 49160 | tf_op jit(solution)/shard_map/ppermute | solution.py:604
  36.5 3.0 %collective-permute-start.28 = (f32[32,128]{1,0:T(8,128)S(1)}, f32[32,128]{1,0:T(8,128)S(1)}, u32[]{:S(2)}, u32[]{:S(2)}) collective-permute-start(f32[32,128]{1,0:T(8,128)S(1)} %get-tuple-element.194), channel_id=1, source_target_pairs={{0,1},{1,0},{2,3},{3,2},{4,5},{5,4},{6,7},{7,6},{8,9},{9,8},{10,11... | collective-permute-start | bytes 49160 | tf_op jit(solution)/shard_map/ppermute | solution.py:579
  36.6 3.9 %collective-permute-start.29 = (f32[32,128]{1,0:T(8,128)S(1)}, f32[32,128]{1,0:T(8,128)S(1)}, u32[]{:S(2)}, u32[]{:S(2)}) collective-permute-start(f32[32,128]{1,0:T(8,128)S(1)} %get-tuple-element.195), channel_id=1, source_target_pairs={{0,32},{32,0},{64,96},{96,64},{1,33},{33,1},{65,97},{97,65},{2,34}... | collective-permute-start | bytes 49160 | tf_op jit(solution)/shard_map/ppermute | solution.py:603
  38.7 1.7 %collective-permute-start.30 = (f32[32,128]{1,0:T(8,128)S(1)}, f32[32,128]{1,0:T(8,128)S(1)}, u32[]{:S(2)}, u32[]{:S(2)}) collective-permute-start(f32[32,128]{1,0:T(8,128)S(1)} %get-tuple-element.196), channel_id=1, source_target_pairs={{0,1},{1,0},{2,3},{3,2},{4,5},{5,4},{6,7},{7,6},{8,9},{9,8},{10,11... | collective-permute-start | bytes 49160 | tf_op jit(solution)/shard_map/ppermute | solution.py:604
  40.7 5.7 %collective-permute-start.31 = (f32[96,128]{1,0:T(8,128)S(1)}, f32[96,128]{1,0:T(8,128)S(1)}, u32[]{:S(2)}, u32[]{:S(2)}) collective-permute-start(f32[96,128]{1,0:T(8,128)S(1)} %get-tuple-element.198), channel_id=1, source_target_pairs={{0,32},{1,2},{2,1},{3,4},{4,3},{5,6},{6,5},{7,8},{8,7},{9,10},{10,... | collective-permute-start | bytes 147464 | tf_op jit(solution)/shard_map/ppermute | solution.py:591
  41.7 1.2 %collective-permute-start.32 = (f32[64,128]{1,0:T(8,128)S(1)}, f32[64,128]{1,0:T(8,128)S(1)}, u32[]{:S(2)}, u32[]{:S(2)}) collective-permute-start(f32[64,128]{1,0:T(8,128)S(1)} %get-tuple-element.199.ma), channel_id=1, source_target_pairs={{0,1},{1,0},{2,3},{3,2},{4,5},{5,4},{6,7},{7,6},{8,9},{9,8},{10,11... | collective-permute-start | bytes 98312 | tf_op jit(solution)/shard_map/ppermute | solution.py:579
  47.3 3.5 %collective-permute-start.33 = (f32[8,128]{1,0:T(8,128)S(1)}, f32[8,128]{1,0:T(8,128)S(1)}, u32[]{:S(2)}, u32[]{:S(2)}) collective-permute-start(f32[8,128]{1,0:T(8,128)S(1)} %get-tuple-element.205), channel_id=1, source_target_pairs={{0,1},{1,0},{2,3},{3,2},{4,5},{5,4},{6,7},{7,6},{8,9},{9,8},{10,11... | collective-permute-start | bytes 12296 | tf_op jit(solution)/shard_map/ppermute | solution.py:579
  47.4 3.8 %collective-permute-start.34 = (f32[8,128]{1,0:T(8,128)S(1)}, f32[8,128]{1,0:T(8,128)S(1)}, u32[]{:S(2)}, u32[]{:S(2)}) collective-permute-start(f32[8,128]{1,0:T(8,128)S(1)} %get-tuple-element.206), channel_id=1, source_target_pairs={{0,32},{32,0},{64,96},{96,64},{1,33},{33,1},{65,97},{97,65},{2,34}... | collective-permute-start | bytes 12296 | tf_op jit(solution)/shard_map/ppermute | solution.py:603
  49.6 1.6 %collective-permute-start.35 = (f32[8,128]{1,0:T(8,128)S(1)}, f32[8,128]{1,0:T(8,128)S(1)}, u32[]{:S(2)}, u32[]{:S(2)}) collective-permute-start(f32[8,128]{1,0:T(8,128)S(1)} %get-tuple-element.207), channel_id=1, source_target_pairs={{0,1},{1,0},{2,3},{3,2},{4,5},{5,4},{6,7},{7,6},{8,9},{9,8},{10,11... | collective-permute-start | bytes 12296 | tf_op jit(solution)/shard_map/ppermute | solution.py:604
  52.8 5.6 %collective-permute-start.6 = (f32[32,128]{1,0:T(8,128)S(1)}, f32[32,128]{1,0:T(8,128)S(1)}, u32[]{:S(2)}, u32[]{:S(2)}) collective-permute-start(f32[32,128]{1,0:T(8,128)S(1)} %get-tuple-element.83), channel_id=1, source_target_pairs={{0,1},{1,0},{2,3},{3,2},{4,5},{5,4},{6,7},{7,6},{8,9},{9,8},{10,11... | collective-permute-start | bytes 49160 | tf_op jit(solution)/shard_map/cond/branch_1_fun/ppermute | solution.py:579
  52.9 5.6 %collective-permute-start.7 = (f32[32,128]{1,0:T(8,128)S(1)}, f32[32,128]{1,0:T(8,128)S(1)}, u32[]{:S(2)}, u32[]{:S(2)}) collective-permute-start(f32[32,128]{1,0:T(8,128)S(1)} %get-tuple-element.84), channel_id=1, source_target_pairs={{0,32},{1,2},{2,1},{3,4},{4,3},{5,6},{6,5},{7,8},{8,7},{9,10},{10,... | collective-permute-start | bytes 49160 | tf_op jit(solution)/shard_map/cond/branch_1_fun/ppermute | solution.py:591
  54.2 4.3 %collective-permute-start.8 = (f32[32,128]{1,0:T(8,128)S(1)}, f32[32,128]{1,0:T(8,128)S(1)}, u32[]{:S(2)}, u32[]{:S(2)}) collective-permute-start(f32[32,128]{1,0:T(8,128)S(1)} %get-tuple-element.85), channel_id=1, source_target_pairs={{0,32},{32,0},{64,96},{96,64},{1,33},{33,1},{65,97},{97,65},{2,34}... | collective-permute-start | bytes 49160 | tf_op jit(solution)/shard_map/cond/branch_1_fun/ppermute | solution.py:603
  56.2 2.3 %collective-permute-start.9 = (f32[32,128]{1,0:T(8,128)S(1)}, f32[32,128]{1,0:T(8,128)S(1)}, u32[]{:S(2)}, u32[]{:S(2)}) collective-permute-start(f32[32,128]{1,0:T(8,128)S(1)} %get-tuple-element.86), channel_id=1, source_target_pairs={{0,1},{1,0},{2,3},{3,2},{4,5},{5,4},{6,7},{7,6},{8,9},{9,8},{10,11... | collective-permute-start | bytes 49160 | tf_op jit(solution)/shard_map/cond/branch_1_fun/ppermute | solution.py:604
  59.7 3.0 %collective-permute-start.10 = (f32[512,128]{1,0:T(8,128)S(1)}, f32[512,128]{1,0:T(8,128)S(1)}, u32[]{:S(2)}, u32[]{:S(2)}) collective-permute-start(f32[512,128]{1,0:T(8,128)S(1)} %get-tuple-element.88), channel_id=1, source_target_pairs={{0,1},{1,0},{2,3},{3,2},{4,5},{5,4},{6,7},{7,6},{8,9},{9,8},{10,11... | collective-permute-start | bytes 786440 | tf_op jit(solution)/shard_map/cond/branch_1_fun/ppermute | solution.py:611
  60.3 7.9 %collective-permute-start.11 = (f32[512,128]{1,0:T(8,128)S(1)}, f32[512,128]{1,0:T(8,128)S(1)}, u32[]{:S(2)}, u32[]{:S(2)}) collective-permute-start(f32[512,128]{1,0:T(8,128)S(1)} %get-tuple-element.89), channel_id=1, source_target_pairs={{0,127},{1,2},{2,1},{3,4},{4,3},{5,6},{6,5},{7,8},{8,7},{9,10},{10... | collective-permute-start | bytes 786440 | tf_op jit(solution)/shard_map/cond/branch_1_fun/ppermute | solution.py:611

commit v5 on v4

--- a/solution.py
+++ b/solution.py
@@ -177,8 +177,8 @@
     block = block + lax.broadcasted_iota(jnp.int32, owner.shape, 1)
     home, place = block // BLK, block % BLK
     leaving = jnp.where(owner > home, BLK - place, jnp.where(owner < home, place + 1, 0))
-    owned[0] = jnp.sum((owner < device).astype(F32)).astype(jnp.int32)
-    owned[1] = jnp.sum((owner == device).astype(F32)).astype(jnp.int32)
+    owned[0:8, :] = jnp.full((8, LANES), jnp.sum((owner < device).astype(F32)))
+    owned[8:16, :] = jnp.full((8, LANES), jnp.sum((owner == device).astype(F32)))
     most[0] = jnp.max(leaving.astype(F32)).astype(jnp.int32)
 
 
@@ -516,7 +516,7 @@
         out[at + STEP : at + STEP + 8, :] = second
 
 
-def last_residual_kernel(src, c, f0, fy, fz, p, r, blocks, *, count):
+def last_residual_kernel(src, c, f0, fy, fz, p, r, blocks):
     t0, here = ZERO(), p[0:BS, :]
     for x in range(BS):
         at = plane(x)
@@ -524,21 +524,25 @@
         r[at, :], t0 = residual_plane(src, c, f0, fy, fz, at, t0, here, after)
         here = after
     for x in range(BS):
-        plane_to_blocks(p[plane(x), :], x, blocks, count * STEP)
-
-
-def final_kernel(ri, gx, gy, ra, rb, rc, rd, pblocks, r, blocks, sa, sb, *, count):
+        plane_to_blocks(p[plane(x), :], x, blocks, BLK * STEP)
+
+
+def final_kernel(ri, gx, gy, ra, rb, rc, rd, pblocks, r, blocks, sa, sb):
     place = Place()
-    even = place.even[0]
     add_all(place, gx, gy, ra[...], rb[...], rc[...], rd[...], r)
 
     for x in range(BS):
-        plane_to_blocks(r[plane(x), :], x, blocks, count * STEP)
+        plane_to_blocks(r[plane(x), :], x, blocks, BLK * STEP)
+    send_blocks_kernel(pblocks, blocks, sa, sb, count=1)
+
+
+def send_blocks_kernel(pblocks, blocks, sa, sb, *, count):
+    even = Place().even[0]
     for n, ref in enumerate((pblocks, blocks)):
         for b in range(count):
             for t in range(0, 256, 32):
-                low = (count + b) * STEP + t
-                high = (BLK + b) * STEP + t
+                low = (BLK + b) * STEP + t
+                high = (2 * BLK - count + b) * STEP + t
                 low, high = ref[low : low + 32, :], ref[high : high + 32, :]
                 at = slice((n * count + b) * 256 + t, (n * count + b) * 256 + t + 32)
                 sa[at, :] = pick(even, high, low)
@@ -548,16 +552,16 @@
 def place_kernel(owned, in_p, in_r, ra, rb, out_p, out_r, seq_p, seq_r, held_p, held_r, sems, *, count):
     place = Place()
     even = place.even[0]
-    start, held = owned[0], owned[1]
-    base = jnp.clip(start - place.device * BLK + count, 0, 2 * count) * STEP
-    valid = row_ids(8) < held
+    start = jnp.max(owned[0:8, :]).astype(jnp.int32)
+    base = jnp.clip(start - place.device * BLK + BLK, 0, 2 * BLK) * STEP
+    valid = row_ids(8).astype(F32) < owned[8:16, :]
     copies = []
     fields = ((seq_p, held_p, out_p), (seq_r, held_r, out_r))
     for n, (seq, tiles, out) in enumerate(fields):
         for b in range(count):
             for t in range(0, 256, 32):
                 at = slice((n * count + b) * 256 + t, (n * count + b) * 256 + t + 32)
-                low, high = b * STEP + t, (count + BLK + b) * STEP + t
+                low, high = (BLK - count + b) * STEP + t, (2 * BLK + b) * STEP + t
                 seq[low : low + 32, :] = pick(even, rb[at, :], ra[at, :])
                 seq[high : high + 32, :] = pick(even, ra[at, :], rb[at, :])
         for part in range(PIECES):
@@ -617,10 +621,11 @@
 
 FULL, TWO, CFIELD = (ROWS, LANES), (2 * BS, LANES), (CROWS, LANES)
 FACE, CFACE = (BS, LANES), (8, LANES)
+ROW = ((2 * BLK + 8) * STEP, LANES)
 
 
 def set_up(levels, new_owner, src, inv):
-    outs = [jax.ShapeDtypeStruct((2,), jnp.int32), jax.ShapeDtypeStruct((1,), jnp.int32)] + [
+    outs = [jax.ShapeDtypeStruct((16, LANES), F32), jax.ShapeDtypeStruct((1,), jnp.int32)] + [
         jax.ShapeDtypeStruct(s, F32) for s in [FULL] * 6 + [TWO] * 2 + [CFIELD] * 2 + [FACE]
     ]
     vm, sm = pl.BlockSpec(memory_space=pltpu.VMEM), pl.BlockSpec(memory_space=pltpu.SMEM)
@@ -628,14 +633,10 @@
         weights_kernel,
         out_shape=outs,
         in_specs=[sm] * 2 + [vm] * 3,
-        out_specs=[sm] * 2 + [vm] * 11,
+        out_specs=[vm, sm] + [vm] * 11,
         compiler_params=pltpu.CompilerParams(vmem_limit_bytes=48 << 20),
         cost_estimate=pl.CostEstimate(flops=4000000, bytes_accessed=6 << 20, transcendentals=0),
     )(*levels, new_owner.reshape(-1, min(LANES, new_owner.size)), src, inv)
-
-
-def row_shape(count):
-    return ((2 * count + 8) * STEP, LANES)
 
 
 def faces_kernel(inv, sa, sb, sc, sd, sems):
@@ -673,7 +674,7 @@
     return pl.pallas_call(
         faces_kernel,
         out_shape=[jax.ShapeDtypeStruct(FACE, F32)] * 4,
-        in_specs=[pl.BlockSpec(memory_space=pl.ANY)],
+        in_specs=[pl.BlockSpec(memory_space=pltpu.HBM)],
         out_specs=[pl.BlockSpec(memory_space=pltpu.VMEM)] * 4,
         scratch_shapes=[pltpu.SemaphoreType.DMA((4,))],
         compiler_params=pltpu.CompilerParams(vmem_limit_bytes=48 << 20),
@@ -682,13 +683,13 @@
 
 
 def place_blocks(count, owned, *arrays):
-    slots, row = (256, CAP, LANES), row_shape(count)
+    slots, row = (256, CAP, LANES), ROW
     vm = pl.BlockSpec(memory_space=pltpu.VMEM)
     anywhere = pl.BlockSpec(memory_space=pl.ANY)
     outs = pl.pallas_call(
         functools.partial(place_kernel, count=count),
         out_shape=[jax.ShapeDtypeStruct(shape, F32) for shape in (slots, slots, row, row)],
-        in_specs=[pl.BlockSpec(memory_space=pltpu.SMEM)] + [vm] * 4,
+        in_specs=[vm] * 5,
         out_specs=[anywhere] * 2 + [vm] * 2,
         scratch_shapes=[vmem(*slots), vmem(*slots), pltpu.SemaphoreType.DMA((2, PIECES))],
         input_output_aliases={1: 2, 2: 3},
@@ -769,26 +770,24 @@
             {0: 0},
         )
 
-    def tail(count, p, sends, fine, gx, gy, owned):
-        halos = swap_faces(*sends)
-        row = row_shape(count)
-        body = functools.partial(last_residual_kernel, count=count)
-        ri, blocks_p = call(body, [FULL, row], [*fine, p])
-        part = (2 * count * 256, LANES)
-        _, blocks_r, sa, sb = call(
-            functools.partial(final_kernel, count=count),
-            [FULL, row, part, part],
-            [ri, gx, gy, *halos, blocks_p],
-            aliases={0: 0},
-        )
-        return place_blocks(count, owned, blocks_p, blocks_r, *swap_blocks(sa, sb))
-
-    return lax.cond(
-        most.reshape(()) <= 1,
-        functools.partial(tail, 1),
-        functools.partial(tail, BLK),
-        p, sends, fine, gx, gy, owned,
-    )
+    halos = swap_faces(*sends)
+    ri, blocks_p = call(last_residual_kernel, [FULL, ROW], [*fine, p])
+    _, blocks_r, sa, sb = call(
+        final_kernel,
+        [FULL, ROW] + [(512, LANES)] * 2,
+        [ri, gx, gy, *halos, blocks_p],
+        aliases={0: 0},
+    )
+
+    def one(owned, blocks_p, blocks_r, sa, sb):
+        return place_blocks(1, owned, blocks_p, blocks_r, *swap_blocks(sa, sb))
+
+    def several(owned, blocks_p, blocks_r, sa, sb):
+        body = functools.partial(send_blocks_kernel, count=BLK)
+        sends = call(body, [(2 * BLK * 256, LANES)] * 2, [blocks_p, blocks_r])
+        return place_blocks(BLK, owned, blocks_p, blocks_r, *swap_blocks(*sends))
+
+    return lax.cond(most.reshape(()) <= 1, one, several, owned, blocks_p, blocks_r, sa, sb)
 
 
 def solution(mesh):

time: 70.4 us -> 70.7 us (level)
    ppermute x7, waiting for transfers between devices: 3.17 us -> 3.89 us  [swap_regions(): inner = lax.ppermute(inner, 'region', [(i, i ^ 1) for i in range(regions)])]
where the time goes in v5:
time: 70.7 us; the launch traced here: 70.6 us
  starting transfers between devices  27.1 us (38%)
  waiting for transfers between devices  22 us (31%)
  Pallas kernels  18.3 us (26%)
  between operations  1.76 us (2%)
  local copies, waits for them, and re-layouts  1.42 us (2%)
    ppermute x7, starting transfers between devices, swap_regions(): inner = lax.ppermute(inner, 'region', [(i, i ^ 1) for i in range(regions)])  15.8 us
    pallas_call x16, Pallas kernels, call(): pl.pallas_call(body, out_shape=outs, in_specs=[pl.BlockSpec(memory_space=...  15.3 us
    ppermute x5, waiting for transfers between devices, swap_far(): return lax.ppermute(value, BOTH, pairs)  10.1 us
    ppermute x5, starting transfers between devices, swap_far(): return lax.ppermute(value, BOTH, pairs)  6.82 us
    ppermute x2, waiting for transfers between devices, swap_blocks(): return (lax.ppermute(first, BOTH, inner), lax.ppermute(second, BOTH, outer))  5.45 us
    ppermute x7, waiting for transfers between devices, swap_regions(): inner = lax.ppermute(inner, 'region', [(i, i ^ 1) for i in range(regions)])  3.89 us
    ppermute x2, starting transfers between devices, swap_blocks(): return (lax.ppermute(first, BOTH, inner), lax.ppermute(second, BOTH, outer))  3.04 us
    ppermute x9, waiting for transfers between devices, swap_near(): lax.ppermute(value, 'member', [(i, i ^ 1) for i in range(lax.axis_size('m...  2.47 us
  transfers between devices with their start and end apart: 30, of which 11 were waited for; matrix products, arithmetic and copies ran while one was open for 0% of the time, Pallas kernels for 9%

profile of v5, /device:TPU:6, one launch (start us, length us, event | category | flops | bytes accessed | tf_op | source)
XLA Modules:
  0.0 70.6 jit_solution(1223719787255259231)
XLA Ops:
  0.6 1.4 %copy-done = f32[3,32,32,128]{3,2,1,0:T(8,128)S(1)} copy-done((f32[3,32,32,128]{3,2,1,0:T(8,128)S(1)}, f32[3,32,32,128]{3,2,1,0:T(8,128)}, u32[]{:S(2)}) %copy-start) | copy-done | bytes 1572888
  2.1 0.1 shard_map.73
  2.2 0.1 collective-permute-start.4
  2.3 3.4 %collective-permute-start.5 = (f32[32,128]{1,0:T(8,128)S(1)}, f32[32,128]{1,0:T(8,128)S(1)}, u32[]{:S(2)}, u32[]{:S(2)}) collective-permute-start(f32[32,128]{1,0:T(8,128)S(1)} %get-tuple-element.107), channel_id=1, source_target_pairs={{0,32},{1,2},{2,1},{3,4},{4,3},{5,6},{6,5},{7,8},{8,7},{9,10},{10,... | collective-permute-start | bytes 49160 | tf_op jit(solution)/shard_map/ppermute | solution.py:595
  5.7 1.9 %collective-permute-start.6 = (f32[32,128]{1,0:T(8,128)S(1)}, f32[32,128]{1,0:T(8,128)S(1)}, u32[]{:S(2)}, u32[]{:S(2)}) collective-permute-start(f32[32,128]{1,0:T(8,128)S(1)} %get-tuple-element.108), channel_id=1, source_target_pairs={{0,32},{32,0},{64,96},{96,64},{1,33},{33,1},{65,97},{97,65},{2,34}... | collective-permute-start | bytes 49160 | tf_op jit(solution)/shard_map/ppermute | solution.py:607
  7.6 0.0 collective-permute-start.7
  7.6 1.5 %shard_map.72 = (f32[16,128]{1,0:T(8,128)S(1)}, s32[1]{0:T(128)}, f32[1024,128]{1,0:T(8,128)S(1)}, f32[1024,128]{1,0:T(8,128)S(1)}, f32[1024,128]{1,0:T(8,128)S(...) custom-call(s32[4]{0:T(128)S(1)} %copy-done.4, ...), custom_call_target="tpu_custom_call" | custom-call | flops 4000000 | bytes 6291456 | tf_op jit(solution)/shard_map/pallas_call | solution.py:632
  9.1 0.0 collective-permute-done.4.ra
  9.2 0.3 collective-permute-done.6.rc
  9.4 0.0 collective-permute-done.7.rd
  9.4 1.6 %shard_map.74 = (f32[1024,128]{1,0:T(8,128)S(1)}, f32[1024,128]{1,0:T(8,128)S(1)}, f32[64,128]{1,0:T(8,128)S(1)}, f32[64,128]{1,0:T(8,128)S(1)}, f32[1024,128]{1...) custom-call(f32[32,128]{1,0:T(8,128)S(1)} %get-tuple-element.99.limi, ...), custom_call_target="tpu_custom_call", output_to_operand_aliasing={{0}: (5, {})} | custom-call | flops 2000000 | bytes 4472832 | tf_op jit(solution)/shard_map/pallas_call | solution.py:38
  11.0 0.3 collective-permute-start.8
  11.4 3.3 %collective-permute-start.9 = (f32[32,128]{1,0:T(8,128)S(1)}, f32[32,128]{1,0:T(8,128)S(1)}, u32[]{:S(2)}, u32[]{:S(2)}) collective-permute-start(f32[32,128]{1,0:T(8,128)S(1)} %get-tuple-element.116), channel_id=1, source_target_pairs={{0,32},{32,0},{64,96},{96,64},{1,33},{33,1},{65,97},{97,65},{2,34}... | collective-permute-start | bytes 49160 | tf_op jit(solution)/shard_map/ppermute | solution.py:607
  14.6 0.2 collective-permute-start.10
  14.8 0.5 shard_map.75.qi
  15.3 0.5 shard_map.76.rest_0_
  15.9 0.5 collective-permute-done.9.rc
  16.4 0.2 shard_map.77
  16.6 0.3 collective-permute-start.11
  16.9 1.3 %collective-permute-done.12.qa = f32[128,128]{1,0:T(8,128)S(1)} collective-permute-done((f32[128,128]{1,0:T(8,128)S(1)}, f32[128,128]{1,0:T(8,128)S(1)}, u32[]{:S(2)}, u32[]{:S(2)}) %collective-permute-start.12) | collective-permute-done | bytes 65568 | tf_op jit(solution)/shard_map/ppermute | solution.py:583
  18.1 4.5 %collective-permute-done.11.qb = f32[160,128]{1,0:T(8,128)S(1)} collective-permute-done((f32[160,128]{1,0:T(8,128)S(1)}, f32[160,128]{1,0:T(8,128)S(1)}, u32[]{:S(2)}, u32[]{:S(2)}) %collective-permute-start.11) | collective-permute-done | bytes 81952 | tf_op jit(solution)/shard_map/ppermute | solution.py:595
  22.6 1.3 %shard_map.78 = (f32[64,128]{1,0:T(8,128)S(1)}, f32[8,128]{1,0:T(8,128)S(1)}, f32[8,128]{1,0:T(8,128)S(1)}, f32[8,128]{1,0:T(8,128)S(1)}, f32[8,128]{1,0:T(8,128)S(1)}, /*index=5*/f32[768,128]{1,0:T(8,128)S(1)}) custom-call(f32[128,128]{1,0:T(8,128)S(1)} %get-tuple-element.122.ma, f32[128,128]{1,0:T(8,128)S(1)} %collective-permute-done.12.qa, ...), custom_call_target="tpu_custom_call" | custom-call | flops 2000000 | bytes 704512 | tf_op jit(solution)/shard_map/pallas_call | solution.py:38
  23.9 0.1 collective-permute-start.13
  24.0 2.2 %collective-permute-start.14 = (f32[8,128]{1,0:T(8,128)S(1)}, f32[8,128]{1,0:T(8,128)S(1)}, u32[]{:S(2)}, u32[]{:S(2)}) collective-permute-start(f32[8,128]{1,0:T(8,128)S(1)} %get-tuple-element.129), channel_id=1, source_target_pairs={{0,32},{32,0},{64,96},{96,64},{1,33},{33,1},{65,97},{97,65},{2,34}... | collective-permute-start | bytes 12296 | tf_op jit(solution)/shard_map/ppermute | solution.py:607
  26.2 0.2 collective-permute-start.15
  26.3 0.3 shard_map.79
  26.7 1.1 %collective-permute-done.14.kc = f32[8,128]{1,0:T(8,128)S(1)} collective-permute-done((f32[8,128]{1,0:T(8,128)S(1)}, f32[8,128]{1,0:T(8,128)S(1)}, u32[]{:S(2)}, u32[]{:S(2)}) %collective-permute-start.14) | collective-permute-done | bytes 4128 | tf_op jit(solution)/shard_map/ppermute | solution.py:607
  27.7 0.0 collective-permute-done.15.kd
  27.7 1.6 %shard_map.80 = (f32[1024,128]{1,0:T(8,128)S(1)}, f32[1024,128]{1,0:T(8,128)S(1)}, f32[32,128]{1,0:T(8,128)S(1)}, f32[32,128]{1,0:T(8,128)S(1)}, f32[32,128]{1,0:T(8,128)S(1)}, /*index=5*/f32[32,128]{1,0:T(8,128)S(1)}) custom-call(f32[1024,128]{1,0:T(8,128)S(1)} %get-tuple-element.125.ri, ...), custom_call_target="tpu_custom_call", output_to_operand_aliasing={{0}: (0, {})} | custom-call | flops 2000000 | bytes 4403200 | tf_op jit(solution)/shard_map/pallas_call | solution.py:38
  29.4 0.1 collective-permute-start.16
  29.5 0.8 %collective-permute-start.17 = (f32[32,128]{1,0:T(8,128)S(1)}, f32[32,128]{1,0:T(8,128)S(1)}, u32[]{:S(2)}, u32[]{:S(2)}) collective-permute-start(f32[32,128]{1,0:T(8,128)S(1)} %get-tuple-element.133), channel_id=1, source_target_pairs={{0,32},{1,2},{2,1},{3,4},{4,3},{5,6},{6,5},{7,8},{8,7},{9,10},{10,... | collective-permute-start | bytes 49160 | tf_op jit(solution)/shard_map/ppermute | solution.py:595
  30.2 2.0 %collective-permute-start.18 = (f32[32,128]{1,0:T(8,128)S(1)}, f32[32,128]{1,0:T(8,128)S(1)}, u32[]{:S(2)}, u32[]{:S(2)}) collective-permute-start(f32[32,128]{1,0:T(8,128)S(1)} %get-tuple-element.134), channel_id=1, source_target_pairs={{0,32},{32,0},{64,96},{96,64},{1,33},{33,1},{65,97},{97,65},{2,34}... | collective-permute-start | bytes 49160 | tf_op jit(solution)/shard_map/ppermute | solution.py:607
  32.3 0.0 collective-permute-start.19
  32.3 0.3 shard_map.81.ri
  32.6 2.2 %collective-permute-done.17.rb = f32[32,128]{1,0:T(8,128)S(1)} collective-permute-done((f32[32,128]{1,0:T(8,128)S(1)}, f32[32,128]{1,0:T(8,128)S(1)}, u32[]{:S(2)}, u32[]{:S(2)}) %collective-permute-start.17) | collective-permute-done | bytes 16416 | tf_op jit(solution)/shard_map/ppermute | solution.py:595
  34.8 1.6 %shard_map.82 = (f32[1024,128]{1,0:T(8,128)S(1)}, f32[1024,128]{1,0:T(8,128)S(1)}, f32[32,128]{1,0:T(8,128)S(1)}, f32[32,128]{1,0:T(8,128)S(1)}, f32[32,128]{1,0:T(8,128)S(1)}, /*index=5*/f32[32,128]{1,0:T(8,128)S(1)}) custom-call(f32[1024,128]{1,0:T(8,128)S(1)} %shard_map.81.ri, ...), custom_call_target="tpu_custom_call", output_to_operand_aliasing={{0}: (0, {})} | custom-call | flops 2000000 | bytes 4407296 | tf_op jit(solution)/shard_map/pallas_call | solution.py:38
  36.5 0.1 collective-permute-start.20
  36.5 2.2 %collective-permute-start.21 = (f32[32,128]{1,0:T(8,128)S(1)}, f32[32,128]{1,0:T(8,128)S(1)}, u32[]{:S(2)}, u32[]{:S(2)}) collective-permute-start(f32[32,128]{1,0:T(8,128)S(1)} %get-tuple-element.138), channel_id=1, source_target_pairs={{0,32},{32,0},{64,96},{96,64},{1,33},{33,1},{65,97},{97,65},{2,34}... | collective-permute-start | bytes 49160 | tf_op jit(solution)/shard_map/ppermute | solution.py:607
  38.7 0.2 collective-permute-start.22
  38.9 0.5 shard_map.83.qi
  39.4 0.0 collective-permute-done.20.ra
  39.5 1.0 %collective-permute-done.21.rc = f32[32,128]{1,0:T(8,128)S(1)} collective-permute-done((f32[32,128]{1,0:T(8,128)S(1)}, f32[32,128]{1,0:T(8,128)S(1)}, u32[]{:S(2)}, u32[]{:S(2)}) %collective-permute-start.21) | collective-permute-done | bytes 16416 | tf_op jit(solution)/shard_map/ppermute | solution.py:607
  40.5 0.0 collective-permute-done.22.rd
  40.5 0.2 shard_map.84
  40.7 1.1 %collective-permute-start.23 = (f32[96,128]{1,0:T(8,128)S(1)}, f32[96,128]{1,0:T(8,128)S(1)}, u32[]{:S(2)}, u32[]{:S(2)}) collective-permute-start(f32[96,128]{1,0:T(8,128)S(1)} %get-tuple-element.141), channel_id=1, source_target_pairs={{0,32},{1,2},{2,1},{3,4},{4,3},{5,6},{6,5},{7,8},{8,7},{9,10},{10,... | collective-permute-start | bytes 147464 | tf_op jit(solution)/shard_map/ppermute | solution.py:595
  41.7 1.2 %collective-permute-done.24.qa = f32[64,128]{1,0:T(8,128)S(1)} collective-permute-done((f32[64,128]{1,0:T(8,128)S(1)}, f32[64,128]{1,0:T(8,128)S(1)}, u32[]{:S(2)}, u32[]{:S(2)}) %collective-permute-start.24) | collective-permute-done | bytes 32800 | tf_op jit(solution)/shard_map/ppermute | solution.py:583
  42.9 3.4 %collective-permute-done.23.qb = f32[96,128]{1,0:T(8,128)S(1)} collective-permute-done((f32[96,128]{1,0:T(8,128)S(1)}, f32[96,128]{1,0:T(8,128)S(1)}, u32[]{:S(2)}, u32[]{:S(2)}) %collective-permute-start.23) | collective-permute-done | bytes 49184 | tf_op jit(solution)/shard_map/ppermute | solution.py:595
  46.4 0.9 %shard_map.85 = (f32[64,128]{1,0:T(8,128)S(1)}, f32[8,128]{1,0:T(8,128)S(1)}, f32[8,128]{1,0:T(8,128)S(1)}, f32[8,128]{1,0:T(8,128)S(1)}, f32[8,128]{1,0:T(8,128)S(1)}) custom-call(f32[64,128]{1,0:T(8,128)S(1)} %get-tuple-element.142.ma, f32[64,128]{1,0:T(8,128)S(1)} %collective-permute-done.24.qa, f32[96,128]{1,0:T(8,128)S(1)} %collective-permute-done.23.qb, ...), custom_call_target="tpu_custom_call" | custom-call | flops 2000000 | bytes 606208 | tf_op jit(solution)/shard_map/pallas_call | solution.py:38
  47.3 0.1 collective-permute-start.25
  47.4 2.2 %collective-permute-start.26 = (f32[8,128]{1,0:T(8,128)S(1)}, f32[8,128]{1,0:T(8,128)S(1)}, u32[]{:S(2)}, u32[]{:S(2)}) collective-permute-start(f32[8,128]{1,0:T(8,128)S(1)} %get-tuple-element.149), channel_id=1, source_target_pairs={{0,32},{32,0},{64,96},{96,64},{1,33},{33,1},{65,97},{97,65},{2,34}... | collective-permute-start | bytes 12296 | tf_op jit(solution)/shard_map/ppermute | solution.py:607
  49.6 0.2 collective-permute-start.27
  49.7 0.4 shard_map.86
  50.1 1.1 %collective-permute-done.26.kc = f32[8,128]{1,0:T(8,128)S(1)} collective-permute-done((f32[8,128]{1,0:T(8,128)S(1)}, f32[8,128]{1,0:T(8,128)S(1)}, u32[]{:S(2)}, u32[]{:S(2)}) %collective-permute-start.26) | collective-permute-done | bytes 4128 | tf_op jit(solution)/shard_map/ppermute | solution.py:607
  51.2 1.8 %shard_map.87 = (f32[1024,128]{1,0:T(8,128)S(1)}, f32[1024,128]{1,0:T(8,128)S(1)}, f32[32,128]{1,0:T(8,128)S(1)}, f32[32,128]{1,0:T(8,128)S(1)}, f32[32,128]{1,0:T(8,128)S(1)}, /*index=5*/f32[32,128]{1,0:T(8,128)S(1)}) custom-call(f32[1024,128]{1,0:T(8,128)S(1)} %get-tuple-element.146.ri, ...), custom_call_target="tpu_custom_call", output_to_operand_aliasing={{0}: (0, {})} | custom-call | flops 2000000 | bytes 4403200 | tf_op jit(solution)/shard_map/pallas_call | solution.py:38
  53.0 0.1 collective-permute-start.28
  53.1 1.3 %collective-permute-start.29 = (f32[32,128]{1,0:T(8,128)S(1)}, f32[32,128]{1,0:T(8,128)S(1)}, u32[]{:S(2)}, u32[]{:S(2)}) collective-permute-start(f32[32,128]{1,0:T(8,128)S(1)} %get-tuple-element.155), channel_id=1, source_target_pairs={{0,32},{1,2},{2,1},{3,4},{4,3},{5,6},{6,5},{7,8},{8,7},{9,10},{10,... | collective-permute-start | bytes 49160 | tf_op jit(solution)/shard_map/ppermute | solution.py:595
  54.4 2.0 %collective-permute-start.30 = (f32[32,128]{1,0:T(8,128)S(1)}, f32[32,128]{1,0:T(8,128)S(1)}, u32[]{:S(2)}, u32[]{:S(2)}) collective-permute-start(f32[32,128]{1,0:T(8,128)S(1)} %get-tuple-element.156), channel_id=1, source_target_pairs={{0,32},{32,0},{64,96},{96,64},{1,33},{33,1},{65,97},{97,65},{2,34}... | collective-permute-start | bytes 49160 | tf_op jit(solution)/shard_map/ppermute | solution.py:607
  57.0 2.2 %shard_map.88 = (f32[1024,128]{1,0:T(8,128)S(1)}, f32[4224,128]{1,0:T(8,128)S(1)}) custom-call(f32[1024,128]{1,0:T(8,128)S(1)} %get-tuple-element.98.src, f32[1024,128]{1,0:T(8,128)S(1)} %get-tuple-element.110.c, f32[1024,128]{1,0:T(8,128)S(1)} %get-tuple-element.100.f0, f32[1024,128]{1,0:T(8,128)S(1)} %get-tuple-element.101.fy, ...), custom_call_target="tpu_custom_call" | custom-call | flops 2000000 | bytes 5832704 | tf_op jit(solution)/shard_map/pallas_call | solution.py:38
  59.3 1.2 %shard_map.89 = (f32[1024,128]{1,0:T(8,128)S(1)}, f32[4224,128]{1,0:T(8,128)S(1)}, f32[512,128]{1,0:T(8,128)S(1)}, f32[512,128]{1,0:T(8,128)S(1)}) custom-call(f32[1024,128]{1,0:T(8,128)S(1)} %get-tuple-element.153.ri, f32[64,128]{1,0:T(8,128)S(1)} %get-tuple-element.114.gx, f32[64,128]{1,0:T(8,128)S(1)} %get-tuple-element.113.gy, ...), custom_call_target="tpu_custom_call", output_to_operand_aliasing={{0}: (0, {})} | custom-call | flops 2000000 | bytes 6029312 | tf_op jit(solution)/shard_map/pallas_call | solution.py:38
  60.5 9.9 %conditional.1 = (f32[6,32768]{1,0:T(8,128)}, f32[6,32768]{1,0:T(8,128)}) conditional(s32[]{:T(128)} %bitcast.15, (f32[4224,128]{1,0:T(8,128)S(1)}, f32[4224,128]{1,0:T(8,128)S(1)}, f32[16,128]{1,0:T(8,128)S(1)}) %tuple.15, (f32[512,128]{1,0:T(8,128)S(1)}, f32[512,128]{1,0:T(8,128)S(1)}, f32[16,128]{1,0:T(8,128)S(1)}, f32[4224,128]{1,0:T(8,128)S(1)}, ...), branch_computations={%region_0.0_spmd, %region_1.0_spmd} | conditional | flops 4000000 | bytes 21102688 | solution.py:790
  60.6 0.6 collective-permute-start.2
  61.1 2.5 %collective-permute-start.3 = (f32[512,128]{1,0:T(8,128)S(1)}, f32[512,128]{1,0:T(8,128)S(1)}, u32[]{:S(2)}, u32[]{:S(2)}) collective-permute-start(f32[512,128]{1,0:T(8,128)S(1)} %get-tuple-element.27), channel_id=1, source_target_pairs={{0,127},{1,2},{2,1},{3,4},{4,3},{5,6},{6,5},{7,8},{8,7},{9,10},{10... | collective-permute-start | bytes 786440 | tf_op jit(solution)/shard_map/cond/branch_1_fun/ppermute | solution.py:615
  63.6 5.5 %collective-permute-done.3.rb = f32[512,128]{1,0:T(8,128)S(1)} collective-permute-done((f32[512,128]{1,0:T(8,128)S(1)}, f32[512,128]{1,0:T(8,128)S(1)}, u32[]{:S(2)}, u32[]{:S(2)}) %collective-permute-start.3) | collective-permute-done | bytes 262176 | tf_op jit(solution)/shard_map/cond/branch_1_fun/ppermute | solution.py:615
  69.0 1.4 %branch_1_fun.1 = (f32[256,6,128]{2,1,0:T(8,128)}, f32[256,6,128]{2,1,0:T(8,128)}, f32[4224,128]{1,0:T(8,128)S(1)}, f32[4224,128]{1,0:T(8,128)S(1)}) custom-call(f32[16,128]{1,0:T(8,128)S(1)} %get-tuple-element.23.owned, f32[4224,128]{1,0:T(8,128)S(1)} %get-tuple-element.24.in_p, ...), custom_call_target="tpu_custom_call", output_to_operand_aliasing={{2}: (1, {}), {3}: (2, {})} | custom-call | flops 2000000 | bytes 6291456 | tf_op jit(solution)/shard_map/cond/branch_1_fun/pallas_call | solution.py:689
  (28 shorter events, 0.1 us)
Async XLA Ops:
  0.6 1.4 %copy-start = (f32[3,32,32,128]{3,2,1,0:T(8,128)S(1)}, f32[3,32,32,128]{3,2,1,0:T(8,128)}, u32[]{:S(2)}) copy-start(f32[3,32,32,128]{3,2,1,0:T(8,128)} %inv.1) | copy-start | bytes 4718596
  2.0 5.6 %copy-start.1 = (f32[3,32,32,128]{3,2,1,0:T(8,128)S(1)}, f32[3,32,32,128]{3,2,1,0:T(8,128)}, u32[]{:S(2)}) copy-start(f32[3,32,32,128]{3,2,1,0:T(8,128)} %inv.1) | copy-start | bytes 4718596
  2.0 5.6 %copy-start.2 = (f32[32,32,128]{2,1,0:T(8,128)S(1)}, f32[32,32,128]{2,1,0:T(8,128)}, u32[]{:S(2)}) copy-start(f32[32,32,128]{2,1,0:T(8,128)} %param.7) | copy-start | bytes 1572868
  2.0 5.6 %copy-start.3 = (s32[512]{0:T(512)S(1)}, s32[512]{0:T(512)}, u32[]{:S(2)}) copy-start(s32[512]{0:T(512)} %param.11) | copy-start | bytes 6148
  2.0 5.6 %copy-start.4 = (s32[4]{0:T(128)S(1)}, s32[4]{0:T(128)}, u32[]{:S(2)}) copy-start(s32[4]{0:T(128)} %levels.1) | copy-start | bytes 52
  2.1 5.6 %copy-start.5 = (s32[3]{0:T(128)S(1)}, s32[3]{0:T(128)}, u32[]{:S(2)}) copy-start(s32[3]{0:T(128)} %level_sweeps.1) | copy-start | bytes 40
  2.2 6.9 %collective-permute-start.4 = (f32[32,128]{1,0:T(8,128)S(1)}, f32[32,128]{1,0:T(8,128)S(1)}, u32[]{:S(2)}, u32[]{:S(2)}) collective-permute-start(f32[32,128]{1,0:T(8,128)S(1)} %get-tuple-element.106), channel_id=1, source_target_pairs={{0,1},{1,0},{2,3},{3,2},{4,5},{5,4},{6,7},{7,6},{8,9},{9,8},{10,11... | collective-permute-start | bytes 49160 | tf_op jit(solution)/shard_map/ppermute | solution.py:583
  2.3 6.8 %collective-permute-start.5 = (f32[32,128]{1,0:T(8,128)S(1)}, f32[32,128]{1,0:T(8,128)S(1)}, u32[]{:S(2)}, u32[]{:S(2)}) collective-permute-start(f32[32,128]{1,0:T(8,128)S(1)} %get-tuple-element.107), channel_id=1, source_target_pairs={{0,32},{1,2},{2,1},{3,4},{4,3},{5,6},{6,5},{7,8},{8,7},{9,10},{10,... | collective-permute-start | bytes 49160 | tf_op jit(solution)/shard_map/ppermute | solution.py:595
  5.7 3.7 %collective-permute-start.6 = (f32[32,128]{1,0:T(8,128)S(1)}, f32[32,128]{1,0:T(8,128)S(1)}, u32[]{:S(2)}, u32[]{:S(2)}) collective-permute-start(f32[32,128]{1,0:T(8,128)S(1)} %get-tuple-element.108), channel_id=1, source_target_pairs={{0,32},{32,0},{64,96},{96,64},{1,33},{33,1},{65,97},{97,65},{2,34}... | collective-permute-start | bytes 49160 | tf_op jit(solution)/shard_map/ppermute | solution.py:607
  7.6 1.8 %collective-permute-start.7 = (f32[32,128]{1,0:T(8,128)S(1)}, f32[32,128]{1,0:T(8,128)S(1)}, u32[]{:S(2)}, u32[]{:S(2)}) collective-permute-start(f32[32,128]{1,0:T(8,128)S(1)} %get-tuple-element.109), channel_id=1, source_target_pairs={{0,1},{1,0},{2,3},{3,2},{4,5},{5,4},{6,7},{7,6},{8,9},{9,8},{10,11... | collective-permute-start | bytes 49160 | tf_op jit(solution)/shard_map/ppermute | solution.py:608
  11.0 4.8 %collective-permute-start.8 = (f32[32,128]{1,0:T(8,128)S(1)}, f32[32,128]{1,0:T(8,128)S(1)}, u32[]{:S(2)}, u32[]{:S(2)}) collective-permute-start(f32[32,128]{1,0:T(8,128)S(1)} %get-tuple-element.115), channel_id=1, source_target_pairs={{0,1},{1,0},{2,3},{3,2},{4,5},{5,4},{6,7},{7,6},{8,9},{9,8},{10,11... | collective-permute-start | bytes 49160 | tf_op jit(solution)/shard_map/ppermute | solution.py:583
  11.4 5.0 %collective-permute-start.9 = (f32[32,128]{1,0:T(8,128)S(1)}, f32[32,128]{1,0:T(8,128)S(1)}, u32[]{:S(2)}, u32[]{:S(2)}) collective-permute-start(f32[32,128]{1,0:T(8,128)S(1)} %get-tuple-element.116), channel_id=1, source_target_pairs={{0,32},{32,0},{64,96},{96,64},{1,33},{33,1},{65,97},{97,65},{2,34}... | collective-permute-start | bytes 49160 | tf_op jit(solution)/shard_map/ppermute | solution.py:607
  14.6 1.7 %collective-permute-start.10 = (f32[32,128]{1,0:T(8,128)S(1)}, f32[32,128]{1,0:T(8,128)S(1)}, u32[]{:S(2)}, u32[]{:S(2)}) collective-permute-start(f32[32,128]{1,0:T(8,128)S(1)} %get-tuple-element.117), channel_id=1, source_target_pairs={{0,1},{1,0},{2,3},{3,2},{4,5},{5,4},{6,7},{7,6},{8,9},{9,8},{10,11... | collective-permute-start | bytes 49160 | tf_op jit(solution)/shard_map/ppermute | solution.py:608
  16.6 6.1 %collective-permute-start.11 = (f32[160,128]{1,0:T(8,128)S(1)}, f32[160,128]{1,0:T(8,128)S(1)}, u32[]{:S(2)}, u32[]{:S(2)}) collective-permute-start(f32[160,128]{1,0:T(8,128)S(1)} %get-tuple-element.121), channel_id=1, source_target_pairs={{0,32},{1,2},{2,1},{3,4},{4,3},{5,6},{6,5},{7,8},{8,7},{9,10},{10,... | collective-permute-start | bytes 245768 | tf_op jit(solution)/shard_map/ppermute | solution.py:595
  16.9 1.3 %collective-permute-start.12 = (f32[128,128]{1,0:T(8,128)S(1)}, f32[128,128]{1,0:T(8,128)S(1)}, u32[]{:S(2)}, u32[]{:S(2)}) collective-permute-start(f32[128,128]{1,0:T(8,128)S(1)} %get-tuple-element.122.ma), channel_id=1, source_target_pairs={{0,1},{1,0},{2,3},{3,2},{4,5},{5,4},{6,7},{7,6},{8,9},{9,8},{10,11... | collective-permute-start | bytes 196616 | tf_op jit(solution)/shard_map/ppermute | solution.py:583
  23.9 2.8 %collective-permute-start.13 = (f32[8,128]{1,0:T(8,128)S(1)}, f32[8,128]{1,0:T(8,128)S(1)}, u32[]{:S(2)}, u32[]{:S(2)}) collective-permute-start(f32[8,128]{1,0:T(8,128)S(1)} %get-tuple-element.128), channel_id=1, source_target_pairs={{0,1},{1,0},{2,3},{3,2},{4,5},{5,4},{6,7},{7,6},{8,9},{9,8},{10,11... | collective-permute-start | bytes 12296 | tf_op jit(solution)/shard_map/ppermute | solution.py:583
  24.0 3.8 %collective-permute-start.14 = (f32[8,128]{1,0:T(8,128)S(1)}, f32[8,128]{1,0:T(8,128)S(1)}, u32[]{:S(2)}, u32[]{:S(2)}) collective-permute-start(f32[8,128]{1,0:T(8,128)S(1)} %get-tuple-element.129), channel_id=1, source_target_pairs={{0,32},{32,0},{64,96},{96,64},{1,33},{33,1},{65,97},{97,65},{2,34}... | collective-permute-start | bytes 12296 | tf_op jit(solution)/shard_map/ppermute | solution.py:607
  26.2 1.6 %collective-permute-start.15 = (f32[8,128]{1,0:T(8,128)S(1)}, f32[8,128]{1,0:T(8,128)S(1)}, u32[]{:S(2)}, u32[]{:S(2)}) collective-permute-start(f32[8,128]{1,0:T(8,128)S(1)} %get-tuple-element.130), channel_id=1, source_target_pairs={{0,1},{1,0},{2,3},{3,2},{4,5},{5,4},{6,7},{7,6},{8,9},{9,8},{10,11... | collective-permute-start | bytes 12296 | tf_op jit(solution)/shard_map/ppermute | solution.py:608
  29.4 3.2 %collective-permute-start.16 = (f32[32,128]{1,0:T(8,128)S(1)}, f32[32,128]{1,0:T(8,128)S(1)}, u32[]{:S(2)}, u32[]{:S(2)}) collective-permute-start(f32[32,128]{1,0:T(8,128)S(1)} %get-tuple-element.132), channel_id=1, source_target_pairs={{0,1},{1,0},{2,3},{3,2},{4,5},{5,4},{6,7},{7,6},{8,9},{9,8},{10,11... | collective-permute-start | bytes 49160 | tf_op jit(solution)/shard_map/ppermute | solution.py:583
  29.5 5.4 %collective-permute-start.17 = (f32[32,128]{1,0:T(8,128)S(1)}, f32[32,128]{1,0:T(8,128)S(1)}, u32[]{:S(2)}, u32[]{:S(2)}) collective-permute-start(f32[32,128]{1,0:T(8,128)S(1)} %get-tuple-element.133), channel_id=1, source_target_pairs={{0,32},{1,2},{2,1},{3,4},{4,3},{5,6},{6,5},{7,8},{8,7},{9,10},{10,... | collective-permute-start | bytes 49160 | tf_op jit(solution)/shard_map/ppermute | solution.py:595
  30.2 4.6 %collective-permute-start.18 = (f32[32,128]{1,0:T(8,128)S(1)}, f32[32,128]{1,0:T(8,128)S(1)}, u32[]{:S(2)}, u32[]{:S(2)}) collective-permute-start(f32[32,128]{1,0:T(8,128)S(1)} %get-tuple-element.134), channel_id=1, source_target_pairs={{0,32},{32,0},{64,96},{96,64},{1,33},{33,1},{65,97},{97,65},{2,34}... | collective-permute-start | bytes 49160 | tf_op jit(solution)/shard_map/ppermute | solution.py:607
  32.3 2.6 %collective-permute-start.19 = (f32[32,128]{1,0:T(8,128)S(1)}, f32[32,128]{1,0:T(8,128)S(1)}, u32[]{:S(2)}, u32[]{:S(2)}) collective-permute-start(f32[32,128]{1,0:T(8,128)S(1)} %get-tuple-element.135), channel_id=1, source_target_pairs={{0,1},{1,0},{2,3},{3,2},{4,5},{5,4},{6,7},{7,6},{8,9},{9,8},{10,11... | collective-permute-start | bytes 49160 | tf_op jit(solution)/shard_map/ppermute | solution.py:608
  36.5 3.0 %collective-permute-start.20 = (f32[32,128]{1,0:T(8,128)S(1)}, f32[32,128]{1,0:T(8,128)S(1)}, u32[]{:S(2)}, u32[]{:S(2)}) collective-permute-start(f32[32,128]{1,0:T(8,128)S(1)} %get-tuple-element.137), channel_id=1, source_target_pairs={{0,1},{1,0},{2,3},{3,2},{4,5},{5,4},{6,7},{7,6},{8,9},{9,8},{10,11... | collective-permute-start | bytes 49160 | tf_op jit(solution)/shard_map/ppermute | solution.py:583
  36.5 3.9 %collective-permute-start.21 = (f32[32,128]{1,0:T(8,128)S(1)}, f32[32,128]{1,0:T(8,128)S(1)}, u32[]{:S(2)}, u32[]{:S(2)}) collective-permute-start(f32[32,128]{1,0:T(8,128)S(1)} %get-tuple-element.138), channel_id=1, source_target_pairs={{0,32},{32,0},{64,96},{96,64},{1,33},{33,1},{65,97},{97,65},{2,34}... | collective-permute-start | bytes 49160 | tf_op jit(solution)/shard_map/ppermute | solution.py:607
  38.7 1.7 %collective-permute-start.22 = (f32[32,128]{1,0:T(8,128)S(1)}, f32[32,128]{1,0:T(8,128)S(1)}, u32[]{:S(2)}, u32[]{:S(2)}) collective-permute-start(f32[32,128]{1,0:T(8,128)S(1)} %get-tuple-element.139), channel_id=1, source_target_pairs={{0,1},{1,0},{2,3},{3,2},{4,5},{5,4},{6,7},{7,6},{8,9},{9,8},{10,11... | collective-permute-start | bytes 49160 | tf_op jit(solution)/shard_map/ppermute | solution.py:608
  40.7 5.7 %collective-permute-start.23 = (f32[96,128]{1,0:T(8,128)S(1)}, f32[96,128]{1,0:T(8,128)S(1)}, u32[]{:S(2)}, u32[]{:S(2)}) collective-permute-start(f32[96,128]{1,0:T(8,128)S(1)} %get-tuple-element.141), channel_id=1, source_target_pairs={{0,32},{1,2},{2,1},{3,4},{4,3},{5,6},{6,5},{7,8},{8,7},{9,10},{10,... | collective-permute-start | bytes 147464 | tf_op jit(solution)/shard_map/ppermute | solution.py:595
  41.7 1.2 %collective-permute-start.24 = (f32[64,128]{1,0:T(8,128)S(1)}, f32[64,128]{1,0:T(8,128)S(1)}, u32[]{:S(2)}, u32[]{:S(2)}) collective-permute-start(f32[64,128]{1,0:T(8,128)S(1)} %get-tuple-element.142.ma), channel_id=1, source_target_pairs={{0,1},{1,0},{2,3},{3,2},{4,5},{5,4},{6,7},{7,6},{8,9},{9,8},{10,11... | collective-permute-start | bytes 98312 | tf_op jit(solution)/shard_map/ppermute | solution.py:583
  47.3 2.8 %collective-permute-start.25 = (f32[8,128]{1,0:T(8,128)S(1)}, f32[8,128]{1,0:T(8,128)S(1)}, u32[]{:S(2)}, u32[]{:S(2)}) collective-permute-start(f32[8,128]{1,0:T(8,128)S(1)} %get-tuple-element.148), channel_id=1, source_target_pairs={{0,1},{1,0},{2,3},{3,2},{4,5},{5,4},{6,7},{7,6},{8,9},{9,8},{10,11... | collective-permute-start | bytes 12296 | tf_op jit(solution)/shard_map/ppermute | solution.py:583
  47.4 3.8 %collective-permute-start.26 = (f32[8,128]{1,0:T(8,128)S(1)}, f32[8,128]{1,0:T(8,128)S(1)}, u32[]{:S(2)}, u32[]{:S(2)}) collective-permute-start(f32[8,128]{1,0:T(8,128)S(1)} %get-tuple-element.149), channel_id=1, source_target_pairs={{0,32},{32,0},{64,96},{96,64},{1,33},{33,1},{65,97},{97,65},{2,34}... | collective-permute-start | bytes 12296 | tf_op jit(solution)/shard_map/ppermute | solution.py:607
  49.6 1.6 %collective-permute-start.27 = (f32[8,128]{1,0:T(8,128)S(1)}, f32[8,128]{1,0:T(8,128)S(1)}, u32[]{:S(2)}, u32[]{:S(2)}) collective-permute-start(f32[8,128]{1,0:T(8,128)S(1)} %get-tuple-element.150), channel_id=1, source_target_pairs={{0,1},{1,0},{2,3},{3,2},{4,5},{5,4},{6,7},{7,6},{8,9},{9,8},{10,11... | collective-permute-start | bytes 12296 | tf_op jit(solution)/shard_map/ppermute | solution.py:608
  53.0 6.3 %collective-permute-start.28 = (f32[32,128]{1,0:T(8,128)S(1)}, f32[32,128]{1,0:T(8,128)S(1)}, u32[]{:S(2)}, u32[]{:S(2)}) collective-permute-start(f32[32,128]{1,0:T(8,128)S(1)} %get-tuple-element.154), channel_id=1, source_target_pairs={{0,1},{1,0},{2,3},{3,2},{4,5},{5,4},{6,7},{7,6},{8,9},{9,8},{10,11... | collective-permute-start | bytes 49160 | tf_op jit(solution)/shard_map/ppermute | solution.py:583
  53.1 6.2 %collective-permute-start.29 = (f32[32,128]{1,0:T(8,128)S(1)}, f32[32,128]{1,0:T(8,128)S(1)}, u32[]{:S(2)}, u32[]{:S(2)}) collective-permute-start(f32[32,128]{1,0:T(8,128)S(1)} %get-tuple-element.155), channel_id=1, source_target_pairs={{0,32},{1,2},{2,1},{3,4},{4,3},{5,6},{6,5},{7,8},{8,7},{9,10},{10,... | collective-permute-start | bytes 49160 | tf_op jit(solution)/shard_map/ppermute | solution.py:595
  54.4 4.9 %collective-permute-start.30 = (f32[32,128]{1,0:T(8,128)S(1)}, f32[32,128]{1,0:T(8,128)S(1)}, u32[]{:S(2)}, u32[]{:S(2)}) collective-permute-start(f32[32,128]{1,0:T(8,128)S(1)} %get-tuple-element.156), channel_id=1, source_target_pairs={{0,32},{32,0},{64,96},{96,64},{1,33},{33,1},{65,97},{97,65},{2,34}... | collective-permute-start | bytes 49160 | tf_op jit(solution)/shard_map/ppermute | solution.py:607
  56.4 2.9 %collective-permute-start.31 = (f32[32,128]{1,0:T(8,128)S(1)}, f32[32,128]{1,0:T(8,128)S(1)}, u32[]{:S(2)}, u32[]{:S(2)}) collective-permute-start(f32[32,128]{1,0:T(8,128)S(1)} %get-tuple-element.157), channel_id=1, source_target_pairs={{0,1},{1,0},{2,3},{3,2},{4,5},{5,4},{6,7},{7,6},{8,9},{9,8},{10,11... | collective-permute-start | bytes 49160 | tf_op jit(solution)/shard_map/ppermute | solution.py:608
  60.6 3.0 %collective-permute-start.2 = (f32[512,128]{1,0:T(8,128)S(1)}, f32[512,128]{1,0:T(8,128)S(1)}, u32[]{:S(2)}, u32[]{:S(2)}) collective-permute-start(f32[512,128]{1,0:T(8,128)S(1)} %get-tuple-element.26), channel_id=1, source_target_pairs={{0,1},{1,0},{2,3},{3,2},{4,5},{5,4},{6,7},{7,6},{8,9},{9,8},{10,11... | collective-permute-start | bytes 786440 | tf_op jit(solution)/shard_map/cond/branch_1_fun/ppermute | solution.py:615
  61.1 7.9 %collective-permute-start.3 = (f32[512,128]{1,0:T(8,128)S(1)}, f32[512,128]{1,0:T(8,128)S(1)}, u32[]{:S(2)}, u32[]{:S(2)}) collective-permute-start(f32[512,128]{1,0:T(8,128)S(1)} %get-tuple-element.27), channel_id=1, source_target_pairs={{0,127},{1,2},{2,1},{3,4},{4,3},{5,6},{6,5},{7,8},{8,7},{9,10},{10... | collective-permute-start | bytes 786440 | tf_op jit(solution)/shard_map/cond/branch_1_fun/ppermute | solution.py:615

commit v6 on v5

--- a/solution.py
+++ b/solution.py
@@ -516,13 +516,7 @@
         out[at + STEP : at + STEP + 8, :] = second
 
 
-def last_residual_kernel(src, c, f0, fy, fz, p, r, blocks):
-    t0, here = ZERO(), p[0:BS, :]
-    for x in range(BS):
-        at = plane(x)
-        after = p[after_plane(x), :]
-        r[at, :], t0 = residual_plane(src, c, f0, fy, fz, at, t0, here, after)
-        here = after
+def pressure_blocks_kernel(p, blocks):
     for x in range(BS):
         plane_to_blocks(p[plane(x), :], x, blocks, BLK * STEP)
 
@@ -674,10 +668,9 @@
     return pl.pallas_call(
         faces_kernel,
         out_shape=[jax.ShapeDtypeStruct(FACE, F32)] * 4,
-        in_specs=[pl.BlockSpec(memory_space=pltpu.HBM)],
-        out_specs=[pl.BlockSpec(memory_space=pltpu.VMEM)] * 4,
+        in_specs=[pl.BlockSpec(memory_space=pl.ANY)],
+        out_specs=[pl.BlockSpec(memory_space=pl.ANY)] * 4,
         scratch_shapes=[pltpu.SemaphoreType.DMA((4,))],
-        compiler_params=pltpu.CompilerParams(vmem_limit_bytes=48 << 20),
         cost_estimate=pl.CostEstimate(flops=2000000000, bytes_accessed=131072, transcendentals=0),
     )(inverse_density)
 
@@ -771,7 +764,8 @@
         )
 
     halos = swap_faces(*sends)
-    ri, blocks_p = call(last_residual_kernel, [FULL, ROW], [*fine, p])
+    (ri,) = call(residual_kernel, [FULL], [*fine, p])
+    (blocks_p,) = call(pressure_blocks_kernel, [ROW], [p])
     _, blocks_r, sa, sb = call(
         final_kernel,
         [FULL, ROW] + [(512, LANES)] * 2,

time: 70.7 us -> 72.1 us (1.020)
  Pallas kernels: 18.3 us -> 20.9 us
  local copies, waits for them, and re-layouts: 1.42 us -> 0.02 us
    pallas_call x1, Pallas kernels: 0.15 us -> 3.15 us  [density_faces(): pl.pallas_call(faces_kernel, out_shape=[jax.ShapeDtypeStruct(FACE, F32)]...]
    unnamed x12 -> x10, local copies, waits for them, and re-layouts: 1.42 us -> 0.02 us
    pallas_call x16 -> x17, Pallas kernels: 15.3 us -> 14.9 us  [call(): pl.pallas_call(body, out_shape=outs, in_specs=[pl.BlockSpec(memory_space=...]
  transfers between devices with their start and end apart: 30 -> 30, of which waited for: 11 -> 11; matrix products, arithmetic and copies ran while one was open for 0% -> 0% of each run, Pallas kernels for 9% -> 8%
where the time goes in v6:
time: 72.1 us; the launch traced here: 72 us
  starting transfers between devices  27.1 us (38%)
  waiting for transfers between devices  22.2 us (31%)
  Pallas kernels  20.9 us (29%)
  between operations  1.81 us (3%)
    ppermute x7, starting transfers between devices, swap_regions(): inner = lax.ppermute(inner, 'region', [(i, i ^ 1) for i in range(regions)])  16 us
    pallas_call x17, Pallas kernels, call(): pl.pallas_call(body, out_shape=outs, in_specs=[pl.BlockSpec(memory_space=...  14.9 us
    ppermute x5, waiting for transfers between devices, swap_far(): return lax.ppermute(value, BOTH, pairs)  10.1 us
    ppermute x5, starting transfers between devices, swap_far(): return lax.ppermute(value, BOTH, pairs)  6.82 us
    ppermute x2, waiting for transfers between devices, swap_blocks(): return (lax.ppermute(first, BOTH, inner), lax.ppermute(second, BOTH, outer))  5.45 us
    ppermute x7, waiting for transfers between devices, swap_regions(): inner = lax.ppermute(inner, 'region', [(i, i ^ 1) for i in range(regions)])  4.1 us
    pallas_call x1, Pallas kernels, density_faces(): pl.pallas_call(faces_kernel, out_shape=[jax.ShapeDtypeStruct(FACE, F32)]...  3.15 us
    ppermute x2, starting transfers between devices, swap_blocks(): return (lax.ppermute(first, BOTH, inner), lax.ppermute(second, BOTH, outer))  3.04 us
  transfers between devices with their start and end apart: 30, of which 11 were waited for; matrix products, arithmetic and copies ran while one was open for 0% of the time, Pallas kernels for 8%

profile of v6, /device:TPU:6, one launch (start us, length us, event | category | flops | bytes accessed | tf_op | source)
XLA Modules:
  0.0 72.0 jit_solution(576132937086266624)
XLA Ops:
  0.7 3.1 %shard_map.73 = (f32[32,128]{1,0:T(8,128)}, f32[32,128]{1,0:T(8,128)}, f32[32,128]{1,0:T(8,128)}, f32[32,128]{1,0:T(8,128)}) custom-call(f32[3,32,32,128]{3,2,1,0:T(8,128)} %inv.1), custom_call_target="tpu_custom_call" | custom-call | flops 2000000000 | bytes 131072 | tf_op jit(solution)/shard_map/pallas_call | solution.py:668
  3.8 0.1 collective-permute-start.4
  3.9 3.4 %collective-permute-start.5 = (f32[32,128]{1,0:T(8,128)}, f32[32,128]{1,0:T(8,128)S(1)}, u32[]{:S(2)}, u32[]{:S(2)}) collective-permute-start(f32[32,128]{1,0:T(8,128)} %get-tuple-element.105), channel_id=1, source_target_pairs={{0,32},{1,2},{2,1},{3,4},{4,3},{5,6},{6,5},{7,8},{8,7},{9,10},{10,... | collective-permute-start | bytes 49160 | tf_op jit(solution)/shard_map/ppermute | solution.py:589
  7.3 1.9 %collective-permute-start.6 = (f32[32,128]{1,0:T(8,128)}, f32[32,128]{1,0:T(8,128)S(1)}, u32[]{:S(2)}, u32[]{:S(2)}) collective-permute-start(f32[32,128]{1,0:T(8,128)} %get-tuple-element.106), channel_id=1, source_target_pairs={{0,32},{32,0},{64,96},{96,64},{1,33},{33,1},{65,97},{97,65},{2,34}... | collective-permute-start | bytes 49160 | tf_op jit(solution)/shard_map/ppermute | solution.py:601
  9.2 0.0 collective-permute-start.7
  9.3 1.5 %shard_map.72 = (f32[16,128]{1,0:T(8,128)S(1)}, s32[1]{0:T(128)}, f32[1024,128]{1,0:T(8,128)S(1)}, f32[1024,128]{1,0:T(8,128)S(1)}, f32[1024,128]{1,0:T(8,128)S(...) custom-call(s32[4]{0:T(128)S(1)} %copy-done.3, ...), custom_call_target="tpu_custom_call" | custom-call | flops 4000000 | bytes 6291456 | tf_op jit(solution)/shard_map/pallas_call | solution.py:626
  10.8 0.0 collective-permute-done.5.rb
  10.8 0.5 collective-permute-done.6.rc
  11.3 0.0 collective-permute-done.7.rd
  11.3 1.6 %shard_map.74 = (f32[1024,128]{1,0:T(8,128)S(1)}, f32[1024,128]{1,0:T(8,128)S(1)}, f32[64,128]{1,0:T(8,128)S(1)}, f32[64,128]{1,0:T(8,128)S(1)}, f32[1024,128]{1...) custom-call(f32[32,128]{1,0:T(8,128)S(1)} %get-tuple-element.97.limi, ...), custom_call_target="tpu_custom_call", output_to_operand_aliasing={{0}: (5, {})} | custom-call | flops 2000000 | bytes 4472832 | tf_op jit(solution)/shard_map/pallas_call | solution.py:38
  12.9 0.1 collective-permute-start.8
  13.0 3.5 %collective-permute-start.9 = (f32[32,128]{1,0:T(8,128)S(1)}, f32[32,128]{1,0:T(8,128)S(1)}, u32[]{:S(2)}, u32[]{:S(2)}) collective-permute-start(f32[32,128]{1,0:T(8,128)S(1)} %get-tuple-element.114), channel_id=1, source_target_pairs={{0,32},{32,0},{64,96},{96,64},{1,33},{33,1},{65,97},{97,65},{2,34}... | collective-permute-start | bytes 49160 | tf_op jit(solution)/shard_map/ppermute | solution.py:601
  16.5 0.2 collective-permute-start.10
  16.6 0.5 shard_map.75.qi
  17.2 0.5 shard_map.76.rest_0_
  17.7 0.5 collective-permute-done.9.rc
  18.2 0.2 shard_map.77
  18.4 0.3 collective-permute-start.11
  18.7 1.3 %collective-permute-done.12.qa = f32[128,128]{1,0:T(8,128)S(1)} collective-permute-done((f32[128,128]{1,0:T(8,128)S(1)}, f32[128,128]{1,0:T(8,128)S(1)}, u32[]{:S(2)}, u32[]{:S(2)}) %collective-permute-start.12) | collective-permute-done | bytes 65568 | tf_op jit(solution)/shard_map/ppermute | solution.py:577
  20.0 4.5 %collective-permute-done.11.qb = f32[160,128]{1,0:T(8,128)S(1)} collective-permute-done((f32[160,128]{1,0:T(8,128)S(1)}, f32[160,128]{1,0:T(8,128)S(1)}, u32[]{:S(2)}, u32[]{:S(2)}) %collective-permute-start.11) | collective-permute-done | bytes 81952 | tf_op jit(solution)/shard_map/ppermute | solution.py:589
  24.4 1.3 %shard_map.78 = (f32[64,128]{1,0:T(8,128)S(1)}, f32[8,128]{1,0:T(8,128)S(1)}, f32[8,128]{1,0:T(8,128)S(1)}, f32[8,128]{1,0:T(8,128)S(1)}, f32[8,128]{1,0:T(8,128)S(1)}, /*index=5*/f32[768,128]{1,0:T(8,128)S(1)}) custom-call(f32[128,128]{1,0:T(8,128)S(1)} %get-tuple-element.120.ma, f32[128,128]{1,0:T(8,128)S(1)} %collective-permute-done.12.qa, ...), custom_call_target="tpu_custom_call" | custom-call | flops 2000000 | bytes 704512 | tf_op jit(solution)/shard_map/pallas_call | solution.py:38
  25.7 0.1 collective-permute-start.13
  25.8 2.2 %collective-permute-start.14 = (f32[8,128]{1,0:T(8,128)S(1)}, f32[8,128]{1,0:T(8,128)S(1)}, u32[]{:S(2)}, u32[]{:S(2)}) collective-permute-start(f32[8,128]{1,0:T(8,128)S(1)} %get-tuple-element.127), channel_id=1, source_target_pairs={{0,32},{32,0},{64,96},{96,64},{1,33},{33,1},{65,97},{97,65},{2,34}... | collective-permute-start | bytes 12296 | tf_op jit(solution)/shard_map/ppermute | solution.py:601
  28.0 0.2 collective-permute-start.15
  28.1 0.3 shard_map.79
  28.5 1.1 %collective-permute-done.14.kc = f32[8,128]{1,0:T(8,128)S(1)} collective-permute-done((f32[8,128]{1,0:T(8,128)S(1)}, f32[8,128]{1,0:T(8,128)S(1)}, u32[]{:S(2)}, u32[]{:S(2)}) %collective-permute-start.14) | collective-permute-done | bytes 4128 | tf_op jit(solution)/shard_map/ppermute | solution.py:601
  29.6 0.0 collective-permute-done.15.kd
  29.6 1.6 %shard_map.80 = (f32[1024,128]{1,0:T(8,128)S(1)}, f32[1024,128]{1,0:T(8,128)S(1)}, f32[32,128]{1,0:T(8,128)S(1)}, f32[32,128]{1,0:T(8,128)S(1)}, f32[32,128]{1,0:T(8,128)S(1)}, /*index=5*/f32[32,128]{1,0:T(8,128)S(1)}) custom-call(f32[1024,128]{1,0:T(8,128)S(1)} %get-tuple-element.123.ri, ...), custom_call_target="tpu_custom_call", output_to_operand_aliasing={{0}: (0, {})} | custom-call | flops 2000000 | bytes 4403200 | tf_op jit(solution)/shard_map/pallas_call | solution.py:38
  31.2 0.1 collective-permute-start.16
  31.3 0.8 %collective-permute-start.17 = (f32[32,128]{1,0:T(8,128)S(1)}, f32[32,128]{1,0:T(8,128)S(1)}, u32[]{:S(2)}, u32[]{:S(2)}) collective-permute-start(f32[32,128]{1,0:T(8,128)S(1)} %get-tuple-element.131), channel_id=1, source_target_pairs={{0,32},{1,2},{2,1},{3,4},{4,3},{5,6},{6,5},{7,8},{8,7},{9,10},{10,... | collective-permute-start | bytes 49160 | tf_op jit(solution)/shard_map/ppermute | solution.py:589
  32.1 2.0 %collective-permute-start.18 = (f32[32,128]{1,0:T(8,128)S(1)}, f32[32,128]{1,0:T(8,128)S(1)}, u32[]{:S(2)}, u32[]{:S(2)}) collective-permute-start(f32[32,128]{1,0:T(8,128)S(1)} %get-tuple-element.132), channel_id=1, source_target_pairs={{0,32},{32,0},{64,96},{96,64},{1,33},{33,1},{65,97},{97,65},{2,34}... | collective-permute-start | bytes 49160 | tf_op jit(solution)/shard_map/ppermute | solution.py:601
  34.1 0.0 collective-permute-start.19
  34.1 0.3 shard_map.81.ri
  34.4 0.0 collective-permute-done.16.ra
  34.4 2.2 %collective-permute-done.17.rb = f32[32,128]{1,0:T(8,128)S(1)} collective-permute-done((f32[32,128]{1,0:T(8,128)S(1)}, f32[32,128]{1,0:T(8,128)S(1)}, u32[]{:S(2)}, u32[]{:S(2)}) %collective-permute-start.17) | collective-permute-done | bytes 16416 | tf_op jit(solution)/shard_map/ppermute | solution.py:589
  36.6 0.0 collective-permute-done.18.rc
  36.7 1.6 %shard_map.82 = (f32[1024,128]{1,0:T(8,128)S(1)}, f32[1024,128]{1,0:T(8,128)S(1)}, f32[32,128]{1,0:T(8,128)S(1)}, f32[32,128]{1,0:T(8,128)S(1)}, f32[32,128]{1,0:T(8,128)S(1)}, /*index=5*/f32[32,128]{1,0:T(8,128)S(1)}) custom-call(f32[1024,128]{1,0:T(8,128)S(1)} %shard_map.81.ri, ...), custom_call_target="tpu_custom_call", output_to_operand_aliasing={{0}: (0, {})} | custom-call | flops 2000000 | bytes 4407296 | tf_op jit(solution)/shard_map/pallas_call | solution.py:38
  38.3 0.1 collective-permute-start.20
  38.4 2.2 %collective-permute-start.21 = (f32[32,128]{1,0:T(8,128)S(1)}, f32[32,128]{1,0:T(8,128)S(1)}, u32[]{:S(2)}, u32[]{:S(2)}) collective-permute-start(f32[32,128]{1,0:T(8,128)S(1)} %get-tuple-element.136), channel_id=1, source_target_pairs={{0,32},{32,0},{64,96},{96,64},{1,33},{33,1},{65,97},{97,65},{2,34}... | collective-permute-start | bytes 49160 | tf_op jit(solution)/shard_map/ppermute | solution.py:601
  40.6 0.2 collective-permute-start.22
  40.7 0.5 shard_map.83.qi
  41.3 1.0 %collective-permute-done.21.rc = f32[32,128]{1,0:T(8,128)S(1)} collective-permute-done((f32[32,128]{1,0:T(8,128)S(1)}, f32[32,128]{1,0:T(8,128)S(1)}, u32[]{:S(2)}, u32[]{:S(2)}) %collective-permute-start.21) | collective-permute-done | bytes 16416 | tf_op jit(solution)/shard_map/ppermute | solution.py:601
  42.3 0.2 shard_map.84
  42.5 1.1 %collective-permute-start.23 = (f32[96,128]{1,0:T(8,128)S(1)}, f32[96,128]{1,0:T(8,128)S(1)}, u32[]{:S(2)}, u32[]{:S(2)}) collective-permute-start(f32[96,128]{1,0:T(8,128)S(1)} %get-tuple-element.139), channel_id=1, source_target_pairs={{0,32},{1,2},{2,1},{3,4},{4,3},{5,6},{6,5},{7,8},{8,7},{9,10},{10,... | collective-permute-start | bytes 147464 | tf_op jit(solution)/shard_map/ppermute | solution.py:589
  43.5 1.2 %collective-permute-done.24.qa = f32[64,128]{1,0:T(8,128)S(1)} collective-permute-done((f32[64,128]{1,0:T(8,128)S(1)}, f32[64,128]{1,0:T(8,128)S(1)}, u32[]{:S(2)}, u32[]{:S(2)}) %collective-permute-start.24) | collective-permute-done | bytes 32800 | tf_op jit(solution)/shard_map/ppermute | solution.py:577
  44.8 3.4 %collective-permute-done.23.qb = f32[96,128]{1,0:T(8,128)S(1)} collective-permute-done((f32[96,128]{1,0:T(8,128)S(1)}, f32[96,128]{1,0:T(8,128)S(1)}, u32[]{:S(2)}, u32[]{:S(2)}) %collective-permute-start.23) | collective-permute-done | bytes 49184 | tf_op jit(solution)/shard_map/ppermute | solution.py:589
  48.2 0.9 %shard_map.85 = (f32[64,128]{1,0:T(8,128)S(1)}, f32[8,128]{1,0:T(8,128)S(1)}, f32[8,128]{1,0:T(8,128)S(1)}, f32[8,128]{1,0:T(8,128)S(1)}, f32[8,128]{1,0:T(8,128)S(1)}) custom-call(f32[64,128]{1,0:T(8,128)S(1)} %get-tuple-element.140.ma, f32[64,128]{1,0:T(8,128)S(1)} %collective-permute-done.24.qa, f32[96,128]{1,0:T(8,128)S(1)} %collective-permute-done.23.qb, ...), custom_call_target="tpu_custom_call" | custom-call | flops 2000000 | bytes 606208 | tf_op jit(solution)/shard_map/pallas_call | solution.py:38
  49.1 0.1 collective-permute-start.25
  49.2 2.2 %collective-permute-start.26 = (f32[8,128]{1,0:T(8,128)S(1)}, f32[8,128]{1,0:T(8,128)S(1)}, u32[]{:S(2)}, u32[]{:S(2)}) collective-permute-start(f32[8,128]{1,0:T(8,128)S(1)} %get-tuple-element.147), channel_id=1, source_target_pairs={{0,32},{32,0},{64,96},{96,64},{1,33},{33,1},{65,97},{97,65},{2,34}... | collective-permute-start | bytes 12296 | tf_op jit(solution)/shard_map/ppermute | solution.py:601
  51.4 0.2 collective-permute-start.27
  51.5 0.4 shard_map.86
  51.9 1.1 %collective-permute-done.26.kc = f32[8,128]{1,0:T(8,128)S(1)} collective-permute-done((f32[8,128]{1,0:T(8,128)S(1)}, f32[8,128]{1,0:T(8,128)S(1)}, u32[]{:S(2)}, u32[]{:S(2)}) %collective-permute-start.26) | collective-permute-done | bytes 4128 | tf_op jit(solution)/shard_map/ppermute | solution.py:601
  53.0 1.8 %shard_map.87 = (f32[1024,128]{1,0:T(8,128)S(1)}, f32[1024,128]{1,0:T(8,128)S(1)}, f32[32,128]{1,0:T(8,128)S(1)}, f32[32,128]{1,0:T(8,128)S(1)}, f32[32,128]{1,0:T(8,128)S(1)}, /*index=5*/f32[32,128]{1,0:T(8,128)S(1)}) custom-call(f32[1024,128]{1,0:T(8,128)S(1)} %get-tuple-element.144.ri, ...), custom_call_target="tpu_custom_call", output_to_operand_aliasing={{0}: (0, {})} | custom-call | flops 2000000 | bytes 4403200 | tf_op jit(solution)/shard_map/pallas_call | solution.py:38
  54.8 0.1 collective-permute-start.28
  54.9 1.3 %collective-permute-start.29 = (f32[32,128]{1,0:T(8,128)S(1)}, f32[32,128]{1,0:T(8,128)S(1)}, u32[]{:S(2)}, u32[]{:S(2)}) collective-permute-start(f32[32,128]{1,0:T(8,128)S(1)} %get-tuple-element.151), channel_id=1, source_target_pairs={{0,32},{1,2},{2,1},{3,4},{4,3},{5,6},{6,5},{7,8},{8,7},{9,10},{10,... | collective-permute-start | bytes 49160 | tf_op jit(solution)/shard_map/ppermute | solution.py:589
  56.2 2.0 %collective-permute-start.30 = (f32[32,128]{1,0:T(8,128)S(1)}, f32[32,128]{1,0:T(8,128)S(1)}, u32[]{:S(2)}, u32[]{:S(2)}) collective-permute-start(f32[32,128]{1,0:T(8,128)S(1)} %get-tuple-element.152), channel_id=1, source_target_pairs={{0,32},{32,0},{64,96},{96,64},{1,33},{33,1},{65,97},{97,65},{2,34}... | collective-permute-start | bytes 49160 | tf_op jit(solution)/shard_map/ppermute | solution.py:601
  58.9 0.3 shard_map.89.ri
  59.2 1.5 %shard_map.88.pblocks = f32[4224,128]{1,0:T(8,128)S(1)} custom-call(f32[1024,128]{1,0:T(8,128)S(1)} %get-tuple-element.149.p), custom_call_target="tpu_custom_call" | custom-call | flops 2000000 | bytes 2686976 | tf_op jit(solution)/shard_map/pallas_call | solution.py:38
  60.7 1.2 %shard_map.90 = (f32[1024,128]{1,0:T(8,128)S(1)}, f32[4224,128]{1,0:T(8,128)S(1)}, f32[512,128]{1,0:T(8,128)S(1)}, f32[512,128]{1,0:T(8,128)S(1)}) custom-call(f32[1024,128]{1,0:T(8,128)S(1)} %shard_map.89.ri, f32[64,128]{1,0:T(8,128)S(1)} %get-tuple-element.112.gx, f32[64,128]{1,0:T(8,128)S(1)} %get-tuple-element.111.gy, ...), custom_call_target="tpu_custom_call", output_to_operand_aliasing={{0}: (0, {})} | custom-call | flops 2000000 | bytes 6029312 | tf_op jit(solution)/shard_map/pallas_call | solution.py:38
  62.0 9.9 %conditional.1 = (f32[6,32768]{1,0:T(8,128)}, f32[6,32768]{1,0:T(8,128)}) conditional(s32[]{:T(128)} %bitcast.15, (f32[4224,128]{1,0:T(8,128)S(1)}, f32[4224,128]{1,0:T(8,128)S(1)}, f32[16,128]{1,0:T(8,128)S(1)}) %tuple.15, (f32[512,128]{1,0:T(8,128)S(1)}, f32[512,128]{1,0:T(8,128)S(1)}, f32[16,128]{1,0:T(8,128)S(1)}, f32[4224,128]{1,0:T(8,128)S(1)}, ...), branch_computations={%region_0.0_spmd, %region_1.0_spmd} | conditional | flops 4000000 | bytes 21102688 | solution.py:784
  62.0 0.6 collective-permute-start.2
  62.6 2.5 %collective-permute-start.3 = (f32[512,128]{1,0:T(8,128)S(1)}, f32[512,128]{1,0:T(8,128)S(1)}, u32[]{:S(2)}, u32[]{:S(2)}) collective-permute-start(f32[512,128]{1,0:T(8,128)S(1)} %get-tuple-element.27), channel_id=1, source_target_pairs={{0,127},{1,2},{2,1},{3,4},{4,3},{5,6},{6,5},{7,8},{8,7},{9,10},{10... | collective-permute-start | bytes 786440 | tf_op jit(solution)/shard_map/cond/branch_1_fun/ppermute | solution.py:609
  65.0 5.5 %collective-permute-done.3.rb = f32[512,128]{1,0:T(8,128)S(1)} collective-permute-done((f32[512,128]{1,0:T(8,128)S(1)}, f32[512,128]{1,0:T(8,128)S(1)}, u32[]{:S(2)}, u32[]{:S(2)}) %collective-permute-start.3) | collective-permute-done | bytes 262176 | tf_op jit(solution)/shard_map/cond/branch_1_fun/ppermute | solution.py:609
  70.5 1.4 %branch_1_fun.1 = (f32[256,6,128]{2,1,0:T(8,128)}, f32[256,6,128]{2,1,0:T(8,128)}, f32[4224,128]{1,0:T(8,128)S(1)}, f32[4224,128]{1,0:T(8,128)S(1)}) custom-call(f32[16,128]{1,0:T(8,128)S(1)} %get-tuple-element.23.owned, f32[4224,128]{1,0:T(8,128)S(1)} %get-tuple-element.24.in_p, ...), custom_call_target="tpu_custom_call", output_to_operand_aliasing={{2}: (1, {}), {3}: (2, {})} | custom-call | flops 2000000 | bytes 6291456 | tf_op jit(solution)/shard_map/cond/branch_1_fun/pallas_call | solution.py:682
  (27 shorter events, 0.1 us)
Async XLA Ops:
  0.6 8.6 %copy-start = (f32[3,32,32,128]{3,2,1,0:T(8,128)S(1)}, f32[3,32,32,128]{3,2,1,0:T(8,128)}, u32[]{:S(2)}) copy-start(f32[3,32,32,128]{3,2,1,0:T(8,128)} %inv.1) | copy-start | bytes 4718596
  0.6 8.6 %copy-start.2 = (s32[512]{0:T(512)S(1)}, s32[512]{0:T(512)}, u32[]{:S(2)}) copy-start(s32[512]{0:T(512)} %param.11) | copy-start | bytes 6148
  0.7 8.6 %copy-start.4 = (s32[3]{0:T(128)S(1)}, s32[3]{0:T(128)}, u32[]{:S(2)}) copy-start(s32[3]{0:T(128)} %level_sweeps.1) | copy-start | bytes 40
  0.7 8.6 %copy-start.3 = (s32[4]{0:T(128)S(1)}, s32[4]{0:T(128)}, u32[]{:S(2)}) copy-start(s32[4]{0:T(128)} %levels.1) | copy-start | bytes 52
  0.7 8.6 %copy-start.1 = (f32[32,32,128]{2,1,0:T(8,128)S(1)}, f32[32,32,128]{2,1,0:T(8,128)}, u32[]{:S(2)}) copy-start(f32[32,32,128]{2,1,0:T(8,128)} %param.7) | copy-start | bytes 1572868
  3.8 6.9 %collective-permute-start.4 = (f32[32,128]{1,0:T(8,128)}, f32[32,128]{1,0:T(8,128)S(1)}, u32[]{:S(2)}, u32[]{:S(2)}) collective-permute-start(f32[32,128]{1,0:T(8,128)} %get-tuple-element.104), channel_id=1, source_target_pairs={{0,1},{1,0},{2,3},{3,2},{4,5},{5,4},{6,7},{7,6},{8,9},{9,8},{10,11... | collective-permute-start | bytes 49160 | tf_op jit(solution)/shard_map/ppermute | solution.py:577
  3.9 6.8 %collective-permute-start.5 = (f32[32,128]{1,0:T(8,128)}, f32[32,128]{1,0:T(8,128)S(1)}, u32[]{:S(2)}, u32[]{:S(2)}) collective-permute-start(f32[32,128]{1,0:T(8,128)} %get-tuple-element.105), channel_id=1, source_target_pairs={{0,32},{1,2},{2,1},{3,4},{4,3},{5,6},{6,5},{7,8},{8,7},{9,10},{10,... | collective-permute-start | bytes 49160 | tf_op jit(solution)/shard_map/ppermute | solution.py:589
  7.3 3.9 %collective-permute-start.6 = (f32[32,128]{1,0:T(8,128)}, f32[32,128]{1,0:T(8,128)S(1)}, u32[]{:S(2)}, u32[]{:S(2)}) collective-permute-start(f32[32,128]{1,0:T(8,128)} %get-tuple-element.106), channel_id=1, source_target_pairs={{0,32},{32,0},{64,96},{96,64},{1,33},{33,1},{65,97},{97,65},{2,34}... | collective-permute-start | bytes 49160 | tf_op jit(solution)/shard_map/ppermute | solution.py:601
  9.2 2.0 %collective-permute-start.7 = (f32[32,128]{1,0:T(8,128)}, f32[32,128]{1,0:T(8,128)S(1)}, u32[]{:S(2)}, u32[]{:S(2)}) collective-permute-start(f32[32,128]{1,0:T(8,128)} %get-tuple-element.107), channel_id=1, source_target_pairs={{0,1},{1,0},{2,3},{3,2},{4,5},{5,4},{6,7},{7,6},{8,9},{9,8},{10,11... | collective-permute-start | bytes 49160 | tf_op jit(solution)/shard_map/ppermute | solution.py:602
  12.9 4.8 %collective-permute-start.8 = (f32[32,128]{1,0:T(8,128)S(1)}, f32[32,128]{1,0:T(8,128)S(1)}, u32[]{:S(2)}, u32[]{:S(2)}) collective-permute-start(f32[32,128]{1,0:T(8,128)S(1)} %get-tuple-element.113), channel_id=1, source_target_pairs={{0,1},{1,0},{2,3},{3,2},{4,5},{5,4},{6,7},{7,6},{8,9},{9,8},{10,11... | collective-permute-start | bytes 49160 | tf_op jit(solution)/shard_map/ppermute | solution.py:577
  13.0 5.2 %collective-permute-start.9 = (f32[32,128]{1,0:T(8,128)S(1)}, f32[32,128]{1,0:T(8,128)S(1)}, u32[]{:S(2)}, u32[]{:S(2)}) collective-permute-start(f32[32,128]{1,0:T(8,128)S(1)} %get-tuple-element.114), channel_id=1, source_target_pairs={{0,32},{32,0},{64,96},{96,64},{1,33},{33,1},{65,97},{97,65},{2,34}... | collective-permute-start | bytes 49160 | tf_op jit(solution)/shard_map/ppermute | solution.py:601
  16.5 1.7 %collective-permute-start.10 = (f32[32,128]{1,0:T(8,128)S(1)}, f32[32,128]{1,0:T(8,128)S(1)}, u32[]{:S(2)}, u32[]{:S(2)}) collective-permute-start(f32[32,128]{1,0:T(8,128)S(1)} %get-tuple-element.115), channel_id=1, source_target_pairs={{0,1},{1,0},{2,3},{3,2},{4,5},{5,4},{6,7},{7,6},{8,9},{9,8},{10,11... | collective-permute-start | bytes 49160 | tf_op jit(solution)/shard_map/ppermute | solution.py:602
  18.4 6.1 %collective-permute-start.11 = (f32[160,128]{1,0:T(8,128)S(1)}, f32[160,128]{1,0:T(8,128)S(1)}, u32[]{:S(2)}, u32[]{:S(2)}) collective-permute-start(f32[160,128]{1,0:T(8,128)S(1)} %get-tuple-element.119), channel_id=1, source_target_pairs={{0,32},{1,2},{2,1},{3,4},{4,3},{5,6},{6,5},{7,8},{8,7},{9,10},{10,... | collective-permute-start | bytes 245768 | tf_op jit(solution)/shard_map/ppermute | solution.py:589
  18.7 1.3 %collective-permute-start.12 = (f32[128,128]{1,0:T(8,128)S(1)}, f32[128,128]{1,0:T(8,128)S(1)}, u32[]{:S(2)}, u32[]{:S(2)}) collective-permute-start(f32[128,128]{1,0:T(8,128)S(1)} %get-tuple-element.120.ma), channel_id=1, source_target_pairs={{0,1},{1,0},{2,3},{3,2},{4,5},{5,4},{6,7},{7,6},{8,9},{9,8},{10,11... | collective-permute-start | bytes 196616 | tf_op jit(solution)/shard_map/ppermute | solution.py:577
  25.7 2.8 %collective-permute-start.13 = (f32[8,128]{1,0:T(8,128)S(1)}, f32[8,128]{1,0:T(8,128)S(1)}, u32[]{:S(2)}, u32[]{:S(2)}) collective-permute-start(f32[8,128]{1,0:T(8,128)S(1)} %get-tuple-element.126), channel_id=1, source_target_pairs={{0,1},{1,0},{2,3},{3,2},{4,5},{5,4},{6,7},{7,6},{8,9},{9,8},{10,11... | collective-permute-start | bytes 12296 | tf_op jit(solution)/shard_map/ppermute | solution.py:577
  25.8 3.8 %collective-permute-start.14 = (f32[8,128]{1,0:T(8,128)S(1)}, f32[8,128]{1,0:T(8,128)S(1)}, u32[]{:S(2)}, u32[]{:S(2)}) collective-permute-start(f32[8,128]{1,0:T(8,128)S(1)} %get-tuple-element.127), channel_id=1, source_target_pairs={{0,32},{32,0},{64,96},{96,64},{1,33},{33,1},{65,97},{97,65},{2,34}... | collective-permute-start | bytes 12296 | tf_op jit(solution)/shard_map/ppermute | solution.py:601
  28.0 1.6 %collective-permute-start.15 = (f32[8,128]{1,0:T(8,128)S(1)}, f32[8,128]{1,0:T(8,128)S(1)}, u32[]{:S(2)}, u32[]{:S(2)}) collective-permute-start(f32[8,128]{1,0:T(8,128)S(1)} %get-tuple-element.128), channel_id=1, source_target_pairs={{0,1},{1,0},{2,3},{3,2},{4,5},{5,4},{6,7},{7,6},{8,9},{9,8},{10,11... | collective-permute-start | bytes 12296 | tf_op jit(solution)/shard_map/ppermute | solution.py:602
  31.2 3.2 %collective-permute-start.16 = (f32[32,128]{1,0:T(8,128)S(1)}, f32[32,128]{1,0:T(8,128)S(1)}, u32[]{:S(2)}, u32[]{:S(2)}) collective-permute-start(f32[32,128]{1,0:T(8,128)S(1)} %get-tuple-element.130), channel_id=1, source_target_pairs={{0,1},{1,0},{2,3},{3,2},{4,5},{5,4},{6,7},{7,6},{8,9},{9,8},{10,11... | collective-permute-start | bytes 49160 | tf_op jit(solution)/shard_map/ppermute | solution.py:577
  31.3 5.4 %collective-permute-start.17 = (f32[32,128]{1,0:T(8,128)S(1)}, f32[32,128]{1,0:T(8,128)S(1)}, u32[]{:S(2)}, u32[]{:S(2)}) collective-permute-start(f32[32,128]{1,0:T(8,128)S(1)} %get-tuple-element.131), channel_id=1, source_target_pairs={{0,32},{1,2},{2,1},{3,4},{4,3},{5,6},{6,5},{7,8},{8,7},{9,10},{10,... | collective-permute-start | bytes 49160 | tf_op jit(solution)/shard_map/ppermute | solution.py:589
  32.1 4.6 %collective-permute-start.18 = (f32[32,128]{1,0:T(8,128)S(1)}, f32[32,128]{1,0:T(8,128)S(1)}, u32[]{:S(2)}, u32[]{:S(2)}) collective-permute-start(f32[32,128]{1,0:T(8,128)S(1)} %get-tuple-element.132), channel_id=1, source_target_pairs={{0,32},{32,0},{64,96},{96,64},{1,33},{33,1},{65,97},{97,65},{2,34}... | collective-permute-start | bytes 49160 | tf_op jit(solution)/shard_map/ppermute | solution.py:601
  34.1 2.6 %collective-permute-start.19 = (f32[32,128]{1,0:T(8,128)S(1)}, f32[32,128]{1,0:T(8,128)S(1)}, u32[]{:S(2)}, u32[]{:S(2)}) collective-permute-start(f32[32,128]{1,0:T(8,128)S(1)} %get-tuple-element.133), channel_id=1, source_target_pairs={{0,1},{1,0},{2,3},{3,2},{4,5},{5,4},{6,7},{7,6},{8,9},{9,8},{10,11... | collective-permute-start | bytes 49160 | tf_op jit(solution)/shard_map/ppermute | solution.py:602
  38.3 3.0 %collective-permute-start.20 = (f32[32,128]{1,0:T(8,128)S(1)}, f32[32,128]{1,0:T(8,128)S(1)}, u32[]{:S(2)}, u32[]{:S(2)}) collective-permute-start(f32[32,128]{1,0:T(8,128)S(1)} %get-tuple-element.135), channel_id=1, source_target_pairs={{0,1},{1,0},{2,3},{3,2},{4,5},{5,4},{6,7},{7,6},{8,9},{9,8},{10,11... | collective-permute-start | bytes 49160 | tf_op jit(solution)/shard_map/ppermute | solution.py:577
  38.4 3.9 %collective-permute-start.21 = (f32[32,128]{1,0:T(8,128)S(1)}, f32[32,128]{1,0:T(8,128)S(1)}, u32[]{:S(2)}, u32[]{:S(2)}) collective-permute-start(f32[32,128]{1,0:T(8,128)S(1)} %get-tuple-element.136), channel_id=1, source_target_pairs={{0,32},{32,0},{64,96},{96,64},{1,33},{33,1},{65,97},{97,65},{2,34}... | collective-permute-start | bytes 49160 | tf_op jit(solution)/shard_map/ppermute | solution.py:601
  40.6 1.7 %collective-permute-start.22 = (f32[32,128]{1,0:T(8,128)S(1)}, f32[32,128]{1,0:T(8,128)S(1)}, u32[]{:S(2)}, u32[]{:S(2)}) collective-permute-start(f32[32,128]{1,0:T(8,128)S(1)} %get-tuple-element.137), channel_id=1, source_target_pairs={{0,1},{1,0},{2,3},{3,2},{4,5},{5,4},{6,7},{7,6},{8,9},{9,8},{10,11... | collective-permute-start | bytes 49160 | tf_op jit(solution)/shard_map/ppermute | solution.py:602
  42.5 5.7 %collective-permute-start.23 = (f32[96,128]{1,0:T(8,128)S(1)}, f32[96,128]{1,0:T(8,128)S(1)}, u32[]{:S(2)}, u32[]{:S(2)}) collective-permute-start(f32[96,128]{1,0:T(8,128)S(1)} %get-tuple-element.139), channel_id=1, source_target_pairs={{0,32},{1,2},{2,1},{3,4},{4,3},{5,6},{6,5},{7,8},{8,7},{9,10},{10,... | collective-permute-start | bytes 147464 | tf_op jit(solution)/shard_map/ppermute | solution.py:589
  43.5 1.2 %collective-permute-start.24 = (f32[64,128]{1,0:T(8,128)S(1)}, f32[64,128]{1,0:T(8,128)S(1)}, u32[]{:S(2)}, u32[]{:S(2)}) collective-permute-start(f32[64,128]{1,0:T(8,128)S(1)} %get-tuple-element.140.ma), channel_id=1, source_target_pairs={{0,1},{1,0},{2,3},{3,2},{4,5},{5,4},{6,7},{7,6},{8,9},{9,8},{10,11... | collective-permute-start | bytes 98312 | tf_op jit(solution)/shard_map/ppermute | solution.py:577
  49.1 2.8 %collective-permute-start.25 = (f32[8,128]{1,0:T(8,128)S(1)}, f32[8,128]{1,0:T(8,128)S(1)}, u32[]{:S(2)}, u32[]{:S(2)}) collective-permute-start(f32[8,128]{1,0:T(8,128)S(1)} %get-tuple-element.146), channel_id=1, source_target_pairs={{0,1},{1,0},{2,3},{3,2},{4,5},{5,4},{6,7},{7,6},{8,9},{9,8},{10,11... | collective-permute-start | bytes 12296 | tf_op jit(solution)/shard_map/ppermute | solution.py:577
  49.2 3.8 %collective-permute-start.26 = (f32[8,128]{1,0:T(8,128)S(1)}, f32[8,128]{1,0:T(8,128)S(1)}, u32[]{:S(2)}, u32[]{:S(2)}) collective-permute-start(f32[8,128]{1,0:T(8,128)S(1)} %get-tuple-element.147), channel_id=1, source_target_pairs={{0,32},{32,0},{64,96},{96,64},{1,33},{33,1},{65,97},{97,65},{2,34}... | collective-permute-start | bytes 12296 | tf_op jit(solution)/shard_map/ppermute | solution.py:601
  51.4 1.6 %collective-permute-start.27 = (f32[8,128]{1,0:T(8,128)S(1)}, f32[8,128]{1,0:T(8,128)S(1)}, u32[]{:S(2)}, u32[]{:S(2)}) collective-permute-start(f32[8,128]{1,0:T(8,128)S(1)} %get-tuple-element.148), channel_id=1, source_target_pairs={{0,1},{1,0},{2,3},{3,2},{4,5},{5,4},{6,7},{7,6},{8,9},{9,8},{10,11... | collective-permute-start | bytes 12296 | tf_op jit(solution)/shard_map/ppermute | solution.py:602
  54.8 5.9 %collective-permute-start.28 = (f32[32,128]{1,0:T(8,128)S(1)}, f32[32,128]{1,0:T(8,128)S(1)}, u32[]{:S(2)}, u32[]{:S(2)}) collective-permute-start(f32[32,128]{1,0:T(8,128)S(1)} %get-tuple-element.150), channel_id=1, source_target_pairs={{0,1},{1,0},{2,3},{3,2},{4,5},{5,4},{6,7},{7,6},{8,9},{9,8},{10,11... | collective-permute-start | bytes 49160 | tf_op jit(solution)/shard_map/ppermute | solution.py:577
  54.9 5.8 %collective-permute-start.29 = (f32[32,128]{1,0:T(8,128)S(1)}, f32[32,128]{1,0:T(8,128)S(1)}, u32[]{:S(2)}, u32[]{:S(2)}) collective-permute-start(f32[32,128]{1,0:T(8,128)S(1)} %get-tuple-element.151), channel_id=1, source_target_pairs={{0,32},{1,2},{2,1},{3,4},{4,3},{5,6},{6,5},{7,8},{8,7},{9,10},{10,... | collective-permute-start | bytes 49160 | tf_op jit(solution)/shard_map/ppermute | solution.py:589
  56.2 4.5 %collective-permute-start.30 = (f32[32,128]{1,0:T(8,128)S(1)}, f32[32,128]{1,0:T(8,128)S(1)}, u32[]{:S(2)}, u32[]{:S(2)}) collective-permute-start(f32[32,128]{1,0:T(8,128)S(1)} %get-tuple-element.152), channel_id=1, source_target_pairs={{0,32},{32,0},{64,96},{96,64},{1,33},{33,1},{65,97},{97,65},{2,34}... | collective-permute-start | bytes 49160 | tf_op jit(solution)/shard_map/ppermute | solution.py:601
  58.2 2.5 %collective-permute-start.31 = (f32[32,128]{1,0:T(8,128)S(1)}, f32[32,128]{1,0:T(8,128)S(1)}, u32[]{:S(2)}, u32[]{:S(2)}) collective-permute-start(f32[32,128]{1,0:T(8,128)S(1)} %get-tuple-element.153), channel_id=1, source_target_pairs={{0,1},{1,0},{2,3},{3,2},{4,5},{5,4},{6,7},{7,6},{8,9},{9,8},{10,11... | collective-permute-start | bytes 49160 | tf_op jit(solution)/shard_map/ppermute | solution.py:602
  62.0 3.0 %collective-permute-start.2 = (f32[512,128]{1,0:T(8,128)S(1)}, f32[512,128]{1,0:T(8,128)S(1)}, u32[]{:S(2)}, u32[]{:S(2)}) collective-permute-start(f32[512,128]{1,0:T(8,128)S(1)} %get-tuple-element.26), channel_id=1, source_target_pairs={{0,1},{1,0},{2,3},{3,2},{4,5},{5,4},{6,7},{7,6},{8,9},{9,8},{10,11... | collective-permute-start | bytes 786440 | tf_op jit(solution)/shard_map/cond/branch_1_fun/ppermute | solution.py:609
  62.6 7.9 %collective-permute-start.3 = (f32[512,128]{1,0:T(8,128)S(1)}, f32[512,128]{1,0:T(8,128)S(1)}, u32[]{:S(2)}, u32[]{:S(2)}) collective-permute-start(f32[512,128]{1,0:T(8,128)S(1)} %get-tuple-element.27), channel_id=1, source_target_pairs={{0,127},{1,2},{2,1},{3,4},{4,3},{5,6},{6,5},{7,8},{8,7},{9,10},{10... | collective-permute-start | bytes 786440 | tf_op jit(solution)/shard_map/cond/branch_1_fun/ppermute | solution.py:609

commit v7 on v6

--- a/solution.py
+++ b/solution.py
@@ -669,8 +669,9 @@
         faces_kernel,
         out_shape=[jax.ShapeDtypeStruct(FACE, F32)] * 4,
         in_specs=[pl.BlockSpec(memory_space=pl.ANY)],
-        out_specs=[pl.BlockSpec(memory_space=pl.ANY)] * 4,
+        out_specs=[pl.BlockSpec(memory_space=pltpu.VMEM)] * 4,
         scratch_shapes=[pltpu.SemaphoreType.DMA((4,))],
+        compiler_params=pltpu.CompilerParams(vmem_limit_bytes=48 << 20),
         cost_estimate=pl.CostEstimate(flops=2000000000, bytes_accessed=131072, transcendentals=0),
     )(inverse_density)
 

time: 72.1 us -> 70.3 us (0.975)
  Pallas kernels: 20.9 us -> 17.9 us
  local copies, waits for them, and re-layouts: 0.02 us -> 1.42 us
    pallas_call x1, Pallas kernels: 3.15 us -> 0.15 us  [density_faces(): pl.pallas_call(faces_kernel, out_shape=[jax.ShapeDtypeStruct(FACE, F32)]...]
    unnamed x10 -> x12, local copies, waits for them, and re-layouts: 0.02 us -> 1.42 us
where the time goes in v7:
time: 70.3 us; the launch traced here: 70.2 us
  starting transfers between devices  27.1 us (39%)
  waiting for transfers between devices  22 us (31%)
  Pallas kernels  17.9 us (25%)
  between operations  1.77 us (3%)
  local copies, waits for them, and re-layouts  1.42 us (2%)
    ppermute x7, starting transfers between devices, swap_regions(): inner = lax.ppermute(inner, 'region', [(i, i ^ 1) for i in range(regions)])  15.8 us
    pallas_call x17, Pallas kernels, call(): pl.pallas_call(body, out_shape=outs, in_specs=[pl.BlockSpec(memory_space=...  14.9 us
    ppermute x5, waiting for transfers between devices, swap_far(): return lax.ppermute(value, BOTH, pairs)  10.1 us
    ppermute x5, starting transfers between devices, swap_far(): return lax.ppermute(value, BOTH, pairs)  6.82 us
    ppermute x2, waiting for transfers between devices, swap_blocks(): return (lax.ppermute(first, BOTH, inner), lax.ppermute(second, BOTH, outer))  5.45 us
    ppermute x7, waiting for transfers between devices, swap_regions(): inner = lax.ppermute(inner, 'region', [(i, i ^ 1) for i in range(regions)])  3.89 us
    ppermute x2, starting transfers between devices, swap_blocks(): return (lax.ppermute(first, BOTH, inner), lax.ppermute(second, BOTH, outer))  3.04 us
    ppermute x9, waiting for transfers between devices, swap_near(): lax.ppermute(value, 'member', [(i, i ^ 1) for i in range(lax.axis_size('m...  2.47 us
  transfers between devices with their start and end apart: 30, of which 11 were waited for; matrix products, arithmetic and copies ran while one was open for 0% of the time, Pallas kernels for 8%

profile of v7, /device:TPU:6, one launch (start us, length us, event | category | flops | bytes accessed | tf_op | source)
XLA Modules:
  0.0 70.2 jit_solution(9736797054366924250)
XLA Ops:
  0.6 1.4 %copy-done = f32[3,32,32,128]{3,2,1,0:T(8,128)S(1)} copy-done((f32[3,32,32,128]{3,2,1,0:T(8,128)S(1)}, f32[3,32,32,128]{3,2,1,0:T(8,128)}, u32[]{:S(2)}) %copy-start) | copy-done | bytes 1572888
  2.1 0.1 shard_map.73
  2.2 0.1 collective-permute-start.4
  2.3 3.4 %collective-permute-start.5 = (f32[32,128]{1,0:T(8,128)S(1)}, f32[32,128]{1,0:T(8,128)S(1)}, u32[]{:S(2)}, u32[]{:S(2)}) collective-permute-start(f32[32,128]{1,0:T(8,128)S(1)} %get-tuple-element.105), channel_id=1, source_target_pairs={{0,32},{1,2},{2,1},{3,4},{4,3},{5,6},{6,5},{7,8},{8,7},{9,10},{10,... | collective-permute-start | bytes 49160 | tf_op jit(solution)/shard_map/ppermute | solution.py:589
  5.7 1.9 %collective-permute-start.6 = (f32[32,128]{1,0:T(8,128)S(1)}, f32[32,128]{1,0:T(8,128)S(1)}, u32[]{:S(2)}, u32[]{:S(2)}) collective-permute-start(f32[32,128]{1,0:T(8,128)S(1)} %get-tuple-element.106), channel_id=1, source_target_pairs={{0,32},{32,0},{64,96},{96,64},{1,33},{33,1},{65,97},{97,65},{2,34}... | collective-permute-start | bytes 49160 | tf_op jit(solution)/shard_map/ppermute | solution.py:601
  7.6 0.0 collective-permute-start.7
  7.6 1.5 %shard_map.72 = (f32[16,128]{1,0:T(8,128)S(1)}, s32[1]{0:T(128)}, f32[1024,128]{1,0:T(8,128)S(1)}, f32[1024,128]{1,0:T(8,128)S(1)}, f32[1024,128]{1,0:T(8,128)S(...) custom-call(s32[4]{0:T(128)S(1)} %copy-done.4, ...), custom_call_target="tpu_custom_call" | custom-call | flops 4000000 | bytes 6291456 | tf_op jit(solution)/shard_map/pallas_call | solution.py:626
  9.1 0.0 collective-permute-done.4.ra
  9.2 0.3 collective-permute-done.6.rc
  9.4 0.0 collective-permute-done.7.rd
  9.4 1.6 %shard_map.74 = (f32[1024,128]{1,0:T(8,128)S(1)}, f32[1024,128]{1,0:T(8,128)S(1)}, f32[64,128]{1,0:T(8,128)S(1)}, f32[64,128]{1,0:T(8,128)S(1)}, f32[1024,128]{1...) custom-call(f32[32,128]{1,0:T(8,128)S(1)} %get-tuple-element.97.limi, ...), custom_call_target="tpu_custom_call", output_to_operand_aliasing={{0}: (5, {})} | custom-call | flops 2000000 | bytes 4472832 | tf_op jit(solution)/shard_map/pallas_call | solution.py:38
  11.0 0.3 collective-permute-start.8
  11.4 3.3 %collective-permute-start.9 = (f32[32,128]{1,0:T(8,128)S(1)}, f32[32,128]{1,0:T(8,128)S(1)}, u32[]{:S(2)}, u32[]{:S(2)}) collective-permute-start(f32[32,128]{1,0:T(8,128)S(1)} %get-tuple-element.114), channel_id=1, source_target_pairs={{0,32},{32,0},{64,96},{96,64},{1,33},{33,1},{65,97},{97,65},{2,34}... | collective-permute-start | bytes 49160 | tf_op jit(solution)/shard_map/ppermute | solution.py:601
  14.6 0.2 collective-permute-start.10
  14.8 0.5 shard_map.75.qi
  15.3 0.5 shard_map.76.rest_0_
  15.9 0.5 collective-permute-done.9.rc
  16.4 0.2 shard_map.77
  16.6 0.3 collective-permute-start.11
  16.9 1.3 %collective-permute-done.12.qa = f32[128,128]{1,0:T(8,128)S(1)} collective-permute-done((f32[128,128]{1,0:T(8,128)S(1)}, f32[128,128]{1,0:T(8,128)S(1)}, u32[]{:S(2)}, u32[]{:S(2)}) %collective-permute-start.12) | collective-permute-done | bytes 65568 | tf_op jit(solution)/shard_map/ppermute | solution.py:577
  18.1 4.5 %collective-permute-done.11.qb = f32[160,128]{1,0:T(8,128)S(1)} collective-permute-done((f32[160,128]{1,0:T(8,128)S(1)}, f32[160,128]{1,0:T(8,128)S(1)}, u32[]{:S(2)}, u32[]{:S(2)}) %collective-permute-start.11) | collective-permute-done | bytes 81952 | tf_op jit(solution)/shard_map/ppermute | solution.py:589
  22.6 1.3 %shard_map.78 = (f32[64,128]{1,0:T(8,128)S(1)}, f32[8,128]{1,0:T(8,128)S(1)}, f32[8,128]{1,0:T(8,128)S(1)}, f32[8,128]{1,0:T(8,128)S(1)}, f32[8,128]{1,0:T(8,128)S(1)}, /*index=5*/f32[768,128]{1,0:T(8,128)S(1)}) custom-call(f32[128,128]{1,0:T(8,128)S(1)} %get-tuple-element.120.ma, f32[128,128]{1,0:T(8,128)S(1)} %collective-permute-done.12.qa, ...), custom_call_target="tpu_custom_call" | custom-call | flops 2000000 | bytes 704512 | tf_op jit(solution)/shard_map/pallas_call | solution.py:38
  23.9 0.1 collective-permute-start.13
  24.0 2.2 %collective-permute-start.14 = (f32[8,128]{1,0:T(8,128)S(1)}, f32[8,128]{1,0:T(8,128)S(1)}, u32[]{:S(2)}, u32[]{:S(2)}) collective-permute-start(f32[8,128]{1,0:T(8,128)S(1)} %get-tuple-element.127), channel_id=1, source_target_pairs={{0,32},{32,0},{64,96},{96,64},{1,33},{33,1},{65,97},{97,65},{2,34}... | collective-permute-start | bytes 12296 | tf_op jit(solution)/shard_map/ppermute | solution.py:601
  26.2 0.2 collective-permute-start.15
  26.3 0.3 shard_map.79
  26.7 1.1 %collective-permute-done.14.kc = f32[8,128]{1,0:T(8,128)S(1)} collective-permute-done((f32[8,128]{1,0:T(8,128)S(1)}, f32[8,128]{1,0:T(8,128)S(1)}, u32[]{:S(2)}, u32[]{:S(2)}) %collective-permute-start.14) | collective-permute-done | bytes 4128 | tf_op jit(solution)/shard_map/ppermute | solution.py:601
  27.7 0.0 collective-permute-done.15.kd
  27.7 1.6 %shard_map.80 = (f32[1024,128]{1,0:T(8,128)S(1)}, f32[1024,128]{1,0:T(8,128)S(1)}, f32[32,128]{1,0:T(8,128)S(1)}, f32[32,128]{1,0:T(8,128)S(1)}, f32[32,128]{1,0:T(8,128)S(1)}, /*index=5*/f32[32,128]{1,0:T(8,128)S(1)}) custom-call(f32[1024,128]{1,0:T(8,128)S(1)} %get-tuple-element.123.ri, ...), custom_call_target="tpu_custom_call", output_to_operand_aliasing={{0}: (0, {})} | custom-call | flops 2000000 | bytes 4403200 | tf_op jit(solution)/shard_map/pallas_call | solution.py:38
  29.4 0.1 collective-permute-start.16
  29.5 0.8 %collective-permute-start.17 = (f32[32,128]{1,0:T(8,128)S(1)}, f32[32,128]{1,0:T(8,128)S(1)}, u32[]{:S(2)}, u32[]{:S(2)}) collective-permute-start(f32[32,128]{1,0:T(8,128)S(1)} %get-tuple-element.131), channel_id=1, source_target_pairs={{0,32},{1,2},{2,1},{3,4},{4,3},{5,6},{6,5},{7,8},{8,7},{9,10},{10,... | collective-permute-start | bytes 49160 | tf_op jit(solution)/shard_map/ppermute | solution.py:589
  30.2 2.0 %collective-permute-start.18 = (f32[32,128]{1,0:T(8,128)S(1)}, f32[32,128]{1,0:T(8,128)S(1)}, u32[]{:S(2)}, u32[]{:S(2)}) collective-permute-start(f32[32,128]{1,0:T(8,128)S(1)} %get-tuple-element.132), channel_id=1, source_target_pairs={{0,32},{32,0},{64,96},{96,64},{1,33},{33,1},{65,97},{97,65},{2,34}... | collective-permute-start | bytes 49160 | tf_op jit(solution)/shard_map/ppermute | solution.py:601
  32.3 0.0 collective-permute-start.19
  32.3 0.3 shard_map.81.ri
  32.6 2.2 %collective-permute-done.17.rb = f32[32,128]{1,0:T(8,128)S(1)} collective-permute-done((f32[32,128]{1,0:T(8,128)S(1)}, f32[32,128]{1,0:T(8,128)S(1)}, u32[]{:S(2)}, u32[]{:S(2)}) %collective-permute-start.17) | collective-permute-done | bytes 16416 | tf_op jit(solution)/shard_map/ppermute | solution.py:589
  34.8 1.6 %shard_map.82 = (f32[1024,128]{1,0:T(8,128)S(1)}, f32[1024,128]{1,0:T(8,128)S(1)}, f32[32,128]{1,0:T(8,128)S(1)}, f32[32,128]{1,0:T(8,128)S(1)}, f32[32,128]{1,0:T(8,128)S(1)}, /*index=5*/f32[32,128]{1,0:T(8,128)S(1)}) custom-call(f32[1024,128]{1,0:T(8,128)S(1)} %shard_map.81.ri, ...), custom_call_target="tpu_custom_call", output_to_operand_aliasing={{0}: (0, {})} | custom-call | flops 2000000 | bytes 4407296 | tf_op jit(solution)/shard_map/pallas_call | solution.py:38
  36.5 0.1 collective-permute-start.20
  36.5 2.2 %collective-permute-start.21 = (f32[32,128]{1,0:T(8,128)S(1)}, f32[32,128]{1,0:T(8,128)S(1)}, u32[]{:S(2)}, u32[]{:S(2)}) collective-permute-start(f32[32,128]{1,0:T(8,128)S(1)} %get-tuple-element.136), channel_id=1, source_target_pairs={{0,32},{32,0},{64,96},{96,64},{1,33},{33,1},{65,97},{97,65},{2,34}... | collective-permute-start | bytes 49160 | tf_op jit(solution)/shard_map/ppermute | solution.py:601
  38.7 0.2 collective-permute-start.22
  38.9 0.5 shard_map.83.qi
  39.4 0.0 collective-permute-done.20.ra
  39.5 1.0 %collective-permute-done.21.rc = f32[32,128]{1,0:T(8,128)S(1)} collective-permute-done((f32[32,128]{1,0:T(8,128)S(1)}, f32[32,128]{1,0:T(8,128)S(1)}, u32[]{:S(2)}, u32[]{:S(2)}) %collective-permute-start.21) | collective-permute-done | bytes 16416 | tf_op jit(solution)/shard_map/ppermute | solution.py:601
  40.5 0.2 shard_map.84
  40.7 1.1 %collective-permute-start.23 = (f32[96,128]{1,0:T(8,128)S(1)}, f32[96,128]{1,0:T(8,128)S(1)}, u32[]{:S(2)}, u32[]{:S(2)}) collective-permute-start(f32[96,128]{1,0:T(8,128)S(1)} %get-tuple-element.139), channel_id=1, source_target_pairs={{0,32},{1,2},{2,1},{3,4},{4,3},{5,6},{6,5},{7,8},{8,7},{9,10},{10,... | collective-permute-start | bytes 147464 | tf_op jit(solution)/shard_map/ppermute | solution.py:589
  41.7 1.2 %collective-permute-done.24.qa = f32[64,128]{1,0:T(8,128)S(1)} collective-permute-done((f32[64,128]{1,0:T(8,128)S(1)}, f32[64,128]{1,0:T(8,128)S(1)}, u32[]{:S(2)}, u32[]{:S(2)}) %collective-permute-start.24) | collective-permute-done | bytes 32800 | tf_op jit(solution)/shard_map/ppermute | solution.py:577
  42.9 3.4 %collective-permute-done.23.qb = f32[96,128]{1,0:T(8,128)S(1)} collective-permute-done((f32[96,128]{1,0:T(8,128)S(1)}, f32[96,128]{1,0:T(8,128)S(1)}, u32[]{:S(2)}, u32[]{:S(2)}) %collective-permute-start.23) | collective-permute-done | bytes 49184 | tf_op jit(solution)/shard_map/ppermute | solution.py:589
  46.4 0.9 %shard_map.85 = (f32[64,128]{1,0:T(8,128)S(1)}, f32[8,128]{1,0:T(8,128)S(1)}, f32[8,128]{1,0:T(8,128)S(1)}, f32[8,128]{1,0:T(8,128)S(1)}, f32[8,128]{1,0:T(8,128)S(1)}) custom-call(f32[64,128]{1,0:T(8,128)S(1)} %get-tuple-element.140.ma, f32[64,128]{1,0:T(8,128)S(1)} %collective-permute-done.24.qa, f32[96,128]{1,0:T(8,128)S(1)} %collective-permute-done.23.qb, ...), custom_call_target="tpu_custom_call" | custom-call | flops 2000000 | bytes 606208 | tf_op jit(solution)/shard_map/pallas_call | solution.py:38
  47.3 0.1 collective-permute-start.25
  47.4 2.2 %collective-permute-start.26 = (f32[8,128]{1,0:T(8,128)S(1)}, f32[8,128]{1,0:T(8,128)S(1)}, u32[]{:S(2)}, u32[]{:S(2)}) collective-permute-start(f32[8,128]{1,0:T(8,128)S(1)} %get-tuple-element.147), channel_id=1, source_target_pairs={{0,32},{32,0},{64,96},{96,64},{1,33},{33,1},{65,97},{97,65},{2,34}... | collective-permute-start | bytes 12296 | tf_op jit(solution)/shard_map/ppermute | solution.py:601
  49.6 0.2 collective-permute-start.27
  49.7 0.4 shard_map.86
  50.1 1.1 %collective-permute-done.26.kc = f32[8,128]{1,0:T(8,128)S(1)} collective-permute-done((f32[8,128]{1,0:T(8,128)S(1)}, f32[8,128]{1,0:T(8,128)S(1)}, u32[]{:S(2)}, u32[]{:S(2)}) %collective-permute-start.26) | collective-permute-done | bytes 4128 | tf_op jit(solution)/shard_map/ppermute | solution.py:601
  51.2 1.8 %shard_map.87 = (f32[1024,128]{1,0:T(8,128)S(1)}, f32[1024,128]{1,0:T(8,128)S(1)}, f32[32,128]{1,0:T(8,128)S(1)}, f32[32,128]{1,0:T(8,128)S(1)}, f32[32,128]{1,0:T(8,128)S(1)}, /*index=5*/f32[32,128]{1,0:T(8,128)S(1)}) custom-call(f32[1024,128]{1,0:T(8,128)S(1)} %get-tuple-element.144.ri, ...), custom_call_target="tpu_custom_call", output_to_operand_aliasing={{0}: (0, {})} | custom-call | flops 2000000 | bytes 4403200 | tf_op jit(solution)/shard_map/pallas_call | solution.py:38
  53.0 0.1 collective-permute-start.28
  53.1 1.3 %collective-permute-start.29 = (f32[32,128]{1,0:T(8,128)S(1)}, f32[32,128]{1,0:T(8,128)S(1)}, u32[]{:S(2)}, u32[]{:S(2)}) collective-permute-start(f32[32,128]{1,0:T(8,128)S(1)} %get-tuple-element.151), channel_id=1, source_target_pairs={{0,32},{1,2},{2,1},{3,4},{4,3},{5,6},{6,5},{7,8},{8,7},{9,10},{10,... | collective-permute-start | bytes 49160 | tf_op jit(solution)/shard_map/ppermute | solution.py:589
  54.4 2.0 %collective-permute-start.30 = (f32[32,128]{1,0:T(8,128)S(1)}, f32[32,128]{1,0:T(8,128)S(1)}, u32[]{:S(2)}, u32[]{:S(2)}) collective-permute-start(f32[32,128]{1,0:T(8,128)S(1)} %get-tuple-element.152), channel_id=1, source_target_pairs={{0,32},{32,0},{64,96},{96,64},{1,33},{33,1},{65,97},{97,65},{2,34}... | collective-permute-start | bytes 49160 | tf_op jit(solution)/shard_map/ppermute | solution.py:601
  57.0 0.3 shard_map.89.ri
  57.4 1.5 %shard_map.88.pblocks = f32[4224,128]{1,0:T(8,128)S(1)} custom-call(f32[1024,128]{1,0:T(8,128)S(1)} %get-tuple-element.149.p), custom_call_target="tpu_custom_call" | custom-call | flops 2000000 | bytes 2686976 | tf_op jit(solution)/shard_map/pallas_call | solution.py:38
  58.9 1.2 %shard_map.90 = (f32[1024,128]{1,0:T(8,128)S(1)}, f32[4224,128]{1,0:T(8,128)S(1)}, f32[512,128]{1,0:T(8,128)S(1)}, f32[512,128]{1,0:T(8,128)S(1)}) custom-call(f32[1024,128]{1,0:T(8,128)S(1)} %shard_map.89.ri, f32[64,128]{1,0:T(8,128)S(1)} %get-tuple-element.112.gx, f32[64,128]{1,0:T(8,128)S(1)} %get-tuple-element.111.gy, ...), custom_call_target="tpu_custom_call", output_to_operand_aliasing={{0}: (0, {})} | custom-call | flops 2000000 | bytes 6029312 | tf_op jit(solution)/shard_map/pallas_call | solution.py:38
  60.1 9.9 %conditional.1 = (f32[6,32768]{1,0:T(8,128)}, f32[6,32768]{1,0:T(8,128)}) conditional(s32[]{:T(128)} %bitcast.15, (f32[4224,128]{1,0:T(8,128)S(1)}, f32[4224,128]{1,0:T(8,128)S(1)}, f32[16,128]{1,0:T(8,128)S(1)}) %tuple.15, (f32[512,128]{1,0:T(8,128)S(1)}, f32[512,128]{1,0:T(8,128)S(1)}, f32[16,128]{1,0:T(8,128)S(1)}, f32[4224,128]{1,0:T(8,128)S(1)}, ...), branch_computations={%region_0.0_spmd, %region_1.0_spmd} | conditional | flops 4000000 | bytes 21102688 | solution.py:785
  60.1 0.6 collective-permute-start.2
  60.7 2.5 %collective-permute-start.3 = (f32[512,128]{1,0:T(8,128)S(1)}, f32[512,128]{1,0:T(8,128)S(1)}, u32[]{:S(2)}, u32[]{:S(2)}) collective-permute-start(f32[512,128]{1,0:T(8,128)S(1)} %get-tuple-element.27), channel_id=1, source_target_pairs={{0,127},{1,2},{2,1},{3,4},{4,3},{5,6},{6,5},{7,8},{8,7},{9,10},{10... | collective-permute-start | bytes 786440 | tf_op jit(solution)/shard_map/cond/branch_1_fun/ppermute | solution.py:609
  63.2 5.5 %collective-permute-done.3.rb = f32[512,128]{1,0:T(8,128)S(1)} collective-permute-done((f32[512,128]{1,0:T(8,128)S(1)}, f32[512,128]{1,0:T(8,128)S(1)}, u32[]{:S(2)}, u32[]{:S(2)}) %collective-permute-start.3) | collective-permute-done | bytes 262176 | tf_op jit(solution)/shard_map/cond/branch_1_fun/ppermute | solution.py:609
  68.6 1.4 %branch_1_fun.1 = (f32[256,6,128]{2,1,0:T(8,128)}, f32[256,6,128]{2,1,0:T(8,128)}, f32[4224,128]{1,0:T(8,128)S(1)}, f32[4224,128]{1,0:T(8,128)S(1)}) custom-call(f32[16,128]{1,0:T(8,128)S(1)} %get-tuple-element.23.owned, f32[4224,128]{1,0:T(8,128)S(1)} %get-tuple-element.24.in_p, ...), custom_call_target="tpu_custom_call", output_to_operand_aliasing={{2}: (1, {}), {3}: (2, {})} | custom-call | flops 2000000 | bytes 6291456 | tf_op jit(solution)/shard_map/cond/branch_1_fun/pallas_call | solution.py:683
  (29 shorter events, 0.1 us)
Async XLA Ops:
  0.6 1.4 %copy-start = (f32[3,32,32,128]{3,2,1,0:T(8,128)S(1)}, f32[3,32,32,128]{3,2,1,0:T(8,128)}, u32[]{:S(2)}) copy-start(f32[3,32,32,128]{3,2,1,0:T(8,128)} %inv.1) | copy-start | bytes 4718596
  2.0 5.6 %copy-start.1 = (f32[3,32,32,128]{3,2,1,0:T(8,128)S(1)}, f32[3,32,32,128]{3,2,1,0:T(8,128)}, u32[]{:S(2)}) copy-start(f32[3,32,32,128]{3,2,1,0:T(8,128)} %inv.1) | copy-start | bytes 4718596
  2.0 5.6 %copy-start.2 = (f32[32,32,128]{2,1,0:T(8,128)S(1)}, f32[32,32,128]{2,1,0:T(8,128)}, u32[]{:S(2)}) copy-start(f32[32,32,128]{2,1,0:T(8,128)} %param.7) | copy-start | bytes 1572868
  2.0 5.6 %copy-start.3 = (s32[512]{0:T(512)S(1)}, s32[512]{0:T(512)}, u32[]{:S(2)}) copy-start(s32[512]{0:T(512)} %param.11) | copy-start | bytes 6148
  2.0 5.6 %copy-start.4 = (s32[4]{0:T(128)S(1)}, s32[4]{0:T(128)}, u32[]{:S(2)}) copy-start(s32[4]{0:T(128)} %levels.1) | copy-start | bytes 52
  2.1 5.6 %copy-start.5 = (s32[3]{0:T(128)S(1)}, s32[3]{0:T(128)}, u32[]{:S(2)}) copy-start(s32[3]{0:T(128)} %level_sweeps.1) | copy-start | bytes 40
  2.2 6.9 %collective-permute-start.4 = (f32[32,128]{1,0:T(8,128)S(1)}, f32[32,128]{1,0:T(8,128)S(1)}, u32[]{:S(2)}, u32[]{:S(2)}) collective-permute-start(f32[32,128]{1,0:T(8,128)S(1)} %get-tuple-element.104), channel_id=1, source_target_pairs={{0,1},{1,0},{2,3},{3,2},{4,5},{5,4},{6,7},{7,6},{8,9},{9,8},{10,11... | collective-permute-start | bytes 49160 | tf_op jit(solution)/shard_map/ppermute | solution.py:577
  2.3 6.8 %collective-permute-start.5 = (f32[32,128]{1,0:T(8,128)S(1)}, f32[32,128]{1,0:T(8,128)S(1)}, u32[]{:S(2)}, u32[]{:S(2)}) collective-permute-start(f32[32,128]{1,0:T(8,128)S(1)} %get-tuple-element.105), channel_id=1, source_target_pairs={{0,32},{1,2},{2,1},{3,4},{4,3},{5,6},{6,5},{7,8},{8,7},{9,10},{10,... | collective-permute-start | bytes 49160 | tf_op jit(solution)/shard_map/ppermute | solution.py:589
  5.7 3.7 %collective-permute-start.6 = (f32[32,128]{1,0:T(8,128)S(1)}, f32[32,128]{1,0:T(8,128)S(1)}, u32[]{:S(2)}, u32[]{:S(2)}) collective-permute-start(f32[32,128]{1,0:T(8,128)S(1)} %get-tuple-element.106), channel_id=1, source_target_pairs={{0,32},{32,0},{64,96},{96,64},{1,33},{33,1},{65,97},{97,65},{2,34}... | collective-permute-start | bytes 49160 | tf_op jit(solution)/shard_map/ppermute | solution.py:601
  7.6 1.8 %collective-permute-start.7 = (f32[32,128]{1,0:T(8,128)S(1)}, f32[32,128]{1,0:T(8,128)S(1)}, u32[]{:S(2)}, u32[]{:S(2)}) collective-permute-start(f32[32,128]{1,0:T(8,128)S(1)} %get-tuple-element.107), channel_id=1, source_target_pairs={{0,1},{1,0},{2,3},{3,2},{4,5},{5,4},{6,7},{7,6},{8,9},{9,8},{10,11... | collective-permute-start | bytes 49160 | tf_op jit(solution)/shard_map/ppermute | solution.py:602
  11.0 4.8 %collective-permute-start.8 = (f32[32,128]{1,0:T(8,128)S(1)}, f32[32,128]{1,0:T(8,128)S(1)}, u32[]{:S(2)}, u32[]{:S(2)}) collective-permute-start(f32[32,128]{1,0:T(8,128)S(1)} %get-tuple-element.113), channel_id=1, source_target_pairs={{0,1},{1,0},{2,3},{3,2},{4,5},{5,4},{6,7},{7,6},{8,9},{9,8},{10,11... | collective-permute-start | bytes 49160 | tf_op jit(solution)/shard_map/ppermute | solution.py:577
  11.4 5.0 %collective-permute-start.9 = (f32[32,128]{1,0:T(8,128)S(1)}, f32[32,128]{1,0:T(8,128)S(1)}, u32[]{:S(2)}, u32[]{:S(2)}) collective-permute-start(f32[32,128]{1,0:T(8,128)S(1)} %get-tuple-element.114), channel_id=1, source_target_pairs={{0,32},{32,0},{64,96},{96,64},{1,33},{33,1},{65,97},{97,65},{2,34}... | collective-permute-start | bytes 49160 | tf_op jit(solution)/shard_map/ppermute | solution.py:601
  14.6 1.7 %collective-permute-start.10 = (f32[32,128]{1,0:T(8,128)S(1)}, f32[32,128]{1,0:T(8,128)S(1)}, u32[]{:S(2)}, u32[]{:S(2)}) collective-permute-start(f32[32,128]{1,0:T(8,128)S(1)} %get-tuple-element.115), channel_id=1, source_target_pairs={{0,1},{1,0},{2,3},{3,2},{4,5},{5,4},{6,7},{7,6},{8,9},{9,8},{10,11... | collective-permute-start | bytes 49160 | tf_op jit(solution)/shard_map/ppermute | solution.py:602
  16.6 6.1 %collective-permute-start.11 = (f32[160,128]{1,0:T(8,128)S(1)}, f32[160,128]{1,0:T(8,128)S(1)}, u32[]{:S(2)}, u32[]{:S(2)}) collective-permute-start(f32[160,128]{1,0:T(8,128)S(1)} %get-tuple-element.119), channel_id=1, source_target_pairs={{0,32},{1,2},{2,1},{3,4},{4,3},{5,6},{6,5},{7,8},{8,7},{9,10},{10,... | collective-permute-start | bytes 245768 | tf_op jit(solution)/shard_map/ppermute | solution.py:589
  16.9 1.3 %collective-permute-start.12 = (f32[128,128]{1,0:T(8,128)S(1)}, f32[128,128]{1,0:T(8,128)S(1)}, u32[]{:S(2)}, u32[]{:S(2)}) collective-permute-start(f32[128,128]{1,0:T(8,128)S(1)} %get-tuple-element.120.ma), channel_id=1, source_target_pairs={{0,1},{1,0},{2,3},{3,2},{4,5},{5,4},{6,7},{7,6},{8,9},{9,8},{10,11... | collective-permute-start | bytes 196616 | tf_op jit(solution)/shard_map/ppermute | solution.py:577
  23.9 2.8 %collective-permute-start.13 = (f32[8,128]{1,0:T(8,128)S(1)}, f32[8,128]{1,0:T(8,128)S(1)}, u32[]{:S(2)}, u32[]{:S(2)}) collective-permute-start(f32[8,128]{1,0:T(8,128)S(1)} %get-tuple-element.126), channel_id=1, source_target_pairs={{0,1},{1,0},{2,3},{3,2},{4,5},{5,4},{6,7},{7,6},{8,9},{9,8},{10,11... | collective-permute-start | bytes 12296 | tf_op jit(solution)/shard_map/ppermute | solution.py:577
  24.0 3.8 %collective-permute-start.14 = (f32[8,128]{1,0:T(8,128)S(1)}, f32[8,128]{1,0:T(8,128)S(1)}, u32[]{:S(2)}, u32[]{:S(2)}) collective-permute-start(f32[8,128]{1,0:T(8,128)S(1)} %get-tuple-element.127), channel_id=1, source_target_pairs={{0,32},{32,0},{64,96},{96,64},{1,33},{33,1},{65,97},{97,65},{2,34}... | collective-permute-start | bytes 12296 | tf_op jit(solution)/shard_map/ppermute | solution.py:601
  26.2 1.6 %collective-permute-start.15 = (f32[8,128]{1,0:T(8,128)S(1)}, f32[8,128]{1,0:T(8,128)S(1)}, u32[]{:S(2)}, u32[]{:S(2)}) collective-permute-start(f32[8,128]{1,0:T(8,128)S(1)} %get-tuple-element.128), channel_id=1, source_target_pairs={{0,1},{1,0},{2,3},{3,2},{4,5},{5,4},{6,7},{7,6},{8,9},{9,8},{10,11... | collective-permute-start | bytes 12296 | tf_op jit(solution)/shard_map/ppermute | solution.py:602
  29.4 3.2 %collective-permute-start.16 = (f32[32,128]{1,0:T(8,128)S(1)}, f32[32,128]{1,0:T(8,128)S(1)}, u32[]{:S(2)}, u32[]{:S(2)}) collective-permute-start(f32[32,128]{1,0:T(8,128)S(1)} %get-tuple-element.130), channel_id=1, source_target_pairs={{0,1},{1,0},{2,3},{3,2},{4,5},{5,4},{6,7},{7,6},{8,9},{9,8},{10,11... | collective-permute-start | bytes 49160 | tf_op jit(solution)/shard_map/ppermute | solution.py:577
  29.5 5.4 %collective-permute-start.17 = (f32[32,128]{1,0:T(8,128)S(1)}, f32[32,128]{1,0:T(8,128)S(1)}, u32[]{:S(2)}, u32[]{:S(2)}) collective-permute-start(f32[32,128]{1,0:T(8,128)S(1)} %get-tuple-element.131), channel_id=1, source_target_pairs={{0,32},{1,2},{2,1},{3,4},{4,3},{5,6},{6,5},{7,8},{8,7},{9,10},{10,... | collective-permute-start | bytes 49160 | tf_op jit(solution)/shard_map/ppermute | solution.py:589
  30.2 4.6 %collective-permute-start.18 = (f32[32,128]{1,0:T(8,128)S(1)}, f32[32,128]{1,0:T(8,128)S(1)}, u32[]{:S(2)}, u32[]{:S(2)}) collective-permute-start(f32[32,128]{1,0:T(8,128)S(1)} %get-tuple-element.132), channel_id=1, source_target_pairs={{0,32},{32,0},{64,96},{96,64},{1,33},{33,1},{65,97},{97,65},{2,34}... | collective-permute-start | bytes 49160 | tf_op jit(solution)/shard_map/ppermute | solution.py:601
  32.3 2.6 %collective-permute-start.19 = (f32[32,128]{1,0:T(8,128)S(1)}, f32[32,128]{1,0:T(8,128)S(1)}, u32[]{:S(2)}, u32[]{:S(2)}) collective-permute-start(f32[32,128]{1,0:T(8,128)S(1)} %get-tuple-element.133), channel_id=1, source_target_pairs={{0,1},{1,0},{2,3},{3,2},{4,5},{5,4},{6,7},{7,6},{8,9},{9,8},{10,11... | collective-permute-start | bytes 49160 | tf_op jit(solution)/shard_map/ppermute | solution.py:602
  36.5 3.0 %collective-permute-start.20 = (f32[32,128]{1,0:T(8,128)S(1)}, f32[32,128]{1,0:T(8,128)S(1)}, u32[]{:S(2)}, u32[]{:S(2)}) collective-permute-start(f32[32,128]{1,0:T(8,128)S(1)} %get-tuple-element.135), channel_id=1, source_target_pairs={{0,1},{1,0},{2,3},{3,2},{4,5},{5,4},{6,7},{7,6},{8,9},{9,8},{10,11... | collective-permute-start | bytes 49160 | tf_op jit(solution)/shard_map/ppermute | solution.py:577
  36.5 3.9 %collective-permute-start.21 = (f32[32,128]{1,0:T(8,128)S(1)}, f32[32,128]{1,0:T(8,128)S(1)}, u32[]{:S(2)}, u32[]{:S(2)}) collective-permute-start(f32[32,128]{1,0:T(8,128)S(1)} %get-tuple-element.136), channel_id=1, source_target_pairs={{0,32},{32,0},{64,96},{96,64},{1,33},{33,1},{65,97},{97,65},{2,34}... | collective-permute-start | bytes 49160 | tf_op jit(solution)/shard_map/ppermute | solution.py:601
  38.7 1.7 %collective-permute-start.22 = (f32[32,128]{1,0:T(8,128)S(1)}, f32[32,128]{1,0:T(8,128)S(1)}, u32[]{:S(2)}, u32[]{:S(2)}) collective-permute-start(f32[32,128]{1,0:T(8,128)S(1)} %get-tuple-element.137), channel_id=1, source_target_pairs={{0,1},{1,0},{2,3},{3,2},{4,5},{5,4},{6,7},{7,6},{8,9},{9,8},{10,11... | collective-permute-start | bytes 49160 | tf_op jit(solution)/shard_map/ppermute | solution.py:602
  40.7 5.7 %collective-permute-start.23 = (f32[96,128]{1,0:T(8,128)S(1)}, f32[96,128]{1,0:T(8,128)S(1)}, u32[]{:S(2)}, u32[]{:S(2)}) collective-permute-start(f32[96,128]{1,0:T(8,128)S(1)} %get-tuple-element.139), channel_id=1, source_target_pairs={{0,32},{1,2},{2,1},{3,4},{4,3},{5,6},{6,5},{7,8},{8,7},{9,10},{10,... | collective-permute-start | bytes 147464 | tf_op jit(solution)/shard_map/ppermute | solution.py:589
  41.7 1.2 %collective-permute-start.24 = (f32[64,128]{1,0:T(8,128)S(1)}, f32[64,128]{1,0:T(8,128)S(1)}, u32[]{:S(2)}, u32[]{:S(2)}) collective-permute-start(f32[64,128]{1,0:T(8,128)S(1)} %get-tuple-element.140.ma), channel_id=1, source_target_pairs={{0,1},{1,0},{2,3},{3,2},{4,5},{5,4},{6,7},{7,6},{8,9},{9,8},{10,11... | collective-permute-start | bytes 98312 | tf_op jit(solution)/shard_map/ppermute | solution.py:577
  47.3 2.8 %collective-permute-start.25 = (f32[8,128]{1,0:T(8,128)S(1)}, f32[8,128]{1,0:T(8,128)S(1)}, u32[]{:S(2)}, u32[]{:S(2)}) collective-permute-start(f32[8,128]{1,0:T(8,128)S(1)} %get-tuple-element.146), channel_id=1, source_target_pairs={{0,1},{1,0},{2,3},{3,2},{4,5},{5,4},{6,7},{7,6},{8,9},{9,8},{10,11... | collective-permute-start | bytes 12296 | tf_op jit(solution)/shard_map/ppermute | solution.py:577
  47.4 3.8 %collective-permute-start.26 = (f32[8,128]{1,0:T(8,128)S(1)}, f32[8,128]{1,0:T(8,128)S(1)}, u32[]{:S(2)}, u32[]{:S(2)}) collective-permute-start(f32[8,128]{1,0:T(8,128)S(1)} %get-tuple-element.147), channel_id=1, source_target_pairs={{0,32},{32,0},{64,96},{96,64},{1,33},{33,1},{65,97},{97,65},{2,34}... | collective-permute-start | bytes 12296 | tf_op jit(solution)/shard_map/ppermute | solution.py:601
  49.6 1.6 %collective-permute-start.27 = (f32[8,128]{1,0:T(8,128)S(1)}, f32[8,128]{1,0:T(8,128)S(1)}, u32[]{:S(2)}, u32[]{:S(2)}) collective-permute-start(f32[8,128]{1,0:T(8,128)S(1)} %get-tuple-element.148), channel_id=1, source_target_pairs={{0,1},{1,0},{2,3},{3,2},{4,5},{5,4},{6,7},{7,6},{8,9},{9,8},{10,11... | collective-permute-start | bytes 12296 | tf_op jit(solution)/shard_map/ppermute | solution.py:602
  53.0 5.9 %collective-permute-start.28 = (f32[32,128]{1,0:T(8,128)S(1)}, f32[32,128]{1,0:T(8,128)S(1)}, u32[]{:S(2)}, u32[]{:S(2)}) collective-permute-start(f32[32,128]{1,0:T(8,128)S(1)} %get-tuple-element.150), channel_id=1, source_target_pairs={{0,1},{1,0},{2,3},{3,2},{4,5},{5,4},{6,7},{7,6},{8,9},{9,8},{10,11... | collective-permute-start | bytes 49160 | tf_op jit(solution)/shard_map/ppermute | solution.py:577
  53.1 5.8 %collective-permute-start.29 = (f32[32,128]{1,0:T(8,128)S(1)}, f32[32,128]{1,0:T(8,128)S(1)}, u32[]{:S(2)}, u32[]{:S(2)}) collective-permute-start(f32[32,128]{1,0:T(8,128)S(1)} %get-tuple-element.151), channel_id=1, source_target_pairs={{0,32},{1,2},{2,1},{3,4},{4,3},{5,6},{6,5},{7,8},{8,7},{9,10},{10,... | collective-permute-start | bytes 49160 | tf_op jit(solution)/shard_map/ppermute | solution.py:589
  54.4 4.5 %collective-permute-start.30 = (f32[32,128]{1,0:T(8,128)S(1)}, f32[32,128]{1,0:T(8,128)S(1)}, u32[]{:S(2)}, u32[]{:S(2)}) collective-permute-start(f32[32,128]{1,0:T(8,128)S(1)} %get-tuple-element.152), channel_id=1, source_target_pairs={{0,32},{32,0},{64,96},{96,64},{1,33},{33,1},{65,97},{97,65},{2,34}... | collective-permute-start | bytes 49160 | tf_op jit(solution)/shard_map/ppermute | solution.py:601
  56.4 2.5 %collective-permute-start.31 = (f32[32,128]{1,0:T(8,128)S(1)}, f32[32,128]{1,0:T(8,128)S(1)}, u32[]{:S(2)}, u32[]{:S(2)}) collective-permute-start(f32[32,128]{1,0:T(8,128)S(1)} %get-tuple-element.153), channel_id=1, source_target_pairs={{0,1},{1,0},{2,3},{3,2},{4,5},{5,4},{6,7},{7,6},{8,9},{9,8},{10,11... | collective-permute-start | bytes 49160 | tf_op jit(solution)/shard_map/ppermute | solution.py:602
  60.1 3.0 %collective-permute-start.2 = (f32[512,128]{1,0:T(8,128)S(1)}, f32[512,128]{1,0:T(8,128)S(1)}, u32[]{:S(2)}, u32[]{:S(2)}) collective-permute-start(f32[512,128]{1,0:T(8,128)S(1)} %get-tuple-element.26), channel_id=1, source_target_pairs={{0,1},{1,0},{2,3},{3,2},{4,5},{5,4},{6,7},{7,6},{8,9},{9,8},{10,11... | collective-permute-start | bytes 786440 | tf_op jit(solution)/shard_map/cond/branch_1_fun/ppermute | solution.py:609
  60.7 7.9 %collective-permute-start.3 = (f32[512,128]{1,0:T(8,128)S(1)}, f32[512,128]{1,0:T(8,128)S(1)}, u32[]{:S(2)}, u32[]{:S(2)}) collective-permute-start(f32[512,128]{1,0:T(8,128)S(1)} %get-tuple-element.27), channel_id=1, source_target_pairs={{0,127},{1,2},{2,1},{3,4},{4,3},{5,6},{6,5},{7,8},{8,7},{9,10},{10... | collective-permute-start | bytes 786440 | tf_op jit(solution)/shard_map/cond/branch_1_fun/ppermute | solution.py:609

commit v8 on v7

--- a/solution.py
+++ b/solution.py
@@ -610,7 +610,9 @@
 
 
 def swap_faces(sa, sb, sc, sd):
-    return (swap_near(sa), swap_far(sb), *swap_regions(sc, sd))
+    far = swap_far(sb)
+    regions = swap_regions(sc, sd)
+    return (swap_near(sa), far, *regions)
 
 
 FULL, TWO, CFIELD = (ROWS, LANES), (2 * BS, LANES), (CROWS, LANES)

time: 70.3 us -> 70.3 us (level)
  no operation moved by 1% of the time
where the time goes in v8:
time: 70.3 us; the launch traced here: 70.2 us
  starting transfers between devices  27.1 us (39%)
  waiting for transfers between devices  22 us (31%)
  Pallas kernels  17.9 us (25%)
  between operations  1.77 us (3%)
  local copies, waits for them, and re-layouts  1.42 us (2%)
    ppermute x7, starting transfers between devices, swap_regions(): inner = lax.ppermute(inner, 'region', [(i, i ^ 1) for i in range(regions)])  15.8 us
    pallas_call x17, Pallas kernels, call(): pl.pallas_call(body, out_shape=outs, in_specs=[pl.BlockSpec(memory_space=...  14.9 us
    ppermute x5, waiting for transfers between devices, swap_far(): return lax.ppermute(value, BOTH, pairs)  10.1 us
    ppermute x5, starting transfers between devices, swap_far(): return lax.ppermute(value, BOTH, pairs)  6.82 us
    ppermute x2, waiting for transfers between devices, swap_blocks(): return (lax.ppermute(first, BOTH, inner), lax.ppermute(second, BOTH, outer))  5.45 us
    ppermute x7, waiting for transfers between devices, swap_regions(): inner = lax.ppermute(inner, 'region', [(i, i ^ 1) for i in range(regions)])  3.89 us
    ppermute x2, starting transfers between devices, swap_blocks(): return (lax.ppermute(first, BOTH, inner), lax.ppermute(second, BOTH, outer))  3.04 us
    ppermute x9, waiting for transfers between devices, swap_near(): lax.ppermute(value, 'member', [(i, i ^ 1) for i in range(lax.axis_size('m...  2.47 us
  transfers between devices with their start and end apart: 30, of which 11 were waited for; matrix products, arithmetic and copies ran while one was open for 0% of the time, Pallas kernels for 8%

profile of v8, /device:TPU:6, one launch (start us, length us, event | category | flops | bytes accessed | tf_op | source)
XLA Modules:
  0.0 70.2 jit_solution(9736797054366924250)
XLA Ops:
  0.6 1.4 %copy-done = f32[3,32,32,128]{3,2,1,0:T(8,128)S(1)} copy-done((f32[3,32,32,128]{3,2,1,0:T(8,128)S(1)}, f32[3,32,32,128]{3,2,1,0:T(8,128)}, u32[]{:S(2)}) %copy-start) | copy-done | bytes 1572888
  2.1 0.1 shard_map.73
  2.2 0.1 collective-permute-start.4
  2.3 3.4 %collective-permute-start.5 = (f32[32,128]{1,0:T(8,128)S(1)}, f32[32,128]{1,0:T(8,128)S(1)}, u32[]{:S(2)}, u32[]{:S(2)}) collective-permute-start(f32[32,128]{1,0:T(8,128)S(1)} %get-tuple-element.105), channel_id=1, source_target_pairs={{0,32},{1,2},{2,1},{3,4},{4,3},{5,6},{6,5},{7,8},{8,7},{9,10},{10,... | collective-permute-start | bytes 49160 | tf_op jit(solution)/shard_map/ppermute | solution.py:589
  5.7 1.9 %collective-permute-start.6 = (f32[32,128]{1,0:T(8,128)S(1)}, f32[32,128]{1,0:T(8,128)S(1)}, u32[]{:S(2)}, u32[]{:S(2)}) collective-permute-start(f32[32,128]{1,0:T(8,128)S(1)} %get-tuple-element.106), channel_id=1, source_target_pairs={{0,32},{32,0},{64,96},{96,64},{1,33},{33,1},{65,97},{97,65},{2,34}... | collective-permute-start | bytes 49160 | tf_op jit(solution)/shard_map/ppermute | solution.py:601
  7.6 0.0 collective-permute-start.7
  7.6 1.5 %shard_map.72 = (f32[16,128]{1,0:T(8,128)S(1)}, s32[1]{0:T(128)}, f32[1024,128]{1,0:T(8,128)S(1)}, f32[1024,128]{1,0:T(8,128)S(1)}, f32[1024,128]{1,0:T(8,128)S(...) custom-call(s32[4]{0:T(128)S(1)} %copy-done.4, ...), custom_call_target="tpu_custom_call" | custom-call | flops 4000000 | bytes 6291456 | tf_op jit(solution)/shard_map/pallas_call | solution.py:628
  9.1 0.0 collective-permute-done.4.ra
  9.2 0.3 collective-permute-done.6.rc
  9.4 0.0 collective-permute-done.7.rd
  9.4 1.6 %shard_map.74 = (f32[1024,128]{1,0:T(8,128)S(1)}, f32[1024,128]{1,0:T(8,128)S(1)}, f32[64,128]{1,0:T(8,128)S(1)}, f32[64,128]{1,0:T(8,128)S(1)}, f32[1024,128]{1...) custom-call(f32[32,128]{1,0:T(8,128)S(1)} %get-tuple-element.97.limi, ...), custom_call_target="tpu_custom_call", output_to_operand_aliasing={{0}: (5, {})} | custom-call | flops 2000000 | bytes 4472832 | tf_op jit(solution)/shard_map/pallas_call | solution.py:38
  11.0 0.3 collective-permute-start.8
  11.4 3.3 %collective-permute-start.9 = (f32[32,128]{1,0:T(8,128)S(1)}, f32[32,128]{1,0:T(8,128)S(1)}, u32[]{:S(2)}, u32[]{:S(2)}) collective-permute-start(f32[32,128]{1,0:T(8,128)S(1)} %get-tuple-element.114), channel_id=1, source_target_pairs={{0,32},{32,0},{64,96},{96,64},{1,33},{33,1},{65,97},{97,65},{2,34}... | collective-permute-start | bytes 49160 | tf_op jit(solution)/shard_map/ppermute | solution.py:601
  14.6 0.2 collective-permute-start.10
  14.8 0.5 shard_map.75.qi
  15.3 0.5 shard_map.76.rest_0_
  15.9 0.5 collective-permute-done.9.rc
  16.4 0.2 shard_map.77
  16.6 0.3 collective-permute-start.11
  16.9 1.3 %collective-permute-done.12.qa = f32[128,128]{1,0:T(8,128)S(1)} collective-permute-done((f32[128,128]{1,0:T(8,128)S(1)}, f32[128,128]{1,0:T(8,128)S(1)}, u32[]{:S(2)}, u32[]{:S(2)}) %collective-permute-start.12) | collective-permute-done | bytes 65568 | tf_op jit(solution)/shard_map/ppermute | solution.py:577
  18.1 4.5 %collective-permute-done.11.qb = f32[160,128]{1,0:T(8,128)S(1)} collective-permute-done((f32[160,128]{1,0:T(8,128)S(1)}, f32[160,128]{1,0:T(8,128)S(1)}, u32[]{:S(2)}, u32[]{:S(2)}) %collective-permute-start.11) | collective-permute-done | bytes 81952 | tf_op jit(solution)/shard_map/ppermute | solution.py:589
  22.6 1.3 %shard_map.78 = (f32[64,128]{1,0:T(8,128)S(1)}, f32[8,128]{1,0:T(8,128)S(1)}, f32[8,128]{1,0:T(8,128)S(1)}, f32[8,128]{1,0:T(8,128)S(1)}, f32[8,128]{1,0:T(8,128)S(1)}, /*index=5*/f32[768,128]{1,0:T(8,128)S(1)}) custom-call(f32[128,128]{1,0:T(8,128)S(1)} %get-tuple-element.120.ma, f32[128,128]{1,0:T(8,128)S(1)} %collective-permute-done.12.qa, ...), custom_call_target="tpu_custom_call" | custom-call | flops 2000000 | bytes 704512 | tf_op jit(solution)/shard_map/pallas_call | solution.py:38
  23.9 0.1 collective-permute-start.13
  24.0 2.2 %collective-permute-start.14 = (f32[8,128]{1,0:T(8,128)S(1)}, f32[8,128]{1,0:T(8,128)S(1)}, u32[]{:S(2)}, u32[]{:S(2)}) collective-permute-start(f32[8,128]{1,0:T(8,128)S(1)} %get-tuple-element.127), channel_id=1, source_target_pairs={{0,32},{32,0},{64,96},{96,64},{1,33},{33,1},{65,97},{97,65},{2,34}... | collective-permute-start | bytes 12296 | tf_op jit(solution)/shard_map/ppermute | solution.py:601
  26.2 0.2 collective-permute-start.15
  26.3 0.3 shard_map.79
  26.7 1.1 %collective-permute-done.14.kc = f32[8,128]{1,0:T(8,128)S(1)} collective-permute-done((f32[8,128]{1,0:T(8,128)S(1)}, f32[8,128]{1,0:T(8,128)S(1)}, u32[]{:S(2)}, u32[]{:S(2)}) %collective-permute-start.14) | collective-permute-done | bytes 4128 | tf_op jit(solution)/shard_map/ppermute | solution.py:601
  27.7 0.0 collective-permute-done.15.kd
  27.7 1.6 %shard_map.80 = (f32[1024,128]{1,0:T(8,128)S(1)}, f32[1024,128]{1,0:T(8,128)S(1)}, f32[32,128]{1,0:T(8,128)S(1)}, f32[32,128]{1,0:T(8,128)S(1)}, f32[32,128]{1,0:T(8,128)S(1)}, /*index=5*/f32[32,128]{1,0:T(8,128)S(1)}) custom-call(f32[1024,128]{1,0:T(8,128)S(1)} %get-tuple-element.123.ri, ...), custom_call_target="tpu_custom_call", output_to_operand_aliasing={{0}: (0, {})} | custom-call | flops 2000000 | bytes 4403200 | tf_op jit(solution)/shard_map/pallas_call | solution.py:38
  29.4 0.1 collective-permute-start.16
  29.5 0.8 %collective-permute-start.17 = (f32[32,128]{1,0:T(8,128)S(1)}, f32[32,128]{1,0:T(8,128)S(1)}, u32[]{:S(2)}, u32[]{:S(2)}) collective-permute-start(f32[32,128]{1,0:T(8,128)S(1)} %get-tuple-element.131), channel_id=1, source_target_pairs={{0,32},{1,2},{2,1},{3,4},{4,3},{5,6},{6,5},{7,8},{8,7},{9,10},{10,... | collective-permute-start | bytes 49160 | tf_op jit(solution)/shard_map/ppermute | solution.py:589
  30.2 2.0 %collective-permute-start.18 = (f32[32,128]{1,0:T(8,128)S(1)}, f32[32,128]{1,0:T(8,128)S(1)}, u32[]{:S(2)}, u32[]{:S(2)}) collective-permute-start(f32[32,128]{1,0:T(8,128)S(1)} %get-tuple-element.132), channel_id=1, source_target_pairs={{0,32},{32,0},{64,96},{96,64},{1,33},{33,1},{65,97},{97,65},{2,34}... | collective-permute-start | bytes 49160 | tf_op jit(solution)/shard_map/ppermute | solution.py:601
  32.3 0.0 collective-permute-start.19
  32.3 0.3 shard_map.81.ri
  32.6 2.2 %collective-permute-done.17.rb = f32[32,128]{1,0:T(8,128)S(1)} collective-permute-done((f32[32,128]{1,0:T(8,128)S(1)}, f32[32,128]{1,0:T(8,128)S(1)}, u32[]{:S(2)}, u32[]{:S(2)}) %collective-permute-start.17) | collective-permute-done | bytes 16416 | tf_op jit(solution)/shard_map/ppermute | solution.py:589
  34.8 1.6 %shard_map.82 = (f32[1024,128]{1,0:T(8,128)S(1)}, f32[1024,128]{1,0:T(8,128)S(1)}, f32[32,128]{1,0:T(8,128)S(1)}, f32[32,128]{1,0:T(8,128)S(1)}, f32[32,128]{1,0:T(8,128)S(1)}, /*index=5*/f32[32,128]{1,0:T(8,128)S(1)}) custom-call(f32[1024,128]{1,0:T(8,128)S(1)} %shard_map.81.ri, ...), custom_call_target="tpu_custom_call", output_to_operand_aliasing={{0}: (0, {})} | custom-call | flops 2000000 | bytes 4407296 | tf_op jit(solution)/shard_map/pallas_call | solution.py:38
  36.5 0.1 collective-permute-start.20
  36.5 2.2 %collective-permute-start.21 = (f32[32,128]{1,0:T(8,128)S(1)}, f32[32,128]{1,0:T(8,128)S(1)}, u32[]{:S(2)}, u32[]{:S(2)}) collective-permute-start(f32[32,128]{1,0:T(8,128)S(1)} %get-tuple-element.136), channel_id=1, source_target_pairs={{0,32},{32,0},{64,96},{96,64},{1,33},{33,1},{65,97},{97,65},{2,34}... | collective-permute-start | bytes 49160 | tf_op jit(solution)/shard_map/ppermute | solution.py:601
  38.7 0.2 collective-permute-start.22
  38.9 0.5 shard_map.83.qi
  39.4 0.0 collective-permute-done.20.ra
  39.5 1.0 %collective-permute-done.21.rc = f32[32,128]{1,0:T(8,128)S(1)} collective-permute-done((f32[32,128]{1,0:T(8,128)S(1)}, f32[32,128]{1,0:T(8,128)S(1)}, u32[]{:S(2)}, u32[]{:S(2)}) %collective-permute-start.21) | collective-permute-done | bytes 16416 | tf_op jit(solution)/shard_map/ppermute | solution.py:601
  40.5 0.2 shard_map.84
  40.7 1.1 %collective-permute-start.23 = (f32[96,128]{1,0:T(8,128)S(1)}, f32[96,128]{1,0:T(8,128)S(1)}, u32[]{:S(2)}, u32[]{:S(2)}) collective-permute-start(f32[96,128]{1,0:T(8,128)S(1)} %get-tuple-element.139), channel_id=1, source_target_pairs={{0,32},{1,2},{2,1},{3,4},{4,3},{5,6},{6,5},{7,8},{8,7},{9,10},{10,... | collective-permute-start | bytes 147464 | tf_op jit(solution)/shard_map/ppermute | solution.py:589
  41.7 1.2 %collective-permute-done.24.qa = f32[64,128]{1,0:T(8,128)S(1)} collective-permute-done((f32[64,128]{1,0:T(8,128)S(1)}, f32[64,128]{1,0:T(8,128)S(1)}, u32[]{:S(2)}, u32[]{:S(2)}) %collective-permute-start.24) | collective-permute-done | bytes 32800 | tf_op jit(solution)/shard_map/ppermute | solution.py:577
  42.9 3.4 %collective-permute-done.23.qb = f32[96,128]{1,0:T(8,128)S(1)} collective-permute-done((f32[96,128]{1,0:T(8,128)S(1)}, f32[96,128]{1,0:T(8,128)S(1)}, u32[]{:S(2)}, u32[]{:S(2)}) %collective-permute-start.23) | collective-permute-done | bytes 49184 | tf_op jit(solution)/shard_map/ppermute | solution.py:589
  46.4 0.9 %shard_map.85 = (f32[64,128]{1,0:T(8,128)S(1)}, f32[8,128]{1,0:T(8,128)S(1)}, f32[8,128]{1,0:T(8,128)S(1)}, f32[8,128]{1,0:T(8,128)S(1)}, f32[8,128]{1,0:T(8,128)S(1)}) custom-call(f32[64,128]{1,0:T(8,128)S(1)} %get-tuple-element.140.ma, f32[64,128]{1,0:T(8,128)S(1)} %collective-permute-done.24.qa, f32[96,128]{1,0:T(8,128)S(1)} %collective-permute-done.23.qb, ...), custom_call_target="tpu_custom_call" | custom-call | flops 2000000 | bytes 606208 | tf_op jit(solution)/shard_map/pallas_call | solution.py:38
  47.3 0.1 collective-permute-start.25
  47.4 2.2 %collective-permute-start.26 = (f32[8,128]{1,0:T(8,128)S(1)}, f32[8,128]{1,0:T(8,128)S(1)}, u32[]{:S(2)}, u32[]{:S(2)}) collective-permute-start(f32[8,128]{1,0:T(8,128)S(1)} %get-tuple-element.147), channel_id=1, source_target_pairs={{0,32},{32,0},{64,96},{96,64},{1,33},{33,1},{65,97},{97,65},{2,34}... | collective-permute-start | bytes 12296 | tf_op jit(solution)/shard_map/ppermute | solution.py:601
  49.6 0.2 collective-permute-start.27
  49.7 0.4 shard_map.86
  50.1 1.1 %collective-permute-done.26.kc = f32[8,128]{1,0:T(8,128)S(1)} collective-permute-done((f32[8,128]{1,0:T(8,128)S(1)}, f32[8,128]{1,0:T(8,128)S(1)}, u32[]{:S(2)}, u32[]{:S(2)}) %collective-permute-start.26) | collective-permute-done | bytes 4128 | tf_op jit(solution)/shard_map/ppermute | solution.py:601
  51.2 1.8 %shard_map.87 = (f32[1024,128]{1,0:T(8,128)S(1)}, f32[1024,128]{1,0:T(8,128)S(1)}, f32[32,128]{1,0:T(8,128)S(1)}, f32[32,128]{1,0:T(8,128)S(1)}, f32[32,128]{1,0:T(8,128)S(1)}, /*index=5*/f32[32,128]{1,0:T(8,128)S(1)}) custom-call(f32[1024,128]{1,0:T(8,128)S(1)} %get-tuple-element.144.ri, ...), custom_call_target="tpu_custom_call", output_to_operand_aliasing={{0}: (0, {})} | custom-call | flops 2000000 | bytes 4403200 | tf_op jit(solution)/shard_map/pallas_call | solution.py:38
  53.0 0.1 collective-permute-start.28
  53.1 1.3 %collective-permute-start.29 = (f32[32,128]{1,0:T(8,128)S(1)}, f32[32,128]{1,0:T(8,128)S(1)}, u32[]{:S(2)}, u32[]{:S(2)}) collective-permute-start(f32[32,128]{1,0:T(8,128)S(1)} %get-tuple-element.151), channel_id=1, source_target_pairs={{0,32},{1,2},{2,1},{3,4},{4,3},{5,6},{6,5},{7,8},{8,7},{9,10},{10,... | collective-permute-start | bytes 49160 | tf_op jit(solution)/shard_map/ppermute | solution.py:589
  54.4 2.0 %collective-permute-start.30 = (f32[32,128]{1,0:T(8,128)S(1)}, f32[32,128]{1,0:T(8,128)S(1)}, u32[]{:S(2)}, u32[]{:S(2)}) collective-permute-start(f32[32,128]{1,0:T(8,128)S(1)} %get-tuple-element.152), channel_id=1, source_target_pairs={{0,32},{32,0},{64,96},{96,64},{1,33},{33,1},{65,97},{97,65},{2,34}... | collective-permute-start | bytes 49160 | tf_op jit(solution)/shard_map/ppermute | solution.py:601
  57.0 0.3 shard_map.89.ri
  57.4 1.5 %shard_map.88.pblocks = f32[4224,128]{1,0:T(8,128)S(1)} custom-call(f32[1024,128]{1,0:T(8,128)S(1)} %get-tuple-element.149.p), custom_call_target="tpu_custom_call" | custom-call | flops 2000000 | bytes 2686976 | tf_op jit(solution)/shard_map/pallas_call | solution.py:38
  58.9 1.2 %shard_map.90 = (f32[1024,128]{1,0:T(8,128)S(1)}, f32[4224,128]{1,0:T(8,128)S(1)}, f32[512,128]{1,0:T(8,128)S(1)}, f32[512,128]{1,0:T(8,128)S(1)}) custom-call(f32[1024,128]{1,0:T(8,128)S(1)} %shard_map.89.ri, f32[64,128]{1,0:T(8,128)S(1)} %get-tuple-element.112.gx, f32[64,128]{1,0:T(8,128)S(1)} %get-tuple-element.111.gy, ...), custom_call_target="tpu_custom_call", output_to_operand_aliasing={{0}: (0, {})} | custom-call | flops 2000000 | bytes 6029312 | tf_op jit(solution)/shard_map/pallas_call | solution.py:38
  60.1 9.9 %conditional.1 = (f32[6,32768]{1,0:T(8,128)}, f32[6,32768]{1,0:T(8,128)}) conditional(s32[]{:T(128)} %bitcast.15, (f32[4224,128]{1,0:T(8,128)S(1)}, f32[4224,128]{1,0:T(8,128)S(1)}, f32[16,128]{1,0:T(8,128)S(1)}) %tuple.15, (f32[512,128]{1,0:T(8,128)S(1)}, f32[512,128]{1,0:T(8,128)S(1)}, f32[16,128]{1,0:T(8,128)S(1)}, f32[4224,128]{1,0:T(8,128)S(1)}, ...), branch_computations={%region_0.0_spmd, %region_1.0_spmd} | conditional | flops 4000000 | bytes 21102688 | solution.py:787
  60.1 0.6 collective-permute-start.2
  60.7 2.5 %collective-permute-start.3 = (f32[512,128]{1,0:T(8,128)S(1)}, f32[512,128]{1,0:T(8,128)S(1)}, u32[]{:S(2)}, u32[]{:S(2)}) collective-permute-start(f32[512,128]{1,0:T(8,128)S(1)} %get-tuple-element.27), channel_id=1, source_target_pairs={{0,127},{1,2},{2,1},{3,4},{4,3},{5,6},{6,5},{7,8},{8,7},{9,10},{10... | collective-permute-start | bytes 786440 | tf_op jit(solution)/shard_map/cond/branch_1_fun/ppermute | solution.py:609
  63.2 5.5 %collective-permute-done.3.rb = f32[512,128]{1,0:T(8,128)S(1)} collective-permute-done((f32[512,128]{1,0:T(8,128)S(1)}, f32[512,128]{1,0:T(8,128)S(1)}, u32[]{:S(2)}, u32[]{:S(2)}) %collective-permute-start.3) | collective-permute-done | bytes 262176 | tf_op jit(solution)/shard_map/cond/branch_1_fun/ppermute | solution.py:609
  68.6 1.4 %branch_1_fun.1 = (f32[256,6,128]{2,1,0:T(8,128)}, f32[256,6,128]{2,1,0:T(8,128)}, f32[4224,128]{1,0:T(8,128)S(1)}, f32[4224,128]{1,0:T(8,128)S(1)}) custom-call(f32[16,128]{1,0:T(8,128)S(1)} %get-tuple-element.23.owned, f32[4224,128]{1,0:T(8,128)S(1)} %get-tuple-element.24.in_p, ...), custom_call_target="tpu_custom_call", output_to_operand_aliasing={{2}: (1, {}), {3}: (2, {})} | custom-call | flops 2000000 | bytes 6291456 | tf_op jit(solution)/shard_map/cond/branch_1_fun/pallas_call | solution.py:685
  (29 shorter events, 0.1 us)
Async XLA Ops:
  0.6 1.4 %copy-start = (f32[3,32,32,128]{3,2,1,0:T(8,128)S(1)}, f32[3,32,32,128]{3,2,1,0:T(8,128)}, u32[]{:S(2)}) copy-start(f32[3,32,32,128]{3,2,1,0:T(8,128)} %inv.1) | copy-start | bytes 4718596
  2.0 5.6 %copy-start.1 = (f32[3,32,32,128]{3,2,1,0:T(8,128)S(1)}, f32[3,32,32,128]{3,2,1,0:T(8,128)}, u32[]{:S(2)}) copy-start(f32[3,32,32,128]{3,2,1,0:T(8,128)} %inv.1) | copy-start | bytes 4718596
  2.0 5.6 %copy-start.2 = (f32[32,32,128]{2,1,0:T(8,128)S(1)}, f32[32,32,128]{2,1,0:T(8,128)}, u32[]{:S(2)}) copy-start(f32[32,32,128]{2,1,0:T(8,128)} %param.7) | copy-start | bytes 1572868
  2.0 5.6 %copy-start.3 = (s32[512]{0:T(512)S(1)}, s32[512]{0:T(512)}, u32[]{:S(2)}) copy-start(s32[512]{0:T(512)} %param.11) | copy-start | bytes 6148
  2.0 5.6 %copy-start.4 = (s32[4]{0:T(128)S(1)}, s32[4]{0:T(128)}, u32[]{:S(2)}) copy-start(s32[4]{0:T(128)} %levels.1) | copy-start | bytes 52
  2.1 5.6 %copy-start.5 = (s32[3]{0:T(128)S(1)}, s32[3]{0:T(128)}, u32[]{:S(2)}) copy-start(s32[3]{0:T(128)} %level_sweeps.1) | copy-start | bytes 40
  2.2 6.9 %collective-permute-start.4 = (f32[32,128]{1,0:T(8,128)S(1)}, f32[32,128]{1,0:T(8,128)S(1)}, u32[]{:S(2)}, u32[]{:S(2)}) collective-permute-start(f32[32,128]{1,0:T(8,128)S(1)} %get-tuple-element.104), channel_id=1, source_target_pairs={{0,1},{1,0},{2,3},{3,2},{4,5},{5,4},{6,7},{7,6},{8,9},{9,8},{10,11... | collective-permute-start | bytes 49160 | tf_op jit(solution)/shard_map/ppermute | solution.py:577
  2.3 6.8 %collective-permute-start.5 = (f32[32,128]{1,0:T(8,128)S(1)}, f32[32,128]{1,0:T(8,128)S(1)}, u32[]{:S(2)}, u32[]{:S(2)}) collective-permute-start(f32[32,128]{1,0:T(8,128)S(1)} %get-tuple-element.105), channel_id=1, source_target_pairs={{0,32},{1,2},{2,1},{3,4},{4,3},{5,6},{6,5},{7,8},{8,7},{9,10},{10,... | collective-permute-start | bytes 49160 | tf_op jit(solution)/shard_map/ppermute | solution.py:589
  5.7 3.7 %collective-permute-start.6 = (f32[32,128]{1,0:T(8,128)S(1)}, f32[32,128]{1,0:T(8,128)S(1)}, u32[]{:S(2)}, u32[]{:S(2)}) collective-permute-start(f32[32,128]{1,0:T(8,128)S(1)} %get-tuple-element.106), channel_id=1, source_target_pairs={{0,32},{32,0},{64,96},{96,64},{1,33},{33,1},{65,97},{97,65},{2,34}... | collective-permute-start | bytes 49160 | tf_op jit(solution)/shard_map/ppermute | solution.py:601
  7.6 1.8 %collective-permute-start.7 = (f32[32,128]{1,0:T(8,128)S(1)}, f32[32,128]{1,0:T(8,128)S(1)}, u32[]{:S(2)}, u32[]{:S(2)}) collective-permute-start(f32[32,128]{1,0:T(8,128)S(1)} %get-tuple-element.107), channel_id=1, source_target_pairs={{0,1},{1,0},{2,3},{3,2},{4,5},{5,4},{6,7},{7,6},{8,9},{9,8},{10,11... | collective-permute-start | bytes 49160 | tf_op jit(solution)/shard_map/ppermute | solution.py:602
  11.0 4.8 %collective-permute-start.8 = (f32[32,128]{1,0:T(8,128)S(1)}, f32[32,128]{1,0:T(8,128)S(1)}, u32[]{:S(2)}, u32[]{:S(2)}) collective-permute-start(f32[32,128]{1,0:T(8,128)S(1)} %get-tuple-element.113), channel_id=1, source_target_pairs={{0,1},{1,0},{2,3},{3,2},{4,5},{5,4},{6,7},{7,6},{8,9},{9,8},{10,11... | collective-permute-start | bytes 49160 | tf_op jit(solution)/shard_map/ppermute | solution.py:577
  11.4 5.0 %collective-permute-start.9 = (f32[32,128]{1,0:T(8,128)S(1)}, f32[32,128]{1,0:T(8,128)S(1)}, u32[]{:S(2)}, u32[]{:S(2)}) collective-permute-start(f32[32,128]{1,0:T(8,128)S(1)} %get-tuple-element.114), channel_id=1, source_target_pairs={{0,32},{32,0},{64,96},{96,64},{1,33},{33,1},{65,97},{97,65},{2,34}... | collective-permute-start | bytes 49160 | tf_op jit(solution)/shard_map/ppermute | solution.py:601
  14.6 1.7 %collective-permute-start.10 = (f32[32,128]{1,0:T(8,128)S(1)}, f32[32,128]{1,0:T(8,128)S(1)}, u32[]{:S(2)}, u32[]{:S(2)}) collective-permute-start(f32[32,128]{1,0:T(8,128)S(1)} %get-tuple-element.115), channel_id=1, source_target_pairs={{0,1},{1,0},{2,3},{3,2},{4,5},{5,4},{6,7},{7,6},{8,9},{9,8},{10,11... | collective-permute-start | bytes 49160 | tf_op jit(solution)/shard_map/ppermute | solution.py:602
  16.6 6.1 %collective-permute-start.11 = (f32[160,128]{1,0:T(8,128)S(1)}, f32[160,128]{1,0:T(8,128)S(1)}, u32[]{:S(2)}, u32[]{:S(2)}) collective-permute-start(f32[160,128]{1,0:T(8,128)S(1)} %get-tuple-element.119), channel_id=1, source_target_pairs={{0,32},{1,2},{2,1},{3,4},{4,3},{5,6},{6,5},{7,8},{8,7},{9,10},{10,... | collective-permute-start | bytes 245768 | tf_op jit(solution)/shard_map/ppermute | solution.py:589
  16.9 1.3 %collective-permute-start.12 = (f32[128,128]{1,0:T(8,128)S(1)}, f32[128,128]{1,0:T(8,128)S(1)}, u32[]{:S(2)}, u32[]{:S(2)}) collective-permute-start(f32[128,128]{1,0:T(8,128)S(1)} %get-tuple-element.120.ma), channel_id=1, source_target_pairs={{0,1},{1,0},{2,3},{3,2},{4,5},{5,4},{6,7},{7,6},{8,9},{9,8},{10,11... | collective-permute-start | bytes 196616 | tf_op jit(solution)/shard_map/ppermute | solution.py:577
  23.9 2.8 %collective-permute-start.13 = (f32[8,128]{1,0:T(8,128)S(1)}, f32[8,128]{1,0:T(8,128)S(1)}, u32[]{:S(2)}, u32[]{:S(2)}) collective-permute-start(f32[8,128]{1,0:T(8,128)S(1)} %get-tuple-element.126), channel_id=1, source_target_pairs={{0,1},{1,0},{2,3},{3,2},{4,5},{5,4},{6,7},{7,6},{8,9},{9,8},{10,11... | collective-permute-start | bytes 12296 | tf_op jit(solution)/shard_map/ppermute | solution.py:577
  24.0 3.8 %collective-permute-start.14 = (f32[8,128]{1,0:T(8,128)S(1)}, f32[8,128]{1,0:T(8,128)S(1)}, u32[]{:S(2)}, u32[]{:S(2)}) collective-permute-start(f32[8,128]{1,0:T(8,128)S(1)} %get-tuple-element.127), channel_id=1, source_target_pairs={{0,32},{32,0},{64,96},{96,64},{1,33},{33,1},{65,97},{97,65},{2,34}... | collective-permute-start | bytes 12296 | tf_op jit(solution)/shard_map/ppermute | solution.py:601
  26.2 1.6 %collective-permute-start.15 = (f32[8,128]{1,0:T(8,128)S(1)}, f32[8,128]{1,0:T(8,128)S(1)}, u32[]{:S(2)}, u32[]{:S(2)}) collective-permute-start(f32[8,128]{1,0:T(8,128)S(1)} %get-tuple-element.128), channel_id=1, source_target_pairs={{0,1},{1,0},{2,3},{3,2},{4,5},{5,4},{6,7},{7,6},{8,9},{9,8},{10,11... | collective-permute-start | bytes 12296 | tf_op jit(solution)/shard_map/ppermute | solution.py:602
  29.4 3.2 %collective-permute-start.16 = (f32[32,128]{1,0:T(8,128)S(1)}, f32[32,128]{1,0:T(8,128)S(1)}, u32[]{:S(2)}, u32[]{:S(2)}) collective-permute-start(f32[32,128]{1,0:T(8,128)S(1)} %get-tuple-element.130), channel_id=1, source_target_pairs={{0,1},{1,0},{2,3},{3,2},{4,5},{5,4},{6,7},{7,6},{8,9},{9,8},{10,11... | collective-permute-start | bytes 49160 | tf_op jit(solution)/shard_map/ppermute | solution.py:577
  29.5 5.4 %collective-permute-start.17 = (f32[32,128]{1,0:T(8,128)S(1)}, f32[32,128]{1,0:T(8,128)S(1)}, u32[]{:S(2)}, u32[]{:S(2)}) collective-permute-start(f32[32,128]{1,0:T(8,128)S(1)} %get-tuple-element.131), channel_id=1, source_target_pairs={{0,32},{1,2},{2,1},{3,4},{4,3},{5,6},{6,5},{7,8},{8,7},{9,10},{10,... | collective-permute-start | bytes 49160 | tf_op jit(solution)/shard_map/ppermute | solution.py:589
  30.2 4.6 %collective-permute-start.18 = (f32[32,128]{1,0:T(8,128)S(1)}, f32[32,128]{1,0:T(8,128)S(1)}, u32[]{:S(2)}, u32[]{:S(2)}) collective-permute-start(f32[32,128]{1,0:T(8,128)S(1)} %get-tuple-element.132), channel_id=1, source_target_pairs={{0,32},{32,0},{64,96},{96,64},{1,33},{33,1},{65,97},{97,65},{2,34}... | collective-permute-start | bytes 49160 | tf_op jit(solution)/shard_map/ppermute | solution.py:601
  32.3 2.6 %collective-permute-start.19 = (f32[32,128]{1,0:T(8,128)S(1)}, f32[32,128]{1,0:T(8,128)S(1)}, u32[]{:S(2)}, u32[]{:S(2)}) collective-permute-start(f32[32,128]{1,0:T(8,128)S(1)} %get-tuple-element.133), channel_id=1, source_target_pairs={{0,1},{1,0},{2,3},{3,2},{4,5},{5,4},{6,7},{7,6},{8,9},{9,8},{10,11... | collective-permute-start | bytes 49160 | tf_op jit(solution)/shard_map/ppermute | solution.py:602
  36.5 3.0 %collective-permute-start.20 = (f32[32,128]{1,0:T(8,128)S(1)}, f32[32,128]{1,0:T(8,128)S(1)}, u32[]{:S(2)}, u32[]{:S(2)}) collective-permute-start(f32[32,128]{1,0:T(8,128)S(1)} %get-tuple-element.135), channel_id=1, source_target_pairs={{0,1},{1,0},{2,3},{3,2},{4,5},{5,4},{6,7},{7,6},{8,9},{9,8},{10,11... | collective-permute-start | bytes 49160 | tf_op jit(solution)/shard_map/ppermute | solution.py:577
  36.5 3.9 %collective-permute-start.21 = (f32[32,128]{1,0:T(8,128)S(1)}, f32[32,128]{1,0:T(8,128)S(1)}, u32[]{:S(2)}, u32[]{:S(2)}) collective-permute-start(f32[32,128]{1,0:T(8,128)S(1)} %get-tuple-element.136), channel_id=1, source_target_pairs={{0,32},{32,0},{64,96},{96,64},{1,33},{33,1},{65,97},{97,65},{2,34}... | collective-permute-start | bytes 49160 | tf_op jit(solution)/shard_map/ppermute | solution.py:601
  38.7 1.7 %collective-permute-start.22 = (f32[32,128]{1,0:T(8,128)S(1)}, f32[32,128]{1,0:T(8,128)S(1)}, u32[]{:S(2)}, u32[]{:S(2)}) collective-permute-start(f32[32,128]{1,0:T(8,128)S(1)} %get-tuple-element.137), channel_id=1, source_target_pairs={{0,1},{1,0},{2,3},{3,2},{4,5},{5,4},{6,7},{7,6},{8,9},{9,8},{10,11... | collective-permute-start | bytes 49160 | tf_op jit(solution)/shard_map/ppermute | solution.py:602
  40.7 5.7 %collective-permute-start.23 = (f32[96,128]{1,0:T(8,128)S(1)}, f32[96,128]{1,0:T(8,128)S(1)}, u32[]{:S(2)}, u32[]{:S(2)}) collective-permute-start(f32[96,128]{1,0:T(8,128)S(1)} %get-tuple-element.139), channel_id=1, source_target_pairs={{0,32},{1,2},{2,1},{3,4},{4,3},{5,6},{6,5},{7,8},{8,7},{9,10},{10,... | collective-permute-start | bytes 147464 | tf_op jit(solution)/shard_map/ppermute | solution.py:589
  41.7 1.2 %collective-permute-start.24 = (f32[64,128]{1,0:T(8,128)S(1)}, f32[64,128]{1,0:T(8,128)S(1)}, u32[]{:S(2)}, u32[]{:S(2)}) collective-permute-start(f32[64,128]{1,0:T(8,128)S(1)} %get-tuple-element.140.ma), channel_id=1, source_target_pairs={{0,1},{1,0},{2,3},{3,2},{4,5},{5,4},{6,7},{7,6},{8,9},{9,8},{10,11... | collective-permute-start | bytes 98312 | tf_op jit(solution)/shard_map/ppermute | solution.py:577
  47.3 2.8 %collective-permute-start.25 = (f32[8,128]{1,0:T(8,128)S(1)}, f32[8,128]{1,0:T(8,128)S(1)}, u32[]{:S(2)}, u32[]{:S(2)}) collective-permute-start(f32[8,128]{1,0:T(8,128)S(1)} %get-tuple-element.146), channel_id=1, source_target_pairs={{0,1},{1,0},{2,3},{3,2},{4,5},{5,4},{6,7},{7,6},{8,9},{9,8},{10,11... | collective-permute-start | bytes 12296 | tf_op jit(solution)/shard_map/ppermute | solution.py:577
  47.4 3.8 %collective-permute-start.26 = (f32[8,128]{1,0:T(8,128)S(1)}, f32[8,128]{1,0:T(8,128)S(1)}, u32[]{:S(2)}, u32[]{:S(2)}) collective-permute-start(f32[8,128]{1,0:T(8,128)S(1)} %get-tuple-element.147), channel_id=1, source_target_pairs={{0,32},{32,0},{64,96},{96,64},{1,33},{33,1},{65,97},{97,65},{2,34}... | collective-permute-start | bytes 12296 | tf_op jit(solution)/shard_map/ppermute | solution.py:601
  49.6 1.6 %collective-permute-start.27 = (f32[8,128]{1,0:T(8,128)S(1)}, f32[8,128]{1,0:T(8,128)S(1)}, u32[]{:S(2)}, u32[]{:S(2)}) collective-permute-start(f32[8,128]{1,0:T(8,128)S(1)} %get-tuple-element.148), channel_id=1, source_target_pairs={{0,1},{1,0},{2,3},{3,2},{4,5},{5,4},{6,7},{7,6},{8,9},{9,8},{10,11... | collective-permute-start | bytes 12296 | tf_op jit(solution)/shard_map/ppermute | solution.py:602
  53.0 5.9 %collective-permute-start.28 = (f32[32,128]{1,0:T(8,128)S(1)}, f32[32,128]{1,0:T(8,128)S(1)}, u32[]{:S(2)}, u32[]{:S(2)}) collective-permute-start(f32[32,128]{1,0:T(8,128)S(1)} %get-tuple-element.150), channel_id=1, source_target_pairs={{0,1},{1,0},{2,3},{3,2},{4,5},{5,4},{6,7},{7,6},{8,9},{9,8},{10,11... | collective-permute-start | bytes 49160 | tf_op jit(solution)/shard_map/ppermute | solution.py:577
  53.1 5.8 %collective-permute-start.29 = (f32[32,128]{1,0:T(8,128)S(1)}, f32[32,128]{1,0:T(8,128)S(1)}, u32[]{:S(2)}, u32[]{:S(2)}) collective-permute-start(f32[32,128]{1,0:T(8,128)S(1)} %get-tuple-element.151), channel_id=1, source_target_pairs={{0,32},{1,2},{2,1},{3,4},{4,3},{5,6},{6,5},{7,8},{8,7},{9,10},{10,... | collective-permute-start | bytes 49160 | tf_op jit(solution)/shard_map/ppermute | solution.py:589
  54.4 4.5 %collective-permute-start.30 = (f32[32,128]{1,0:T(8,128)S(1)}, f32[32,128]{1,0:T(8,128)S(1)}, u32[]{:S(2)}, u32[]{:S(2)}) collective-permute-start(f32[32,128]{1,0:T(8,128)S(1)} %get-tuple-element.152), channel_id=1, source_target_pairs={{0,32},{32,0},{64,96},{96,64},{1,33},{33,1},{65,97},{97,65},{2,34}... | collective-permute-start | bytes 49160 | tf_op jit(solution)/shard_map/ppermute | solution.py:601
  56.4 2.5 %collective-permute-start.31 = (f32[32,128]{1,0:T(8,128)S(1)}, f32[32,128]{1,0:T(8,128)S(1)}, u32[]{:S(2)}, u32[]{:S(2)}) collective-permute-start(f32[32,128]{1,0:T(8,128)S(1)} %get-tuple-element.153), channel_id=1, source_target_pairs={{0,1},{1,0},{2,3},{3,2},{4,5},{5,4},{6,7},{7,6},{8,9},{9,8},{10,11... | collective-permute-start | bytes 49160 | tf_op jit(solution)/shard_map/ppermute | solution.py:602
  60.1 3.0 %collective-permute-start.2 = (f32[512,128]{1,0:T(8,128)S(1)}, f32[512,128]{1,0:T(8,128)S(1)}, u32[]{:S(2)}, u32[]{:S(2)}) collective-permute-start(f32[512,128]{1,0:T(8,128)S(1)} %get-tuple-element.26), channel_id=1, source_target_pairs={{0,1},{1,0},{2,3},{3,2},{4,5},{5,4},{6,7},{7,6},{8,9},{9,8},{10,11... | collective-permute-start | bytes 786440 | tf_op jit(solution)/shard_map/cond/branch_1_fun/ppermute | solution.py:609
  60.7 7.9 %collective-permute-start.3 = (f32[512,128]{1,0:T(8,128)S(1)}, f32[512,128]{1,0:T(8,128)S(1)}, u32[]{:S(2)}, u32[]{:S(2)}) collective-permute-start(f32[512,128]{1,0:T(8,128)S(1)} %get-tuple-element.27), channel_id=1, source_target_pairs={{0,127},{1,2},{2,1},{3,4},{4,3},{5,6},{6,5},{7,8},{8,7},{9,10},{10... | collective-permute-start | bytes 786440 | tf_op jit(solution)/shard_map/cond/branch_1_fun/ppermute | solution.py:609
